TPU v7x, 32 devices: a whole 2x2x4 slice. The times are simulated.
32 devices in a mesh: section: 2 (over core), dp: 16 (over z, y, x).
Axes of the slice: x: 2, y: 2, z: 4, core: 2. Of those that a mesh axis runs over, the one named last changes fastest.
Arguments:
- ends_in: bfloat16 [2, 8192, 768], P('section', 'dp'), may hold values from -6 to 6
- lengths: int32 [32, 4], P('dp'), may hold values from 0 to 256, as said below
- qkv_weight: bfloat16 [2, 768, 2304], P('section', 'dp'), may hold values from -0.21875 to 0.21875
- qkv_bias: bfloat16 [2, 2304], P('section', 'dp'), may hold values from -1.796875 to 1.796875
- out_weight: bfloat16 [2, 768, 768], P('section', 'dp'), may hold values from -1.75 to 1.75
- up_weight: bfloat16 [2, 768, 3072], P('section', 'dp'), may hold values from -0.21875 to 0.21875
- up_bias: bfloat16 [2, 3072], P('section', 'dp'), may hold values from -1.796875 to 1.796875
- down_weight: bfloat16 [2, 3072, 768], P('section', 'dp'), may hold values from -0.109375 to 0.109375
- out_biases: bfloat16 [2, 2, 768], P('section', None, 'dp'), may hold values from -1.796875 to 1.796875
- norm_gains: bfloat16 [2, 2, 768], P('section', None, 'dp'), may hold values from 0.25 to 1.75
- norm_biases: bfloat16 [2, 2, 768], P('section', None, 'dp'), may hold values from -1.796875 to 1.796875
Outputs:
- ends_out: float32 [2, 8192, 768], P('section', 'dp')
- qkv_weight_grad: float32 [2, 768, 2304], P('section', 'dp')
- qkv_bias_grad: float32 [2, 2304], P('section', 'dp')
- out_weight_grad: float32 [2, 768, 768], P('section', 'dp')
- up_weight_grad: float32 [2, 768, 3072], P('section', 'dp')
- up_bias_grad: float32 [2, 3072], P('section', 'dp')
- down_weight_grad: float32 [2, 3072, 768], P('section', 'dp')
- out_biases_grad: float32 [2, 2, 768], P('section', None, 'dp')
- norm_gains_grad: float32 [2, 2, 768], P('section', None, 'dp')
- norm_biases_grad: float32 [2, 2, 768], P('section', None, 'dp')
Inputs may be any that keep to these rules, and one draw needn't show every extreme that they name: `lengths`: row r describes micro-batch r % 2 of data device r // 2: its sequences fill the block's slots in order from slot 0; each row sums to 256 or less, and some row holds a single sequence of 256 tokens.
All inputs are finite; a program needn't handle non-finite values.
Results may differ from a plain program's by a relative error of at most 0.01.
Values may be sent and summed in bfloat16 or wider, within the bound.
No kernel may reach another device: no remote copies, remote signals or barrier semaphores. Data moves between devices by JAX's collectives and lax.ppermute only.
A program may use at most 320 MiB of HBM per device.

v0:
```python
from functools import partial
import math

import jax
import jax.numpy as jnp
from jax import lax
from jax.sharding import PartitionSpec as P

HD = 64
ROT = 16


eps = 1e-05
masked_score = -1e30


def from_behind(value, axis, steps):
    count = lax.axis_size(axis)
    initial, last = (max(0, -steps), min(count, count - steps))
    return lax.ppermute(value, axis, [(source, source + steps) for source in range(initial, last)])


def product_plain(left, right):
    return jnp.dot(left, right, preferred_element_type=jnp.float32)


def product_transposed(left, right):
    return lax.dot_general(
        left, right, (((1,), (1,)), ((), ())), preferred_element_type=jnp.float32
    )


def product_leftwise(left, right):
    return lax.dot_general(
        left, right, (((0,), (0,)), ((), ())), preferred_element_type=jnp.float32
    )


def layouts(lengths, slot_count):
    ends_at = jnp.cumsum(lengths, axis=1)
    indices = jnp.arange(slot_count, dtype=jnp.int32)
    passed = indices[None, :, None] >= ends_at[:, None, :]
    segments = jnp.sum(passed.astype(jnp.int32), axis=2)
    starts = jnp.sum(jnp.where(passed, lengths[:, None, :], 0), axis=2)
    return (segments, indices[None, :] - starts)


def rotary_tables(positions):
    freqs = 10000.0 ** (-2.0 * jnp.arange(ROT // 2, dtype=jnp.float32) / ROT)
    angles = positions.astype(jnp.float32)[:, None] * freqs[None, :]
    angles = jnp.concatenate([angles, angles], axis=1)
    return (jnp.cos(angles)[:, None, :], jnp.sin(angles)[:, None, :])


def rotate(values, cosine, sine_table):
    head_part = values[..., :ROT]
    half = ROT // 2
    turned = jnp.concatenate([-head_part[..., half:], head_part[..., :half]], axis=-1)
    return jnp.concatenate([head_part * cosine + turned * sine_table, values[..., ROT:]], axis=-1)


def unrotate(grads, cosine, sine_table):
    head_part = grads[..., :ROT]
    half = ROT // 2
    turned = head_part * sine_table
    back_part = jnp.concatenate([turned[..., half:], -turned[..., :half]], axis=-1)
    return jnp.concatenate([head_part * cosine + back_part, grads[..., ROT:]], axis=-1)


def normalize(residual, gains, shifts):
    centre = jnp.mean(residual, axis=-1, keepdims=True)
    centred = residual - centre
    spread = jnp.mean(centred * centred, axis=-1, keepdims=True)
    unit_rows = centred * lax.rsqrt(spread + eps)
    return (unit_rows * gains[0] + shifts[0], unit_rows * gains[1] + shifts[1])


def allowed_mask(segment):
    indices = jnp.arange(segment.shape[0], dtype=jnp.int32)
    return (segment[:, None] == segment[None, :]) & (indices[None, :] <= indices[:, None])


def score_block(query_rows, keys_r, allowed_rows):
    scores = jnp.einsum("qhd,khd->hqk", query_rows, keys_r, preferred_element_type=jnp.float32) * (
        1.0 / math.sqrt(HD)
    )
    return jnp.where(allowed_rows[None], scores, masked_score)


def layer_forward(entry, segment, positions, weights):
    weight_qkv, bias_qkv, weight_out, weight_up, bias_up, weight_down, bias_out, gains, shifts = (
        weights
    )
    residual = entry.astype(jnp.float32)
    normed_attn, normed_mlp = normalize(
        residual, gains.astype(jnp.float32), shifts.astype(jnp.float32)
    )
    length = residual.shape[0]
    features = residual.shape[1]
    head_count = features // HD
    projected = (
        product_plain(normed_attn.astype(jnp.bfloat16), weight_qkv) + bias_qkv.astype(jnp.float32)
    ).reshape(length, 3, head_count, HD)
    cosine, sine_table = rotary_tables(positions)
    queries = rotate(projected[:, 0], cosine, sine_table).astype(jnp.bfloat16)
    keys_r = rotate(projected[:, 1], cosine, sine_table).astype(jnp.bfloat16)
    values_r = projected[:, 2].astype(jnp.bfloat16)
    allowed = allowed_mask(segment)
    scores = score_block(queries, keys_r, allowed)
    row_peak = jnp.max(scores, axis=-1, keepdims=True)
    raised = jnp.exp(scores - row_peak)
    row_total = jnp.sum(raised, axis=-1, keepdims=True)
    probabilities = (raised / row_total).astype(jnp.bfloat16)
    pieces = [
        jnp.einsum("hqk,khd->qhd", probabilities, values_r, preferred_element_type=jnp.float32)
    ]
    log_parts = [(row_peak + jnp.log(row_total))[..., 0]]
    attended = jnp.concatenate(pieces, axis=0).reshape(length, features).astype(jnp.bfloat16)
    log_totals = jnp.concatenate(log_parts, axis=1)
    attn_out = product_plain(attended, weight_out) + bias_out[0].astype(jnp.float32)
    hidden = product_plain(normed_mlp.astype(jnp.bfloat16), weight_up) + bias_up.astype(jnp.float32)
    activated = jax.nn.gelu(hidden, approximate=False).astype(jnp.bfloat16)
    mlp_out = product_plain(activated, weight_down) + bias_out[1].astype(jnp.float32)
    produced = residual + attn_out + mlp_out
    return (produced, (queries, keys_r, values_r, log_totals, attended, hidden, activated))


def mlp_part(grad_in, normed_mlp_r, saved, weights):
    weight_qkv, bias_qkv, weight_out, weight_up, bias_up, weight_down, bias_out, gains, shifts = (
        weights
    )
    queries, keys_r, values_r, log_totals, attended, hidden, activated = saved
    grad_rows = grad_in.astype(jnp.float32)
    column_sum = jnp.sum(grad_rows, axis=0)
    grad_bias_out = jnp.stack([column_sum, column_sum])
    grad_weight_down = product_leftwise(activated, grad_in)
    grad_activated = product_transposed(grad_in, weight_down)
    gelu_value, gelu_back = jax.vjp(partial(jax.nn.gelu, approximate=False), hidden)
    grad_hidden = gelu_back(grad_activated)[0].astype(jnp.bfloat16)
    grad_weight_up = product_leftwise(normed_mlp_r, grad_hidden)
    grad_bias_up = jnp.sum(grad_hidden.astype(jnp.float32), axis=0)
    grad_normed_mlp = product_transposed(grad_hidden, weight_up)
    grad_weight_out = product_leftwise(attended, grad_in)
    return (
        grad_normed_mlp,
        (grad_weight_out, grad_weight_up, grad_bias_up, grad_weight_down, grad_bias_out),
    )


def attn_part(grad_in, normed_attn_r, segment, positions, saved, weights):
    weight_qkv, bias_qkv, weight_out, weight_up, bias_up, weight_down, bias_out, gains, shifts = (
        weights
    )
    queries, keys_r, values_r, log_totals, attended, hidden, activated = saved
    length = grad_in.shape[0]
    features = grad_in.shape[1]
    head_count = features // HD
    scale_factor = 1.0 / math.sqrt(HD)
    grad_attended = (
        product_transposed(grad_in, weight_out).astype(jnp.bfloat16).reshape(length, head_count, HD)
    )
    allowed = allowed_mask(segment)
    cosine, sine_table = rotary_tables(positions)
    scores = score_block(queries, keys_r, allowed)
    probabilities = jnp.exp(scores - log_totals[..., None])
    grad_values = jnp.einsum(
        "hqk,qhd->khd",
        probabilities.astype(jnp.bfloat16),
        grad_attended,
        preferred_element_type=jnp.float32,
    )
    grad_probs = jnp.einsum(
        "qhd,khd->hqk", grad_attended, values_r, preferred_element_type=jnp.float32
    )
    inner_sum = jnp.sum(grad_probs * probabilities, axis=-1, keepdims=True)
    grad_scores = (probabilities * (grad_probs - inner_sum)).astype(jnp.bfloat16)
    query_parts = [
        jnp.einsum("hqk,khd->qhd", grad_scores, keys_r, preferred_element_type=jnp.float32)
        * scale_factor
    ]
    grad_keys = (
        jnp.einsum("hqk,qhd->khd", grad_scores, queries, preferred_element_type=jnp.float32)
        * scale_factor
    )
    grad_queries = unrotate(jnp.concatenate(query_parts, axis=0), cosine, sine_table)
    grad_keys = unrotate(grad_keys, cosine, sine_table)
    grad_projected = (
        jnp.stack([grad_queries, grad_keys, grad_values], axis=1)
        .reshape(length, 3 * features)
        .astype(jnp.bfloat16)
    )
    grad_weight_qkv = product_leftwise(normed_attn_r, grad_projected)
    grad_bias_qkv = jnp.sum(grad_projected.astype(jnp.float32), axis=0)
    grad_normed_attn = product_transposed(grad_projected, weight_qkv)
    return (grad_normed_attn, (grad_weight_qkv, grad_bias_qkv))


def layer_backward(grad_in, entry, segment, positions, saved, weights):
    gains = weights[7]
    shifts = weights[8]
    residual = entry.astype(jnp.float32)
    (normed_attn, normed_mlp), norm_back = jax.vjp(
        normalize, residual, gains.astype(jnp.float32), shifts.astype(jnp.float32)
    )
    grad_normed_mlp, mlp_grads = mlp_part(grad_in, normed_mlp.astype(jnp.bfloat16), saved, weights)
    grad_normed_attn, attn_grads = attn_part(
        grad_in, normed_attn.astype(jnp.bfloat16), segment, positions, saved, weights
    )
    grad_residual, grad_gains, grad_shifts = norm_back((grad_normed_attn, grad_normed_mlp))
    grads_layer = (
        attn_grads[0],
        attn_grads[1],
        mlp_grads[0],
        mlp_grads[1],
        mlp_grads[2],
        mlp_grads[3],
        mlp_grads[4],
        grad_gains,
        grad_shifts,
    )
    return (grad_in.astype(jnp.float32) + grad_residual, grads_layer)


def forward_zeros(length, features, hidden_width):
    head_count = features // HD
    kept = (
        jnp.zeros((length, head_count, HD), jnp.bfloat16),
        jnp.zeros((length, head_count, HD), jnp.bfloat16),
        jnp.zeros((length, head_count, HD), jnp.bfloat16),
        jnp.zeros((head_count, length), jnp.float32),
        jnp.zeros((length, features), jnp.bfloat16),
        jnp.zeros((length, hidden_width), jnp.float32),
        jnp.zeros((length, hidden_width), jnp.bfloat16),
    )
    return (jnp.zeros((length, features), jnp.float32), kept)


def backward_zeros(length, features, weights):
    return (
        jnp.zeros((length, features), jnp.float32),
        tuple((jnp.zeros(stacked.shape, jnp.float32) for stacked in weights)),
    )


def skip_forward(length, features, hidden_width, *operands):
    return forward_zeros(length, features, hidden_width)


def skip_backward(length, features, *operands):
    return backward_zeros(length, features, operands[-1])


def take(stacked, picked):
    return lax.dynamic_index_in_dim(stacked, picked, 0, keepdims=False)


def store(stacked, value, picked, active):
    current = take(stacked, picked)
    return lax.dynamic_update_index_in_dim(stacked, jnp.where(active, value, current), picked, 0)


def on_device(
    ends_in,
    lengths,
    qkv_weight,
    qkv_bias,
    out_weight,
    up_weight,
    up_bias,
    down_weight,
    out_biases,
    norm_gains,
    norm_biases,
):
    section_index = lax.axis_index("section")
    is_first = section_index == 0
    micro_count = lengths.shape[0]
    slot_count = ends_in.shape[1] // micro_count
    features = ends_in.shape[2]
    weights = (
        lax.all_gather(qkv_weight[0], "dp", axis=0, tiled=True),
        lax.all_gather(qkv_bias[0], "dp", axis=0, tiled=True),
        lax.all_gather(out_weight[0], "dp", axis=0, tiled=True),
        lax.all_gather(up_weight[0], "dp", axis=0, tiled=True),
        lax.all_gather(up_bias[0], "dp", axis=0, tiled=True),
        lax.all_gather(down_weight[0], "dp", axis=0, tiled=True),
        lax.all_gather(out_biases[0], "dp", axis=1, tiled=True),
        lax.all_gather(norm_gains[0], "dp", axis=1, tiled=True),
        lax.all_gather(norm_biases[0], "dp", axis=1, tiled=True),
    )
    hidden_width = weights[3].shape[1]
    own_rows = ends_in[0].reshape(micro_count, slot_count, features)
    segments, positions = layouts(lengths, slot_count)
    zero_saved = forward_zeros(slot_count, features, hidden_width)[1]
    stash = jax.tree.map(
        lambda shaped: jnp.zeros((micro_count,) + shaped.shape, shaped.dtype), zero_saved
    )
    kept_inputs = jnp.zeros((micro_count, slot_count, features), jnp.bfloat16)
    results = jnp.zeros((micro_count, slot_count, features), jnp.float32)
    arrived = jnp.zeros((slot_count, features), jnp.bfloat16)
    for moment in range(micro_count + 1):
        index_now = moment - section_index
        active = (index_now >= 0) & (index_now < micro_count)
        picked = jnp.clip(index_now, 0, micro_count - 1)
        entry = jnp.where(is_first, take(own_rows, picked), arrived)
        segment_now = take(segments, picked)
        position_now = take(positions, picked)
        produced, saved = lax.cond(
            active,
            layer_forward,
            partial(skip_forward, slot_count, features, hidden_width),
            entry,
            segment_now,
            position_now,
            weights,
        )
        kept_inputs = store(kept_inputs, entry, picked, active)
        stash = jax.tree.map(
            lambda stacked, value: store(stacked, value, picked, active), stash, saved
        )
        results = store(results, produced, picked, active & jnp.logical_not(is_first))
        arrived = from_behind(produced.astype(jnp.bfloat16), "section", 1)
    totals = backward_zeros(slot_count, features, weights)[1]
    incoming = jnp.zeros((slot_count, features), jnp.bfloat16)
    for moment in range(micro_count + 1):
        index_now = moment - (1 - section_index)
        active = (index_now >= 0) & (index_now < micro_count)
        picked = jnp.clip(index_now, 0, micro_count - 1)
        grad_entry = jnp.where(is_first, incoming, take(own_rows, picked))
        saved = jax.tree.map(lambda stacked: take(stacked, picked), stash)
        entry_rows = take(kept_inputs, picked)
        segment_now = take(segments, picked)
        position_now = take(positions, picked)
        sent, layer_grads = lax.cond(
            active,
            layer_backward,
            partial(skip_backward, slot_count, features),
            grad_entry,
            entry_rows,
            segment_now,
            position_now,
            saved,
            weights,
        )
        totals = jax.tree.map(jnp.add, totals, layer_grads)
        results = store(results, sent, picked, active & is_first)
        incoming = from_behind(sent.astype(jnp.bfloat16), "section", -1)
    summed = (
        lax.psum_scatter(totals[0], "dp", scatter_dimension=0, tiled=True),
        lax.psum_scatter(totals[1], "dp", scatter_dimension=0, tiled=True),
        lax.psum_scatter(totals[2], "dp", scatter_dimension=0, tiled=True),
        lax.psum_scatter(totals[3], "dp", scatter_dimension=0, tiled=True),
        lax.psum_scatter(totals[4], "dp", scatter_dimension=0, tiled=True),
        lax.psum_scatter(totals[5], "dp", scatter_dimension=0, tiled=True),
        lax.psum_scatter(totals[6], "dp", scatter_dimension=1, tiled=True),
        lax.psum_scatter(totals[7], "dp", scatter_dimension=1, tiled=True),
        lax.psum_scatter(totals[8], "dp", scatter_dimension=1, tiled=True),
    )
    ends_out = results.reshape(1, micro_count * slot_count, features)
    return (
        ends_out,
        summed[0][None],
        summed[1][None],
        summed[2][None],
        summed[3][None],
        summed[4][None],
        summed[5][None],
        summed[6][None],
        summed[7][None],
        summed[8][None],
    )


def solution(mesh):
    return jax.shard_map(
        on_device,
        mesh=mesh,
        in_specs=(
            P("section", "dp", None),
            P("dp", None),
            P("section", "dp", None),
            P("section", "dp"),
            P("section", "dp", None),
            P("section", "dp", None),
            P("section", "dp"),
            P("section", "dp", None),
            P("section", None, "dp"),
            P("section", None, "dp"),
            P("section", None, "dp"),
        ),
        out_specs=(
            P("section", "dp", None),
            P("section", "dp", None),
            P("section", "dp"),
            P("section", "dp", None),
            P("section", "dp", None),
            P("section", "dp"),
            P("section", "dp", None),
            P("section", None, "dp"),
            P("section", None, "dp"),
            P("section", None, "dp"),
        ),
        check_vma=False,
    )
```

profile of v0, /device:TPU:1, one launch (start us, length us, event | category | flops | bytes accessed | tf_op | source)
XLA Modules:
  0.0 1647.1 jit_solution(7167156043635274506)
XLA Ops:
  10.8 36.7 %all-gather = bf16[1,2,768]{1,0,2:T(2,128)(2,1)S(1)} all-gather(bf16[1,2,48]{1,0,2:T(2,128)(2,1)S(1)} %copy.156), channel_id=2, replica_groups=mesh['section'=2,'dp'=16] {'dp'}, dimensions={2}, use_global_device_ids=true | all-gather | bytes 3264 | tf_op jit(solution)/shard_map/all_gather | solution.py:288
  48.6 31.5 %all-gather.1 = bf16[1,2,768]{1,0,2:T(2,128)(2,1)S(1)} all-gather(bf16[1,2,48]{1,0,2:T(2,128)(2,1)S(1)} %copy.158), channel_id=3, replica_groups=mesh['section'=2,'dp'=16] {'dp'}, dimensions={2}, use_global_device_ids=true | all-gather | bytes 3264 | tf_op jit(solution)/shard_map/all_gather | solution.py:289
  86.0 32.9 %all-gather.5 = bf16[1,2,768]{1,0,2:T(2,128)(2,1)S(1)} all-gather(bf16[1,2,48]{1,0,2:T(2,128)(2,1)S(1)} %copy.160), channel_id=7, replica_groups=mesh['section'=2,'dp'=16] {'dp'}, dimensions={2}, use_global_device_ids=true | all-gather | bytes 3264 | tf_op jit(solution)/shard_map/all_gather | solution.py:287
  119.7 60.3 %all-reduce.17 = (bf16[2304]{0:T(1024)(128)(2,1)S(1)}, bf16[3072]{0:T(1024)(128)(2,1)S(1)}) all-reduce(bf16[2304]{0:T(1024)(128)(2,1)S(1)} %dynamic-update-slice, bf16[3072]{0:T(1024)(128)(2,1)S(1)} %dynamic-update-slice.1), channel_id=5, replica_groups=mesh['section'=2,'dp'=16] {'dp'}, use_global_device_ids=true, to_apply=%add.12 | all-reduce | flops 5376 | bytes 21504 | tf_op jit(solution)/shard_map/all_gather | solution.py:282
  181.1 46.3 %all-gather.18.cloned.1.call-done = bf16[1,768,3072]{2,1,0:T(8,128)(2,1)} async-done(((bf16[1,48,3072]{2,1,0:T(8,128)(2,1)}), bf16[1,768,3072]{2,1,0:T(8,128)(2,1)}) %all-gather.18.cloned.1.call-update) | async-done | bytes 4718608 | tf_op jit(solution)/shard_map/all_gather | solution.py:284
  227.4 82.2 %all-gather.20.cloned.1.call-done = bf16[1,3072,768]{2,1,0:T(8,128)(2,1)} async-done(((bf16[1,192,768]{2,1,0:T(8,128)(2,1)}), bf16[1,3072,768]{2,1,0:T(8,128)(2,1)}) %all-gather.20.cloned.1.call-update) | async-done | bytes 4718608 | tf_op jit(solution)/shard_map/all_gather | solution.py:286
  310.5 6.3 conditional.6
  316.8 8.2 collective-permute-start
  341.1 6.6 collective-permute-done
  349.7 36.1 %conditional.7 = (f32[256,768]{1,0:T(8,128)}, bf16[256,12,64]{0,2,1:T(8,128)(2,1)}, bf16[256,12,64]{0,2,1:T(8,128)(2,1)}, bf16[256,12,64]{0,2,1:T(8,128)(2,1)}, ...) conditional(s32[]{:T(128)} %convert_element_type.572, () %tuple.82, ...), branch_computations={%region_9.10_spmd, %region_10.15_spmd} | conditional | flops 3894179072 | bytes 60955408 | solution.py:308
  350.2 10.9 fusion.47
  415.5 35.5 %conditional.8 = (f32[256,768]{1,0:T(8,128)}, bf16[256,12,64]{0,2,1:T(8,128)(2,1)}, bf16[256,12,64]{0,2,1:T(8,128)(2,1)}, bf16[256,12,64]{0,2,1:T(8,128)(2,1)}, ...) conditional(s32[]{:T(128)} %convert_element_type.574, () %tuple.84, ...), branch_computations={%region_15.16_spmd, %region_16.21_spmd} | conditional | flops 3894179072 | bytes 75119464 | solution.py:308
  416.1 10.8 fusion.92
  467.3 49.7 %conditional.9 = (f32[256,768]{1,0:T(8,128)S(1)}, f32[768,2304]{1,0:T(8,128)}, f32[2304]{0:T(1024)S(1)}, f32[768,768]{1,0:T(8,128)}, f32[768,3072]{1,0:T(8,128)}...) conditional(s32[]{:T(128)} %convert_element_type.576, () %tuple.86, ...), branch_computations={%region_21.22_spmd, %region_22.35_spmd} | conditional | flops 7831047680 | bytes 190930640 | solution.py:334
  484.1 9.6 convert_reduce_fusion.9
  510.1 6.6 fusion.159
  522.4 50.3 %conditional.10 = (f32[256,768]{1,0:T(8,128)S(1)}, f32[768,2304]{1,0:T(8,128)}, f32[2304]{0:T(1024)S(1)}, f32[768,768]{1,0:T(8,128)}, f32[768,3072]{1,0:T(8,128)...) conditional(s32[]{:T(128)} %convert_element_type.577, () %tuple.88, ...), branch_computations={%region_35.36_spmd, %region_36.49_spmd} | conditional | flops 7831047680 | bytes 187776656 | solution.py:334
  539.5 10.0 convert_reduce_fusion.13
  560.7 5.2 fusion.284
  566.0 6.6 fusion.253
  579.1 18.6 %conditional.11 = (f32[256,768]{1,0:T(8,128)}, f32[768,2304]{1,0:T(8,128)}, f32[2304]{0:T(1024)S(1)}, f32[768,768]{1,0:T(8,128)S(1)}, f32[768,3072]{1,0:T(8,128)...) conditional(s32[]{:T(128)} %convert_element_type.579, () %tuple.90, ...), branch_computations={%region_49.50_spmd, %region_50.63_spmd} | conditional | flops 7831047680 | bytes 194031216 | solution.py:334
  607.3 11.3 add_add_fusion.5
  618.6 14.8 add_add_fusion.4
  633.5 14.0 add_add_fusion.3
  653.1 60.2 %all-reduce.16 = (f32[2304]{0:T(1024)S(1)}, f32[3072]{0:T(1024)S(1)}) all-reduce(f32[2304]{0:T(1024)S(1)} %add_add_fusion.8, f32[3072]{0:T(1024)S(1)} %add_add_fusion.7), channel_id=12, replica_groups=mesh['section'=2,'dp'=16] {'dp'}, use_global_device_ids=true, to_apply=%region_64.65.clone | all-reduce | flops 5376 | bytes 43008
  714.7 32.5 %reduce-scatter.22.cloned.1.call-done = f32[48,2]{1,0:T(8,128)} async-done(((f32[768,2]{1,0:T(8,128)}), f32[48,2]{1,0:T(8,128)}) %reduce-scatter.22.cloned.1.call-update) | async-done | bytes 400
  748.6 124.6 %reduce-scatter.24.cloned.1.call-done = f32[48,2]{1,0:T(8,128)} async-done(((f32[768,2]{1,0:T(8,128)}), f32[48,2]{1,0:T(8,128)}) %reduce-scatter.24.cloned.1.call-update) | async-done | bytes 400
  874.5 124.0 %reduce-scatter.26.cloned.1.call-done = f32[48,2]{1,0:T(8,128)} async-done(((f32[768,2]{1,0:T(8,128)}), f32[48,2]{1,0:T(8,128)}) %reduce-scatter.26.cloned.1.call-update) | async-done | bytes 400
  999.9 131.6 %reduce-scatter.16.cloned.1.call-done = f32[48,768]{1,0:T(8,128)} async-done(((f32[768,768]{1,0:T(8,128)}), f32[48,768]{1,0:T(8,128)}) %reduce-scatter.16.cloned.1.call-update) | async-done | bytes 147472 | tf_op jit(solution)/shard_map/reduce_scatter | solution.py:351
  1131.5 155.7 %reduce-scatter.14.cloned.1.call-done = f32[48,2304]{1,0:T(8,128)} async-done(((f32[768,2304]{1,0:T(8,128)}), f32[48,2304]{1,0:T(8,128)}) %reduce-scatter.14.cloned.1.call-update) | async-done | bytes 442384 | tf_op jit(solution)/shard_map/reduce_scatter | solution.py:349
  1287.3 175.9 %reduce-scatter.18.cloned.1.call-done = f32[48,3072]{1,0:T(8,128)} async-done(((f32[768,3072]{1,0:T(8,128)}), f32[48,3072]{1,0:T(8,128)}) %reduce-scatter.18.cloned.1.call-update) | async-done | bytes 589840 | tf_op jit(solution)/shard_map/reduce_scatter | solution.py:352
  1463.2 177.1 %reduce-scatter.20.cloned.1.call-done = f32[192,768]{1,0:T(8,128)} async-done(((f32[3072,768]{1,0:T(8,128)}), f32[192,768]{1,0:T(8,128)}) %reduce-scatter.20.cloned.1.call-update) | async-done | bytes 589840 | tf_op jit(solution)/shard_map/reduce_scatter | solution.py:354
  (563 shorter events, 235.8 us)
Async XLA Ops:
  7.2 172.8 %copy-start.113 = (s32[2,4]{1,0:T(2,128)S(1)}, s32[2,4]{1,0:T(2,128)}, u32[]{:S(2)}) copy-start(s32[2,4]{1,0:T(2,128)} %param.24) | copy-start | bytes 100
  7.2 172.9 %copy-start.24 = (bf16[1,512,768]{2,1,0:T(8,128)(2,1)S(1)}, bf16[1,512,768]{2,1,0:T(8,128)(2,1)}, u32[]{:S(2)}) copy-start(bf16[1,512,768]{2,1,0:T(8,128)(2,1)} %param.23) | copy-start | bytes 2359300
  7.2 173.8 %all-gather.16.cloned.1.call-start = ((), (), s32[]{:S(2)}) async-start(), calls=%async_computation.12 | async-start | bytes 1253376 | tf_op jit(solution)/shard_map/all_gather | solution.py:283
  7.9 173.1 %all-gather.14.cloned.1.call-start = ((), (), s32[]{:S(2)}) async-start(), calls=%async_computation.11 | async-start | bytes 3760128 | tf_op jit(solution)/shard_map/all_gather | solution.py:281
  8.7 218.7 %all-gather.18.cloned.1.call-start = ((), (), s32[]{:S(2)}) async-start(), calls=%async_computation.13 | async-start | bytes 5013504 | tf_op jit(solution)/shard_map/all_gather | solution.py:284
  9.4 300.1 %all-gather.20.cloned.1.call-start = ((), (), s32[]{:S(2)}) async-start(), calls=%async_computation.14 | async-start | bytes 5013504 | tf_op jit(solution)/shard_map/all_gather | solution.py:286
  10.0 737.2 %reduce-scatter.22.cloned.1.call-start = ((), (), s32[]{:S(2)}) async-start(), calls=%async_computation.15 | async-start | bytes 417792
  180.0 129.7 %copy-start.69 = (bf16[2304]{0:T(1024)(128)(2,1)}, bf16[2304]{0:T(1024)(128)(2,1)S(1)}, u32[]{:S(2)}) copy-start(bf16[2304]{0:T(1024)(128)(2,1)S(1)} %get-tuple-element.1211) | copy-start | bytes 13828
  180.0 129.7 %copy-start.72 = (bf16[3072]{0:T(1024)(128)(2,1)}, bf16[3072]{0:T(1024)(128)(2,1)S(1)}, u32[]{:S(2)}) copy-start(bf16[3072]{0:T(1024)(128)(2,1)S(1)} %get-tuple-element.1212) | copy-start | bytes 18436
  180.0 287.3 %copy-start.92 = (s32[2,256]{1,0:T(2,128)}, s32[2,256]{1,0:T(2,128)S(1)}, u32[]{:S(2)}) copy-start(s32[2,256]{1,0:T(2,128)S(1)} %get-tuple-element.1208) | copy-start | bytes 6148
  181.0 128.7 %copy-start.94 = (s32[2,256]{1,0:T(2,128)}, s32[2,256]{1,0:T(2,128)S(1)}, u32[]{:S(2)}) copy-start(s32[2,256]{1,0:T(2,128)S(1)} %iota_subtract_fusion) | copy-start | bytes 6148
  316.8 30.9 %collective-permute-start = (bf16[256,768]{1,0:T(8,128)(2,1)S(1)}, bf16[256,768]{1,0:T(8,128)(2,1)S(1)}, u32[]{:S(2)}, u32[]{:S(2)}) collective-permute-start(bf16[256,768]{1,0:T(8,128)(2,1)S(1)} %convert_element_type.573), channel_id=1, source_target_pairs={{0,16},{1,17},{2,18},{3,19},{4,20},{5,21},{6,22},{7,23},{8,24},{9,... | collective-permute-start | bytes 1179656 | tf_op jit(solution)/shard_map/ppermute | solution.py:20
  330.8 18.8 %slice-start.6 = ((s8[4718592]{0:T(1024)(128)(4,1)}), s8[4194304]{0:T(1024)(128)(4,1)S(1)}, s32[]{:S(2)}) async-start(s8[4718592]{0:T(1024)(128)(4,1)} %bitcast.836), calls=%async_computation.24 | async-start | bytes 8388608
  330.8 18.8 %slice-start.16 = ((s8[4718592]{0:T(1024)(128)(4,1)}), s8[4194304]{0:T(1024)(128)(4,1)S(1)}, s32[]{:S(2)}) async-start(s8[4718592]{0:T(1024)(128)(4,1)} %bitcast.853), calls=%async_computation.34 | async-start | bytes 8388608
  334.0 15.6 slice-start.7
  334.0 15.6 slice-start.17
  337.5 12.2 copy-start.73
  337.5 12.2 copy-start.114
  349.7 15.8 copy-start.32
  387.0 28.3 %collective-permute-start.1 = (bf16[256,768]{1,0:T(8,128)(2,1)S(1)}, bf16[256,768]{1,0:T(8,128)(2,1)S(1)}, u32[]{:S(2)}, u32[]{:S(2)}) collective-permute-start(bf16[256,768]{1,0:T(8,128)(2,1)S(1)} %convert_element_type.575), channel_id=1, source_target_pairs={{0,16},{1,17},{2,18},{3,19},{4,20},{5,21},{6,22},{7,23},{8,24},{9,... | collective-permute-start | bytes 1179656 | tf_op jit(solution)/shard_map/ppermute | solution.py:20
  401.1 14.5 copy-start.11
  401.9 13.5 slice-start.8
  415.6 15.6 copy-start.30
  519.8 2.6 collective-permute-start.2
  575.4 3.6 collective-permute-start.3
  599.4 273.7 %reduce-scatter.24.cloned.1.call-start = ((), (), s32[]{:S(2)}) async-start(), calls=%async_computation.16 | async-start | bytes 417792
  601.1 397.4 %reduce-scatter.26.cloned.1.call-start = ((), (), s32[]{:S(2)}) async-start(), calls=%async_computation.17 | async-start | bytes 417792
  602.9 528.6 %reduce-scatter.16.cloned.1.call-start = ((), (), s32[]{:S(2)}) async-start(), calls=%async_computation.8 | async-start | bytes 2506752 | tf_op jit(solution)/shard_map/reduce_scatter | solution.py:351
  607.2 680.0 %reduce-scatter.14.cloned.1.call-start = ((), (), s32[]{:S(2)}) async-start(), calls=%async_computation.7 | async-start | bytes 7520256 | tf_op jit(solution)/shard_map/reduce_scatter | solution.py:349
  618.5 844.7 %reduce-scatter.18.cloned.1.call-start = ((), (), s32[]{:S(2)}) async-start(), calls=%async_computation.9 | async-start | bytes 10027008 | tf_op jit(solution)/shard_map/reduce_scatter | solution.py:352
  633.4 1006.9 %reduce-scatter.20.cloned.1.call-start = ((), (), s32[]{:S(2)}) async-start(), calls=%async_computation.10 | async-start | bytes 10027008 | tf_op jit(solution)/shard_map/reduce_scatter | solution.py:354
  714.7 925.6 %copy-start.3 = (f32[2,256,768]{2,1,0:T(8,128)}, f32[2,256,768]{2,1,0:T(8,128)S(1)}, u32[]{:S(2)}) copy-start(f32[2,256,768]{2,1,0:T(8,128)S(1)} %bitcast_dynamic-update-slice_fusion.6) | copy-start | bytes 4718596
  (108 other events, 485.8 us)
Sparse Core Ops, SparseCore 0:
  10.8 58.4 all-gather.15
  72.1 72.9 all-gather.13
  147.9 79.4 all-gather.17
  230.0 79.4 all-gather.19
  599.5 147.6 reduce-scatter.21
  752.4 120.6 reduce-scatter.23
  877.8 120.7 reduce-scatter.25
  1004.8 126.6 reduce-scatter.15
  1137.4 149.7 reduce-scatter.13
  1293.4 169.7 reduce-scatter.17
  1470.4 169.8 reduce-scatter.19
where the time goes:
time: 1650 us
  waiting for transfers between devices  1060 us (64%)
  blocking collectives  222 us (13%)
  matrix products  119 us (7%)
  other arithmetic  108 us (7%)
  local copies, waits for them, and re-layouts  97.3 us (6%)
  between operations  17.8 us (1%)
    unnamed x14, waiting for transfers between devices  284 us
    reduce_scatter x1, waiting for transfers between devices, on_device(): lax.psum_scatter(totals[5], 'dp', scatter_dimension=0, tiled=True)  177 us
    reduce_scatter x1, waiting for transfers between devices, on_device(): lax.psum_scatter(totals[3], 'dp', scatter_dimension=0, tiled=True)  176 us
    reduce_scatter x1, waiting for transfers between devices, on_device(): lax.psum_scatter(totals[0], 'dp', scatter_dimension=0, tiled=True)  156 us
    reduce_scatter x1, waiting for transfers between devices, on_device(): lax.psum_scatter(totals[2], 'dp', scatter_dimension=0, tiled=True)  132 us
    all_gather x1, waiting for transfers between devices, on_device(): lax.all_gather(down_weight[0], 'dp', axis=0, tiled=True)  82.2 us
    all_gather x1, blocking collectives, on_device(): lax.all_gather(qkv_bias[0], 'dp', axis=0, tiled=True)  60.3 us
    unnamed x1, blocking collectives  60.2 us
  transfers between devices with their start and end apart: 15, of which 12 were waited for; matrix products, arithmetic and copies ran while one was open for 6% of the time, Pallas kernels for 0%

commit v1 on v0

--- a/solution.py
+++ b/solution.py
@@ -4,6 +4,8 @@
 import jax
 import jax.numpy as jnp
 from jax import lax
+from jax.experimental import pallas as pl
+from jax.experimental.pallas import tpu as pltpu
 from jax.sharding import PartitionSpec as P
 
 HD = 64
@@ -12,12 +14,6 @@
 
 eps = 1e-05
 masked_score = -1e30
-
-
-def from_behind(value, axis, steps):
-    count = lax.axis_size(axis)
-    initial, last = (max(0, -steps), min(count, count - steps))
-    return lax.ppermute(value, axis, [(source, source + steps) for source in range(initial, last)])
 
 
 def product_plain(left, right):
@@ -221,42 +217,127 @@
     return (grad_in.astype(jnp.float32) + grad_residual, grads_layer)
 
 
-def forward_zeros(length, features, hidden_width):
-    head_count = features // HD
-    kept = (
-        jnp.zeros((length, head_count, HD), jnp.bfloat16),
-        jnp.zeros((length, head_count, HD), jnp.bfloat16),
-        jnp.zeros((length, head_count, HD), jnp.bfloat16),
-        jnp.zeros((head_count, length), jnp.float32),
-        jnp.zeros((length, features), jnp.bfloat16),
-        jnp.zeros((length, hidden_width), jnp.float32),
-        jnp.zeros((length, hidden_width), jnp.bfloat16),
-    )
-    return (jnp.zeros((length, features), jnp.float32), kept)
-
-
-def backward_zeros(length, features, weights):
-    return (
-        jnp.zeros((length, features), jnp.float32),
-        tuple((jnp.zeros(stacked.shape, jnp.float32) for stacked in weights)),
-    )
-
-
-def skip_forward(length, features, hidden_width, *operands):
-    return forward_zeros(length, features, hidden_width)
-
-
-def skip_backward(length, features, *operands):
-    return backward_zeros(length, features, operands[-1])
-
-
-def take(stacked, picked):
-    return lax.dynamic_index_in_dim(stacked, picked, 0, keepdims=False)
-
-
-def store(stacked, value, picked, active):
-    current = take(stacked, picked)
-    return lax.dynamic_update_index_in_dim(stacked, jnp.where(active, value, current), picked, 0)
+SQUARE = 4
+RING = 4
+
+
+def swap_cores(value):
+    return lax.ppermute(value, "section", [(0, 1), (1, 0)])
+
+
+def swap_square(value, bit):
+    count = lax.axis_size("dp")
+    return lax.ppermute(value, "dp", [(i, i ^ bit) for i in range(count)])
+
+
+def ring_on(value):
+    count = lax.axis_size("dp")
+    return lax.ppermute(value, "dp", [(i, (i + SQUARE) % count) for i in range(count)])
+
+
+def small_slice():
+    return lax.axis_size("dp") == SQUARE * RING
+
+
+def place_kernel(spot_ref, own, first, second, far_low, far_high, out, sems):
+    spot = spot_ref[0]
+    half = RING // 2
+    copies = [
+        pltpu.make_async_copy(own, out.at[:, spot], sems.at[0]),
+        pltpu.make_async_copy(first, out.at[:, spot ^ 1], sems.at[1]),
+        pltpu.make_async_copy(second, out.at[:, spot ^ 2], sems.at[2]),
+        pltpu.make_async_copy(far_low, out.at[pl.ds(0, half), spot ^ 3], sems.at[3]),
+        pltpu.make_async_copy(far_high, out.at[pl.ds(half, half), spot ^ 3], sems.at[4]),
+    ]
+    for copy in copies:
+        copy.start()
+    for copy in copies:
+        copy.wait()
+
+
+def place_blocks(spot, blocks):
+    _, rows, columns = blocks[0].shape
+    any_space = pl.BlockSpec(memory_space=pl.ANY)
+    return pl.pallas_call(
+        place_kernel,
+        out_shape=jax.ShapeDtypeStruct((RING, SQUARE, rows, columns), blocks[0].dtype),
+        in_specs=[pl.BlockSpec(memory_space=pltpu.SMEM)] + [any_space] * 5,
+        out_specs=any_space,
+        scratch_shapes=[pltpu.SemaphoreType.DMA((5,))],
+        name="place_blocks",
+    )(spot, *blocks)
+
+
+def gather_rows(piece):
+    rows, columns = piece.shape
+    if not small_slice():
+        return lax.all_gather(piece, "dp", axis=0, tiled=True)
+    place = lax.axis_index("dp")
+    level = place // SQUARE
+    spot = (place % SQUARE).astype(jnp.int32).reshape(1)
+    held = [piece]
+    for _ in range(RING - 1):
+        held.append(ring_on(held[-1]))
+    doubled = jnp.stack([held[3], held[2], held[1], held[0], held[3], held[2], held[1]])
+    column = lax.dynamic_slice_in_dim(doubled, RING - 1 - level, RING, 0)
+    first = swap_square(column, 1)
+    second = swap_square(column, 2)
+    half = RING // 2
+    far_low = swap_square(first[:half], 2)
+    far_high = swap_square(second[half:], 1)
+    whole = place_blocks(spot, (column, first, second, far_low, far_high))
+    return whole.reshape(RING * SQUARE * rows, columns)
+
+
+def scatter_rows(summed):
+    rows = summed.shape[0] // lax.axis_size("dp")
+    columns = summed.shape[1]
+    if not small_slice():
+        return lax.psum_scatter(summed, "dp", scatter_dimension=0, tiled=True)
+    place = lax.axis_index("dp")
+    level = place // SQUARE
+    spot = place % SQUARE
+    blocks = summed.reshape(RING, SQUARE, rows, columns)
+
+    def block(index):
+        return lax.dynamic_index_in_dim(blocks, index, 1, keepdims=False)
+
+    half = RING // 2
+    wire = jnp.bfloat16
+    far = block(spot ^ 3).astype(wire)
+    far_low = swap_square(far[:half], 1)
+    far_high = swap_square(far[half:], 2)
+    first = block(spot ^ 1)
+    second = block(spot ^ 2)
+    first = jnp.concatenate([first[:half], first[half:] + far_high.astype(jnp.float32)])
+    second = jnp.concatenate([second[:half] + far_low.astype(jnp.float32), second[half:]])
+    from_first = swap_square(first.astype(wire), 1)
+    from_second = swap_square(second.astype(wire), 2)
+    column = block(spot) + from_first.astype(jnp.float32) + from_second.astype(jnp.float32)
+
+    def rung(back):
+        return lax.dynamic_index_in_dim(column, (level - back) % RING, 0, keepdims=False)
+
+    travelling = rung(1)
+    for step in range(1, RING):
+        travelling = ring_on(travelling.astype(wire)).astype(jnp.float32) + rung(step + 1)
+    return travelling
+
+
+def halves_joined(is_first, mine, other):
+    return jnp.where(
+        is_first, jnp.concatenate([mine, other], axis=1), jnp.concatenate([other, mine], axis=1)
+    )
+
+
+def half_of(array, which):
+    width = array.shape[1] // 2
+    return lax.dynamic_slice_in_dim(array, which * width, width, 1)
+
+
+def half_slots(array, which):
+    length = array.shape[0] // 2
+    return lax.dynamic_slice_in_dim(array, which * length, length, 0)
 
 
 def on_device(
@@ -274,100 +355,169 @@
 ):
     section_index = lax.axis_index("section")
     is_first = section_index == 0
-    micro_count = lengths.shape[0]
-    slot_count = ends_in.shape[1] // micro_count
     features = ends_in.shape[2]
-    weights = (
-        lax.all_gather(qkv_weight[0], "dp", axis=0, tiled=True),
-        lax.all_gather(qkv_bias[0], "dp", axis=0, tiled=True),
-        lax.all_gather(out_weight[0], "dp", axis=0, tiled=True),
-        lax.all_gather(up_weight[0], "dp", axis=0, tiled=True),
-        lax.all_gather(up_bias[0], "dp", axis=0, tiled=True),
-        lax.all_gather(down_weight[0], "dp", axis=0, tiled=True),
-        lax.all_gather(out_biases[0], "dp", axis=1, tiled=True),
-        lax.all_gather(norm_gains[0], "dp", axis=1, tiled=True),
-        lax.all_gather(norm_biases[0], "dp", axis=1, tiled=True),
-    )
-    hidden_width = weights[3].shape[1]
-    own_rows = ends_in[0].reshape(micro_count, slot_count, features)
+    count = lax.axis_size("dp")
+    own_rows = ends_in[0]
+    slot_count = own_rows.shape[0] // 2
+    kept_rows = half_slots(own_rows, section_index)
+    other_rows = swap_cores(half_slots(own_rows, 1 - section_index))
+    entry = jnp.where(is_first, kept_rows, other_rows)
+    cotangent = jnp.where(is_first, other_rows, kept_rows)
     segments, positions = layouts(lengths, slot_count)
-    zero_saved = forward_zeros(slot_count, features, hidden_width)[1]
-    stash = jax.tree.map(
-        lambda shaped: jnp.zeros((micro_count,) + shaped.shape, shaped.dtype), zero_saved
-    )
-    kept_inputs = jnp.zeros((micro_count, slot_count, features), jnp.bfloat16)
-    results = jnp.zeros((micro_count, slot_count, features), jnp.float32)
-    arrived = jnp.zeros((slot_count, features), jnp.bfloat16)
-    for moment in range(micro_count + 1):
-        index_now = moment - section_index
-        active = (index_now >= 0) & (index_now < micro_count)
-        picked = jnp.clip(index_now, 0, micro_count - 1)
-        entry = jnp.where(is_first, take(own_rows, picked), arrived)
-        segment_now = take(segments, picked)
-        position_now = take(positions, picked)
-        produced, saved = lax.cond(
-            active,
-            layer_forward,
-            partial(skip_forward, slot_count, features, hidden_width),
-            entry,
-            segment_now,
-            position_now,
-            weights,
+    segment = lax.dynamic_index_in_dim(segments, section_index, 0, keepdims=False)
+    position = lax.dynamic_index_in_dim(positions, section_index, 0, keepdims=False)
+
+    def both(shard):
+        kept = half_of(shard, section_index)
+        other = swap_cores(half_of(shard, 1 - section_index))
+        return (jnp.where(is_first, kept, other), jnp.where(is_first, other, kept))
+
+    small_shapes = [
+        (qkv_bias.shape[1],),
+        (up_bias.shape[1],),
+        out_biases.shape[1:],
+        norm_gains.shape[1:],
+        norm_biases.shape[1:],
+    ]
+    small_own = jnp.concatenate(
+        [a[0].reshape(-1) for a in (qkv_bias, up_bias, out_biases, norm_gains, norm_biases)]
+    )
+    small_other = swap_cores(small_own)
+    small_both = jnp.where(
+        is_first,
+        jnp.concatenate([small_own, small_other]),
+        jnp.concatenate([small_other, small_own]),
+    )
+    small_full = gather_rows(small_both[None])
+    small_full = small_full.reshape(count, 2, small_own.shape[0])
+
+    def small_of(layer):
+        rows = small_full[:, layer]
+        found = []
+        at = 0
+        for shape in small_shapes:
+            size = math.prod(shape)
+            part = rows[:, at : at + size].reshape((count,) + shape)
+            at += size
+            if len(shape) == 2:
+                part = part.transpose(1, 0, 2).reshape(shape[0], count * shape[1])
+            else:
+                part = part.reshape(count * shape[0])
+            found.append(part)
+        return found
+
+    narrow = jnp.concatenate([qkv_weight[0], out_weight[0]], axis=1)
+    pieces = (both(qkv_weight[0]), both(out_weight[0]), both(up_weight[0]), both(down_weight[0]))
+    qkv_width = qkv_weight.shape[2]
+    weights = []
+    for layer in range(2):
+        joined = []
+        packed = (
+            jnp.concatenate([pieces[0][layer], pieces[1][layer]], axis=1),
+            pieces[2][layer],
+            pieces[3][layer],
         )
-        kept_inputs = store(kept_inputs, entry, picked, active)
-        stash = jax.tree.map(
-            lambda stacked, value: store(stacked, value, picked, active), stash, saved
+        for piece in packed:
+            mine = gather_rows(piece)
+            joined.append((mine, swap_cores(mine)))
+        cut = qkv_width // 2
+        weight_qkv = halves_joined(is_first, joined[0][0][:, :cut], joined[0][1][:, :cut])
+        weight_out = halves_joined(is_first, joined[0][0][:, cut:], joined[0][1][:, cut:])
+        weight_up = halves_joined(is_first, *joined[1])
+        weight_down = halves_joined(is_first, *joined[2])
+        bias_qkv, bias_up, bias_out, gains, shifts = small_of(layer)
+        weights.append(
+            (
+                weight_qkv,
+                bias_qkv,
+                weight_out,
+                weight_up,
+                bias_up,
+                weight_down,
+                bias_out,
+                gains,
+                shifts,
+            )
         )
-        results = store(results, produced, picked, active & jnp.logical_not(is_first))
-        arrived = from_behind(produced.astype(jnp.bfloat16), "section", 1)
-    totals = backward_zeros(slot_count, features, weights)[1]
-    incoming = jnp.zeros((slot_count, features), jnp.bfloat16)
-    for moment in range(micro_count + 1):
-        index_now = moment - (1 - section_index)
-        active = (index_now >= 0) & (index_now < micro_count)
-        picked = jnp.clip(index_now, 0, micro_count - 1)
-        grad_entry = jnp.where(is_first, incoming, take(own_rows, picked))
-        saved = jax.tree.map(lambda stacked: take(stacked, picked), stash)
-        entry_rows = take(kept_inputs, picked)
-        segment_now = take(segments, picked)
-        position_now = take(positions, picked)
-        sent, layer_grads = lax.cond(
-            active,
-            layer_backward,
-            partial(skip_backward, slot_count, features),
-            grad_entry,
-            entry_rows,
-            segment_now,
-            position_now,
-            saved,
-            weights,
-        )
-        totals = jax.tree.map(jnp.add, totals, layer_grads)
-        results = store(results, sent, picked, active & is_first)
-        incoming = from_behind(sent.astype(jnp.bfloat16), "section", -1)
-    summed = (
-        lax.psum_scatter(totals[0], "dp", scatter_dimension=0, tiled=True),
-        lax.psum_scatter(totals[1], "dp", scatter_dimension=0, tiled=True),
-        lax.psum_scatter(totals[2], "dp", scatter_dimension=0, tiled=True),
-        lax.psum_scatter(totals[3], "dp", scatter_dimension=0, tiled=True),
-        lax.psum_scatter(totals[4], "dp", scatter_dimension=0, tiled=True),
-        lax.psum_scatter(totals[5], "dp", scatter_dimension=0, tiled=True),
-        lax.psum_scatter(totals[6], "dp", scatter_dimension=1, tiled=True),
-        lax.psum_scatter(totals[7], "dp", scatter_dimension=1, tiled=True),
-        lax.psum_scatter(totals[8], "dp", scatter_dimension=1, tiled=True),
-    )
-    ends_out = results.reshape(1, micro_count * slot_count, features)
+
+    middle, saved_lower = layer_forward(entry, segment, position, weights[0])
+    middle = middle.astype(jnp.bfloat16)
+    produced, saved_upper = layer_forward(middle, segment, position, weights[1])
+    grad_middle, grads_upper = layer_backward(
+        cotangent, middle, segment, position, saved_upper, weights[1]
+    )
+    grad_entry, grads_lower = layer_backward(
+        grad_middle.astype(jnp.bfloat16), entry, segment, position, saved_lower, weights[0]
+    )
+
+    def reduce_half(*grads):
+        sent = [half_of(g, 1 - section_index).astype(jnp.bfloat16) for g in grads]
+        kept = [half_of(g, section_index).astype(jnp.float32) for g in grads]
+        sent = jnp.concatenate(sent, axis=1) if len(sent) > 1 else sent[0]
+        kept = jnp.concatenate(kept, axis=1) if len(kept) > 1 else kept[0]
+        return scatter_rows(kept + swap_cores(sent).astype(jnp.float32))
+
+    reduced = []
+    for grads in (grads_upper, grads_lower):
+        down = reduce_half(grads[5])
+        up = reduce_half(grads[3])
+        narrow = reduce_half(grads[0], grads[2])
+        reduced.append((narrow, up, down))
+    reduced = reduced[::-1]
+
+    def finish(upper_lower):
+        lower, upper = upper_lower
+        mine = jnp.where(is_first, lower, upper)
+        other = swap_cores(jnp.where(is_first, upper, lower))
+        return halves_joined(is_first, mine, other)
+
+    cut = qkv_width // 2
+    total_qkv = finish((reduced[0][0][:, :cut], reduced[1][0][:, :cut]))
+    total_out = finish((reduced[0][0][:, cut:], reduced[1][0][:, cut:]))
+    total_up = finish((reduced[0][1], reduced[1][1]))
+    total_down = finish((reduced[0][2], reduced[1][2]))
+
+    def small_rows(grads):
+        parts = []
+        for index in (1, 4, 6, 7, 8):
+            grad = grads[index].astype(jnp.float32)
+            if grad.ndim == 2:
+                part = grad.reshape(grad.shape[0], count, -1).transpose(1, 0, 2)
+                parts.append(part.reshape(count, -1))
+            else:
+                parts.append(grad.reshape(count, -1))
+        return jnp.concatenate(parts, axis=1)
+
+    small_lower = small_rows(grads_lower)
+    small_upper = small_rows(grads_upper)
+    small_kept = jnp.where(is_first, small_lower, small_upper)
+    small_sent = jnp.where(is_first, small_upper, small_lower)
+    small_total = scatter_rows(small_kept + swap_cores(small_sent))[0]
+    small_outs = []
+    at = 0
+    for shape in small_shapes:
+        size = math.prod(shape)
+        small_outs.append(small_total[at : at + size].reshape((1,) + shape))
+        at += size
+
+    crossing = swap_cores(jnp.where(is_first, produced, grad_entry))
+    staying = jnp.where(is_first, grad_entry, produced)
+    ends_out = jnp.where(
+        is_first,
+        jnp.concatenate([staying, crossing]),
+        jnp.concatenate([crossing, staying]),
+    )
     return (
-        ends_out,
-        summed[0][None],
-        summed[1][None],
-        summed[2][None],
-        summed[3][None],
-        summed[4][None],
-        summed[5][None],
-        summed[6][None],
-        summed[7][None],
-        summed[8][None],
+        ends_out[None],
+        total_qkv[None],
+        small_outs[0],
+        total_out[None],
+        total_up[None],
+        small_outs[1],
+        total_down[None],
+        small_outs[2],
+        small_outs[3],
+        small_outs[4],
     )
 
 

time: 1650 us -> 1140 us (0.69)
  waiting for transfers between devices: 1060 us -> 224 us
  Pallas kernels: 0 us -> 439 us
  blocking collectives: 222 us -> 0 us
  starting transfers between devices: 13.9 us -> 113 us
  local copies, waits for them, and re-layouts: 97.3 us -> 164 us
  other arithmetic: 108 us -> 64.7 us
    reduce_scatter x4 -> x0, waiting for transfers between devices: 640 us -> none  [the longest x1 177 us: on_device(): lax.psum_scatter(totals[5], 'dp', scatter_dimension=0, tiled=True)]
    pallas_call x0 -> x7, Pallas kernels: none -> 439 us  [place_blocks(): pl.pallas_call(place_kernel, out_shape=jax.ShapeDtypeStruct((RING, SQUARE...]
    unnamed x14 -> x0, waiting for transfers between devices: 284 us -> none
    ppermute x4 -> x122, waiting for transfers between devices: 9.2 us -> 224 us  [the longest x56 133 us: swap_square(): return lax.ppermute(value, 'dp', [(i, i ^ bit) for i in range(count)])]
    all_gather x4 -> x0, blocking collectives: 161 us -> none  [the longest x1 60.3 us: on_device(): lax.all_gather(qkv_bias[0], 'dp', axis=0, tiled=True)]
    all_gather x4 -> x0, waiting for transfers between devices: 129 us -> none  [the longest x1 82.2 us: on_device(): lax.all_gather(down_weight[0], 'dp', axis=0, tiled=True)]
    ppermute x4 -> x122, starting transfers between devices: 13.5 us -> 113 us  [the longest x56 51.4 us: swap_square(): return lax.ppermute(value, 'dp', [(i, i ^ bit) for i in range(count)])]
    unnamed x1 -> x0, blocking collectives: 60.2 us -> none
  transfers between devices with their start and end apart: 15 -> 122, of which waited for: 12 -> 51; matrix products, arithmetic and copies ran while one was open for 6% -> 25% of each run, Pallas kernels for 0% -> 39%
where the time goes in v1:
time: 1140 us; the launch traced here: 1130 us
  Pallas kernels  439 us (39%)
  waiting for transfers between devices  224 us (20%)
  local copies, waits for them, and re-layouts  164 us (14%)
  matrix products  119 us (10%)
  starting transfers between devices  113 us (10%)
  other arithmetic  64.7 us (6%)
    pallas_call x7, Pallas kernels, place_blocks(): pl.pallas_call(place_kernel, out_shape=jax.ShapeDtypeStruct((RING, SQUARE...  439 us
    ppermute x56, waiting for transfers between devices, swap_square(): return lax.ppermute(value, 'dp', [(i, i ^ bit) for i in range(count)])  133 us
    ppermute x42, waiting for transfers between devices, ring_on(): lax.ppermute(value, 'dp', [(i, (i + SQUARE) % count) for i in range(count)])  91.1 us
    ppermute x56, starting transfers between devices, swap_square(): return lax.ppermute(value, 'dp', [(i, i ^ bit) for i in range(count)])  51.4 us
    dot_general x8, matrix products, product_plain(): return jnp.dot(left, right, preferred_element_type=jnp.float32)  49.7 us
    ppermute x24, starting transfers between devices, swap_cores(): return lax.ppermute(value, 'section', [(0, 1), (1, 0)])  46.9 us
    dot_general x8, matrix products, product_transposed(): lax.dot_general(left, right, (((1,), (1,)), ((), ())), preferred_element_...  32.8 us
    unnamed x391, local copies, waits for them, and re-layouts  31 us
  transfers between devices with their start and end apart: 122, of which 51 were waited for; matrix products, arithmetic and copies ran while one was open for 25% of the time, Pallas kernels for 39%

profile of v1, /device:TPU:1, one launch (start us, length us, event | category | flops | bytes accessed | tf_op | source)
XLA Modules:
  0.0 1128.4 jit_solution(17138970023833958079)
XLA Ops:
  35.9 5.0 collective-permute-start.19
  62.0 5.5 collective-permute-done.54
  96.6 12.0 %collective-permute-done.39 = bf16[48,1536]{1,0:T(8,128)(2,1)S(1)} collective-permute-done((bf16[48,1536]{1,0:T(8,128)(2,1)S(1)}, bf16[48,1536]{1,0:T(8,128)(2,1)S(1)}, u32[]{:S(2)}, u32[]{:S(2)}) %collective-permute-start.39) | collective-permute-done | bytes 147488 | tf_op jit(solution)/shard_map/ppermute | solution.py:235
  115.8 17.6 %collective-permute-done.15.second = bf16[4,48,1536]{2,1,0:T(8,128)(2,1)S(1)} collective-permute-done((bf16[4,48,1536]{2,1,0:T(8,128)(2,1)S(1)}, bf16[4,48,1536]{2,1,0:T(8,128)(2,1)S(1)}, u32[]{:S(2)}, u32[]{:S(2)}) %collective-permute-start.15) | collective-permute-done | bytes 589856 | tf_op jit(solution)/shard_map/ppermute | solution.py:230
  146.1 72.6 %place_blocks.8 = bf16[4,4,48,1536]{3,2,1,0:T(8,128)(2,1)} custom-call(s32[1]{0:T(128)} %bitcast.2.spot_ref, bf16[4,48,1536]{2,1,0:T(8,128)(2,1)} %copy-done.44, bf16[4,48,1536]{2,1,0:T(8,128)(2,1)} %copy-done.69, bf16[4,48,1536]{2,1,0:T(8,128)(2,1)} %copy-done.68, bf16[2,48,1536]{2,1,0:T(8,128)(2,1)} %copy-done.101, ...), custom_call_target="tpu_custom_call" | custom-call | tf_op jit(solution)/shard_map/place_blocks/pallas_call | solution.py:261
  218.8 6.0 collective-permute-start.18
  236.0 11.6 %collective-permute-done.59.far_high = bf16[2,48,1536]{2,1,0:T(8,128)(2,1)S(1)} collective-permute-done((bf16[2,48,1536]{2,1,0:T(8,128)(2,1)S(1)}, bf16[2,48,1536]{2,1,0:T(8,128)(2,1)S(1)}, u32[]{:S(2)}, u32[]{:S(2)}) %collective-permute-start.59) | collective-permute-done | bytes 294944 | tf_op jit(solution)/shard_map/ppermute | solution.py:230
  258.5 72.6 %place_blocks.13 = bf16[4,4,48,1536]{3,2,1,0:T(8,128)(2,1)} custom-call(s32[1]{0:T(128)} %bitcast.2.spot_ref, bf16[4,48,1536]{2,1,0:T(8,128)(2,1)} %copy-done.42, bf16[4,48,1536]{2,1,0:T(8,128)(2,1)} %collective-permute-done.56.first, bf16[4,48,1536]{2,1,0:T(8,128)(2,1)} %collective-permute-done.57.second, bf16[2,48,1536]{2,1,0:T(8,128)(2,1)} %copy-done.100, ...), custom_call_target="tpu_custom_call" | custom-call | tf_op jit(solution)/shard_map/place_blocks/pallas_call | solution.py:261
  371.7 5.0 collective-permute-done.51.far_high
  384.5 72.6 %place_blocks.9 = bf16[4,4,48,1536]{3,2,1,0:T(8,128)(2,1)} custom-call(s32[1]{0:T(128)} %bitcast.2.spot_ref, bf16[4,48,1536]{2,1,0:T(8,128)(2,1)} %copy-done.41, bf16[4,48,1536]{2,1,0:T(8,128)(2,1)} %collective-permute-done.23.first, bf16[4,48,1536]{2,1,0:T(8,128)(2,1)} %copy-done.66, bf16[2,48,1536]{2,1,0:T(8,128)(2,1)} %collective-permute-done.25.far_low, ...), custom_call_target="tpu_custom_call" | custom-call | tf_op jit(solution)/shard_map/place_blocks/pallas_call | solution.py:261
  457.1 72.6 %place_blocks.12 = bf16[4,4,192,384]{3,2,1,0:T(8,128)(2,1)} custom-call(s32[1]{0:T(128)} %bitcast.2.spot_ref, bf16[4,192,384]{2,1,0:T(8,128)(2,1)} %copy-done.43, bf16[4,192,384]{2,1,0:T(8,128)(2,1)} %collective-permute-done.48.first, bf16[4,192,384]{2,1,0:T(8,128)(2,1)} %collective-permute-done.49.second, ...), custom_call_target="tpu_custom_call" | custom-call | tf_op jit(solution)/shard_map/place_blocks/pallas_call | solution.py:261
  533.4 72.6 %place_blocks.10 = bf16[4,4,192,384]{3,2,1,0:T(8,128)(2,1)} custom-call(s32[1]{0:T(128)} %bitcast.2.spot_ref, bf16[4,192,384]{2,1,0:T(8,128)(2,1)} %constant_dynamic-slice_fusion.17.own, bf16[4,192,384]{2,1,0:T(8,128)(2,1)} %collective-permute-done.32.first, bf16[4,192,384]{2,1,0:T(8,128)(2,1)} %copy-done.67, ...), custom_call_target="tpu_custom_call" | custom-call | tf_op jit(solution)/shard_map/place_blocks/pallas_call | solution.py:261
  606.6 72.6 %place_blocks.11 = bf16[4,4,48,1536]{3,2,1,0:T(8,128)(2,1)} custom-call(s32[1]{0:T(128)} %bitcast.2.spot_ref, bf16[4,48,1536]{2,1,0:T(8,128)(2,1)} %copy-done.40, bf16[4,48,1536]{2,1,0:T(8,128)(2,1)} %copy-done.65, bf16[4,48,1536]{2,1,0:T(8,128)(2,1)} %copy-done.64, bf16[2,48,1536]{2,1,0:T(8,128)(2,1)} %collective-permute-done.42.far_low, ...), custom_call_target="tpu_custom_call" | custom-call | tf_op jit(solution)/shard_map/place_blocks/pallas_call | solution.py:261
  701.5 14.8 %multiply_convert_fusion.3 = (bf16[256,3072]{1,0:T(8,128)(2,1)S(1)}, f32[256,3072]{1,0:T(8,128)}, f32[256,3072]{1,0:T(8,128)}) fusion(f32[3072]{0:T(1024)S(1)} %copy-done.145, bf16[768,1536]{1,0:T(8,128)(2,1)} %collective-permute-done.27, bf16[768,1536]{1,0:T(8,128)(2,1)} %bitcast.34, pred[]{:T(512)S(6)} %eq.86, ...), kind=kOutput, calls=%fused_computation.52 | convolution fusion | flops 1282277376 | bytes 12996609 | tf_op jit(solution)/shard_map/dot_general | solution.py:20
  716.4 6.6 convolution_add_fusion.7
  748.6 12.2 %multiply_convert_fusion = (bf16[256,3072]{1,0:T(8,128)(2,1)}, f32[256,3072]{1,0:T(8,128)S(1)}, f32[256,3072]{1,0:T(8,128)S(1)}) fusion(f32[3072]{0:T(1024)S(1)} %copy-done.143, bf16[768,1536]{1,0:T(8,128)(2,1)} %collective-permute-done.44, bf16[768,1536]{1,0:T(8,128)(2,1)S(1)} %bitcast.606, pred[]{:T(512)S(6)} %eq.86, f32[256,768]{1,0:T(8,128)S(1)} %copy-done.5, ...), kind=kOutput, calls=%fused_computation.28 | convolution fusion | flops 1282080768 | bytes 13389825 | tf_op jit(solution)/shard_map/dot_general | solution.py:20
  760.8 6.1 convert_reduce_fusion
  767.0 5.6 multiply_reduce_fusion.3
  794.8 5.2 fusion.206
  800.0 5.0 fusion.226
  814.2 7.4 convert_reduce_fusion.1
  840.7 6.8 fusion.200
  847.5 6.3 fusion.65
  860.5 8.2 convolution_add_fusion.6
  920.7 5.2 convert_add_fusion.1
  929.0 5.8 maximum_add_fusion
  944.5 5.2 dynamic-slice_bitcast_fusion.9
  999.1 10.3 collective-permute-done.74
  1012.8 9.3 collective-permute-done.66
  1025.4 9.3 collective-permute-done.100
  1036.8 23.2 %collective-permute-done.109 = bf16[4,192,384]{2,1,0:T(8,128)(2,1)S(1)} collective-permute-done((bf16[4,192,384]{2,1,0:T(8,128)(2,1)S(1)}, bf16[4,192,384]{2,1,0:T(8,128)(2,1)S(1)}, u32[]{:S(2)}, u32[]{:S(2)}) %collective-permute-start.109) | collective-permute-done | bytes 589856 | tf_op jit(solution)/shard_map/ppermute | solution.py:230
  1063.4 9.2 collective-permute-done.117
  (980 shorter events, 464.1 us)
Async XLA Ops:
  5.3 43.9 %collective-permute-start.10 = (bf16[48,384]{1,0:T(8,128)(2,1)S(1)}, bf16[48,384]{1,0:T(8,128)(2,1)S(1)}, u32[]{:S(2)}, u32[]{:S(2)}) collective-permute-start(bf16[48,384]{1,0:T(8,128)(2,1)S(1)} %dynamic-slice_bitcast_fusion.16), channel_id=1, source_target_pairs={{0,16},{16,0},{1,17},{17,1},{2,18},{18,2},{3,19},{19,3},{4,20},{20... | collective-permute-start | bytes 110600 | tf_op jit(solution)/shard_map/ppermute | solution.py:225
  6.7 42.6 %collective-permute-start.9 = (bf16[48,1152]{1,0:T(8,128)(2,1)S(1)}, bf16[48,1152]{1,0:T(8,128)(2,1)S(1)}, u32[]{:S(2)}, u32[]{:S(2)}) collective-permute-start(bf16[48,1152]{1,0:T(8,128)(2,1)S(1)} %dynamic-slice_bitcast_fusion.15), channel_id=1, source_target_pairs={{0,16},{16,0},{1,17},{17,1},{2,18},{18,2},{3,19},{19,3},{4,20},{20... | collective-permute-start | bytes 331784 | tf_op jit(solution)/shard_map/ppermute | solution.py:225
  7.7 41.9 %collective-permute-start.28 = (bf16[192,384]{1,0:T(8,128)(2,1)S(1)}, bf16[192,384]{1,0:T(8,128)(2,1)S(1)}, u32[]{:S(2)}, u32[]{:S(2)}) collective-permute-start(bf16[192,384]{1,0:T(8,128)(2,1)S(1)} %dynamic-slice_bitcast_fusion.13), channel_id=1, source_target_pairs={{0,16},{16,0},{1,17},{17,1},{2,18},{18,2},{3,19},{19,3},{4,20},{20... | collective-permute-start | bytes 442376 | tf_op jit(solution)/shard_map/ppermute | solution.py:225
  83.3 55.2 %collective-permute-start = (bf16[256,768]{1,0:T(8,128)(2,1)S(1)}, bf16[256,768]{1,0:T(8,128)(2,1)S(1)}, u32[]{:S(2)}, u32[]{:S(2)}) collective-permute-start(bf16[256,768]{1,0:T(8,128)(2,1)S(1)} %dynamic-slice_bitcast_fusion.12), channel_id=1, source_target_pairs={{0,16},{16,0},{1,17},{17,1},{2,18},{18,2},{3,19},{19,3},{4,20},{20... | collective-permute-start | bytes 1179656 | tf_op jit(solution)/shard_map/ppermute | solution.py:225
  108.6 110.2 %collective-permute-start.57 = (bf16[4,48,1536]{2,1,0:T(8,128)(2,1)S(1)}, bf16[4,48,1536]{2,1,0:T(8,128)(2,1)}, u32[]{:S(2)}, u32[]{:S(2)}) collective-permute-start(bf16[4,48,1536]{2,1,0:T(8,128)(2,1)S(1)} %constant_dynamic-slice_fusion.14.own), channel_id=1, source_target_pairs={{0,2},{1,3},{2,0},{3,1},{4,6},{5,7},{6,4},{7,5},{8,10},{9,11},{10,... | collective-permute-start | bytes 1769480 | tf_op jit(solution)/shard_map/ppermute | solution.py:230
  110.2 116.2 %collective-permute-start.56 = (bf16[4,48,1536]{2,1,0:T(8,128)(2,1)S(1)}, bf16[4,48,1536]{2,1,0:T(8,128)(2,1)}, u32[]{:S(2)}, u32[]{:S(2)}) collective-permute-start(bf16[4,48,1536]{2,1,0:T(8,128)(2,1)S(1)} %constant_dynamic-slice_fusion.14.own), channel_id=1, source_target_pairs={{0,1},{1,0},{2,3},{3,2},{4,5},{5,4},{6,7},{7,6},{8,9},{9,8},{10,11... | collective-permute-start | bytes 1769480 | tf_op jit(solution)/shard_map/ppermute | solution.py:230
  138.6 92.9 %collective-permute-start.41 = (bf16[4,48,1536]{2,1,0:T(8,128)(2,1)S(1)}, bf16[4,48,1536]{2,1,0:T(8,128)(2,1)S(1)}, u32[]{:S(2)}, u32[]{:S(2)}) collective-permute-start(bf16[4,48,1536]{2,1,0:T(8,128)(2,1)S(1)} %constant_dynamic-slice_fusion.16.own), channel_id=1, source_target_pairs={{0,2},{1,3},{2,0},{3,1},{4,6},{5,7},{6,4},{7,5},{8,10},{9,11},{10,... | collective-permute-start | bytes 1769480 | tf_op jit(solution)/shard_map/ppermute | solution.py:230
  143.6 89.0 %collective-permute-start.40 = (bf16[4,48,1536]{2,1,0:T(8,128)(2,1)S(1)}, bf16[4,48,1536]{2,1,0:T(8,128)(2,1)S(1)}, u32[]{:S(2)}, u32[]{:S(2)}) collective-permute-start(bf16[4,48,1536]{2,1,0:T(8,128)(2,1)S(1)} %constant_dynamic-slice_fusion.16.own), channel_id=1, source_target_pairs={{0,1},{1,0},{2,3},{3,2},{4,5},{5,4},{6,7},{7,6},{8,9},{9,8},{10,11... | collective-permute-start | bytes 1769480 | tf_op jit(solution)/shard_map/ppermute | solution.py:230
  144.8 87.8 %collective-permute-start.24 = (bf16[4,48,1536]{2,1,0:T(8,128)(2,1)S(1)}, bf16[4,48,1536]{2,1,0:T(8,128)(2,1)S(1)}, u32[]{:S(2)}, u32[]{:S(2)}) collective-permute-start(bf16[4,48,1536]{2,1,0:T(8,128)(2,1)S(1)} %constant_dynamic-slice_fusion.18.own), channel_id=1, source_target_pairs={{0,2},{1,3},{2,0},{3,1},{4,6},{5,7},{6,4},{7,5},{8,10},{9,11},{10,... | collective-permute-start | bytes 1769480 | tf_op jit(solution)/shard_map/ppermute | solution.py:230
  218.8 460.4 %collective-permute-start.18 = (bf16[768,1536]{1,0:T(8,128)(2,1)}, bf16[768,1536]{1,0:T(8,128)(2,1)}, u32[]{:S(2)}, u32[]{:S(2)}) collective-permute-start(bf16[768,1536]{1,0:T(8,128)(2,1)} %bitcast.585), channel_id=1, source_target_pairs={{0,16},{16,0},{1,17},{17,1},{2,18},{18,2},{3,19},{19,3},{4,20},{20... | collective-permute-start | bytes 7077896 | tf_op jit(solution)/shard_map/ppermute | solution.py:225
  226.4 104.8 %collective-permute-start.23 = (bf16[4,48,1536]{2,1,0:T(8,128)(2,1)S(1)}, bf16[4,48,1536]{2,1,0:T(8,128)(2,1)}, u32[]{:S(2)}, u32[]{:S(2)}) collective-permute-start(bf16[4,48,1536]{2,1,0:T(8,128)(2,1)S(1)} %constant_dynamic-slice_fusion.18.own), channel_id=1, source_target_pairs={{0,1},{1,0},{2,3},{3,2},{4,5},{5,4},{6,7},{7,6},{8,9},{9,8},{10,11... | collective-permute-start | bytes 1769480 | tf_op jit(solution)/shard_map/ppermute | solution.py:230
  231.5 102.6 %collective-permute-start.33 = (bf16[4,192,384]{2,1,0:T(8,128)(2,1)}, bf16[4,192,384]{2,1,0:T(8,128)(2,1)S(1)}, u32[]{:S(2)}, u32[]{:S(2)}) collective-permute-start(bf16[4,192,384]{2,1,0:T(8,128)(2,1)} %constant_dynamic-slice_fusion.17.own), channel_id=1, source_target_pairs={{0,2},{1,3},{2,0},{3,1},{4,6},{5,7},{6,4},{7,5},{8,10},{9,11},{10,... | collective-permute-start | bytes 1769480 | tf_op jit(solution)/shard_map/ppermute | solution.py:230
  247.6 90.8 %collective-permute-start.49 = (bf16[4,192,384]{2,1,0:T(8,128)(2,1)S(1)}, bf16[4,192,384]{2,1,0:T(8,128)(2,1)}, u32[]{:S(2)}, u32[]{:S(2)}) collective-permute-start(bf16[4,192,384]{2,1,0:T(8,128)(2,1)S(1)} %constant_dynamic-slice_fusion.15.own), channel_id=1, source_target_pairs={{0,2},{1,3},{2,0},{3,1},{4,6},{5,7},{6,4},{7,5},{8,10},{9,11},{10,... | collective-permute-start | bytes 1769480 | tf_op jit(solution)/shard_map/ppermute | solution.py:230
  253.4 85.3 %collective-permute-start.48 = (bf16[4,192,384]{2,1,0:T(8,128)(2,1)S(1)}, bf16[4,192,384]{2,1,0:T(8,128)(2,1)}, u32[]{:S(2)}, u32[]{:S(2)}) collective-permute-start(bf16[4,192,384]{2,1,0:T(8,128)(2,1)S(1)} %constant_dynamic-slice_fusion.15.own), channel_id=1, source_target_pairs={{0,1},{1,0},{2,3},{3,2},{4,5},{5,4},{6,7},{7,6},{8,9},{9,8},{10,11... | collective-permute-start | bytes 1769480 | tf_op jit(solution)/shard_map/ppermute | solution.py:230
  331.2 358.1 %collective-permute-start.60 = (bf16[768,1536]{1,0:T(8,128)(2,1)}, bf16[768,1536]{1,0:T(8,128)(2,1)}, u32[]{:S(2)}, u32[]{:S(2)}) collective-permute-start(bf16[768,1536]{1,0:T(8,128)(2,1)} %bitcast.588), channel_id=1, source_target_pairs={{0,16},{16,0},{1,17},{17,1},{2,18},{18,2},{3,19},{19,3},{4,20},{20... | collective-permute-start | bytes 7077896 | tf_op jit(solution)/shard_map/ppermute | solution.py:225
  370.3 235.7 %collective-permute-start.43 = (bf16[2,48,1536]{2,1,0:T(8,128)(2,1)}, bf16[2,48,1536]{2,1,0:T(8,128)(2,1)}, u32[]{:S(2)}, u32[]{:S(2)}) collective-permute-start(bf16[2,48,1536]{2,1,0:T(8,128)(2,1)} %slice.796), channel_id=1, source_target_pairs={{0,1},{1,0},{2,3},{3,2},{4,5},{5,4},{6,7},{7,6},{8,9},{9,8},{10,11... | collective-permute-start | bytes 884744 | tf_op jit(solution)/shard_map/ppermute | solution.py:230
  376.6 229.5 %collective-permute-start.42 = (bf16[2,48,1536]{2,1,0:T(8,128)(2,1)}, bf16[2,48,1536]{2,1,0:T(8,128)(2,1)}, u32[]{:S(2)}, u32[]{:S(2)}) collective-permute-start(bf16[2,48,1536]{2,1,0:T(8,128)(2,1)} %slice.795), channel_id=1, source_target_pairs={{0,2},{1,3},{2,0},{3,1},{4,6},{5,7},{6,4},{7,5},{8,10},{9,11},{10,... | collective-permute-start | bytes 884744 | tf_op jit(solution)/shard_map/ppermute | solution.py:230
  377.2 152.5 %collective-permute-start.34 = (bf16[2,192,384]{2,1,0:T(8,128)(2,1)}, bf16[2,192,384]{2,1,0:T(8,128)(2,1)}, u32[]{:S(2)}, u32[]{:S(2)}) collective-permute-start(bf16[2,192,384]{2,1,0:T(8,128)(2,1)} %slice.787), channel_id=1, source_target_pairs={{0,2},{1,3},{2,0},{3,1},{4,6},{5,7},{6,4},{7,5},{8,10},{9,11},{10,... | collective-permute-start | bytes 884744 | tf_op jit(solution)/shard_map/ppermute | solution.py:230
  529.8 231.1 %collective-permute-start.52 = (bf16[3072,384]{1,0:T(8,128)(2,1)}, bf16[3072,384]{1,0:T(8,128)(2,1)}, u32[]{:S(2)}, u32[]{:S(2)}) collective-permute-start(bf16[3072,384]{1,0:T(8,128)(2,1)} %bitcast.599), channel_id=1, source_target_pairs={{0,16},{16,0},{1,17},{17,1},{2,18},{18,2},{3,19},{19,3},{4,20},{20... | collective-permute-start | bytes 7077896 | tf_op jit(solution)/shard_map/ppermute | solution.py:225
  606.0 110.3 %collective-permute-start.36 = (bf16[3072,384]{1,0:T(8,128)(2,1)}, bf16[3072,384]{1,0:T(8,128)(2,1)}, u32[]{:S(2)}, u32[]{:S(2)}) collective-permute-start(bf16[3072,384]{1,0:T(8,128)(2,1)} %bitcast.602), channel_id=1, source_target_pairs={{0,16},{16,0},{1,17},{17,1},{2,18},{18,2},{3,19},{19,3},{4,20},{20... | collective-permute-start | bytes 7077896 | tf_op jit(solution)/shard_map/ppermute | solution.py:225
  606.1 95.4 %collective-permute-start.27 = (bf16[768,1536]{1,0:T(8,128)(2,1)}, bf16[768,1536]{1,0:T(8,128)(2,1)}, u32[]{:S(2)}, u32[]{:S(2)}) collective-permute-start(bf16[768,1536]{1,0:T(8,128)(2,1)} %bitcast.34), channel_id=1, source_target_pairs={{0,16},{16,0},{1,17},{17,1},{2,18},{18,2},{3,19},{19,3},{4,20},{20... | collective-permute-start | bytes 7077896 | tf_op jit(solution)/shard_map/ppermute | solution.py:225
  679.2 69.3 %collective-permute-start.44 = (bf16[768,1536]{1,0:T(8,128)(2,1)}, bf16[768,1536]{1,0:T(8,128)(2,1)}, u32[]{:S(2)}, u32[]{:S(2)}) collective-permute-start(bf16[768,1536]{1,0:T(8,128)(2,1)} %bitcast.605), channel_id=1, source_target_pairs={{0,16},{16,0},{1,17},{17,1},{2,18},{18,2},{3,19},{19,3},{4,20},{20... | collective-permute-start | bytes 7077896 | tf_op jit(solution)/shard_map/ppermute | solution.py:225
  811.4 106.4 %collective-permute-start.70 = (bf16[768,1536]{1,0:T(8,128)(2,1)}, bf16[768,1536]{1,0:T(8,128)(2,1)}, u32[]{:S(2)}, u32[]{:S(2)}) collective-permute-start(bf16[768,1536]{1,0:T(8,128)(2,1)} %pad_maximum_fusion.1), channel_id=1, source_target_pairs={{0,16},{16,0},{1,17},{17,1},{2,18},{18,2},{3,19},{19,3},{4,20},{20... | collective-permute-start | bytes 7077896 | tf_op jit(solution)/shard_map/ppermute | solution.py:225
  870.5 43.8 %collective-permute-start.61 = (f32[256,768]{1,0:T(8,128)}, f32[256,768]{1,0:T(8,128)}, u32[]{:S(2)}, u32[]{:S(2)}) collective-permute-start(f32[256,768]{1,0:T(8,128)} %get-tuple-element.76), channel_id=1, source_target_pairs={{0,16},{16,0},{1,17},{17,1},{2,18},{18,2},{3,19},{19,3},{4,20},{20... | collective-permute-start | bytes 2359304 | tf_op jit(solution)/shard_map/ppermute | solution.py:225
  889.8 30.9 %collective-permute-start.105 = (bf16[3072,384]{1,0:T(8,128)(2,1)}, bf16[3072,384]{1,0:T(8,128)(2,1)}, u32[]{:S(2)}, u32[]{:S(2)}) collective-permute-start(bf16[3072,384]{1,0:T(8,128)(2,1)} %dynamic-slice_convert_fusion.1), channel_id=1, source_target_pairs={{0,16},{16,0},{1,17},{17,1},{2,18},{18,2},{3,19},{19,3},{4,20},{20... | collective-permute-start | bytes 7077896 | tf_op jit(solution)/shard_map/ppermute | solution.py:225
  906.9 30.2 %collective-permute-start.96 = (bf16[768,1536]{1,0:T(8,128)(2,1)}, bf16[768,1536]{1,0:T(8,128)(2,1)}, u32[]{:S(2)}, u32[]{:S(2)}) collective-permute-start(bf16[768,1536]{1,0:T(8,128)(2,1)} %dynamic-slice_convert_fusion.2), channel_id=1, source_target_pairs={{0,16},{16,0},{1,17},{17,1},{2,18},{18,2},{3,19},{19,3},{4,20},{20... | collective-permute-start | bytes 7077896 | tf_op jit(solution)/shard_map/ppermute | solution.py:225
  917.8 35.3 %collective-permute-start.113 = (bf16[3072,384]{1,0:T(8,128)(2,1)}, bf16[3072,384]{1,0:T(8,128)(2,1)}, u32[]{:S(2)}, u32[]{:S(2)}) collective-permute-start(bf16[3072,384]{1,0:T(8,128)(2,1)} %dynamic-slice_convert_fusion), channel_id=1, source_target_pairs={{0,16},{16,0},{1,17},{17,1},{2,18},{18,2},{3,19},{19,3},{4,20},{20... | collective-permute-start | bytes 7077896 | tf_op jit(solution)/shard_map/ppermute | solution.py:225
  998.5 36.2 %collective-permute-start.100 = (bf16[4,48,1536]{2,1,0:T(8,128)(2,1)S(1)}, bf16[4,48,1536]{2,1,0:T(8,128)(2,1)S(1)}, u32[]{:S(2)}, u32[]{:S(2)}) collective-permute-start(bf16[4,48,1536]{2,1,0:T(8,128)(2,1)S(1)} %pad_maximum_fusion.9), channel_id=1, source_target_pairs={{0,2},{1,3},{2,0},{3,1},{4,6},{5,7},{6,4},{7,5},{8,10},{9,11},{10,... | collective-permute-start | bytes 1769480 | tf_op jit(solution)/shard_map/ppermute | solution.py:230
  1010.9 50.9 %collective-permute-start.92 = (bf16[4,48,1536]{2,1,0:T(8,128)(2,1)S(1)}, bf16[4,48,1536]{2,1,0:T(8,128)(2,1)S(1)}, u32[]{:S(2)}, u32[]{:S(2)}) collective-permute-start(bf16[4,48,1536]{2,1,0:T(8,128)(2,1)S(1)} %pad_maximum_fusion.7), channel_id=1, source_target_pairs={{0,2},{1,3},{2,0},{3,1},{4,6},{5,7},{6,4},{7,5},{8,10},{9,11},{10,... | collective-permute-start | bytes 1769480 | tf_op jit(solution)/shard_map/ppermute | solution.py:230
  1022.0 37.9 %collective-permute-start.109 = (bf16[4,192,384]{2,1,0:T(8,128)(2,1)S(1)}, bf16[4,192,384]{2,1,0:T(8,128)(2,1)S(1)}, u32[]{:S(2)}, u32[]{:S(2)}) collective-permute-start(bf16[4,192,384]{2,1,0:T(8,128)(2,1)S(1)} %pad_maximum_fusion.11), channel_id=1, source_target_pairs={{0,2},{1,3},{2,0},{3,1},{4,6},{5,7},{6,4},{7,5},{8,10},{9,11},{10,... | collective-permute-start | bytes 1769480 | tf_op jit(solution)/shard_map/ppermute | solution.py:230
  1022.7 38.7 %collective-permute-start.107 = (bf16[4,192,384]{2,1,0:T(8,128)(2,1)S(1)}, bf16[4,192,384]{2,1,0:T(8,128)(2,1)S(1)}, u32[]{:S(2)}, u32[]{:S(2)}) collective-permute-start(bf16[4,192,384]{2,1,0:T(8,128)(2,1)S(1)} %pad_maximum_fusion.10), channel_id=1, source_target_pairs={{0,1},{1,0},{2,3},{3,2},{4,5},{5,4},{6,7},{7,6},{8,9},{9,8},{10,11... | collective-permute-start | bytes 1769480 | tf_op jit(solution)/shard_map/ppermute | solution.py:230
  1036.2 36.4 %collective-permute-start.117 = (bf16[4,192,384]{2,1,0:T(8,128)(2,1)S(1)}, bf16[4,192,384]{2,1,0:T(8,128)(2,1)S(1)}, u32[]{:S(2)}, u32[]{:S(2)}) collective-permute-start(bf16[4,192,384]{2,1,0:T(8,128)(2,1)S(1)} %pad_maximum_fusion.13), channel_id=1, source_target_pairs={{0,2},{1,3},{2,0},{3,1},{4,6},{5,7},{6,4},{7,5},{8,10},{9,11},{10,... | collective-permute-start | bytes 1769480 | tf_op jit(solution)/shard_map/ppermute | solution.py:230
  (262 other events, 4924.3 us)

commit v2 on v1

v2 whole, which is shorter than its diff:
```python
import math

import jax
import jax.numpy as jnp
from jax import lax
from jax.experimental import pallas as pl
from jax.experimental.pallas import tpu as pltpu
from jax.sharding import PartitionSpec as P

HD = 64
ROT = 16
LANES = 128
TILES = 3


eps = 1e-05
masked_score = -1e30
vmem_bytes = 48 * 1024 * 1024


def product(left, right):
    return jnp.dot(left, right, preferred_element_type=jnp.float32)


def product_transposed(left, right):
    return lax.dot_general(
        left, right, (((1,), (1,)), ((), ())), preferred_element_type=jnp.float32
    )


def layouts(lengths, slot_count):
    ends_at = jnp.cumsum(lengths)
    indices = jnp.arange(slot_count, dtype=jnp.int32)
    passed = indices[:, None] >= ends_at[None, :]
    segments = jnp.sum(passed.astype(jnp.int32), axis=1)
    starts = jnp.sum(jnp.where(passed, lengths[None, :], 0), axis=1)
    return (segments, indices - starts)


def rotary_tables(positions):
    lane = jnp.arange(LANES, dtype=jnp.int32) % HD
    half = ROT // 2
    freqs = 10000.0 ** (-2.0 * (lane % half).astype(jnp.float32) / ROT)
    angles = positions.astype(jnp.float32)[:, None] * freqs[None, :]
    cosine = jnp.where(lane < ROT, jnp.cos(angles), 1.0)
    sine = jnp.sin(angles)
    ahead = jnp.where(lane < half, -sine, 0.0)
    behind = jnp.where((lane >= half) & (lane < ROT), sine, 0.0)
    return jnp.stack([cosine, ahead, behind])


def allowed_transposed(segment):
    indices = jnp.arange(segment.shape[0], dtype=jnp.int32)
    allowed = (segment[:, None] == segment[None, :]) & (indices[:, None] <= indices[None, :])
    return allowed.astype(jnp.float32)


def turned(values, tables, back):
    half = ROT // 2
    parts = []
    for at in range(0, values.shape[1], LANES):
        part = values[:, at : at + LANES]
        moved = (
            pltpu.roll(part, LANES - half, 1) * tables[1] + pltpu.roll(part, half, 1) * tables[2]
        )
        kept = part * tables[0]
        parts.append(kept - moved if back else kept + moved)
    return jnp.concatenate(parts, axis=1)


def unit_rows(rows):
    centred = rows - jnp.mean(rows, axis=-1, keepdims=True)
    spread = jnp.mean(centred * centred, axis=-1, keepdims=True)
    scale = lax.rsqrt(spread + eps)
    return (centred * scale, scale)


def lane_half(which, width):
    return pl.ds(pl.multiple_of(which * width, LANES), width)


def head_lanes(values, which):
    lane = lax.broadcasted_iota(jnp.int32, values.shape, 1)
    return jnp.where((lane < HD) == (which == 0), values, jnp.zeros_like(values))


def scores_of(key_pair, query_pair, which, allowed):
    scores = product_transposed(head_lanes(key_pair, which), query_pair) * (1.0 / math.sqrt(HD))
    return jnp.where(allowed, scores, masked_score)


def attn_forward_kernel(
    side, rows, tables, mask, norms, bias_qkv, bias_out, mine, other, qkv, logs, attended, passed
):
    width = mine.shape[1] // 4
    entry = rows[...].astype(jnp.float32)
    unit, _ = unit_rows(entry)
    normed = (unit * norms[0:1] + norms[2:3]).astype(jnp.bfloat16)
    allowed = mask[...] > 0.5
    for at, weight in enumerate((mine, other)):
        half = side[0] if at == 0 else 1 - side[0]
        parts = []
        for part in range(3):
            cut = slice(part * width, (part + 1) * width)
            value = product(normed, weight[:, cut]) + bias_qkv[at : at + 1, cut]
            if part < 2:
                value = turned(value, tables, False)
            value = value.astype(jnp.bfloat16)
            qkv[at, :, cut] = value
            parts.append(value)
        queries, keys, values = parts
        values = values.T
        outs = []
        for pair in range(width // LANES):
            cut = slice(pair * LANES, (pair + 1) * LANES)
            for which in range(2):
                head = 2 * pair + which
                scores = scores_of(keys[:, cut], queries[:, cut], which, allowed)
                peak = jnp.max(scores, axis=0, keepdims=True)
                raised = jnp.exp(scores - peak)
                total = jnp.sum(raised, axis=0, keepdims=True)
                chances = (raised * (1.0 / total)).astype(jnp.bfloat16)
                outs.append(product(values[head * HD : (head + 1) * HD], chances))
                logs[at, head : head + 1, :] = peak + jnp.log(total)
        mixed = jnp.concatenate(outs, axis=0).T.astype(jnp.bfloat16)
        attended[:, lane_half(half, width)] = mixed
    mixed = attended[...]
    for at, weight in enumerate((mine, other)):
        half = side[0] if at == 0 else 1 - side[0]
        lanes = lane_half(half, width)
        passed[:, lanes] = (
            rows[:, lanes].astype(jnp.float32)
            + product(mixed, weight[:, 3 * width :])
            + bias_out[0:1, lanes]
        )


def whole_blocks(count):
    return [pl.BlockSpec(memory_space=pltpu.VMEM)] * count


def attn_forward(side, rows, tables, mask, small, mine, other):
    length, features = rows.shape
    width = features // 2
    heads = width // HD
    return pl.pallas_call(
        attn_forward_kernel,
        out_shape=(
            jax.ShapeDtypeStruct((2, length, 3 * width), jnp.bfloat16),
            jax.ShapeDtypeStruct((2, heads, length), jnp.float32),
            jax.ShapeDtypeStruct((length, features), jnp.bfloat16),
            jax.ShapeDtypeStruct((length, features), jnp.float32),
        ),
        in_specs=[pl.BlockSpec(memory_space=pltpu.SMEM)] + whole_blocks(8),
        out_specs=tuple(whole_blocks(4)),
        compiler_params=pltpu.CompilerParams(vmem_limit_bytes=vmem_bytes),
        cost_estimate=pl.CostEstimate(
            flops=2 * length * features * features * 5,
            bytes_accessed=8 * features * features,
            transcendentals=length * length * features // HD,
        ),
        name="attn_forward",
    )(side, rows, tables, mask, small["norms"], small["qkv"], small["out"], mine, other)


def tile_of(step, side):
    half = jnp.where(step < TILES, side[0], 1 - side[0])
    return half * TILES + step % TILES


def first_tile(step):
    return jnp.minimum(step, TILES - 1)


def second_tile(step):
    return jnp.maximum(step - TILES, 0)


def mlp_forward_kernel(
    side, rows, passed, norms, bias_up, bias_out, up_mine, up_other, down_mine, down_other,
    active, slope, produced, normed, sum_mine, sum_other
):
    step = pl.program_id(0)

    @pl.when(step == 0)
    def _():
        unit, _ = unit_rows(rows[...].astype(jnp.float32))
        normed[...] = (unit * norms[1:2] + norms[3:4]).astype(jnp.bfloat16)
        sum_mine[...] = jnp.zeros_like(sum_mine)
        sum_other[...] = jnp.zeros_like(sum_other)

    weight = jnp.where(step < TILES, up_mine[...], up_other[...])
    hidden = product(normed[...], weight) + bias_up[...]
    bell = 0.5 * (1.0 + lax.erf(hidden * (1.0 / math.sqrt(2.0))))
    density = jnp.exp(-0.5 * hidden * hidden) * (1.0 / math.sqrt(2.0 * math.pi))
    slope[...] = bell + hidden * density
    lit = (hidden * bell).astype(jnp.bfloat16)
    active[...] = lit
    sum_mine[...] += product(lit, down_mine[...])
    sum_other[...] += product(lit, down_other[...])

    @pl.when(step == 2 * TILES - 1)
    def _():
        width = sum_mine.shape[1]
        for half, total in ((side[0], sum_mine), (1 - side[0], sum_other)):
            lanes = lane_half(half, width)
            produced[:, lanes] = (
                passed[:, lanes] + total[...] + bias_out[1:2, lanes]
            ).astype(produced.dtype)


def mlp_forward(side, rows, passed, small, weights, kind):
    up_mine, up_other, down_mine, down_other = weights
    length, features = rows.shape
    hidden = down_mine.shape[0]
    tile = hidden // (2 * TILES)
    width = features // 2

    def fixed(*shape):
        return pl.BlockSpec(shape, lambda step, side: (0,) * len(shape))

    tiled = pl.BlockSpec((length, tile), lambda step, side: (0, tile_of(step, side)))
    down_spec = pl.BlockSpec((tile, width), lambda step, side: (tile_of(step, side), 0))
    return pl.pallas_call(
        mlp_forward_kernel,
        out_shape=(
            jax.ShapeDtypeStruct((length, hidden), jnp.bfloat16),
            jax.ShapeDtypeStruct((length, hidden), jnp.float32),
            jax.ShapeDtypeStruct((length, features), kind),
        ),
        grid_spec=pltpu.PrefetchScalarGridSpec(
            num_scalar_prefetch=1,
            grid=(2 * TILES,),
            in_specs=[
                fixed(length, features),
                fixed(length, features),
                fixed(4, features),
                pl.BlockSpec((1, tile), lambda step, side: (0, tile_of(step, side))),
                fixed(2, features),
                pl.BlockSpec((features, tile), lambda step, side: (0, first_tile(step))),
                pl.BlockSpec((features, tile), lambda step, side: (0, second_tile(step))),
                down_spec,
                down_spec,
            ],
            out_specs=(tiled, tiled, fixed(length, features)),
            scratch_shapes=[
                pltpu.VMEM((length, features), jnp.bfloat16),
                pltpu.VMEM((length, width), jnp.float32),
                pltpu.VMEM((length, width), jnp.float32),
            ],
        ),
        compiler_params=pltpu.CompilerParams(vmem_limit_bytes=vmem_bytes),
        cost_estimate=pl.CostEstimate(
            flops=4 * length * features * hidden,
            bytes_accessed=4 * features * hidden + 6 * length * hidden,
            transcendentals=2 * length * hidden,
        ),
        name="mlp_forward",
    )(
        side, rows, passed, small["norms"], small["up"], small["out"],
        up_mine, up_other, down_mine, down_other,
    )


def mlp_backward_kernel(
    side, rows, grad, norms, active, slope, up_mine, up_other, down_mine, down_other,
    up_kept, up_sent, down_kept, down_sent, bias_grad, grad_normed, normed
):
    step = pl.program_id(0)
    width = down_mine.shape[1]

    @pl.when(step == 0)
    def _():
        unit, _ = unit_rows(rows[...].astype(jnp.float32))
        normed[...] = (unit * norms[1:2] + norms[3:4]).T.astype(jnp.bfloat16)
        grad_normed[...] = jnp.zeros_like(grad_normed)

    grad_mine = grad[:, lane_half(side[0], width)]
    grad_other = grad[:, lane_half(1 - side[0], width)]
    weight = jnp.where(step < TILES, up_mine[...], up_other[...])
    lit = active[...].T
    down_kept[...] = product(lit, grad_mine).astype(jnp.bfloat16)
    down_sent[...] = product(lit, grad_other).astype(jnp.bfloat16)
    back = product_transposed(grad_mine, down_mine[...])
    back += product_transposed(grad_other, down_other[...])
    back = (back * slope[...]).astype(jnp.bfloat16)
    bias_grad[...] = jnp.sum(back.astype(jnp.float32), axis=0, keepdims=True)
    up_grad = product(normed[...], back).astype(jnp.bfloat16)

    @pl.when(step < TILES)
    def _():
        up_kept[...] = up_grad

    @pl.when(step >= TILES)
    def _():
        up_sent[...] = up_grad

    grad_normed[...] += product_transposed(back, weight)


def mlp_backward(side, rows, grad, small, saved, weights):
    active, slope = saved
    up_mine, up_other, down_mine, down_other = weights
    length, features = rows.shape
    hidden = down_mine.shape[0]
    tile = hidden // (2 * TILES)
    width = features // 2

    def fixed(*shape):
        return pl.BlockSpec(shape, lambda step, side: (0,) * len(shape))

    tiled = pl.BlockSpec((length, tile), lambda step, side: (0, tile_of(step, side)))
    down_spec = pl.BlockSpec((tile, width), lambda step, side: (tile_of(step, side), 0))
    up_first = pl.BlockSpec((features, tile), lambda step, side: (0, first_tile(step)))
    up_second = pl.BlockSpec((features, tile), lambda step, side: (0, second_tile(step)))
    return pl.pallas_call(
        mlp_backward_kernel,
        out_shape=(
            jax.ShapeDtypeStruct((features, hidden // 2), jnp.bfloat16),
            jax.ShapeDtypeStruct((features, hidden // 2), jnp.bfloat16),
            jax.ShapeDtypeStruct((hidden, width), jnp.bfloat16),
            jax.ShapeDtypeStruct((hidden, width), jnp.bfloat16),
            jax.ShapeDtypeStruct((1, hidden), jnp.float32),
            jax.ShapeDtypeStruct((length, features), jnp.float32),
        ),
        grid_spec=pltpu.PrefetchScalarGridSpec(
            num_scalar_prefetch=1,
            grid=(2 * TILES,),
            in_specs=[
                fixed(length, features),
                fixed(length, features),
                fixed(4, features),
                tiled,
                tiled,
                up_first,
                up_second,
                down_spec,
                down_spec,
            ],
            out_specs=(
                up_first,
                up_second,
                down_spec,
                down_spec,
                pl.BlockSpec((1, tile), lambda step, side: (0, tile_of(step, side))),
                fixed(length, features),
            ),
            scratch_shapes=[pltpu.VMEM((features, length), jnp.bfloat16)],
        ),
        compiler_params=pltpu.CompilerParams(vmem_limit_bytes=vmem_bytes),
        cost_estimate=pl.CostEstimate(
            flops=8 * length * features * hidden,
            bytes_accessed=8 * features * hidden + 6 * length * hidden,
            transcendentals=0,
        ),
        name="mlp_backward",
    )(
        side, rows, grad, small["norms"], active, slope,
        up_mine, up_other, down_mine, down_other,
    )


def attn_backward_kernel(
    side, rows, grad, tables, mask, norms, qkv, logs, attended, grad_mlp, mine, other,
    kept, sent, bias_grad, sums, passed, mixed_back
):
    width = mine.shape[1] // 4
    unit, scale = unit_rows(rows[...].astype(jnp.float32))
    normed = (unit * norms[0:1] + norms[2:3]).T.astype(jnp.bfloat16)
    allowed = mask[...] > 0.5
    mixed = attended[...].T
    back = None
    for at, (weight, result) in enumerate(((mine, kept), (other, sent))):
        half = side[0] if at == 0 else 1 - side[0]
        part = grad[:, lane_half(half, width)]
        result[:, 3 * width :] = product(mixed, part).astype(jnp.bfloat16)
        term = product_transposed(part, weight[:, 3 * width :])
        back = term if back is None else back + term
    mixed_back[...] = back.astype(jnp.bfloat16)
    grad_attn = None
    for at, (weight, result) in enumerate(((mine, kept), (other, sent))):
        half = side[0] if at == 0 else 1 - side[0]
        queries = qkv[at, :, 0:width]
        keys = qkv[at, :, width : 2 * width]
        values = qkv[at, :, 2 * width :]
        keys_turned = keys.T
        grad_out = mixed_back[:, lane_half(half, width)]
        query_grads, key_grads, value_grads = [], [], []
        for pair in range(width // LANES):
            cut = slice(pair * LANES, (pair + 1) * LANES)
            key_pair, value_pair = [], []
            for which in range(2):
                head = 2 * pair + which
                scores = scores_of(keys[:, cut], queries[:, cut], which, allowed)
                chances = jnp.exp(scores - logs[at, head : head + 1, :])
                value_pair.append(product(chances.astype(jnp.bfloat16), grad_out[:, cut]))
                slopes = product_transposed(head_lanes(values[:, cut], which), grad_out[:, cut])
                inner = jnp.sum(slopes * chances, axis=0, keepdims=True)
                slopes = (chances * (slopes - inner)).astype(jnp.bfloat16)
                key_pair.append(product(slopes, queries[:, cut]))
                query_grads.append(product(keys_turned[head * HD : (head + 1) * HD], slopes))
            lane = lax.broadcasted_iota(jnp.int32, key_pair[0].shape, 1)
            key_grads.append(jnp.where(lane < HD, key_pair[0], key_pair[1]))
            value_grads.append(jnp.where(lane < HD, value_pair[0], value_pair[1]))
        factor = 1.0 / math.sqrt(HD)
        query_grad = turned(jnp.concatenate(query_grads, axis=0).T * factor, tables, True)
        key_grad = turned(jnp.concatenate(key_grads, axis=1) * factor, tables, True)
        value_grad = jnp.concatenate(value_grads, axis=1)
        for index, part in enumerate((query_grad, key_grad, value_grad)):
            cut = slice(index * width, (index + 1) * width)
            part = part.astype(jnp.bfloat16)
            bias_grad[at : at + 1, cut] = jnp.sum(
                part.astype(jnp.float32), axis=0, keepdims=True
            )
            result[:, cut] = product(normed, part).astype(jnp.bfloat16)
            term = product_transposed(part, weight[:, cut])
            grad_attn = term if grad_attn is None else grad_attn + term
    grad_up = grad_mlp[...]
    grad_rows = grad[...].astype(jnp.float32)
    sums[0:1] = jnp.sum(unit * grad_attn, axis=0, keepdims=True)
    sums[1:2] = jnp.sum(unit * grad_up, axis=0, keepdims=True)
    sums[2:3] = jnp.sum(grad_attn, axis=0, keepdims=True)
    sums[3:4] = jnp.sum(grad_up, axis=0, keepdims=True)
    sums[4:5] = jnp.sum(grad_rows, axis=0, keepdims=True)
    inward = grad_attn * norms[0:1] + grad_up * norms[1:2]
    level = jnp.mean(inward, axis=-1, keepdims=True)
    along = jnp.mean(inward * unit, axis=-1, keepdims=True)
    passed[...] = (grad_rows + (inward - level - unit * along) * scale).astype(passed.dtype)


def attn_backward(side, rows, grad, tables, mask, small, saved, grad_mlp, mine, other, kind):
    qkv, logs, attended = saved
    length, features = rows.shape
    return pl.pallas_call(
        attn_backward_kernel,
        out_shape=(
            jax.ShapeDtypeStruct(mine.shape, jnp.bfloat16),
            jax.ShapeDtypeStruct(mine.shape, jnp.bfloat16),
            jax.ShapeDtypeStruct((2, 3 * features // 2), jnp.float32),
            jax.ShapeDtypeStruct((5, features), jnp.float32),
            jax.ShapeDtypeStruct((length, features), kind),
        ),
        in_specs=[pl.BlockSpec(memory_space=pltpu.SMEM)] + whole_blocks(11),
        out_specs=tuple(whole_blocks(5)),
        scratch_shapes=[pltpu.VMEM((length, features), jnp.bfloat16)],
        compiler_params=pltpu.CompilerParams(vmem_limit_bytes=vmem_bytes),
        cost_estimate=pl.CostEstimate(
            flops=2 * length * features * features * 12,
            bytes_accessed=16 * features * features,
            transcendentals=length * length * features // HD,
        ),
        name="attn_backward",
    )(
        side, rows, grad, tables, mask, small["norms"], qkv, logs, attended, grad_mlp, mine, other
    )


SQUARE = 4
RING = 4


def swap_cores(value):
    return lax.ppermute(value, "section", [(0, 1), (1, 0)])


def swap_square(value, bit):
    count = lax.axis_size("dp")
    return lax.ppermute(value, "dp", [(i, i ^ bit) for i in range(count)])


def ring_on(value):
    count = lax.axis_size("dp")
    return lax.ppermute(value, "dp", [(i, (i + SQUARE) % count) for i in range(count)])


def small_slice():
    return lax.axis_size("dp") == SQUARE * RING


def place_kernel(spot_ref, own, first, second, far_low, far_high, out, sems):
    spot = spot_ref[0]
    half = RING // 2
    copies = [
        pltpu.make_async_copy(own, out.at[:, spot], sems.at[0]),
        pltpu.make_async_copy(first, out.at[:, spot ^ 1], sems.at[1]),
        pltpu.make_async_copy(second, out.at[:, spot ^ 2], sems.at[2]),
        pltpu.make_async_copy(far_low, out.at[pl.ds(0, half), spot ^ 3], sems.at[3]),
        pltpu.make_async_copy(far_high, out.at[pl.ds(half, half), spot ^ 3], sems.at[4]),
    ]
    for copy in copies:
        copy.start()
    for copy in copies:
        copy.wait()


def place_blocks(spot, blocks):
    _, rows, columns = blocks[0].shape
    any_space = pl.BlockSpec(memory_space=pl.ANY)
    return pl.pallas_call(
        place_kernel,
        out_shape=jax.ShapeDtypeStruct((RING, SQUARE, rows, columns), blocks[0].dtype),
        in_specs=[pl.BlockSpec(memory_space=pltpu.SMEM)] + [any_space] * 5,
        out_specs=pl.BlockSpec(memory_space=pltpu.VMEM),
        scratch_shapes=[pltpu.SemaphoreType.DMA((5,))],
        compiler_params=pltpu.CompilerParams(vmem_limit_bytes=vmem_bytes),
        name="place_blocks",
    )(spot, *blocks)


def gather_rows(piece):
    rows, columns = piece.shape
    if not small_slice():
        return lax.all_gather(piece, "dp", axis=0, tiled=True)
    place = lax.axis_index("dp")
    level = place // SQUARE
    spot = (place % SQUARE).astype(jnp.int32).reshape(1)
    held = [piece]
    for _ in range(RING - 1):
        held.append(ring_on(held[-1]))
    doubled = jnp.stack([held[3], held[2], held[1], held[0], held[3], held[2], held[1]])
    column = lax.dynamic_slice_in_dim(doubled, RING - 1 - level, RING, 0)
    first = swap_square(column, 1)
    second = swap_square(column, 2)
    half = RING // 2
    far_low = swap_square(first[:half], 2)
    far_high = swap_square(second[half:], 1)
    whole = place_blocks(spot, (column, first, second, far_low, far_high))
    return whole.reshape(RING * SQUARE * rows, columns)


def scatter_rows(summed):
    rows = summed.shape[0] // lax.axis_size("dp")
    columns = summed.shape[1]
    if not small_slice():
        return lax.psum_scatter(summed, "dp", scatter_dimension=0, tiled=True)
    place = lax.axis_index("dp")
    level = place // SQUARE
    spot = place % SQUARE
    blocks = summed.reshape(RING, SQUARE, rows, columns)

    def block(index):
        return lax.dynamic_index_in_dim(blocks, index, 1, keepdims=False)

    half = RING // 2
    wire = jnp.bfloat16
    far = block(spot ^ 3).astype(wire)
    far_low = swap_square(far[:half], 1)
    far_high = swap_square(far[half:], 2)
    first = block(spot ^ 1)
    second = block(spot ^ 2)
    first = jnp.concatenate([first[:half], first[half:] + far_high.astype(jnp.float32)])
    second = jnp.concatenate([second[:half] + far_low.astype(jnp.float32), second[half:]])
    from_first = swap_square(first.astype(wire), 1)
    from_second = swap_square(second.astype(wire), 2)
    column = block(spot) + from_first.astype(jnp.float32) + from_second.astype(jnp.float32)

    def rung(back):
        return lax.dynamic_index_in_dim(column, (level - back) % RING, 0, keepdims=False)

    travelling = rung(1)
    for step in range(1, RING):
        travelling = ring_on(travelling.astype(wire)).astype(jnp.float32) + rung(step + 1)
    return travelling


def half_of(array, which):
    width = array.shape[1] // 2
    return lax.dynamic_slice_in_dim(array, which * width, width, 1)


def half_slots(array, which):
    length = array.shape[0] // 2
    return lax.dynamic_slice_in_dim(array, which * length, length, 0)


def ordered(is_first, mine, other):
    return (jnp.where(is_first, mine, other), jnp.where(is_first, other, mine))


def on_device(
    ends_in,
    lengths,
    qkv_weight,
    qkv_bias,
    out_weight,
    up_weight,
    up_bias,
    down_weight,
    out_biases,
    norm_gains,
    norm_biases,
):
    section_index = lax.axis_index("section")
    is_first = section_index == 0
    side = section_index.astype(jnp.int32).reshape(1)
    features = ends_in.shape[2]
    width = features // 2
    count = lax.axis_size("dp")
    own_rows = ends_in[0]
    slot_count = own_rows.shape[0] // 2
    kept_rows = half_slots(own_rows, section_index)
    other_rows = swap_cores(half_slots(own_rows, 1 - section_index))
    entry, cotangent = ordered(is_first, kept_rows, other_rows)
    segment, position = layouts(
        lax.dynamic_index_in_dim(lengths, section_index, 0, keepdims=False), slot_count
    )
    tables = rotary_tables(position)
    mask = allowed_transposed(segment)

    def both(take):
        kept = take(section_index)
        other = swap_cores(take(1 - section_index))
        return ordered(is_first, kept, other)

    def take_narrow(which):
        thirds = [
            qkv_weight[0, :, part * features : (part + 1) * features] for part in range(3)
        ]
        return jnp.concatenate([half_of(part, which) for part in thirds + [out_weight[0]]], axis=1)

    pieces = (
        both(take_narrow),
        both(lambda which: half_of(up_weight[0], which)),
        both(lambda which: half_of(down_weight[0], which)),
    )

    small_shapes = [
        (qkv_bias.shape[1],),
        (up_bias.shape[1],),
        out_biases.shape[1:],
        norm_gains.shape[1:],
        norm_biases.shape[1:],
    ]
    small_own = jnp.concatenate(
        [a[0].reshape(-1) for a in (qkv_bias, up_bias, out_biases, norm_gains, norm_biases)]
    )
    small_both = jnp.concatenate(ordered(is_first, small_own, swap_cores(small_own)))
    small_full = gather_rows(small_both[None])
    small_full = small_full.reshape(count, 2, small_own.shape[0]).astype(jnp.float32)

    def small_of(layer):
        rows = small_full[:, layer]
        found = []
        at = 0
        for shape in small_shapes:
            size = math.prod(shape)
            part = rows[:, at : at + size].reshape((count,) + shape)
            at += size
            if len(shape) == 2:
                part = part.transpose(1, 0, 2).reshape(shape[0], count * shape[1])
            else:
                part = part.reshape(1, count * shape[0])
            found.append(part)
        bias_qkv, bias_up, bias_out, gains, shifts = found
        bias_qkv = bias_qkv.reshape(3, 2, width).transpose(1, 0, 2).reshape(2, 3 * width)
        return dict(
            qkv=jnp.where(is_first, bias_qkv, bias_qkv[::-1]),
            up=bias_up,
            out=bias_out,
            norms=jnp.concatenate([gains, shifts]),
        )

    gathered = []
    for layer in range(2):
        found = []
        for piece in pieces:
            mine = gather_rows(piece[layer])
            found.append((mine, swap_cores(mine)))
        gathered.append(found)
    small = [small_of(layer) for layer in range(2)]

    def forward(rows, layer, kind):
        narrow, up, down = gathered[layer]
        qkv, logs, attended, passed = attn_forward(side, rows, tables, mask, small[layer], *narrow)
        active, slope, produced = mlp_forward(
            side, rows, passed, small[layer], up + down, kind
        )
        return (produced, (qkv, logs, attended), (active, slope))

    def backward(rows, grad, layer, attn_saved, mlp_saved, kind):
        narrow, up, down = gathered[layer]
        up_kept, up_sent, down_kept, down_sent, bias_up, grad_mlp = mlp_backward(
            side, rows, grad, small[layer], mlp_saved, up + down
        )
        kept, sent, bias_qkv, sums, passed = attn_backward(
            side, rows, grad, tables, mask, small[layer], attn_saved, grad_mlp, *narrow, kind
        )
        bias_qkv = jnp.where(is_first, bias_qkv, bias_qkv[::-1])
        bias_qkv = bias_qkv.reshape(2, 3, width).transpose(1, 0, 2).reshape(1, 6 * width)
        vectors = (
            bias_qkv,
            bias_up,
            jnp.concatenate([sums[4:5], sums[4:5]]),
            sums[0:2],
            sums[2:4],
        )
        return (passed, ((down_kept, down_sent), (up_kept, up_sent), (kept, sent)), vectors)

    middle, attn_lower, mlp_lower = forward(entry, 0, jnp.bfloat16)
    produced, attn_upper, mlp_upper = forward(middle, 1, jnp.float32)
    grad_middle, grads_upper, vectors_upper = backward(
        middle, cotangent, 1, attn_upper, mlp_upper, jnp.bfloat16
    )
    grad_entry, grads_lower, vectors_lower = backward(
        entry, grad_middle, 0, attn_lower, mlp_lower, jnp.float32
    )

    def reduce_half(kept, sent):
        return scatter_rows(kept.astype(jnp.float32) + swap_cores(sent).astype(jnp.float32))

    reduced_upper = [reduce_half(*pair) for pair in grads_upper]
    reduced_lower = [reduce_half(*pair) for pair in grads_lower]

    def finish(lower, upper):
        mine, leaving = ordered(is_first, lower, upper)
        return ordered(is_first, mine, swap_cores(leaving))

    down_halves, up_halves, narrow_halves = (
        finish(*pair) for pair in zip(reduced_lower, reduced_upper)
    )
    total_down = jnp.concatenate(down_halves, axis=1)
    total_up = jnp.concatenate(up_halves, axis=1)
    total_qkv = jnp.concatenate(
        [
            part[:, at * width : (at + 1) * width]
            for at in range(3)
            for part in narrow_halves
        ],
        axis=1,
    )
    total_out = jnp.concatenate([part[:, 3 * width :] for part in narrow_halves], axis=1)

    def small_rows(vectors):
        parts = []
        for grad in vectors:
            part = grad.reshape(grad.shape[0], count, -1).transpose(1, 0, 2)
            parts.append(part.reshape(count, -1))
        return jnp.concatenate(parts, axis=1)

    small_kept, small_sent = ordered(
        is_first, small_rows(vectors_lower), small_rows(vectors_upper)
    )
    small_total = scatter_rows(small_kept + swap_cores(small_sent))[0]
    small_outs = []
    at = 0
    for shape in small_shapes:
        size = math.prod(shape)
        small_outs.append(small_total[at : at + size].reshape((1,) + shape))
        at += size

    staying, leaving = ordered(is_first, grad_entry, produced)
    ends_out = jnp.concatenate(ordered(is_first, staying, swap_cores(leaving)))
    return (
        ends_out[None],
        total_qkv[None],
        small_outs[0],
        total_out[None],
        total_up[None],
        small_outs[1],
        total_down[None],
        small_outs[2],
        small_outs[3],
        small_outs[4],
    )


def solution(mesh):
    return jax.shard_map(
        on_device,
        mesh=mesh,
        in_specs=(
            P("section", "dp", None),
            P("dp", None),
            P("section", "dp", None),
            P("section", "dp"),
            P("section", "dp", None),
            P("section", "dp", None),
            P("section", "dp"),
            P("section", "dp", None),
            P("section", None, "dp"),
            P("section", None, "dp"),
            P("section", None, "dp"),
        ),
        out_specs=(
            P("section", "dp", None),
            P("section", "dp", None),
            P("section", "dp"),
            P("section", "dp", None),
            P("section", "dp", None),
            P("section", "dp"),
            P("section", "dp", None),
            P("section", None, "dp"),
            P("section", None, "dp"),
            P("section", None, "dp"),
        ),
        check_vma=False,
    )
```

time: 1140 us -> 553 us (0.49)
  Pallas kernels: 439 us -> 105 us
  matrix products: 119 us -> 0 us
  local copies, waits for them, and re-layouts: 164 us -> 52.2 us
  other arithmetic: 64.7 us -> 30.8 us
    pallas_call x7, Pallas kernels: 439 us -> 13.8 us  [place_blocks(): pl.pallas_call(place_kernel, out_shape=jax.ShapeDtypeStruct((RING, SQUARE...]
    dot_general x36 -> x0, matrix products: 119 us -> none  [the longest x8 49.7 us: product_plain(): return jnp.dot(left, right, preferred_element_type=jnp.float32)]
    pallas_call x0 -> x8, Pallas kernels: none -> 90.7 us  [the longest x2 29.8 us: mlp_backward(): pl.pallas_call(mlp_backward_kernel, out_shape=(jax.ShapeDtypeStruct((feat...]
    convert_element_type x22 -> x1, local copies, waits for them, and re-layouts: 31.8 us -> 1.01 us  [on_device(): small_full.reshape(count, 2, small_own.shape[0]).astype(jnp.float32)]
    ppermute x24 -> x22, starting transfers between devices: 46.9 us -> 63.2 us  [swap_cores(): return lax.ppermute(value, 'section', [(0, 1), (1, 0)])]
    slice x20 -> x13, local copies, waits for them, and re-layouts: 16.1 us -> 1.31 us  [the longest x1 0.97 us: take_narrow(): qkv_weight[0, :, part * features:(part + 1) * features]]
    unnamed x391 -> x177, local copies, waits for them, and re-layouts: 31 us -> 18.3 us
  transfers between devices with their start and end apart: 122 -> 120, of which waited for: 51 -> 54; matrix products, arithmetic and copies ran while one was open for 25% -> 10% of each run, Pallas kernels for 39% -> 7%
where the time goes in v2:
time: 553 us; the launch traced here: 547 us
  waiting for transfers between devices  234 us (42%)
  starting transfers between devices  122 us (22%)
  Pallas kernels  105 us (19%)
  local copies, waits for them, and re-layouts  52.2 us (9%)
  other arithmetic  30.8 us (6%)
    ppermute x56, waiting for transfers between devices, swap_square(): return lax.ppermute(value, 'dp', [(i, i ^ bit) for i in range(count)])  142 us
    ppermute x42, waiting for transfers between devices, ring_on(): lax.ppermute(value, 'dp', [(i, (i + SQUARE) % count) for i in range(count)])  91.2 us
    ppermute x22, starting transfers between devices, swap_cores(): return lax.ppermute(value, 'section', [(0, 1), (1, 0)])  63.2 us
    ppermute x56, starting transfers between devices, swap_square(): return lax.ppermute(value, 'dp', [(i, i ^ bit) for i in range(count)])  44.8 us
    pallas_call x2, Pallas kernels, mlp_backward(): pl.pallas_call(mlp_backward_kernel, out_shape=(jax.ShapeDtypeStruct((feat...  29.8 us
    pallas_call x2, Pallas kernels, attn_backward(): pl.pallas_call(attn_backward_kernel, out_shape=(jax.ShapeDtypeStruct(mine...  24.7 us
    pallas_call x2, Pallas kernels, mlp_forward(): pl.pallas_call(mlp_forward_kernel, out_shape=(jax.ShapeDtypeStruct((lengt...  19.6 us
    unnamed x177, local copies, waits for them, and re-layouts  18.3 us
  transfers between devices with their start and end apart: 120, of which 54 were waited for; matrix products, arithmetic and copies ran while one was open for 10% of the time, Pallas kernels for 7%

profile of v2, /device:TPU:1, one launch (start us, length us, event | category | flops | bytes accessed | tf_op | source)
XLA Modules:
  0.0 546.9 jit_solution(9782409640486393444)
XLA Ops:
  67.1 5.3 collective-permute-done.38
  83.2 15.6 %collective-permute-done.15.far_low = bf16[2,48,1536]{2,1,0:T(8,128)(2,1)S(1)} collective-permute-done((bf16[2,48,1536]{2,1,0:T(8,128)(2,1)S(1)}, bf16[2,48,1536]{2,1,0:T(8,128)(2,1)S(1)}, u32[]{:S(2)}, u32[]{:S(2)}) %collective-permute-start.15) | collective-permute-done | bytes 294944 | tf_op jit(solution)/shard_map/ppermute | solution.py:468
  99.6 7.7 %collective-permute-done.16.far_high = bf16[2,48,1536]{2,1,0:T(8,128)(2,1)S(1)} collective-permute-done((bf16[2,48,1536]{2,1,0:T(8,128)(2,1)S(1)}, bf16[2,48,1536]{2,1,0:T(8,128)(2,1)S(1)}, u32[]{:S(2)}, u32[]{:S(2)}) %collective-permute-start.16) | collective-permute-done | bytes 294944 | tf_op jit(solution)/shard_map/ppermute | solution.py:468
  111.9 10.7 %collective-permute-start.17 = (bf16[768,1536]{1,0:T(8,128)(2,1)S(1)}, bf16[768,1536]{1,0:T(8,128)(2,1)}, u32[]{:S(2)}, u32[]{:S(2)}) collective-permute-start(bf16[768,1536]{1,0:T(8,128)(2,1)S(1)} %bitcast.509), channel_id=1, source_target_pairs={{0,16},{16,0},{1,17},{17,1},{2,18},{18,2},{3,19},{19,3},{4,20},{20... | collective-permute-start | bytes 7077896 | tf_op jit(solution)/shard_map/ppermute | solution.py:463
  131.4 7.0 %collective-permute-done.47.first = bf16[4,48,1536]{2,1,0:T(8,128)(2,1)} collective-permute-done((bf16[4,48,1536]{2,1,0:T(8,128)(2,1)}, bf16[4,48,1536]{2,1,0:T(8,128)(2,1)}, u32[]{:S(2)}, u32[]{:S(2)}) %collective-permute-start.47) | collective-permute-done | bytes 589856 | tf_op jit(solution)/shard_map/ppermute | solution.py:468
  141.4 9.7 %collective-permute-done.55.first = bf16[4,192,384]{2,1,0:T(8,128)(2,1)} collective-permute-done((bf16[4,192,384]{2,1,0:T(8,128)(2,1)}, bf16[4,192,384]{2,1,0:T(8,128)(2,1)}, u32[]{:S(2)}, u32[]{:S(2)}) %collective-permute-start.55) | collective-permute-done | bytes 589856 | tf_op jit(solution)/shard_map/ppermute | solution.py:468
  154.0 5.3 collective-permute-done.24.far_low
  174.3 20.4 %collective-permute-start = (bf16[256,768]{1,0:T(8,128)(2,1)}, bf16[256,768]{1,0:T(8,128)(2,1)}, u32[]{:S(2)}, u32[]{:S(2)}) collective-permute-start(bf16[256,768]{1,0:T(8,128)(2,1)} %dynamic-slice_bitcast_fusion.12), channel_id=1, source_target_pairs={{0,16},{16,0},{1,17},{17,1},{2,18},{18,2},{3,19},{19,3},{4,20},{20... | collective-permute-start | bytes 1179656 | tf_op jit(solution)/shard_map/ppermute | solution.py:463
  221.6 8.0 %attn_forward.2 = (bf16[2,256,1152]{2,1,0:T(8,128)(2,1)S(1)}, f32[2,6,256]{2,1,0:T(8,128)S(1)}, bf16[256,768]{1,0:T(8,128)(2,1)S(1)}, f32[256,768]{1,0:T(8,128)S(1)}) custom-call(s32[1]{0:T(128)} %bitcast.side, bf16[256,768]{1,0:T(8,128)(2,1)S(1)} %get-tuple-element.108.rows, f32[3,256,128]{2,1,0:T(8,128)S(1)} %pad_maximum_fusion.12.tables, ...), custom_call_target="tpu_custom_call" | custom-call | flops 1509949440 | bytes 4718592 | tf_op jit(solution)/shard_map/attn_forward/pallas_call | solution.py:146
  229.5 9.9 %mlp_forward.2 = (bf16[256,3072]{1,0:T(8,128)(2,1)S(1)}, f32[256,3072]{1,0:T(8,128)}, bf16[256,768]{1,0:T(8,128)(2,1)S(1)}) custom-call(s32[1]{0:T(128)} %bitcast.side, bf16[256,768]{1,0:T(8,128)(2,1)S(1)} %get-tuple-element.108.rows, f32[256,768]{1,0:T(8,128)S(1)} %get-tuple-element.46.passed, f32[4,768]{1,0:T(4,128)S(1)} %pad_maximum_fusion.15.norms, ...), custom_call_target="tpu_custom_call" | custom-call | flops 2415919104 | bytes 14155776 | tf_op jit(solution)/shard_map/mlp_forward/pallas_call | solution.py:224
  239.5 8.7 %attn_forward.3 = (bf16[2,256,1152]{2,1,0:T(8,128)(2,1)S(1)}, f32[2,6,256]{2,1,0:T(8,128)S(1)}, bf16[256,768]{1,0:T(8,128)(2,1)S(1)}, f32[256,768]{1,0:T(8,128)S(1)}) custom-call(s32[1]{0:T(128)} %bitcast.side, bf16[256,768]{1,0:T(8,128)(2,1)S(1)} %get-tuple-element.47.rows, f32[3,256,128]{2,1,0:T(8,128)S(1)} %pad_maximum_fusion.12.tables, ...), custom_call_target="tpu_custom_call" | custom-call | flops 1509949440 | bytes 4718592 | tf_op jit(solution)/shard_map/attn_forward/pallas_call | solution.py:146
  248.2 9.7 %mlp_forward.3 = (bf16[256,3072]{1,0:T(8,128)(2,1)S(1)}, f32[256,3072]{1,0:T(8,128)}, f32[256,768]{1,0:T(8,128)S(1)}) custom-call(s32[1]{0:T(128)} %bitcast.side, bf16[256,768]{1,0:T(8,128)(2,1)S(1)} %get-tuple-element.47.rows, f32[256,768]{1,0:T(8,128)S(1)} %get-tuple-element.51.passed, f32[4,768]{1,0:T(4,128)S(1)} %pad_maximum_fusion.16.norms, ...), custom_call_target="tpu_custom_call" | custom-call | flops 2415919104 | bytes 14155776 | tf_op jit(solution)/shard_map/mlp_forward/pallas_call | solution.py:224
  257.9 15.0 %mlp_backward.2 = (bf16[768,1536]{1,0:T(8,128)(2,1)S(1)}, bf16[768,1536]{1,0:T(8,128)(2,1)}, bf16[3072,384]{1,0:T(8,128)(2,1)}, bf16[3072,384]{1,0:T(8,128)(2,1)...) custom-call(s32[1]{0:T(128)} %bitcast.side, bf16[256,768]{1,0:T(8,128)(2,1)S(1)} %get-tuple-element.47.rows, ...), custom_call_target="tpu_custom_call" | custom-call | flops 4831838208 | bytes 23592960 | tf_op jit(solution)/shard_map/mlp_backward/pallas_call | solution.py:316
  274.3 12.3 %attn_backward.2 = (bf16[768,1536]{1,0:T(8,128)(2,1)}, bf16[768,1536]{1,0:T(8,128)(2,1)}, f32[2,1152]{1,0:T(2,128)S(1)}, f32[5,768]{1,0:T(8,128)S(1)}, bf16[256,768]{1,0:T(8,128)(2,1)S(1)}) custom-call(s32[1]{0:T(128)} %bitcast.side, bf16[256,768]{1,0:T(8,128)(2,1)S(1)} %get-tuple-element.47.rows, bf16[256,768]{1,0:T(8,128)(2,1)S(1)} %get-tuple-element.107.grad, ...), custom_call_target="tpu_custom_call" | custom-call | flops 3623878656 | bytes 9437184 | tf_op jit(solution)/shard_map/attn_backward/pallas_call | solution.py:434
  286.7 14.8 %mlp_backward.3 = (bf16[768,1536]{1,0:T(8,128)(2,1)S(1)}, bf16[768,1536]{1,0:T(8,128)(2,1)}, bf16[3072,384]{1,0:T(8,128)(2,1)}, bf16[3072,384]{1,0:T(8,128)(2,1)...) custom-call(s32[1]{0:T(128)} %bitcast.side, bf16[256,768]{1,0:T(8,128)(2,1)S(1)} %get-tuple-element.108.rows, ...), custom_call_target="tpu_custom_call" | custom-call | flops 4831838208 | bytes 23592960 | tf_op jit(solution)/shard_map/mlp_backward/pallas_call | solution.py:316
  302.9 12.4 %attn_backward.3 = (bf16[768,1536]{1,0:T(8,128)(2,1)}, bf16[768,1536]{1,0:T(8,128)(2,1)}, f32[2,1152]{1,0:T(2,128)S(1)}, f32[5,768]{1,0:T(8,128)S(1)}, f32[256,768]{1,0:T(8,128)S(1)}) custom-call(s32[1]{0:T(128)} %bitcast.side, bf16[256,768]{1,0:T(8,128)(2,1)S(1)} %get-tuple-element.108.rows, bf16[256,768]{1,0:T(8,128)(2,1)S(1)} %get-tuple-element.55.grad, ...), custom_call_target="tpu_custom_call" | custom-call | flops 3623878656 | bytes 9437184 | tf_op jit(solution)/shard_map/attn_backward/pallas_call | solution.py:434
  332.6 4.2 collective-permute-done.84
  337.1 4.4 collective-permute-start.86
  341.5 5.3 collective-permute-start.94
  384.7 4.6 collective-permute-done.72
  391.0 4.5 collective-permute-done.89
  397.4 4.5 collective-permute-done.97
  403.9 4.4 collective-permute-done.106
  410.3 4.3 collective-permute-done.114
  416.6 11.6 %collective-permute-done.65 = bf16[4,48,1536]{2,1,0:T(8,128)(2,1)S(1)} collective-permute-done((bf16[4,48,1536]{2,1,0:T(8,128)(2,1)S(1)}, bf16[4,48,1536]{2,1,0:T(8,128)(2,1)S(1)}, u32[]{:S(2)}, u32[]{:S(2)}) %collective-permute-start.65) | collective-permute-done | bytes 589856 | tf_op jit(solution)/shard_map/ppermute | solution.py:468
  429.8 11.1 %collective-permute-done.73 = bf16[4,48,1536]{2,1,0:T(8,128)(2,1)S(1)} collective-permute-done((bf16[4,48,1536]{2,1,0:T(8,128)(2,1)S(1)}, bf16[4,48,1536]{2,1,0:T(8,128)(2,1)S(1)}, u32[]{:S(2)}, u32[]{:S(2)}) %collective-permute-start.73) | collective-permute-done | bytes 589856 | tf_op jit(solution)/shard_map/ppermute | solution.py:468
  442.4 11.0 %collective-permute-done.90 = bf16[4,48,1536]{2,1,0:T(8,128)(2,1)S(1)} collective-permute-done((bf16[4,48,1536]{2,1,0:T(8,128)(2,1)S(1)}, bf16[4,48,1536]{2,1,0:T(8,128)(2,1)S(1)}, u32[]{:S(2)}, u32[]{:S(2)}) %collective-permute-start.90) | collective-permute-done | bytes 589856 | tf_op jit(solution)/shard_map/ppermute | solution.py:468
  455.0 23.7 %collective-permute-done.107 = bf16[4,192,384]{2,1,0:T(8,128)(2,1)S(1)} collective-permute-done((bf16[4,192,384]{2,1,0:T(8,128)(2,1)S(1)}, bf16[4,192,384]{2,1,0:T(8,128)(2,1)S(1)}, u32[]{:S(2)}, u32[]{:S(2)}) %collective-permute-start.107) | collective-permute-done | bytes 589856 | tf_op jit(solution)/shard_map/ppermute | solution.py:468
  479.6 11.8 %collective-permute-done.115 = bf16[4,192,384]{2,1,0:T(8,128)(2,1)S(1)} collective-permute-done((bf16[4,192,384]{2,1,0:T(8,128)(2,1)S(1)}, bf16[4,192,384]{2,1,0:T(8,128)(2,1)S(1)}, u32[]{:S(2)}, u32[]{:S(2)}) %collective-permute-start.115) | collective-permute-done | bytes 589856 | tf_op jit(solution)/shard_map/ppermute | solution.py:468
  491.8 3.8 collective-permute-start.67
  528.5 4.9 collective-permute-start.77
  534.9 4.9 collective-permute-start.102
  (653 shorter events, 252.4 us)
Async XLA Ops:
  73.6 38.3 %collective-permute-start.22 = (bf16[4,48,1536]{2,1,0:T(8,128)(2,1)S(1)}, bf16[4,48,1536]{2,1,0:T(8,128)(2,1)S(1)}, u32[]{:S(2)}, u32[]{:S(2)}) collective-permute-start(bf16[4,48,1536]{2,1,0:T(8,128)(2,1)S(1)} %constant_dynamic-slice_fusion.14.own), channel_id=1, source_target_pairs={{0,1},{1,0},{2,3},{3,2},{4,5},{5,4},{6,7},{7,6},{8,9},{9,8},{10,11... | collective-permute-start | bytes 1769480 | tf_op jit(solution)/shard_map/ppermute | solution.py:468
  75.5 36.4 %collective-permute-start.23 = (bf16[4,48,1536]{2,1,0:T(8,128)(2,1)S(1)}, bf16[4,48,1536]{2,1,0:T(8,128)(2,1)S(1)}, u32[]{:S(2)}, u32[]{:S(2)}) collective-permute-start(bf16[4,48,1536]{2,1,0:T(8,128)(2,1)S(1)} %constant_dynamic-slice_fusion.14.own), channel_id=1, source_target_pairs={{0,2},{1,3},{2,0},{3,1},{4,6},{5,7},{6,4},{7,5},{8,10},{9,11},{10,... | collective-permute-start | bytes 1769480 | tf_op jit(solution)/shard_map/ppermute | solution.py:468
  78.7 44.0 %collective-permute-start.31 = (bf16[4,192,384]{2,1,0:T(8,128)(2,1)S(1)}, bf16[4,192,384]{2,1,0:T(8,128)(2,1)S(1)}, u32[]{:S(2)}, u32[]{:S(2)}) collective-permute-start(bf16[4,192,384]{2,1,0:T(8,128)(2,1)S(1)} %constant_dynamic-slice_fusion.13.own), channel_id=1, source_target_pairs={{0,1},{1,0},{2,3},{3,2},{4,5},{5,4},{6,7},{7,6},{8,9},{9,8},{10,11... | collective-permute-start | bytes 1769480 | tf_op jit(solution)/shard_map/ppermute | solution.py:468
  82.8 24.5 %collective-permute-start.16 = (bf16[2,48,1536]{2,1,0:T(8,128)(2,1)S(1)}, bf16[2,48,1536]{2,1,0:T(8,128)(2,1)S(1)}, u32[]{:S(2)}, u32[]{:S(2)}) collective-permute-start(bf16[2,48,1536]{2,1,0:T(8,128)(2,1)S(1)} %slice.554), channel_id=1, source_target_pairs={{0,1},{1,0},{2,3},{3,2},{4,5},{5,4},{6,7},{7,6},{8,9},{9,8},{10,11... | collective-permute-start | bytes 884744 | tf_op jit(solution)/shard_map/ppermute | solution.py:468
  111.9 105.9 %collective-permute-start.17 = (bf16[768,1536]{1,0:T(8,128)(2,1)S(1)}, bf16[768,1536]{1,0:T(8,128)(2,1)}, u32[]{:S(2)}, u32[]{:S(2)}) collective-permute-start(bf16[768,1536]{1,0:T(8,128)(2,1)S(1)} %bitcast.509), channel_id=1, source_target_pairs={{0,16},{16,0},{1,17},{17,1},{2,18},{18,2},{3,19},{19,3},{4,20},{20... | collective-permute-start | bytes 7077896 | tf_op jit(solution)/shard_map/ppermute | solution.py:463
  125.2 25.9 %collective-permute-start.55 = (bf16[4,192,384]{2,1,0:T(8,128)(2,1)}, bf16[4,192,384]{2,1,0:T(8,128)(2,1)}, u32[]{:S(2)}, u32[]{:S(2)}) collective-permute-start(bf16[4,192,384]{2,1,0:T(8,128)(2,1)} %constant_dynamic-slice_fusion.10.own), channel_id=1, source_target_pairs={{0,1},{1,0},{2,3},{3,2},{4,5},{5,4},{6,7},{7,6},{8,9},{9,8},{10,11... | collective-permute-start | bytes 1769480 | tf_op jit(solution)/shard_map/ppermute | solution.py:468
  127.6 25.5 %collective-permute-start.56 = (bf16[4,192,384]{2,1,0:T(8,128)(2,1)}, bf16[4,192,384]{2,1,0:T(8,128)(2,1)}, u32[]{:S(2)}, u32[]{:S(2)}) collective-permute-start(bf16[4,192,384]{2,1,0:T(8,128)(2,1)} %constant_dynamic-slice_fusion.10.own), channel_id=1, source_target_pairs={{0,2},{1,3},{2,0},{3,1},{4,6},{5,7},{6,4},{7,5},{8,10},{9,11},{10,... | collective-permute-start | bytes 1769480 | tf_op jit(solution)/shard_map/ppermute | solution.py:468
  140.4 24.4 %collective-permute-start.25 = (bf16[2,48,1536]{2,1,0:T(8,128)(2,1)S(1)}, bf16[2,48,1536]{2,1,0:T(8,128)(2,1)S(1)}, u32[]{:S(2)}, u32[]{:S(2)}) collective-permute-start(bf16[2,48,1536]{2,1,0:T(8,128)(2,1)S(1)} %slice.557), channel_id=1, source_target_pairs={{0,1},{1,0},{2,3},{3,2},{4,5},{5,4},{6,7},{7,6},{8,9},{9,8},{10,11... | collective-permute-start | bytes 884744 | tf_op jit(solution)/shard_map/ppermute | solution.py:468
  167.3 29.3 %collective-permute-start.49 = (bf16[2,48,1536]{2,1,0:T(8,128)(2,1)}, bf16[2,48,1536]{2,1,0:T(8,128)(2,1)}, u32[]{:S(2)}, u32[]{:S(2)}) collective-permute-start(bf16[2,48,1536]{2,1,0:T(8,128)(2,1)} %slice.568), channel_id=1, source_target_pairs={{0,2},{1,3},{2,0},{3,1},{4,6},{5,7},{6,4},{7,5},{8,10},{9,11},{10,... | collective-permute-start | bytes 884744 | tf_op jit(solution)/shard_map/ppermute | solution.py:468
  173.0 34.5 %collective-permute-start.50 = (bf16[2,48,1536]{2,1,0:T(8,128)(2,1)}, bf16[2,48,1536]{2,1,0:T(8,128)(2,1)}, u32[]{:S(2)}, u32[]{:S(2)}) collective-permute-start(bf16[2,48,1536]{2,1,0:T(8,128)(2,1)} %slice.569), channel_id=1, source_target_pairs={{0,1},{1,0},{2,3},{3,2},{4,5},{5,4},{6,7},{7,6},{8,9},{9,8},{10,11... | collective-permute-start | bytes 884744 | tf_op jit(solution)/shard_map/ppermute | solution.py:468
  173.5 34.2 %collective-permute-start.57 = (bf16[2,192,384]{2,1,0:T(8,128)(2,1)}, bf16[2,192,384]{2,1,0:T(8,128)(2,1)}, u32[]{:S(2)}, u32[]{:S(2)}) collective-permute-start(bf16[2,192,384]{2,1,0:T(8,128)(2,1)} %slice.570), channel_id=1, source_target_pairs={{0,2},{1,3},{2,0},{3,1},{4,6},{5,7},{6,4},{7,5},{8,10},{9,11},{10,... | collective-permute-start | bytes 884744 | tf_op jit(solution)/shard_map/ppermute | solution.py:468
  174.3 43.1 %collective-permute-start = (bf16[256,768]{1,0:T(8,128)(2,1)}, bf16[256,768]{1,0:T(8,128)(2,1)}, u32[]{:S(2)}, u32[]{:S(2)}) collective-permute-start(bf16[256,768]{1,0:T(8,128)(2,1)} %dynamic-slice_bitcast_fusion.12), channel_id=1, source_target_pairs={{0,16},{16,0},{1,17},{17,1},{2,18},{18,2},{3,19},{19,3},{4,20},{20... | collective-permute-start | bytes 1179656 | tf_op jit(solution)/shard_map/ppermute | solution.py:463
  207.5 22.0 %collective-permute-start.26 = (bf16[768,1536]{1,0:T(8,128)(2,1)}, bf16[768,1536]{1,0:T(8,128)(2,1)}, u32[]{:S(2)}, u32[]{:S(2)}) collective-permute-start(bf16[768,1536]{1,0:T(8,128)(2,1)} %bitcast.36.up_mine), channel_id=1, source_target_pairs={{0,16},{16,0},{1,17},{17,1},{2,18},{18,2},{3,19},{19,3},{4,20},{20... | collective-permute-start | bytes 7077896 | tf_op jit(solution)/shard_map/ppermute | solution.py:463
  207.8 21.8 %collective-permute-start.35 = (bf16[3072,384]{1,0:T(8,128)(2,1)}, bf16[3072,384]{1,0:T(8,128)(2,1)}, u32[]{:S(2)}, u32[]{:S(2)}) collective-permute-start(bf16[3072,384]{1,0:T(8,128)(2,1)} %bitcast.43.down_mine), channel_id=1, source_target_pairs={{0,16},{16,0},{1,17},{17,1},{2,18},{18,2},{3,19},{19,3},{4,20},{20... | collective-permute-start | bytes 7077896 | tf_op jit(solution)/shard_map/ppermute | solution.py:463
  214.2 25.3 %collective-permute-start.43 = (bf16[768,1536]{1,0:T(8,128)(2,1)}, bf16[768,1536]{1,0:T(8,128)(2,1)}, u32[]{:S(2)}, u32[]{:S(2)}) collective-permute-start(bf16[768,1536]{1,0:T(8,128)(2,1)} %bitcast.55.mine), channel_id=1, source_target_pairs={{0,16},{16,0},{1,17},{17,1},{2,18},{18,2},{3,19},{19,3},{4,20},{20... | collective-permute-start | bytes 7077896 | tf_op jit(solution)/shard_map/ppermute | solution.py:463
  217.4 30.7 %collective-permute-start.51 = (bf16[768,1536]{1,0:T(8,128)(2,1)}, bf16[768,1536]{1,0:T(8,128)(2,1)}, u32[]{:S(2)}, u32[]{:S(2)}) collective-permute-start(bf16[768,1536]{1,0:T(8,128)(2,1)} %bitcast.60.up_mine), channel_id=1, source_target_pairs={{0,16},{16,0},{1,17},{17,1},{2,18},{18,2},{3,19},{19,3},{4,20},{20... | collective-permute-start | bytes 7077896 | tf_op jit(solution)/shard_map/ppermute | solution.py:463
  217.8 30.3 %collective-permute-start.59 = (bf16[3072,384]{1,0:T(8,128)(2,1)}, bf16[3072,384]{1,0:T(8,128)(2,1)}, u32[]{:S(2)}, u32[]{:S(2)}) collective-permute-start(bf16[3072,384]{1,0:T(8,128)(2,1)} %bitcast.65.down_mine), channel_id=1, source_target_pairs={{0,16},{16,0},{1,17},{17,1},{2,18},{18,2},{3,19},{19,3},{4,20},{20... | collective-permute-start | bytes 7077896 | tf_op jit(solution)/shard_map/ppermute | solution.py:463
  319.6 31.9 %collective-permute-start.61 = (bf16[768,1536]{1,0:T(8,128)(2,1)}, bf16[768,1536]{1,0:T(8,128)(2,1)}, u32[]{:S(2)}, u32[]{:S(2)}) collective-permute-start(bf16[768,1536]{1,0:T(8,128)(2,1)} %get-tuple-element.65), channel_id=1, source_target_pairs={{0,16},{16,0},{1,17},{17,1},{2,18},{18,2},{3,19},{19,3},{4,20},{20... | collective-permute-start | bytes 7077896 | tf_op jit(solution)/shard_map/ppermute | solution.py:463
  326.2 29.6 %collective-permute-start.69 = (bf16[768,1536]{1,0:T(8,128)(2,1)}, bf16[768,1536]{1,0:T(8,128)(2,1)}, u32[]{:S(2)}, u32[]{:S(2)}) collective-permute-start(bf16[768,1536]{1,0:T(8,128)(2,1)} %get-tuple-element.67), channel_id=1, source_target_pairs={{0,16},{16,0},{1,17},{17,1},{2,18},{18,2},{3,19},{19,3},{4,20},{20... | collective-permute-start | bytes 7077896 | tf_op jit(solution)/shard_map/ppermute | solution.py:463
  328.3 21.7 %collective-permute-start.60 = (f32[256,768]{1,0:T(8,128)S(1)}, f32[256,768]{1,0:T(8,128)S(1)}, u32[]{:S(2)}, u32[]{:S(2)}) collective-permute-start(f32[256,768]{1,0:T(8,128)S(1)} %broadcast_select_fusion.2), channel_id=1, source_target_pairs={{0,16},{16,0},{1,17},{17,1},{2,18},{18,2},{3,19},{19,3},{4,20},{20... | collective-permute-start | bytes 2359304 | tf_op jit(solution)/shard_map/ppermute | solution.py:463
  337.1 22.1 %collective-permute-start.86 = (bf16[768,1536]{1,0:T(8,128)(2,1)}, bf16[768,1536]{1,0:T(8,128)(2,1)}, u32[]{:S(2)}, u32[]{:S(2)}) collective-permute-start(bf16[768,1536]{1,0:T(8,128)(2,1)} %get-tuple-element.75), channel_id=1, source_target_pairs={{0,16},{16,0},{1,17},{17,1},{2,18},{18,2},{3,19},{19,3},{4,20},{20... | collective-permute-start | bytes 7077896 | tf_op jit(solution)/shard_map/ppermute | solution.py:463
  341.5 21.8 %collective-permute-start.94 = (bf16[768,1536]{1,0:T(8,128)(2,1)}, bf16[768,1536]{1,0:T(8,128)(2,1)}, u32[]{:S(2)}, u32[]{:S(2)}) collective-permute-start(bf16[768,1536]{1,0:T(8,128)(2,1)} %get-tuple-element.77), channel_id=1, source_target_pairs={{0,16},{16,0},{1,17},{17,1},{2,18},{18,2},{3,19},{19,3},{4,20},{20... | collective-permute-start | bytes 7077896 | tf_op jit(solution)/shard_map/ppermute | solution.py:463
  403.4 24.8 %collective-permute-start.65 = (bf16[4,48,1536]{2,1,0:T(8,128)(2,1)S(1)}, bf16[4,48,1536]{2,1,0:T(8,128)(2,1)S(1)}, u32[]{:S(2)}, u32[]{:S(2)}) collective-permute-start(bf16[4,48,1536]{2,1,0:T(8,128)(2,1)S(1)} %pad_maximum_fusion.1), channel_id=1, source_target_pairs={{0,2},{1,3},{2,0},{3,1},{4,6},{5,7},{6,4},{7,5},{8,10},{9,11},{10,... | collective-permute-start | bytes 1769480 | tf_op jit(solution)/shard_map/ppermute | solution.py:468
  409.8 31.1 %collective-permute-start.73 = (bf16[4,48,1536]{2,1,0:T(8,128)(2,1)S(1)}, bf16[4,48,1536]{2,1,0:T(8,128)(2,1)S(1)}, u32[]{:S(2)}, u32[]{:S(2)}) collective-permute-start(bf16[4,48,1536]{2,1,0:T(8,128)(2,1)S(1)} %pad_maximum_fusion.3), channel_id=1, source_target_pairs={{0,2},{1,3},{2,0},{3,1},{4,6},{5,7},{6,4},{7,5},{8,10},{9,11},{10,... | collective-permute-start | bytes 1769480 | tf_op jit(solution)/shard_map/ppermute | solution.py:468
  414.6 26.5 %collective-permute-start.71 = (bf16[4,48,1536]{2,1,0:T(8,128)(2,1)S(1)}, bf16[4,48,1536]{2,1,0:T(8,128)(2,1)S(1)}, u32[]{:S(2)}, u32[]{:S(2)}) collective-permute-start(bf16[4,48,1536]{2,1,0:T(8,128)(2,1)S(1)} %pad_maximum_fusion.2), channel_id=1, source_target_pairs={{0,1},{1,0},{2,3},{3,2},{4,5},{5,4},{6,7},{7,6},{8,9},{9,8},{10,11... | collective-permute-start | bytes 1769480 | tf_op jit(solution)/shard_map/ppermute | solution.py:468
  416.1 37.4 %collective-permute-start.90 = (bf16[4,48,1536]{2,1,0:T(8,128)(2,1)S(1)}, bf16[4,48,1536]{2,1,0:T(8,128)(2,1)S(1)}, u32[]{:S(2)}, u32[]{:S(2)}) collective-permute-start(bf16[4,48,1536]{2,1,0:T(8,128)(2,1)S(1)} %pad_maximum_fusion.5), channel_id=1, source_target_pairs={{0,2},{1,3},{2,0},{3,1},{4,6},{5,7},{6,4},{7,5},{8,10},{9,11},{10,... | collective-permute-start | bytes 1769480 | tf_op jit(solution)/shard_map/ppermute | solution.py:468
  428.2 25.4 %collective-permute-start.88 = (bf16[4,48,1536]{2,1,0:T(8,128)(2,1)S(1)}, bf16[4,48,1536]{2,1,0:T(8,128)(2,1)S(1)}, u32[]{:S(2)}, u32[]{:S(2)}) collective-permute-start(bf16[4,48,1536]{2,1,0:T(8,128)(2,1)S(1)} %pad_maximum_fusion.4), channel_id=1, source_target_pairs={{0,1},{1,0},{2,3},{3,2},{4,5},{5,4},{6,7},{7,6},{8,9},{9,8},{10,11... | collective-permute-start | bytes 1769480 | tf_op jit(solution)/shard_map/ppermute | solution.py:468
  428.3 50.9 %collective-permute-start.98 = (bf16[4,48,1536]{2,1,0:T(8,128)(2,1)S(1)}, bf16[4,48,1536]{2,1,0:T(8,128)(2,1)S(1)}, u32[]{:S(2)}, u32[]{:S(2)}) collective-permute-start(bf16[4,48,1536]{2,1,0:T(8,128)(2,1)S(1)} %pad_maximum_fusion.7), channel_id=1, source_target_pairs={{0,2},{1,3},{2,0},{3,1},{4,6},{5,7},{6,4},{7,5},{8,10},{9,11},{10,... | collective-permute-start | bytes 1769480 | tf_op jit(solution)/shard_map/ppermute | solution.py:468
  440.8 37.9 %collective-permute-start.107 = (bf16[4,192,384]{2,1,0:T(8,128)(2,1)S(1)}, bf16[4,192,384]{2,1,0:T(8,128)(2,1)S(1)}, u32[]{:S(2)}, u32[]{:S(2)}) collective-permute-start(bf16[4,192,384]{2,1,0:T(8,128)(2,1)S(1)} %pad_maximum_fusion.9), channel_id=1, source_target_pairs={{0,2},{1,3},{2,0},{3,1},{4,6},{5,7},{6,4},{7,5},{8,10},{9,11},{10,... | collective-permute-start | bytes 1769480 | tf_op jit(solution)/shard_map/ppermute | solution.py:468
  441.1 37.8 %collective-permute-start.105 = (bf16[4,192,384]{2,1,0:T(8,128)(2,1)S(1)}, bf16[4,192,384]{2,1,0:T(8,128)(2,1)S(1)}, u32[]{:S(2)}, u32[]{:S(2)}) collective-permute-start(bf16[4,192,384]{2,1,0:T(8,128)(2,1)S(1)} %pad_maximum_fusion.8), channel_id=1, source_target_pairs={{0,1},{1,0},{2,3},{3,2},{4,5},{5,4},{6,7},{7,6},{8,9},{9,8},{10,11... | collective-permute-start | bytes 1769480 | tf_op jit(solution)/shard_map/ppermute | solution.py:468
  453.5 25.8 %collective-permute-start.96 = (bf16[4,48,1536]{2,1,0:T(8,128)(2,1)S(1)}, bf16[4,48,1536]{2,1,0:T(8,128)(2,1)S(1)}, u32[]{:S(2)}, u32[]{:S(2)}) collective-permute-start(bf16[4,48,1536]{2,1,0:T(8,128)(2,1)S(1)} %pad_maximum_fusion.6), channel_id=1, source_target_pairs={{0,1},{1,0},{2,3},{3,2},{4,5},{5,4},{6,7},{7,6},{8,9},{9,8},{10,11... | collective-permute-start | bytes 1769480 | tf_op jit(solution)/shard_map/ppermute | solution.py:468
  453.6 37.8 %collective-permute-start.115 = (bf16[4,192,384]{2,1,0:T(8,128)(2,1)S(1)}, bf16[4,192,384]{2,1,0:T(8,128)(2,1)S(1)}, u32[]{:S(2)}, u32[]{:S(2)}) collective-permute-start(bf16[4,192,384]{2,1,0:T(8,128)(2,1)S(1)} %pad_maximum_fusion.11), channel_id=1, source_target_pairs={{0,2},{1,3},{2,0},{3,1},{4,6},{5,7},{6,4},{7,5},{8,10},{9,11},{10,... | collective-permute-start | bytes 1769480 | tf_op jit(solution)/shard_map/ppermute | solution.py:468
  (150 other events, 1861.6 us)

commit v3 on v2

--- a/solution.py
+++ b/solution.py
@@ -457,6 +457,7 @@
 
 SQUARE = 4
 RING = 4
+LAG = 2
 
 
 def swap_cores(value):
@@ -468,9 +469,10 @@
     return lax.ppermute(value, "dp", [(i, i ^ bit) for i in range(count)])
 
 
-def ring_on(value):
+def shift_ring(value, steps):
     count = lax.axis_size("dp")
-    return lax.ppermute(value, "dp", [(i, (i + SQUARE) % count) for i in range(count)])
+    pairs = [(i, (i + SQUARE * steps) % count) for i in range(count)]
+    return lax.ppermute(value, "dp", pairs)
 
 
 def small_slice():
@@ -507,60 +509,169 @@
     )(spot, *blocks)
 
 
-def gather_rows(piece):
-    rows, columns = piece.shape
+def after(values, earlier):
+    flat, shape = jax.tree.flatten(values)
+    waited = jax.tree.leaves(earlier)
+    if not waited:
+        return values
+    tied = lax.optimization_barrier(tuple(flat) + tuple(waited))
+    return jax.tree.unflatten(shape, tied[: len(flat)])
+
+
+def gather_whole(piece):
+    return lax.all_gather(piece, "dp", axis=0, tiled=True)
+
+
+def column_moved(piece):
+    return [piece] + [shift_ring(piece, steps) for steps in range(1, RING)]
+
+
+def column_kernel(level_ref, *refs):
+    held, out, sems = refs[:RING], refs[RING], refs[RING + 1]
+    level = level_ref[0]
+    copies = [
+        pltpu.make_async_copy(part, out.at[lax.rem(level + RING - steps, RING)], sems.at[steps])
+        for steps, part in enumerate(held)
+    ]
+    for copy in copies:
+        copy.start()
+    for copy in copies:
+        copy.wait()
+
+
+def column_placed(held):
+    level = (lax.axis_index("dp") // SQUARE).astype(jnp.int32).reshape(1)
+    return pl.pallas_call(
+        column_kernel,
+        out_shape=jax.ShapeDtypeStruct((RING,) + held[0].shape, held[0].dtype),
+        in_specs=[pl.BlockSpec(memory_space=pltpu.SMEM)]
+        + [pl.BlockSpec(memory_space=pl.ANY)] * RING,
+        out_specs=pl.BlockSpec(memory_space=pltpu.VMEM),
+        scratch_shapes=[pltpu.SemaphoreType.DMA((RING,))],
+        name="place_column",
+    )(level, *held)
+
+
+def gather_stages(piece, tied):
+    held = column_moved(tied(piece))
+    yield held[1:]
+    column = tied(column_placed(held))
+    first = swap_square(column, 1)
+    second = swap_square(column, 2)
+    yield (first, second)
+    half = RING // 2
+    low, high = tied((first[:half], second[half:]))
+    far_low = swap_square(low, 2)
+    far_high = swap_square(high, 1)
+    yield (far_low, far_high)
+    spot = (lax.axis_index("dp") % SQUARE).astype(jnp.int32).reshape(1)
+    whole = place_blocks(spot, (column, first, second, far_low, far_high))
+    whole = tied(whole.reshape(RING * SQUARE * piece.shape[0], piece.shape[1]))
+    other = swap_cores(whole)
+    yield other
+    return (whole, other)
+
+
+def gather_small(piece):
     if not small_slice():
-        return lax.all_gather(piece, "dp", axis=0, tiled=True)
+        return gather_whole(piece)
+    spot = lax.axis_index("dp") % SQUARE
+    level = lax.axis_index("dp") // SQUARE
+    order = (level - jnp.arange(RING)) % RING
+    column = jnp.take(jnp.stack(column_moved(piece)), order, axis=0)
+    blocks = [column] + [swap_square(column, bit) for bit in range(1, SQUARE)]
+    stacked = jnp.stack(blocks, axis=1)
+    order = jnp.arange(SQUARE) ^ spot
+    return jnp.take(stacked, order, axis=1).reshape(RING * SQUARE * piece.shape[0], -1)
+
+
+def scatter_stages(kept, sent, tied):
+    wire = jnp.bfloat16
+    rows = kept.shape[0] // (RING * SQUARE)
+    columns = kept.shape[1]
     place = lax.axis_index("dp")
     level = place // SQUARE
-    spot = (place % SQUARE).astype(jnp.int32).reshape(1)
-    held = [piece]
-    for _ in range(RING - 1):
-        held.append(ring_on(held[-1]))
-    doubled = jnp.stack([held[3], held[2], held[1], held[0], held[3], held[2], held[1]])
-    column = lax.dynamic_slice_in_dim(doubled, RING - 1 - level, RING, 0)
-    first = swap_square(column, 1)
-    second = swap_square(column, 2)
+    spot = place % SQUARE
+    received = swap_cores(tied(sent))
+    yield received
+    kept = kept.reshape(RING, SQUARE, rows, columns)
+    received = received.reshape(RING, SQUARE, rows, columns)
+
+    def block(index):
+        mine = lax.dynamic_index_in_dim(kept, index, 1, keepdims=False)
+        theirs = lax.dynamic_index_in_dim(received, index, 1, keepdims=False)
+        return mine.astype(jnp.float32) + theirs.astype(jnp.float32)
+
     half = RING // 2
-    far_low = swap_square(first[:half], 2)
-    far_high = swap_square(second[half:], 1)
-    whole = place_blocks(spot, (column, first, second, far_low, far_high))
-    return whole.reshape(RING * SQUARE * rows, columns)
-
-
-def scatter_rows(summed):
-    rows = summed.shape[0] // lax.axis_size("dp")
-    columns = summed.shape[1]
+    far = block(spot ^ 3).astype(wire)
+    low, high = tied((far[:half], far[half:]))
+    far_low = swap_square(low, 1)
+    far_high = swap_square(high, 2)
+    yield (far_low, far_high)
+    first = block(spot ^ 1)
+    second = block(spot ^ 2)
+    first = jnp.concatenate([first[:half], first[half:] + far_high.astype(jnp.float32)])
+    second = jnp.concatenate([second[:half] + far_low.astype(jnp.float32), second[half:]])
+    first, second = tied((first.astype(wire), second.astype(wire)))
+    from_first = swap_square(first, 1)
+    from_second = swap_square(second, 2)
+    yield (from_first, from_second)
+    column = block(spot) + from_first.astype(jnp.float32) + from_second.astype(jnp.float32)
+    column = [lax.dynamic_index_in_dim(column, (level + steps) % RING, 0, keepdims=False) for steps in range(RING)]
+    moving = tied(tuple(part.astype(wire) for part in column[1:]))
+    moved = [shift_ring(part, steps + 1) for steps, part in enumerate(moving)]
+    yield tuple(moved)
+    total = column[0]
+    for part in moved:
+        total = total + part.astype(jnp.float32)
+    return total
+
+
+def scatter_small(kept, sent):
+    summed = kept + swap_cores(sent)
     if not small_slice():
         return lax.psum_scatter(summed, "dp", scatter_dimension=0, tiled=True)
     place = lax.axis_index("dp")
     level = place // SQUARE
     spot = place % SQUARE
-    blocks = summed.reshape(RING, SQUARE, rows, columns)
+    blocks = summed.reshape(RING, SQUARE, -1)
 
     def block(index):
         return lax.dynamic_index_in_dim(blocks, index, 1, keepdims=False)
 
-    half = RING // 2
-    wire = jnp.bfloat16
-    far = block(spot ^ 3).astype(wire)
-    far_low = swap_square(far[:half], 1)
-    far_high = swap_square(far[half:], 2)
-    first = block(spot ^ 1)
-    second = block(spot ^ 2)
-    first = jnp.concatenate([first[:half], first[half:] + far_high.astype(jnp.float32)])
-    second = jnp.concatenate([second[:half] + far_low.astype(jnp.float32), second[half:]])
-    from_first = swap_square(first.astype(wire), 1)
-    from_second = swap_square(second.astype(wire), 2)
-    column = block(spot) + from_first.astype(jnp.float32) + from_second.astype(jnp.float32)
-
-    def rung(back):
-        return lax.dynamic_index_in_dim(column, (level - back) % RING, 0, keepdims=False)
-
-    travelling = rung(1)
-    for step in range(1, RING):
-        travelling = ring_on(travelling.astype(wire)).astype(jnp.float32) + rung(step + 1)
-    return travelling
+    column = block(spot)
+    for bit in range(1, SQUARE):
+        column = column + swap_square(block(spot ^ bit), bit)
+    total = lax.dynamic_index_in_dim(column, level, 0, keepdims=True)
+    for steps in range(1, RING):
+        part = lax.dynamic_index_in_dim(column, (level + steps) % RING, 0, keepdims=True)
+        total = total + shift_ring(part, steps)
+    return total
+
+
+class Rounds:
+    def __init__(self, lag):
+        self.lag = lag
+        self.made = []
+        self.current = []
+
+    def tied(self, values):
+        at = len(self.made) - self.lag
+        return after(values, self.made[at]) if at >= 0 else values
+
+    def note(self, values):
+        self.current.append(values)
+
+    def close(self):
+        self.made.append(self.current)
+        self.current = []
+
+
+def advance(stages, rounds, results, name):
+    try:
+        rounds.note(next(stages))
+    except StopIteration as ended:
+        results[name] = ended.value
 
 
 def half_of(array, which):
@@ -635,7 +746,7 @@
         [a[0].reshape(-1) for a in (qkv_bias, up_bias, out_biases, norm_gains, norm_biases)]
     )
     small_both = jnp.concatenate(ordered(is_first, small_own, swap_cores(small_own)))
-    small_full = gather_rows(small_both[None])
+    small_full = gather_small(small_both[None])
     small_full = small_full.reshape(count, 2, small_own.shape[0]).astype(jnp.float32)
 
     def small_of(layer):
@@ -660,63 +771,130 @@
             norms=jnp.concatenate([gains, shifts]),
         )
 
-    gathered = []
-    for layer in range(2):
-        found = []
-        for piece in pieces:
-            mine = gather_rows(piece[layer])
-            found.append((mine, swap_cores(mine)))
-        gathered.append(found)
     small = [small_of(layer) for layer in range(2)]
-
-    def forward(rows, layer, kind):
-        narrow, up, down = gathered[layer]
-        qkv, logs, attended, passed = attn_forward(side, rows, tables, mask, small[layer], *narrow)
-        active, slope, produced = mlp_forward(
-            side, rows, passed, small[layer], up + down, kind
+    flat_pieces = [piece[layer] for layer in range(2) for piece in pieces]
+    kept_forward = {}
+
+    def attn_step(layer, rows, weights):
+        kept_forward[layer, "rows"] = rows
+        made = attn_forward(side, rows, tables, mask, small[layer], *weights)
+        kept_forward[layer, "attn"] = made
+        return made
+
+    def mlp_step(layer, up, down, kind):
+        passed = kept_forward[layer, "attn"][3]
+        rows = kept_forward[layer, "rows"]
+        made = mlp_forward(side, rows, passed, small[layer], up + down, kind)
+        kept_forward[layer, "mlp"] = made
+        return made
+
+    def mlp_back(layer, grad):
+        rows = kept_forward[layer, "rows"]
+        return mlp_backward(
+            side, rows, grad, small[layer], kept_forward[layer, "mlp"][:2],
+            gathered[layer][1] + gathered[layer][2],
         )
-        return (produced, (qkv, logs, attended), (active, slope))
-
-    def backward(rows, grad, layer, attn_saved, mlp_saved, kind):
-        narrow, up, down = gathered[layer]
-        up_kept, up_sent, down_kept, down_sent, bias_up, grad_mlp = mlp_backward(
-            side, rows, grad, small[layer], mlp_saved, up + down
+
+    def attn_back(layer, grad, grad_mlp, kind):
+        return attn_backward(
+            side, kept_forward[layer, "rows"], grad, tables, mask, small[layer],
+            kept_forward[layer, "attn"][:3], grad_mlp, *gathered[layer][0], kind,
         )
-        kept, sent, bias_qkv, sums, passed = attn_backward(
-            side, rows, grad, tables, mask, small[layer], attn_saved, grad_mlp, *narrow, kind
-        )
+
+    def vectors_of(bias_qkv, bias_up, sums):
         bias_qkv = jnp.where(is_first, bias_qkv, bias_qkv[::-1])
         bias_qkv = bias_qkv.reshape(2, 3, width).transpose(1, 0, 2).reshape(1, 6 * width)
-        vectors = (
-            bias_qkv,
-            bias_up,
-            jnp.concatenate([sums[4:5], sums[4:5]]),
-            sums[0:2],
-            sums[2:4],
-        )
-        return (passed, ((down_kept, down_sent), (up_kept, up_sent), (kept, sent)), vectors)
-
-    middle, attn_lower, mlp_lower = forward(entry, 0, jnp.bfloat16)
-    produced, attn_upper, mlp_upper = forward(middle, 1, jnp.float32)
-    grad_middle, grads_upper, vectors_upper = backward(
-        middle, cotangent, 1, attn_upper, mlp_upper, jnp.bfloat16
-    )
-    grad_entry, grads_lower, vectors_lower = backward(
-        entry, grad_middle, 0, attn_lower, mlp_lower, jnp.float32
-    )
-
-    def reduce_half(kept, sent):
-        return scatter_rows(kept.astype(jnp.float32) + swap_cores(sent).astype(jnp.float32))
-
-    reduced_upper = [reduce_half(*pair) for pair in grads_upper]
-    reduced_lower = [reduce_half(*pair) for pair in grads_lower]
+        double = jnp.concatenate([sums[4:5], sums[4:5]])
+        return (bias_qkv, bias_up, double, sums[0:2], sums[2:4])
+
+    whole = {}
+    if small_slice():
+        rounds = Rounds(LAG)
+        tied = rounds.tied
+        chunks = [gather_stages(piece, tied) for piece in flat_pieces]
+        for turn in range(len(chunks) + 4):
+            for index in range(len(chunks)):
+                if index <= turn <= index + 4:
+                    advance(chunks[index], rounds, whole, index)
+            if turn == 4:
+                rounds.note(attn_step(0, entry, whole[0]))
+            if turn == 6:
+                rounds.note(mlp_step(0, whole[1], whole[2], jnp.bfloat16))
+            if turn == 7:
+                middle = kept_forward[0, "mlp"][2]
+                rounds.note(attn_step(1, middle, whole[3]))
+            rounds.close()
+        mlp_step(1, whole[4], whole[5], jnp.float32)
+    else:
+        for index, piece in enumerate(flat_pieces):
+            mine = gather_whole(piece)
+            whole[index] = (mine, swap_cores(mine))
+        attn_step(0, entry, whole[0])
+        mlp_step(0, whole[1], whole[2], jnp.bfloat16)
+        attn_step(1, kept_forward[0, "mlp"][2], whole[3])
+        mlp_step(1, whole[4], whole[5], jnp.float32)
+    gathered = [[whole[0], whole[1], whole[2]], [whole[3], whole[4], whole[5]]]
+    produced = kept_forward[1, "mlp"][2]
+
+    reduced = {}
+    if small_slice():
+        rounds = Rounds(LAG)
+        tied = rounds.tied
+        stages = {}
+        plan = {
+            "down1": (0, 1, 2, 3, 4),
+            "up1": (0, 1, 3, 4, 5),
+            "narrow1": (1, 2, 4, 5, 6),
+            "down0": (2, 3, 5, 6, 7),
+            "up0": (2, 4, 6, 7, 8),
+            "narrow0": (3, 5, 7, 8, 9),
+        }
+        upper = mlp_back(1, cotangent)
+        stages["down1"] = scatter_stages(upper[2], upper[3], tied)
+        stages["up1"] = scatter_stages(upper[0], upper[1], tied)
+        for turn in range(10):
+            for name, when in plan.items():
+                if turn in when:
+                    advance(stages[name], rounds, reduced, name)
+            if turn == 0:
+                upper_attn = attn_back(1, cotangent, upper[5], jnp.bfloat16)
+                stages["narrow1"] = scatter_stages(upper_attn[0], upper_attn[1], tied)
+                rounds.note(upper_attn)
+            if turn == 1:
+                lower = mlp_back(0, upper_attn[4])
+                stages["down0"] = scatter_stages(lower[2], lower[3], tied)
+                stages["up0"] = scatter_stages(lower[0], lower[1], tied)
+                rounds.note(lower)
+            if turn == 2:
+                lower_attn = attn_back(0, upper_attn[4], lower[5], jnp.float32)
+                stages["narrow0"] = scatter_stages(lower_attn[0], lower_attn[1], tied)
+                rounds.note(lower_attn)
+            rounds.close()
+    else:
+        upper = mlp_back(1, cotangent)
+        upper_attn = attn_back(1, cotangent, upper[5], jnp.bfloat16)
+        lower = mlp_back(0, upper_attn[4])
+        lower_attn = attn_back(0, upper_attn[4], lower[5], jnp.float32)
+        for layer, mlp, attn in ((1, upper, upper_attn), (0, lower, lower_attn)):
+            for name, kept, sent in (
+                ("down", mlp[2], mlp[3]),
+                ("up", mlp[0], mlp[1]),
+                ("narrow", attn[0], attn[1]),
+            ):
+                summed = kept.astype(jnp.float32) + swap_cores(sent).astype(jnp.float32)
+                reduced[name + str(layer)] = lax.psum_scatter(
+                    summed, "dp", scatter_dimension=0, tiled=True
+                )
+    grad_entry = lower_attn[4]
+    vectors_upper = vectors_of(upper_attn[2], upper[4], upper_attn[3])
+    vectors_lower = vectors_of(lower_attn[2], lower[4], lower_attn[3])
 
     def finish(lower, upper):
         mine, leaving = ordered(is_first, lower, upper)
         return ordered(is_first, mine, swap_cores(leaving))
 
     down_halves, up_halves, narrow_halves = (
-        finish(*pair) for pair in zip(reduced_lower, reduced_upper)
+        finish(reduced[name + "0"], reduced[name + "1"]) for name in ("down", "up", "narrow")
     )
     total_down = jnp.concatenate(down_halves, axis=1)
     total_up = jnp.concatenate(up_halves, axis=1)
@@ -740,7 +918,7 @@
     small_kept, small_sent = ordered(
         is_first, small_rows(vectors_lower), small_rows(vectors_upper)
     )
-    small_total = scatter_rows(small_kept + swap_cores(small_sent))[0]
+    small_total = scatter_small(small_kept, small_sent)[0]
     small_outs = []
     at = 0
     for shape in small_shapes:

time: 553 us -> 529 us (0.957)
  waiting for transfers between devices: 234 us -> 158 us
  starting transfers between devices: 122 us -> 175 us
  Pallas kernels: 105 us -> 116 us
  other arithmetic: 30.8 us -> 23.5 us
    ppermute x56 -> x54, waiting for transfers between devices: 142 us -> 90.3 us  [swap_square(): return lax.ppermute(value, 'dp', [(i, i ^ bit) for i in range(count)])]
    ppermute x42, starting transfers between devices: 14.1 us -> 65.1 us  [shift_ring(): return lax.ppermute(value, 'dp', pairs)]
    ppermute x42, waiting for transfers between devices: 91.2 us -> 67 us  [shift_ring(): return lax.ppermute(value, 'dp', pairs)]
    pallas_call x0 -> x6, Pallas kernels: none -> 12 us  [column_placed(): pl.pallas_call(column_kernel, out_shape=jax.ShapeDtypeStruct((RING,) + he...]
    ppermute x56 -> x54, starting transfers between devices: 44.8 us -> 48.2 us  [swap_square(): return lax.ppermute(value, 'dp', [(i, i ^ bit) for i in range(count)])]
    slice x38 -> x34, local copies, waits for them, and re-layouts: 11.9 us -> 14.4 us  [the longest x12 13.7 us: gather_stages(): low, high = tied((first[:half], second[half:]))]
    unnamed x177 -> x134, local copies, waits for them, and re-layouts: 18.3 us -> 20.2 us
    pallas_call x7 -> x6, Pallas kernels: 13.8 us -> 13.4 us  [place_blocks(): pl.pallas_call(place_kernel, out_shape=jax.ShapeDtypeStruct((RING, SQUARE...]
  transfers between devices with their start and end apart: 120 -> 118, of which waited for: 54 -> 39; matrix products, arithmetic and copies ran while one was open for 10% -> 9% of each run, Pallas kernels for 7% -> 15%
where the time goes in v3:
time: 529 us; the launch traced here: 522 us
  starting transfers between devices  175 us (33%)
  waiting for transfers between devices  158 us (30%)
  Pallas kernels  116 us (22%)
  local copies, waits for them, and re-layouts  47.5 us (9%)
  other arithmetic  23.5 us (4%)
    ppermute x54, waiting for transfers between devices, swap_square(): return lax.ppermute(value, 'dp', [(i, i ^ bit) for i in range(count)])  90.3 us
    ppermute x42, waiting for transfers between devices, shift_ring(): return lax.ppermute(value, 'dp', pairs)  67 us
    ppermute x42, starting transfers between devices, shift_ring(): return lax.ppermute(value, 'dp', pairs)  65.1 us
    ppermute x22, starting transfers between devices, swap_cores(): return lax.ppermute(value, 'section', [(0, 1), (1, 0)])  61.3 us
    ppermute x54, starting transfers between devices, swap_square(): return lax.ppermute(value, 'dp', [(i, i ^ bit) for i in range(count)])  48.2 us
    pallas_call x2, Pallas kernels, mlp_backward(): pl.pallas_call(mlp_backward_kernel, out_shape=(jax.ShapeDtypeStruct((feat...  29.9 us
    pallas_call x2, Pallas kernels, attn_backward(): pl.pallas_call(attn_backward_kernel, out_shape=(jax.ShapeDtypeStruct(mine...  24.9 us
    unnamed x134, local copies, waits for them, and re-layouts  20.2 us
  transfers between devices with their start and end apart: 118, of which 39 were waited for; matrix products, arithmetic and copies ran while one was open for 9% of the time, Pallas kernels for 15%

profile of v3, /device:TPU:1, one launch (start us, length us, event | category | flops | bytes accessed | tf_op | source)
XLA Modules:
  0.0 522.2 jit_solution(5611391118832232386)
XLA Ops:
  13.6 6.8 %collective-permute-done.10.refs_2_ = bf16[48,1536]{1,0:T(8,128)(2,1)S(1)} collective-permute-done((bf16[48,1536]{1,0:T(8,128)(2,1)S(1)}, bf16[48,1536]{1,0:T(8,128)(2,1)S(1)}, u32[]{:S(2)}, u32[]{:S(2)}) %collective-permute-start.10) | collective-permute-done | bytes 147488 | tf_op jit(solution)/shard_map/ppermute | solution.py:475
  32.5 4.4 collective-permute-start.1
  47.5 4.6 collective-permute-start.4
  52.1 13.0 %collective-permute-done.14.far_low = bf16[2,48,1536]{2,1,0:T(8,128)(2,1)S(1)} collective-permute-done((bf16[2,48,1536]{2,1,0:T(8,128)(2,1)S(1)}, bf16[2,48,1536]{2,1,0:T(8,128)(2,1)S(1)}, u32[]{:S(2)}, u32[]{:S(2)}) %collective-permute-start.14) | collective-permute-done | bytes 294944 | tf_op jit(solution)/shard_map/ppermute | solution.py:469
  107.9 6.5 %collective-permute-done.35.refs_2_ = bf16[48,1536]{1,0:T(8,128)(2,1)} collective-permute-done((bf16[48,1536]{1,0:T(8,128)(2,1)S(1)}, bf16[48,1536]{1,0:T(8,128)(2,1)}, u32[]{:S(2)}, u32[]{:S(2)}) %collective-permute-start.35) | collective-permute-done | bytes 147488 | tf_op jit(solution)/shard_map/ppermute | solution.py:475
  114.5 5.0 collective-permute-done.36.refs_3_
  127.7 7.7 %collective-permute-done.38.first = bf16[4,48,1536]{2,1,0:T(8,128)(2,1)} collective-permute-done((bf16[4,48,1536]{2,1,0:T(8,128)(2,1)}, bf16[4,48,1536]{2,1,0:T(8,128)(2,1)}, u32[]{:S(2)}, u32[]{:S(2)}) %collective-permute-start.38) | collective-permute-done | bytes 589856 | tf_op jit(solution)/shard_map/ppermute | solution.py:469
  153.9 4.5 collective-permute-start.37
  159.3 8.0 %attn_forward.2 = (bf16[2,256,1152]{2,1,0:T(8,128)(2,1)S(1)}, f32[2,6,256]{2,1,0:T(8,128)S(1)}, bf16[256,768]{1,0:T(8,128)(2,1)S(1)}, f32[256,768]{1,0:T(8,128)S(1)}) custom-call(s32[1]{0:T(128)} %bitcast.side, bf16[256,768]{1,0:T(8,128)(2,1)S(1)} %get-tuple-element.271.rows, f32[3,256,128]{2,1,0:T(8,128)S(1)} %pad_maximum_fusion.12.tables, ...), custom_call_target="tpu_custom_call" | custom-call | flops 1509949440 | bytes 4718592 | tf_op jit(solution)/shard_map/attn_forward/pallas_call | solution.py:146
  175.8 5.3 %collective-permute-done.50.refs_1_ = bf16[192,384]{1,0:T(8,128)(2,1)} collective-permute-done((bf16[192,384]{1,0:T(8,128)(2,1)}, bf16[192,384]{1,0:T(8,128)(2,1)}, u32[]{:S(2)}, u32[]{:S(2)}) %collective-permute-start.50) | collective-permute-done | bytes 147488 | tf_op jit(solution)/shard_map/ppermute | solution.py:475
  181.2 5.8 %collective-permute-done.51.refs_2_ = bf16[192,384]{1,0:T(8,128)(2,1)} collective-permute-done((bf16[192,384]{1,0:T(8,128)(2,1)}, bf16[192,384]{1,0:T(8,128)(2,1)}, u32[]{:S(2)}, u32[]{:S(2)}) %collective-permute-start.51) | collective-permute-done | bytes 147488 | tf_op jit(solution)/shard_map/ppermute | solution.py:475
  193.4 6.8 %collective-permute-done.47.second = bf16[4,48,1536]{2,1,0:T(8,128)(2,1)} collective-permute-done((bf16[4,48,1536]{2,1,0:T(8,128)(2,1)}, bf16[4,48,1536]{2,1,0:T(8,128)(2,1)}, u32[]{:S(2)}, u32[]{:S(2)}) %collective-permute-start.47) | collective-permute-done | bytes 589856 | tf_op jit(solution)/shard_map/ppermute | solution.py:469
  206.9 5.9 %collective-permute-done.55.second = bf16[4,192,384]{2,1,0:T(8,128)(2,1)S(1)} collective-permute-done((bf16[4,192,384]{2,1,0:T(8,128)(2,1)}, bf16[4,192,384]{2,1,0:T(8,128)(2,1)S(1)}, u32[]{:S(2)}, u32[]{:S(2)}) %collective-permute-start.55) | collective-permute-done | bytes 589856 | tf_op jit(solution)/shard_map/ppermute | solution.py:469
  223.3 5.4 %collective-permute-start.53 = (bf16[768,1536]{1,0:T(8,128)(2,1)}, bf16[768,1536]{1,0:T(8,128)(2,1)}, u32[]{:S(2)}, u32[]{:S(2)}) collective-permute-start(bf16[768,1536]{1,0:T(8,128)(2,1)} %bitcast.49.up_mine), channel_id=1, source_target_pairs={{0,16},{16,0},{1,17},{17,1},{2,18},{18,2},{3,19},{19,3},{4,20},{20... | collective-permute-start | bytes 7077896 | tf_op jit(solution)/shard_map/ppermute | solution.py:464
  228.6 9.7 %mlp_forward.2 = (bf16[256,3072]{1,0:T(8,128)(2,1)S(1)}, f32[256,3072]{1,0:T(8,128)}, bf16[256,768]{1,0:T(8,128)(2,1)S(1)}) custom-call(s32[1]{0:T(128)} %bitcast.side, bf16[256,768]{1,0:T(8,128)(2,1)S(1)} %get-tuple-element.271.rows, f32[256,768]{1,0:T(8,128)S(1)} %copy-done.23, f32[4,768]{1,0:T(4,128)S(1)} %pad_maximum_fusion.15.norms, ...), custom_call_target="tpu_custom_call" | custom-call | flops 2415919104 | bytes 14155776 | tf_op jit(solution)/shard_map/mlp_forward/pallas_call | solution.py:224
  244.5 8.0 %attn_forward.3 = (bf16[2,256,1152]{2,1,0:T(8,128)(2,1)S(1)}, f32[2,6,256]{2,1,0:T(8,128)S(1)}, bf16[256,768]{1,0:T(8,128)(2,1)S(1)}, f32[256,768]{1,0:T(8,128)S(1)}) custom-call(s32[1]{0:T(128)} %bitcast.side, bf16[256,768]{1,0:T(8,128)(2,1)S(1)} %copy-done.13, f32[3,256,128]{2,1,0:T(8,128)S(1)} %pad_maximum_fusion.12.tables, f32[256,256]{1,0:T(8,128)S(1)} %fusion.55.mask, ...), custom_call_target="tpu_custom_call" | custom-call | flops 1509949440 | bytes 4718592 | tf_op jit(solution)/shard_map/attn_forward/pallas_call | solution.py:146
  252.5 9.8 %mlp_forward.3 = (bf16[256,3072]{1,0:T(8,128)(2,1)S(1)}, f32[256,3072]{1,0:T(8,128)}, f32[256,768]{1,0:T(8,128)S(1)}) custom-call(s32[1]{0:T(128)} %bitcast.side, bf16[256,768]{1,0:T(8,128)(2,1)S(1)} %copy-done.13, f32[256,768]{1,0:T(8,128)S(1)} %get-tuple-element.140.passed, f32[4,768]{1,0:T(4,128)S(1)} %pad_maximum_fusion.16.norms, ...), custom_call_target="tpu_custom_call" | custom-call | flops 2415919104 | bytes 14155776 | tf_op jit(solution)/shard_map/mlp_forward/pallas_call | solution.py:224
  262.4 14.8 %mlp_backward.2 = (bf16[768,1536]{1,0:T(8,128)(2,1)S(1)}, bf16[768,1536]{1,0:T(8,128)(2,1)}, bf16[3072,384]{1,0:T(8,128)(2,1)}, bf16[3072,384]{1,0:T(8,128)(2,1)...) custom-call(s32[1]{0:T(128)} %bitcast.side, bf16[256,768]{1,0:T(8,128)(2,1)S(1)} %copy-done.13, ...), custom_call_target="tpu_custom_call" | custom-call | flops 4831838208 | bytes 23592960 | tf_op jit(solution)/shard_map/mlp_backward/pallas_call | solution.py:316
  278.6 12.4 %attn_backward.2 = (bf16[768,1536]{1,0:T(8,128)(2,1)}, bf16[768,1536]{1,0:T(8,128)(2,1)}, f32[2,1152]{1,0:T(2,128)S(1)}, f32[5,768]{1,0:T(8,128)S(1)}, bf16[256,768]{1,0:T(8,128)(2,1)S(1)}) custom-call(s32[1]{0:T(128)} %bitcast.side, bf16[256,768]{1,0:T(8,128)(2,1)S(1)} %copy-done.13, bf16[256,768]{1,0:T(8,128)(2,1)S(1)} %copy-done.24, ...), custom_call_target="tpu_custom_call" | custom-call | flops 3623878656 | bytes 9437184 | tf_op jit(solution)/shard_map/attn_backward/pallas_call | solution.py:434
  295.2 15.1 %mlp_backward.3 = (bf16[768,1536]{1,0:T(8,128)(2,1)S(1)}, bf16[768,1536]{1,0:T(8,128)(2,1)}, bf16[3072,384]{1,0:T(8,128)(2,1)}, bf16[3072,384]{1,0:T(8,128)(2,1)...) custom-call(s32[1]{0:T(128)} %bitcast.side, bf16[256,768]{1,0:T(8,128)(2,1)S(1)} %get-tuple-element.271.rows, ...), custom_call_target="tpu_custom_call" | custom-call | flops 4831838208 | bytes 23592960 | tf_op jit(solution)/shard_map/mlp_backward/pallas_call | solution.py:316
  311.7 12.4 %attn_backward.3 = (bf16[768,1536]{1,0:T(8,128)(2,1)}, bf16[768,1536]{1,0:T(8,128)(2,1)}, f32[2,1152]{1,0:T(2,128)S(1)}, f32[5,768]{1,0:T(8,128)S(1)}, f32[256,768]{1,0:T(8,128)S(1)}) custom-call(s32[1]{0:T(128)} %bitcast.side, bf16[256,768]{1,0:T(8,128)(2,1)S(1)} %get-tuple-element.271.rows, bf16[256,768]{1,0:T(8,128)(2,1)S(1)} %get-tuple-element.155.grad, ...), custom_call_target="tpu_custom_call" | custom-call | flops 3623878656 | bytes 9437184 | tf_op jit(solution)/shard_map/attn_backward/pallas_call | solution.py:434
  340.6 4.0 collective-permute-start.66
  366.0 4.9 collective-permute-start.82
  374.4 12.1 %collective-permute-done.69 = bf16[4,192,384]{2,1,0:T(8,128)(2,1)S(1)} collective-permute-done((bf16[4,192,384]{2,1,0:T(8,128)(2,1)S(1)}, bf16[4,192,384]{2,1,0:T(8,128)(2,1)S(1)}, u32[]{:S(2)}, u32[]{:S(2)}) %collective-permute-start.69) | collective-permute-done | bytes 589856 | tf_op jit(solution)/shard_map/ppermute | solution.py:469
  386.7 5.6 %collective-permute-start.67 = (bf16[768,1536]{1,0:T(8,128)(2,1)S(1)}, bf16[768,1536]{1,0:T(8,128)(2,1)S(1)}, u32[]{:S(2)}, u32[]{:S(2)}) collective-permute-start(bf16[768,1536]{1,0:T(8,128)(2,1)S(1)} %copy-done.57), channel_id=1, source_target_pairs={{0,16},{16,0},{1,17},{17,1},{2,18},{18,2},{3,19},{19,3},{4,20},{20... | collective-permute-start | bytes 7077896 | tf_op jit(solution)/shard_map/ppermute | solution.py:464
  422.3 9.3 %collective-permute-done.78 = bf16[2,48,1536]{2,1,0:T(8,128)(2,1)S(1)} collective-permute-done((bf16[2,48,1536]{2,1,0:T(8,128)(2,1)S(1)}, bf16[2,48,1536]{2,1,0:T(8,128)(2,1)S(1)}, u32[]{:S(2)}, u32[]{:S(2)}) %collective-permute-start.78) | collective-permute-done | bytes 294944 | tf_op jit(solution)/shard_map/ppermute | solution.py:469
  433.8 7.6 %collective-permute-done.79 = bf16[2,48,1536]{2,1,0:T(8,128)(2,1)S(1)} collective-permute-done((bf16[2,48,1536]{2,1,0:T(8,128)(2,1)S(1)}, bf16[2,48,1536]{2,1,0:T(8,128)(2,1)S(1)}, u32[]{:S(2)}, u32[]{:S(2)}) %collective-permute-start.79) | collective-permute-done | bytes 294944 | tf_op jit(solution)/shard_map/ppermute | solution.py:469
  441.3 5.4 %collective-permute-start.94 = (bf16[48,1536]{1,0:T(8,128)(2,1)S(1)}, bf16[48,1536]{1,0:T(8,128)(2,1)S(1)}, u32[]{:S(2)}, u32[]{:S(2)}) collective-permute-start(bf16[48,1536]{1,0:T(8,128)(2,1)S(1)} %get-tuple-element.203), channel_id=1, source_target_pairs={{0,12},{1,13},{2,14},{3,15},{4,0},{5,1},{6,2},{7,3},{8,4},{9,5},{1... | collective-permute-start | bytes 442376 | tf_op jit(solution)/shard_map/ppermute | solution.py:475
  461.0 4.5 collective-permute-start.90
  471.5 7.3 %collective-permute-start.99 = (bf16[192,384]{1,0:T(8,128)(2,1)S(1)}, bf16[192,384]{1,0:T(8,128)(2,1)S(1)}, u32[]{:S(2)}, u32[]{:S(2)}) collective-permute-start(bf16[192,384]{1,0:T(8,128)(2,1)S(1)} %get-tuple-element.208), channel_id=1, source_target_pairs={{0,12},{1,13},{2,14},{3,15},{4,0},{5,1},{6,2},{7,3},{8,4},{9,5},{1... | collective-permute-start | bytes 442376 | tf_op jit(solution)/shard_map/ppermute | solution.py:475
  484.8 14.1 %collective-permute-start.117 = (f32[192,384]{1,0:T(8,128)S(1)}, f32[192,384]{1,0:T(8,128)S(1)}, u32[]{:S(2)}, u32[]{:S(2)}) collective-permute-start(f32[192,384]{1,0:T(8,128)S(1)} %get-tuple-element.223), channel_id=1, source_target_pairs={{0,16},{16,0},{1,17},{17,1},{2,18},{18,2},{3,19},{19,3},{4,20},{20... | collective-permute-start | bytes 884744 | tf_op jit(solution)/shard_map/ppermute | solution.py:464
  508.9 9.9 %collective-permute-done.103 = bf16[48,1536]{1,0:T(8,128)(2,1)S(1)} collective-permute-done((bf16[48,1536]{1,0:T(8,128)(2,1)S(1)}, bf16[48,1536]{1,0:T(8,128)(2,1)S(1)}, u32[]{:S(2)}, u32[]{:S(2)}) %collective-permute-start.103) | collective-permute-done | bytes 147488 | tf_op jit(solution)/shard_map/ppermute | solution.py:475
  (581 shorter events, 262.9 us)
Async XLA Ops:
  2.8 22.7 %collective-permute-start.16 = (bf16[48,1536]{1,0:T(8,128)(2,1)S(1)}, bf16[48,1536]{1,0:T(8,128)(2,1)S(1)}, u32[]{:S(2)}, u32[]{:S(2)}) collective-permute-start(bf16[48,1536]{1,0:T(8,128)(2,1)S(1)} %dynamic-slice_bitcast_fusion.2), channel_id=1, source_target_pairs={{0,16},{16,0},{1,17},{17,1},{2,18},{18,2},{3,19},{19,3},{4,20},{20... | collective-permute-start | bytes 442376 | tf_op jit(solution)/shard_map/ppermute | solution.py:464
  23.0 21.5 %collective-permute-start.12 = (bf16[4,48,1536]{2,1,0:T(8,128)(2,1)}, bf16[4,48,1536]{2,1,0:T(8,128)(2,1)S(1)}, u32[]{:S(2)}, u32[]{:S(2)}) collective-permute-start(bf16[4,48,1536]{2,1,0:T(8,128)(2,1)} %place_column.6.own), channel_id=1, source_target_pairs={{0,1},{1,0},{2,3},{3,2},{4,5},{5,4},{6,7},{7,6},{8,9},{9,8},{10,11... | collective-permute-start | bytes 1769480 | tf_op jit(solution)/shard_map/ppermute | solution.py:469
  24.3 20.5 %collective-permute-start.13 = (bf16[4,48,1536]{2,1,0:T(8,128)(2,1)}, bf16[4,48,1536]{2,1,0:T(8,128)(2,1)S(1)}, u32[]{:S(2)}, u32[]{:S(2)}) collective-permute-start(bf16[4,48,1536]{2,1,0:T(8,128)(2,1)} %place_column.6.own), channel_id=1, source_target_pairs={{0,2},{1,3},{2,0},{3,1},{4,6},{5,7},{6,4},{7,5},{8,10},{9,11},{10,... | collective-permute-start | bytes 1769480 | tf_op jit(solution)/shard_map/ppermute | solution.py:469
  44.2 32.8 %collective-permute-start.21 = (bf16[4,48,1536]{2,1,0:T(8,128)(2,1)}, bf16[4,48,1536]{2,1,0:T(8,128)(2,1)}, u32[]{:S(2)}, u32[]{:S(2)}) collective-permute-start(bf16[4,48,1536]{2,1,0:T(8,128)(2,1)} %place_column.7.own), channel_id=1, source_target_pairs={{0,1},{1,0},{2,3},{3,2},{4,5},{5,4},{6,7},{7,6},{8,9},{9,8},{10,11... | collective-permute-start | bytes 1769480 | tf_op jit(solution)/shard_map/ppermute | solution.py:469
  44.6 37.0 %collective-permute-start.22 = (bf16[4,48,1536]{2,1,0:T(8,128)(2,1)}, bf16[4,48,1536]{2,1,0:T(8,128)(2,1)}, u32[]{:S(2)}, u32[]{:S(2)}) collective-permute-start(bf16[4,48,1536]{2,1,0:T(8,128)(2,1)} %place_column.7.own), channel_id=1, source_target_pairs={{0,2},{1,3},{2,0},{3,1},{4,6},{5,7},{6,4},{7,5},{8,10},{9,11},{10,... | collective-permute-start | bytes 1769480 | tf_op jit(solution)/shard_map/ppermute | solution.py:469
  44.9 20.2 %collective-permute-start.14 = (bf16[2,48,1536]{2,1,0:T(8,128)(2,1)S(1)}, bf16[2,48,1536]{2,1,0:T(8,128)(2,1)S(1)}, u32[]{:S(2)}, u32[]{:S(2)}) collective-permute-start(bf16[2,48,1536]{2,1,0:T(8,128)(2,1)S(1)} %slice.503), channel_id=1, source_target_pairs={{0,2},{1,3},{2,0},{3,1},{4,6},{5,7},{6,4},{7,5},{8,10},{9,11},{10,... | collective-permute-start | bytes 884744 | tf_op jit(solution)/shard_map/ppermute | solution.py:469
  46.2 20.8 %collective-permute-start.15 = (bf16[2,48,1536]{2,1,0:T(8,128)(2,1)S(1)}, bf16[2,48,1536]{2,1,0:T(8,128)(2,1)S(1)}, u32[]{:S(2)}, u32[]{:S(2)}) collective-permute-start(bf16[2,48,1536]{2,1,0:T(8,128)(2,1)S(1)} %slice.504), channel_id=1, source_target_pairs={{0,1},{1,0},{2,3},{3,2},{4,5},{5,4},{6,7},{7,6},{8,9},{9,8},{10,11... | collective-permute-start | bytes 884744 | tf_op jit(solution)/shard_map/ppermute | solution.py:469
  47.5 25.6 %collective-permute-start.4 = (bf16[1,1248]{1,0:T(2,128)(2,1)S(1)}, bf16[1,1248]{1,0:T(2,128)(2,1)S(1)}, u32[]{:S(2)}, u32[]{:S(2)}) collective-permute-start(bf16[1,1248]{1,0:T(2,128)(2,1)S(1)} %broadcast_in_dim.99), channel_id=1, source_target_pairs={{0,12},{1,13},{2,14},{3,15},{4,0},{5,1},{6,2},{7,3},{8,4},{9,5},{1... | collective-permute-start | bytes 7496 | tf_op jit(solution)/shard_map/ppermute | solution.py:475
  73.2 66.6 %collective-permute-start.20 = (bf16[768,1536]{1,0:T(8,128)(2,1)S(1)}, bf16[768,1536]{1,0:T(8,128)(2,1)}, u32[]{:S(2)}, u32[]{:S(2)}) collective-permute-start(bf16[768,1536]{1,0:T(8,128)(2,1)S(1)} %bitcast.452), channel_id=1, source_target_pairs={{0,16},{16,0},{1,17},{17,1},{2,18},{18,2},{3,19},{19,3},{4,20},{20... | collective-permute-start | bytes 7077896 | tf_op jit(solution)/shard_map/ppermute | solution.py:464
  93.1 28.6 %collective-permute-start.30 = (bf16[4,192,384]{2,1,0:T(8,128)(2,1)}, bf16[4,192,384]{2,1,0:T(8,128)(2,1)}, u32[]{:S(2)}, u32[]{:S(2)}) collective-permute-start(bf16[4,192,384]{2,1,0:T(8,128)(2,1)} %place_column.8.own), channel_id=1, source_target_pairs={{0,1},{1,0},{2,3},{3,2},{4,5},{5,4},{6,7},{7,6},{8,9},{9,8},{10,11... | collective-permute-start | bytes 1769480 | tf_op jit(solution)/shard_map/ppermute | solution.py:469
  97.7 72.4 %collective-permute-start.29 = (bf16[768,1536]{1,0:T(8,128)(2,1)}, bf16[768,1536]{1,0:T(8,128)(2,1)}, u32[]{:S(2)}, u32[]{:S(2)}) collective-permute-start(bf16[768,1536]{1,0:T(8,128)(2,1)} %bitcast.38.up_mine), channel_id=1, source_target_pairs={{0,16},{16,0},{1,17},{17,1},{2,18},{18,2},{3,19},{19,3},{4,20},{20... | collective-permute-start | bytes 7077896 | tf_op jit(solution)/shard_map/ppermute | solution.py:464
  146.1 24.0 %collective-permute-start.42 = (bf16[48,1536]{1,0:T(8,128)(2,1)}, bf16[48,1536]{1,0:T(8,128)(2,1)S(1)}, u32[]{:S(2)}, u32[]{:S(2)}) collective-permute-start(bf16[48,1536]{1,0:T(8,128)(2,1)} %get-tuple-element.132.refs_0_), channel_id=1, source_target_pairs={{0,4},{1,5},{2,6},{3,7},{4,8},{5,9},{6,10},{7,11},{8,12},{9,13},{1... | collective-permute-start | bytes 442376 | tf_op jit(solution)/shard_map/ppermute | solution.py:475
  153.9 60.6 %collective-permute-start.37 = (bf16[3072,384]{1,0:T(8,128)(2,1)}, bf16[3072,384]{1,0:T(8,128)(2,1)}, u32[]{:S(2)}, u32[]{:S(2)}) collective-permute-start(bf16[3072,384]{1,0:T(8,128)(2,1)} %bitcast.41.down_mine), channel_id=1, source_target_pairs={{0,16},{16,0},{1,17},{17,1},{2,18},{18,2},{3,19},{19,3},{4,20},{20... | collective-permute-start | bytes 7077896 | tf_op jit(solution)/shard_map/ppermute | solution.py:464
  170.9 71.3 %collective-permute-start.45 = (bf16[768,1536]{1,0:T(8,128)(2,1)S(1)}, bf16[768,1536]{1,0:T(8,128)(2,1)}, u32[]{:S(2)}, u32[]{:S(2)}) collective-permute-start(bf16[768,1536]{1,0:T(8,128)(2,1)S(1)} %bitcast.455), channel_id=1, source_target_pairs={{0,16},{16,0},{1,17},{17,1},{2,18},{18,2},{3,19},{19,3},{4,20},{20... | collective-permute-start | bytes 7077896 | tf_op jit(solution)/shard_map/ppermute | solution.py:464
  191.1 21.8 %collective-permute-start.55 = (bf16[4,192,384]{2,1,0:T(8,128)(2,1)}, bf16[4,192,384]{2,1,0:T(8,128)(2,1)S(1)}, u32[]{:S(2)}, u32[]{:S(2)}) collective-permute-start(bf16[4,192,384]{2,1,0:T(8,128)(2,1)} %place_column.11.own), channel_id=1, source_target_pairs={{0,2},{1,3},{2,0},{3,1},{4,6},{5,7},{6,4},{7,5},{8,10},{9,11},{10,... | collective-permute-start | bytes 1769480 | tf_op jit(solution)/shard_map/ppermute | solution.py:469
  214.4 25.1 %collective-permute-start.56 = (bf16[2,192,384]{2,1,0:T(8,128)(2,1)}, bf16[2,192,384]{2,1,0:T(8,128)(2,1)}, u32[]{:S(2)}, u32[]{:S(2)}) collective-permute-start(bf16[2,192,384]{2,1,0:T(8,128)(2,1)} %slice.520), channel_id=1, source_target_pairs={{0,2},{1,3},{2,0},{3,1},{4,6},{5,7},{6,4},{7,5},{8,10},{9,11},{10,... | collective-permute-start | bytes 884744 | tf_op jit(solution)/shard_map/ppermute | solution.py:469
  216.6 22.9 %collective-permute-start.57 = (bf16[2,192,384]{2,1,0:T(8,128)(2,1)}, bf16[2,192,384]{2,1,0:T(8,128)(2,1)}, u32[]{:S(2)}, u32[]{:S(2)}) collective-permute-start(bf16[2,192,384]{2,1,0:T(8,128)(2,1)} %slice.521), channel_id=1, source_target_pairs={{0,1},{1,0},{2,3},{3,2},{4,5},{5,4},{6,7},{7,6},{8,9},{9,8},{10,11... | collective-permute-start | bytes 884744 | tf_op jit(solution)/shard_map/ppermute | solution.py:469
  223.3 29.2 %collective-permute-start.53 = (bf16[768,1536]{1,0:T(8,128)(2,1)}, bf16[768,1536]{1,0:T(8,128)(2,1)}, u32[]{:S(2)}, u32[]{:S(2)}) collective-permute-start(bf16[768,1536]{1,0:T(8,128)(2,1)} %bitcast.49.up_mine), channel_id=1, source_target_pairs={{0,16},{16,0},{1,17},{17,1},{2,18},{18,2},{3,19},{19,3},{4,20},{20... | collective-permute-start | bytes 7077896 | tf_op jit(solution)/shard_map/ppermute | solution.py:464
  291.0 58.2 %collective-permute-start.60 = (bf16[3072,384]{1,0:T(8,128)(2,1)}, bf16[3072,384]{1,0:T(8,128)(2,1)}, u32[]{:S(2)}, u32[]{:S(2)}) collective-permute-start(bf16[3072,384]{1,0:T(8,128)(2,1)} %get-tuple-element.162), channel_id=1, source_target_pairs={{0,16},{16,0},{1,17},{17,1},{2,18},{18,2},{3,19},{19,3},{4,20},{20... | collective-permute-start | bytes 7077896 | tf_op jit(solution)/shard_map/ppermute | solution.py:464
  291.4 61.6 %collective-permute-start.63 = (bf16[768,1536]{1,0:T(8,128)(2,1)}, bf16[768,1536]{1,0:T(8,128)(2,1)}, u32[]{:S(2)}, u32[]{:S(2)}) collective-permute-start(bf16[768,1536]{1,0:T(8,128)(2,1)} %get-tuple-element.164), channel_id=1, source_target_pairs={{0,16},{16,0},{1,17},{17,1},{2,18},{18,2},{3,19},{19,3},{4,20},{20... | collective-permute-start | bytes 7077896 | tf_op jit(solution)/shard_map/ppermute | solution.py:464
  326.5 21.4 %collective-permute-start.59 = (f32[256,768]{1,0:T(8,128)S(1)}, f32[256,768]{1,0:T(8,128)S(1)}, u32[]{:S(2)}, u32[]{:S(2)}) collective-permute-start(f32[256,768]{1,0:T(8,128)S(1)} %broadcast_select_fusion.2), channel_id=1, source_target_pairs={{0,16},{16,0},{1,17},{17,1},{2,18},{18,2},{3,19},{19,3},{4,20},{20... | collective-permute-start | bytes 2359304 | tf_op jit(solution)/shard_map/ppermute | solution.py:464
  357.5 45.1 %collective-permute-start.75 = (bf16[3072,384]{1,0:T(8,128)(2,1)S(1)}, bf16[3072,384]{1,0:T(8,128)(2,1)S(1)}, u32[]{:S(2)}, u32[]{:S(2)}) collective-permute-start(bf16[3072,384]{1,0:T(8,128)(2,1)S(1)} %copy-done.59), channel_id=1, source_target_pairs={{0,16},{16,0},{1,17},{17,1},{2,18},{18,2},{3,19},{19,3},{4,20},{20... | collective-permute-start | bytes 7077896 | tf_op jit(solution)/shard_map/ppermute | solution.py:464
  366.0 37.5 %collective-permute-start.82 = (bf16[768,1536]{1,0:T(8,128)(2,1)S(1)}, bf16[768,1536]{1,0:T(8,128)(2,1)S(1)}, u32[]{:S(2)}, u32[]{:S(2)}) collective-permute-start(bf16[768,1536]{1,0:T(8,128)(2,1)S(1)} %copy-done.58), channel_id=1, source_target_pairs={{0,16},{16,0},{1,17},{17,1},{2,18},{18,2},{3,19},{19,3},{4,20},{20... | collective-permute-start | bytes 7077896 | tf_op jit(solution)/shard_map/ppermute | solution.py:464
  373.3 23.3 %collective-permute-start.73 = (bf16[4,48,1536]{2,1,0:T(8,128)(2,1)S(1)}, bf16[4,48,1536]{2,1,0:T(8,128)(2,1)S(1)}, u32[]{:S(2)}, u32[]{:S(2)}) collective-permute-start(bf16[4,48,1536]{2,1,0:T(8,128)(2,1)S(1)} %pad_maximum_fusion.2), channel_id=1, source_target_pairs={{0,1},{1,0},{2,3},{3,2},{4,5},{5,4},{6,7},{7,6},{8,9},{9,8},{10,11... | collective-permute-start | bytes 1769480 | tf_op jit(solution)/shard_map/ppermute | solution.py:469
  415.5 31.2 %collective-permute-start.84 = (bf16[4,48,1536]{2,1,0:T(8,128)(2,1)S(1)}, bf16[4,48,1536]{2,1,0:T(8,128)(2,1)S(1)}, u32[]{:S(2)}, u32[]{:S(2)}) collective-permute-start(bf16[4,48,1536]{2,1,0:T(8,128)(2,1)S(1)} %pad_maximum_fusion.7), channel_id=1, source_target_pairs={{0,2},{1,3},{2,0},{3,1},{4,6},{5,7},{6,4},{7,5},{8,10},{9,11},{10,... | collective-permute-start | bytes 1769480 | tf_op jit(solution)/shard_map/ppermute | solution.py:469
  416.4 31.1 %collective-permute-start.83 = (bf16[4,48,1536]{2,1,0:T(8,128)(2,1)S(1)}, bf16[4,48,1536]{2,1,0:T(8,128)(2,1)S(1)}, u32[]{:S(2)}, u32[]{:S(2)}) collective-permute-start(bf16[4,48,1536]{2,1,0:T(8,128)(2,1)S(1)} %pad_maximum_fusion.6), channel_id=1, source_target_pairs={{0,1},{1,0},{2,3},{3,2},{4,5},{5,4},{6,7},{7,6},{8,9},{9,8},{10,11... | collective-permute-start | bytes 1769480 | tf_op jit(solution)/shard_map/ppermute | solution.py:469
  416.5 34.2 %collective-permute-start.92 = (bf16[48,1536]{1,0:T(8,128)(2,1)S(1)}, bf16[48,1536]{1,0:T(8,128)(2,1)S(1)}, u32[]{:S(2)}, u32[]{:S(2)}) collective-permute-start(bf16[48,1536]{1,0:T(8,128)(2,1)S(1)} %get-tuple-element.201), channel_id=1, source_target_pairs={{0,4},{1,5},{2,6},{3,7},{4,8},{5,9},{6,10},{7,11},{8,12},{9,13},{1... | collective-permute-start | bytes 442376 | tf_op jit(solution)/shard_map/ppermute | solution.py:475
  419.0 31.8 %collective-permute-start.93 = (bf16[48,1536]{1,0:T(8,128)(2,1)S(1)}, bf16[48,1536]{1,0:T(8,128)(2,1)S(1)}, u32[]{:S(2)}, u32[]{:S(2)}) collective-permute-start(bf16[48,1536]{1,0:T(8,128)(2,1)S(1)} %get-tuple-element.202), channel_id=1, source_target_pairs={{0,8},{1,9},{2,10},{3,11},{4,12},{5,13},{6,14},{7,15},{8,0},{9,1},... | collective-permute-start | bytes 442376 | tf_op jit(solution)/shard_map/ppermute | solution.py:475
  459.4 43.6 %collective-permute-start.91 = (bf16[4,48,1536]{2,1,0:T(8,128)(2,1)S(1)}, bf16[4,48,1536]{2,1,0:T(8,128)(2,1)S(1)}, u32[]{:S(2)}, u32[]{:S(2)}) collective-permute-start(bf16[4,48,1536]{2,1,0:T(8,128)(2,1)S(1)} %pad_maximum_fusion.5), channel_id=1, source_target_pairs={{0,2},{1,3},{2,0},{3,1},{4,6},{5,7},{6,4},{7,5},{8,10},{9,11},{10,... | collective-permute-start | bytes 1769480 | tf_op jit(solution)/shard_map/ppermute | solution.py:469
  461.0 42.0 %collective-permute-start.90 = (bf16[4,48,1536]{2,1,0:T(8,128)(2,1)S(1)}, bf16[4,48,1536]{2,1,0:T(8,128)(2,1)S(1)}, u32[]{:S(2)}, u32[]{:S(2)}) collective-permute-start(bf16[4,48,1536]{2,1,0:T(8,128)(2,1)S(1)} %pad_maximum_fusion.4), channel_id=1, source_target_pairs={{0,1},{1,0},{2,3},{3,2},{4,5},{5,4},{6,7},{7,6},{8,9},{9,8},{10,11... | collective-permute-start | bytes 1769480 | tf_op jit(solution)/shard_map/ppermute | solution.py:469
  484.8 21.9 %collective-permute-start.117 = (f32[192,384]{1,0:T(8,128)S(1)}, f32[192,384]{1,0:T(8,128)S(1)}, u32[]{:S(2)}, u32[]{:S(2)}) collective-permute-start(f32[192,384]{1,0:T(8,128)S(1)} %get-tuple-element.223), channel_id=1, source_target_pairs={{0,16},{16,0},{1,17},{17,1},{2,18},{18,2},{3,19},{19,3},{4,20},{20... | collective-permute-start | bytes 884744 | tf_op jit(solution)/shard_map/ppermute | solution.py:464
  499.0 20.8 %collective-permute-start.116 = (f32[48,1536]{1,0:T(8,128)S(1)}, f32[48,1536]{1,0:T(8,128)S(1)}, u32[]{:S(2)}, u32[]{:S(2)}) collective-permute-start(f32[48,1536]{1,0:T(8,128)S(1)} %get-tuple-element.226), channel_id=1, source_target_pairs={{0,16},{16,0},{1,17},{17,1},{2,18},{18,2},{3,19},{19,3},{4,20},{20... | collective-permute-start | bytes 884744 | tf_op jit(solution)/shard_map/ppermute | solution.py:464
  (149 other events, 1637.6 us)

commit v4 on v3

--- a/solution.py
+++ b/solution.py
@@ -811,19 +811,24 @@
     if small_slice():
         rounds = Rounds(LAG)
         tied = rounds.tied
-        chunks = [gather_stages(piece, tied) for piece in flat_pieces]
+        rows, columns = flat_pieces[3].shape
+        deep = flat_pieces[5].reshape(-1, rows, width).transpose(1, 0, 2).reshape(rows, -1)
+        packed = gather_whole(jnp.concatenate([flat_pieces[3], flat_pieces[4], deep], axis=1))
+        chunks = [gather_stages(piece, tied) for piece in flat_pieces[:3]]
         for turn in range(len(chunks) + 4):
             for index in range(len(chunks)):
                 if index <= turn <= index + 4:
                     advance(chunks[index], rounds, whole, index)
             if turn == 4:
                 rounds.note(attn_step(0, entry, whole[0]))
-            if turn == 6:
-                rounds.note(mlp_step(0, whole[1], whole[2], jnp.bfloat16))
-            if turn == 7:
-                middle = kept_forward[0, "mlp"][2]
-                rounds.note(attn_step(1, middle, whole[3]))
             rounds.close()
+        mlp_step(0, whole[1], whole[2], jnp.bfloat16)
+        packed = after(packed, kept_forward[0, "attn"][3])
+        deep = packed[:, 2 * columns :].reshape(count, rows, -1, width).transpose(0, 2, 1, 3)
+        parts = (packed[:, :columns], packed[:, columns : 2 * columns], deep.reshape(-1, width))
+        for index, part in enumerate(parts):
+            whole[3 + index] = (part, swap_cores(part))
+        attn_step(1, kept_forward[0, "mlp"][2], whole[3])
         mlp_step(1, whole[4], whole[5], jnp.float32)
     else:
         for index, piece in enumerate(flat_pieces):
@@ -861,12 +866,14 @@
                 stages["narrow1"] = scatter_stages(upper_attn[0], upper_attn[1], tied)
                 rounds.note(upper_attn)
             if turn == 1:
-                lower = mlp_back(0, upper_attn[4])
+                lower = mlp_back(0, after(upper_attn[4], rounds.made[-1]))
                 stages["down0"] = scatter_stages(lower[2], lower[3], tied)
                 stages["up0"] = scatter_stages(lower[0], lower[1], tied)
                 rounds.note(lower)
             if turn == 2:
-                lower_attn = attn_back(0, upper_attn[4], lower[5], jnp.float32)
+                lower_attn = attn_back(
+                    0, upper_attn[4], after(lower[5], rounds.made[-1]), jnp.float32
+                )
                 stages["narrow0"] = scatter_stages(lower_attn[0], lower_attn[1], tied)
                 rounds.note(lower_attn)
             rounds.close()

time: 529 us -> 502 us (0.949)
  starting transfers between devices: 175 us -> 135 us
  waiting for transfers between devices: 158 us -> 121 us
  local copies, waits for them, and re-layouts: 47.5 us -> 74.1 us
  other arithmetic: 23.5 us -> 45.8 us
  between operations: 2.76 us -> 16 us
  Pallas kernels: 116 us -> 103 us
    ppermute x54 -> x42, waiting for transfers between devices: 90.3 us -> 65.9 us  [swap_square(): return lax.ppermute(value, 'dp', [(i, i ^ bit) for i in range(count)])]
    ppermute x22, starting transfers between devices: 61.3 us -> 37.9 us  [swap_cores(): return lax.ppermute(value, 'section', [(0, 1), (1, 0)])]
    ppermute x54 -> x42, starting transfers between devices: 48.2 us -> 35.1 us  [swap_square(): return lax.ppermute(value, 'dp', [(i, i ^ bit) for i in range(count)])]
    ppermute x42 -> x33, waiting for transfers between devices: 67 us -> 54.1 us  [shift_ring(): return lax.ppermute(value, 'dp', pairs)]
    pallas_call x6 -> x3, Pallas kernels: 13.4 us -> 6.16 us  [place_blocks(): pl.pallas_call(place_kernel, out_shape=jax.ShapeDtypeStruct((RING, SQUARE...]
    slice x12 -> x6, local copies, waits for them, and re-layouts: 13.7 us -> 6.88 us  [gather_stages(): low, high = tied((first[:half], second[half:]))]
    another operation x13, other arithmetic: 0.92 us -> 7 us
    pallas_call x6 -> x3, Pallas kernels: 12 us -> 5.93 us  [column_placed(): pl.pallas_call(column_kernel, out_shape=jax.ShapeDtypeStruct((RING,) + he...]
  transfers between devices with their start and end apart: 118 -> 98, of which waited for: 39 -> 29; matrix products, arithmetic and copies ran while one was open for 9% -> 19% of each run, Pallas kernels for 15% -> 16%
where the time goes in v4:
time: 502 us; the launch traced here: 495 us
  starting transfers between devices  135 us (27%)
  waiting for transfers between devices  121 us (24%)
  Pallas kernels  103 us (21%)
  local copies, waits for them, and re-layouts  74.1 us (15%)
  other arithmetic  45.8 us (9%)
  between operations  16 us (3%)
    ppermute x42, waiting for transfers between devices, swap_square(): return lax.ppermute(value, 'dp', [(i, i ^ bit) for i in range(count)])  65.9 us
    ppermute x33, starting transfers between devices, shift_ring(): return lax.ppermute(value, 'dp', pairs)  62.4 us
    ppermute x33, waiting for transfers between devices, shift_ring(): return lax.ppermute(value, 'dp', pairs)  54.1 us
    ppermute x22, starting transfers between devices, swap_cores(): return lax.ppermute(value, 'section', [(0, 1), (1, 0)])  37.9 us
    ppermute x42, starting transfers between devices, swap_square(): return lax.ppermute(value, 'dp', [(i, i ^ bit) for i in range(count)])  35.1 us
    pallas_call x2, Pallas kernels, mlp_backward(): pl.pallas_call(mlp_backward_kernel, out_shape=(jax.ShapeDtypeStruct((feat...  30 us
    pallas_call x2, Pallas kernels, attn_backward(): pl.pallas_call(attn_backward_kernel, out_shape=(jax.ShapeDtypeStruct(mine...  24.9 us
    unnamed x179, local copies, waits for them, and re-layouts  22.7 us
  transfers between devices with their start and end apart: 98, of which 29 were waited for; matrix products, arithmetic and copies ran while one was open for 19% of the time, Pallas kernels for 16%

profile of v4, /device:TPU:1, one launch (start us, length us, event | category | flops | bytes accessed | tf_op | source)
XLA Modules:
  0.0 495.4 jit_solution(14707547191184869311)
XLA Ops:
  24.7 10.8 %collective-permute-done.10.refs_2_ = bf16[48,1536]{1,0:T(8,128)(2,1)S(1)} collective-permute-done((bf16[48,1536]{1,0:T(8,128)(2,1)S(1)}, bf16[48,1536]{1,0:T(8,128)(2,1)S(1)}, u32[]{:S(2)}, u32[]{:S(2)}) %collective-permute-start.10) | collective-permute-done | bytes 147488 | tf_op jit(solution)/shard_map/ppermute | solution.py:475
  40.7 6.1 %collective-permute-start.4 = (bf16[1,1248]{1,0:T(2,128)(2,1)S(1)}, bf16[1,1248]{1,0:T(2,128)(2,1)S(1)}, u32[]{:S(2)}, u32[]{:S(2)}) collective-permute-start(bf16[1,1248]{1,0:T(2,128)(2,1)S(1)} %broadcast_in_dim.99), channel_id=1, source_target_pairs={{0,12},{1,13},{2,14},{3,15},{4,0},{5,1},{6,2},{7,3},{8,4},{9,5},{1... | collective-permute-start | bytes 7496 | tf_op jit(solution)/shard_map/ppermute | solution.py:475
  50.2 3.3 collective-permute-done.2
  58.5 6.1 %collective-permute-done.14.far_low = bf16[2,48,1536]{2,1,0:T(8,128)(2,1)S(1)} collective-permute-done((bf16[2,48,1536]{2,1,0:T(8,128)(2,1)S(1)}, bf16[2,48,1536]{2,1,0:T(8,128)(2,1)S(1)}, u32[]{:S(2)}, u32[]{:S(2)}) %collective-permute-start.14) | collective-permute-done | bytes 294944 | tf_op jit(solution)/shard_map/ppermute | solution.py:469
  66.6 4.4 collective-permute-done.15.far_high
  83.9 7.3 %collective-permute-start.26 = (bf16[192,384]{1,0:T(8,128)(2,1)S(1)}, bf16[192,384]{1,0:T(8,128)(2,1)S(1)}, u32[]{:S(2)}, u32[]{:S(2)}) collective-permute-start(bf16[192,384]{1,0:T(8,128)(2,1)S(1)} %get-tuple-element.109.refs_0_), channel_id=1, source_target_pairs={{0,4},{1,5},{2,6},{3,7},{4,8},{5,9},{6,10},{7,11},{8,12},{9,13},{1... | collective-permute-start | bytes 442376 | tf_op jit(solution)/shard_map/ppermute | solution.py:475
  97.3 12.9 %collective-permute-done.27.refs_2_ = bf16[192,384]{1,0:T(8,128)(2,1)S(1)} collective-permute-done((bf16[192,384]{1,0:T(8,128)(2,1)S(1)}, bf16[192,384]{1,0:T(8,128)(2,1)S(1)}, u32[]{:S(2)}, u32[]{:S(2)}) %collective-permute-start.27) | collective-permute-done | bytes 147488 | tf_op jit(solution)/shard_map/ppermute | solution.py:475
  125.5 9.7 %collective-permute-done.30.first = bf16[4,192,384]{2,1,0:T(8,128)(2,1)} collective-permute-done((bf16[4,192,384]{2,1,0:T(8,128)(2,1)}, bf16[4,192,384]{2,1,0:T(8,128)(2,1)}, u32[]{:S(2)}, u32[]{:S(2)}) %collective-permute-start.30) | collective-permute-done | bytes 589856 | tf_op jit(solution)/shard_map/ppermute | solution.py:469
  137.3 4.3 collective-permute-done.31.second
  151.9 5.1 %collective-permute-start.29 = (bf16[768,1536]{1,0:T(8,128)(2,1)}, bf16[768,1536]{1,0:T(8,128)(2,1)}, u32[]{:S(2)}, u32[]{:S(2)}) collective-permute-start(bf16[768,1536]{1,0:T(8,128)(2,1)} %bitcast.38.up_mine), channel_id=1, source_target_pairs={{0,16},{16,0},{1,17},{17,1},{2,18},{18,2},{3,19},{19,3},{4,20},{20... | collective-permute-start | bytes 7077896 | tf_op jit(solution)/shard_map/ppermute | solution.py:464
  160.0 8.0 %attn_forward.2 = (bf16[2,256,1152]{2,1,0:T(8,128)(2,1)S(1)}, f32[2,6,256]{2,1,0:T(8,128)S(1)}, bf16[256,768]{1,0:T(8,128)(2,1)S(1)}, f32[256,768]{1,0:T(8,128)S(1)}) custom-call(s32[1]{0:T(128)} %bitcast.side, bf16[256,768]{1,0:T(8,128)(2,1)S(1)} %get-tuple-element.250.rows, f32[3,256,128]{2,1,0:T(8,128)S(1)} %pad_maximum_fusion.13.tables, ...), custom_call_target="tpu_custom_call" | custom-call | flops 1509949440 | bytes 4718592 | tf_op jit(solution)/shard_map/attn_forward/pallas_call | solution.py:146
  170.7 5.7 %fusion.101 = (bf16[768,1536]{1,0:T(8,128)(2,1)}, bf16[768,1536]{1,0:T(8,128)(2,1)}, bf16[768,1536]{1,0:T(8,128)(2,1)S(1)}) fusion(bf16[768,4608]{1,0:T(8,128)(2,1)} %all-gather.2.cloned.1.call-done), kind=kLoop, calls=%fused_computation.310 | loop fusion | bytes 14155776 | tf_op jit(solution)/shard_map/slice | solution.py:827
  176.9 5.5 %reshape.770 = bf16[16,48,4,384]{3,2,1,0:T(4,128)(2,1)} reshape(bf16[768,1536]{1,0:T(8,128)(2,1)} %get-tuple-element.208) | data formatting | bytes 4718592 | tf_op jit(solution)/shard_map/reshape | solution.py:827
  182.4 3.5 copy.140
  194.8 9.9 %mlp_forward.2 = (bf16[256,3072]{1,0:T(8,128)(2,1)S(1)}, f32[256,3072]{1,0:T(8,128)}, bf16[256,768]{1,0:T(8,128)(2,1)S(1)}) custom-call(s32[1]{0:T(128)} %bitcast.side, bf16[256,768]{1,0:T(8,128)(2,1)S(1)} %get-tuple-element.250.rows, f32[256,768]{1,0:T(8,128)S(1)} %copy-done.16, f32[4,768]{1,0:T(4,128)S(1)} %pad_maximum_fusion.16.norms, ...), custom_call_target="tpu_custom_call" | custom-call | flops 2415919104 | bytes 14155776 | tf_op jit(solution)/shard_map/mlp_forward/pallas_call | solution.py:224
  205.9 8.1 %attn_forward.3 = (bf16[2,256,1152]{2,1,0:T(8,128)(2,1)S(1)}, f32[2,6,256]{2,1,0:T(8,128)S(1)}, bf16[256,768]{1,0:T(8,128)(2,1)S(1)}, f32[256,768]{1,0:T(8,128)S(1)}) custom-call(s32[1]{0:T(128)} %bitcast.side, bf16[256,768]{1,0:T(8,128)(2,1)S(1)} %get-tuple-element.115.rows, f32[3,256,128]{2,1,0:T(8,128)S(1)} %pad_maximum_fusion.13.tables, ...), custom_call_target="tpu_custom_call" | custom-call | flops 1509949440 | bytes 4718592 | tf_op jit(solution)/shard_map/attn_forward/pallas_call | solution.py:146
  214.0 10.3 %mlp_forward.3 = (bf16[256,3072]{1,0:T(8,128)(2,1)S(1)}, f32[256,3072]{1,0:T(8,128)}, f32[256,768]{1,0:T(8,128)S(1)}) custom-call(s32[1]{0:T(128)} %bitcast.side, bf16[256,768]{1,0:T(8,128)(2,1)S(1)} %get-tuple-element.115.rows, f32[256,768]{1,0:T(8,128)S(1)} %get-tuple-element.120.passed, f32[4,768]{1,0:T(4,128)S(1)} %pad_maximum_fusion.17.norms, ...), custom_call_target="tpu_custom_call" | custom-call | flops 2415919104 | bytes 14155776 | tf_op jit(solution)/shard_map/mlp_forward/pallas_call | solution.py:224
  224.3 15.0 %mlp_backward.2 = (bf16[768,1536]{1,0:T(8,128)(2,1)S(1)}, bf16[768,1536]{1,0:T(8,128)(2,1)}, bf16[3072,384]{1,0:T(8,128)(2,1)}, bf16[3072,384]{1,0:T(8,128)(2,1)...) custom-call(s32[1]{0:T(128)} %bitcast.side, bf16[256,768]{1,0:T(8,128)(2,1)S(1)} %get-tuple-element.115.rows, ...), custom_call_target="tpu_custom_call" | custom-call | flops 4831838208 | bytes 23592960 | tf_op jit(solution)/shard_map/mlp_backward/pallas_call | solution.py:316
  245.6 12.4 %attn_backward.2 = (bf16[768,1536]{1,0:T(8,128)(2,1)}, bf16[768,1536]{1,0:T(8,128)(2,1)}, f32[2,1152]{1,0:T(2,128)S(1)}, f32[5,768]{1,0:T(8,128)S(1)}, bf16[256,768]{1,0:T(8,128)(2,1)S(1)}) custom-call(s32[1]{0:T(128)} %bitcast.side, bf16[256,768]{1,0:T(8,128)(2,1)S(1)} %copy-done.10, bf16[256,768]{1,0:T(8,128)(2,1)S(1)} %copy-done.17, ...), custom_call_target="tpu_custom_call" | custom-call | flops 3623878656 | bytes 9437184 | tf_op jit(solution)/shard_map/attn_backward/pallas_call | solution.py:434
  260.3 3.5 convert_add_fusion.9
  270.7 14.9 %mlp_backward.3 = (bf16[768,1536]{1,0:T(8,128)(2,1)S(1)}, bf16[768,1536]{1,0:T(8,128)(2,1)}, bf16[3072,384]{1,0:T(8,128)(2,1)}, bf16[3072,384]{1,0:T(8,128)(2,1)...) custom-call(s32[1]{0:T(128)} %bitcast.side, bf16[256,768]{1,0:T(8,128)(2,1)S(1)} %get-tuple-element.250.rows, ...), custom_call_target="tpu_custom_call" | custom-call | flops 4831838208 | bytes 23592960 | tf_op jit(solution)/shard_map/mlp_backward/pallas_call | solution.py:316
  300.9 12.5 %attn_backward.3 = (bf16[768,1536]{1,0:T(8,128)(2,1)}, bf16[768,1536]{1,0:T(8,128)(2,1)}, f32[2,1152]{1,0:T(2,128)S(1)}, f32[5,768]{1,0:T(8,128)S(1)}, f32[256,768]{1,0:T(8,128)S(1)}) custom-call(s32[1]{0:T(128)} %bitcast.side, bf16[256,768]{1,0:T(8,128)(2,1)S(1)} %get-tuple-element.250.rows, bf16[256,768]{1,0:T(8,128)(2,1)S(1)} %copy-done.33, ...), custom_call_target="tpu_custom_call" | custom-call | flops 3623878656 | bytes 9437184 | tf_op jit(solution)/shard_map/attn_backward/pallas_call | solution.py:434
  351.1 6.6 %collective-permute-done.52 = bf16[4,48,1536]{2,1,0:T(8,128)(2,1)} collective-permute-done((bf16[4,48,1536]{2,1,0:T(8,128)(2,1)}, bf16[4,48,1536]{2,1,0:T(8,128)(2,1)}, u32[]{:S(2)}, u32[]{:S(2)}) %collective-permute-start.52) | collective-permute-done | bytes 589856 | tf_op jit(solution)/shard_map/ppermute | solution.py:469
  379.2 5.0 %collective-permute-done.75 = bf16[2,48,1536]{2,1,0:T(8,128)(2,1)S(1)} collective-permute-done((bf16[2,48,1536]{2,1,0:T(8,128)(2,1)S(1)}, bf16[2,48,1536]{2,1,0:T(8,128)(2,1)S(1)}, u32[]{:S(2)}, u32[]{:S(2)}) %collective-permute-start.75) | collective-permute-done | bytes 294944 | tf_op jit(solution)/shard_map/ppermute | solution.py:469
  393.2 12.5 %collective-permute-done.57 = bf16[2,48,1536]{2,1,0:T(8,128)(2,1)S(1)} collective-permute-done((bf16[2,48,1536]{2,1,0:T(8,128)(2,1)S(1)}, bf16[2,48,1536]{2,1,0:T(8,128)(2,1)S(1)}, u32[]{:S(2)}, u32[]{:S(2)}) %collective-permute-start.57) | collective-permute-done | bytes 294944 | tf_op jit(solution)/shard_map/ppermute | solution.py:469
  406.0 5.3 %collective-permute-done.58 = bf16[2,48,1536]{2,1,0:T(8,128)(2,1)S(1)} collective-permute-done((bf16[2,48,1536]{2,1,0:T(8,128)(2,1)S(1)}, bf16[2,48,1536]{2,1,0:T(8,128)(2,1)S(1)}, u32[]{:S(2)}, u32[]{:S(2)}) %collective-permute-start.58) | collective-permute-done | bytes 294944 | tf_op jit(solution)/shard_map/ppermute | solution.py:469
  428.0 6.1 %collective-permute-start.76 = (bf16[192,384]{1,0:T(8,128)(2,1)S(1)}, bf16[192,384]{1,0:T(8,128)(2,1)S(1)}, u32[]{:S(2)}, u32[]{:S(2)}) collective-permute-start(bf16[192,384]{1,0:T(8,128)(2,1)S(1)} %get-tuple-element.182), channel_id=1, source_target_pairs={{0,4},{1,5},{2,6},{3,7},{4,8},{5,9},{6,10},{7,11},{8,12},{9,13},{1... | collective-permute-start | bytes 442376 | tf_op jit(solution)/shard_map/ppermute | solution.py:475
  437.3 7.8 %collective-permute-start.78 = (bf16[192,384]{1,0:T(8,128)(2,1)S(1)}, bf16[192,384]{1,0:T(8,128)(2,1)S(1)}, u32[]{:S(2)}, u32[]{:S(2)}) collective-permute-start(bf16[192,384]{1,0:T(8,128)(2,1)S(1)} %get-tuple-element.184), channel_id=1, source_target_pairs={{0,12},{1,13},{2,14},{3,15},{4,0},{5,1},{6,2},{7,3},{8,4},{9,5},{1... | collective-permute-start | bytes 442376 | tf_op jit(solution)/shard_map/ppermute | solution.py:475
  448.3 5.9 %collective-permute-done.94 = bf16[48,1536]{1,0:T(8,128)(2,1)S(1)} collective-permute-done((bf16[48,1536]{1,0:T(8,128)(2,1)S(1)}, bf16[48,1536]{1,0:T(8,128)(2,1)S(1)}, u32[]{:S(2)}, u32[]{:S(2)}) %collective-permute-start.94) | collective-permute-done | bytes 147488 | tf_op jit(solution)/shard_map/ppermute | solution.py:475
  454.2 11.0 %collective-permute-start.96 = (f32[192,384]{1,0:T(8,128)S(1)}, f32[192,384]{1,0:T(8,128)S(1)}, u32[]{:S(2)}, u32[]{:S(2)}) collective-permute-start(f32[192,384]{1,0:T(8,128)S(1)} %get-tuple-element.199), channel_id=1, source_target_pairs={{0,16},{16,0},{1,17},{17,1},{2,18},{18,2},{3,19},{19,3},{4,20},{20... | collective-permute-start | bytes 884744 | tf_op jit(solution)/shard_map/ppermute | solution.py:464
  465.4 4.0 collective-permute-start.95
  475.2 9.9 %collective-permute-done.82 = bf16[48,1536]{1,0:T(8,128)(2,1)S(1)} collective-permute-done((bf16[48,1536]{1,0:T(8,128)(2,1)S(1)}, bf16[48,1536]{1,0:T(8,128)(2,1)S(1)}, u32[]{:S(2)}, u32[]{:S(2)}) %collective-permute-start.82) | collective-permute-done | bytes 147488 | tf_op jit(solution)/shard_map/ppermute | solution.py:475
  (580 shorter events, 226.2 us)
Async XLA Ops:
  7.2 163.5 %all-gather.2.cloned.1.call-start = ((), (), s32[]{:S(2)}) async-start(), calls=%async_computation | async-start | bytes 7520256 | tf_op jit(solution)/shard_map/all_gather | solution.py:522
  13.8 26.9 %collective-permute-start.1 = (bf16[624]{0:T(1024)(128)(2,1)S(1)}, bf16[624]{0:T(1024)(128)(2,1)S(1)}, u32[]{:S(2)}, u32[]{:S(2)}) collective-permute-start(bf16[624]{0:T(1024)(128)(2,1)S(1)} %concatenate.96), channel_id=1, source_target_pairs={{0,16},{16,0},{1,17},{17,1},{2,18},{18,2},{3,19},{19,3},{4,20},{20... | collective-permute-start | bytes 3752 | tf_op jit(solution)/shard_map/ppermute | solution.py:464
  75.9 84.0 %collective-permute-start.20 = (bf16[768,1536]{1,0:T(8,128)(2,1)S(1)}, bf16[768,1536]{1,0:T(8,128)(2,1)}, u32[]{:S(2)}, u32[]{:S(2)}) collective-permute-start(bf16[768,1536]{1,0:T(8,128)(2,1)S(1)} %bitcast.455), channel_id=1, source_target_pairs={{0,16},{16,0},{1,17},{17,1},{2,18},{18,2},{3,19},{19,3},{4,20},{20... | collective-permute-start | bytes 7077896 | tf_op jit(solution)/shard_map/ppermute | solution.py:464
  82.5 32.9 %collective-permute-start.21 = (bf16[4,48,1536]{2,1,0:T(8,128)(2,1)}, bf16[4,48,1536]{2,1,0:T(8,128)(2,1)}, u32[]{:S(2)}, u32[]{:S(2)}) collective-permute-start(bf16[4,48,1536]{2,1,0:T(8,128)(2,1)} %place_column.4.own), channel_id=1, source_target_pairs={{0,1},{1,0},{2,3},{3,2},{4,5},{5,4},{6,7},{7,6},{8,9},{9,8},{10,11... | collective-permute-start | bytes 1769480 | tf_op jit(solution)/shard_map/ppermute | solution.py:469
  96.4 26.2 %collective-permute-start.22 = (bf16[4,48,1536]{2,1,0:T(8,128)(2,1)}, bf16[4,48,1536]{2,1,0:T(8,128)(2,1)}, u32[]{:S(2)}, u32[]{:S(2)}) collective-permute-start(bf16[4,48,1536]{2,1,0:T(8,128)(2,1)} %place_column.4.own), channel_id=1, source_target_pairs={{0,2},{1,3},{2,0},{3,1},{4,6},{5,7},{6,4},{7,5},{8,10},{9,11},{10,... | collective-permute-start | bytes 1769480 | tf_op jit(solution)/shard_map/ppermute | solution.py:469
  112.9 22.3 %collective-permute-start.30 = (bf16[4,192,384]{2,1,0:T(8,128)(2,1)}, bf16[4,192,384]{2,1,0:T(8,128)(2,1)}, u32[]{:S(2)}, u32[]{:S(2)}) collective-permute-start(bf16[4,192,384]{2,1,0:T(8,128)(2,1)} %place_column.5.own), channel_id=1, source_target_pairs={{0,1},{1,0},{2,3},{3,2},{4,5},{5,4},{6,7},{7,6},{8,9},{9,8},{10,11... | collective-permute-start | bytes 1769480 | tf_op jit(solution)/shard_map/ppermute | solution.py:469
  113.9 27.7 %collective-permute-start.31 = (bf16[4,192,384]{2,1,0:T(8,128)(2,1)}, bf16[4,192,384]{2,1,0:T(8,128)(2,1)}, u32[]{:S(2)}, u32[]{:S(2)}) collective-permute-start(bf16[4,192,384]{2,1,0:T(8,128)(2,1)} %place_column.5.own), channel_id=1, source_target_pairs={{0,2},{1,3},{2,0},{3,1},{4,6},{5,7},{6,4},{7,5},{8,10},{9,11},{10,... | collective-permute-start | bytes 1769480 | tf_op jit(solution)/shard_map/ppermute | solution.py:469
  115.4 28.1 %collective-permute-start = (bf16[256,768]{1,0:T(8,128)(2,1)S(1)}, bf16[256,768]{1,0:T(8,128)(2,1)S(1)}, u32[]{:S(2)}, u32[]{:S(2)}) collective-permute-start(bf16[256,768]{1,0:T(8,128)(2,1)S(1)} %copy-done.58), channel_id=1, source_target_pairs={{0,16},{16,0},{1,17},{17,1},{2,18},{18,2},{3,19},{19,3},{4,20},{20... | collective-permute-start | bytes 1179656 | tf_op jit(solution)/shard_map/ppermute | solution.py:464
  124.3 23.6 %collective-permute-start.23 = (bf16[2,48,1536]{2,1,0:T(8,128)(2,1)}, bf16[2,48,1536]{2,1,0:T(8,128)(2,1)}, u32[]{:S(2)}, u32[]{:S(2)}) collective-permute-start(bf16[2,48,1536]{2,1,0:T(8,128)(2,1)} %slice.494), channel_id=1, source_target_pairs={{0,2},{1,3},{2,0},{3,1},{4,6},{5,7},{6,4},{7,5},{8,10},{9,11},{10,... | collective-permute-start | bytes 884744 | tf_op jit(solution)/shard_map/ppermute | solution.py:469
  151.9 41.8 %collective-permute-start.29 = (bf16[768,1536]{1,0:T(8,128)(2,1)}, bf16[768,1536]{1,0:T(8,128)(2,1)}, u32[]{:S(2)}, u32[]{:S(2)}) collective-permute-start(bf16[768,1536]{1,0:T(8,128)(2,1)} %bitcast.38.up_mine), channel_id=1, source_target_pairs={{0,16},{16,0},{1,17},{17,1},{2,18},{18,2},{3,19},{19,3},{4,20},{20... | collective-permute-start | bytes 7077896 | tf_op jit(solution)/shard_map/ppermute | solution.py:464
  159.9 33.7 %collective-permute-start.34 = (bf16[3072,384]{1,0:T(8,128)(2,1)}, bf16[3072,384]{1,0:T(8,128)(2,1)}, u32[]{:S(2)}, u32[]{:S(2)}) collective-permute-start(bf16[3072,384]{1,0:T(8,128)(2,1)} %bitcast.41.down_mine), channel_id=1, source_target_pairs={{0,16},{16,0},{1,17},{17,1},{2,18},{18,2},{3,19},{19,3},{4,20},{20... | collective-permute-start | bytes 7077896 | tf_op jit(solution)/shard_map/ppermute | solution.py:464
  176.4 29.5 %collective-permute-start.35 = (bf16[768,1536]{1,0:T(8,128)(2,1)S(1)}, bf16[768,1536]{1,0:T(8,128)(2,1)}, u32[]{:S(2)}, u32[]{:S(2)}) collective-permute-start(bf16[768,1536]{1,0:T(8,128)(2,1)S(1)} %get-tuple-element.210.mine), channel_id=1, source_target_pairs={{0,16},{16,0},{1,17},{17,1},{2,18},{18,2},{3,19},{19,3},{4,20},{20... | collective-permute-start | bytes 7077896 | tf_op jit(solution)/shard_map/ppermute | solution.py:464
  176.9 37.1 %collective-permute-start.36 = (bf16[768,1536]{1,0:T(8,128)(2,1)}, bf16[768,1536]{1,0:T(8,128)(2,1)}, u32[]{:S(2)}, u32[]{:S(2)}) collective-permute-start(bf16[768,1536]{1,0:T(8,128)(2,1)} %get-tuple-element.209.up_mine), channel_id=1, source_target_pairs={{0,16},{16,0},{1,17},{17,1},{2,18},{18,2},{3,19},{19,3},{4,20},{20... | collective-permute-start | bytes 7077896 | tf_op jit(solution)/shard_map/ppermute | solution.py:464
  185.9 28.1 %collective-permute-start.37 = (bf16[3072,384]{1,0:T(8,128)(2,1)}, bf16[3072,384]{1,0:T(8,128)(2,1)}, u32[]{:S(2)}, u32[]{:S(2)}) collective-permute-start(bf16[3072,384]{1,0:T(8,128)(2,1)} %bitcast.51.down_mine), channel_id=1, source_target_pairs={{0,16},{16,0},{1,17},{17,1},{2,18},{18,2},{3,19},{19,3},{4,20},{20... | collective-permute-start | bytes 7077896 | tf_op jit(solution)/shard_map/ppermute | solution.py:464
  258.0 30.3 %collective-permute-start.44 = (bf16[768,1536]{1,0:T(8,128)(2,1)}, bf16[768,1536]{1,0:T(8,128)(2,1)}, u32[]{:S(2)}, u32[]{:S(2)}) collective-permute-start(bf16[768,1536]{1,0:T(8,128)(2,1)} %get-tuple-element.131), channel_id=1, source_target_pairs={{0,16},{16,0},{1,17},{17,1},{2,18},{18,2},{3,19},{19,3},{4,20},{20... | collective-permute-start | bytes 7077896 | tf_op jit(solution)/shard_map/ppermute | solution.py:464
  264.9 31.2 %collective-permute-start.40 = (bf16[2,192,384]{2,1,0:T(8,128)(2,1)}, bf16[2,192,384]{2,1,0:T(8,128)(2,1)}, u32[]{:S(2)}, u32[]{:S(2)}) collective-permute-start(bf16[2,192,384]{2,1,0:T(8,128)(2,1)} %get-tuple-element.268), channel_id=1, source_target_pairs={{0,1},{1,0},{2,3},{3,2},{4,5},{5,4},{6,7},{7,6},{8,9},{9,8},{10,11... | collective-permute-start | bytes 884744 | tf_op jit(solution)/shard_map/ppermute | solution.py:469
  265.7 31.1 %collective-permute-start.41 = (bf16[2,192,384]{2,1,0:T(8,128)(2,1)}, bf16[2,192,384]{2,1,0:T(8,128)(2,1)}, u32[]{:S(2)}, u32[]{:S(2)}) collective-permute-start(bf16[2,192,384]{2,1,0:T(8,128)(2,1)} %get-tuple-element.267), channel_id=1, source_target_pairs={{0,2},{1,3},{2,0},{3,1},{4,6},{5,7},{6,4},{7,5},{8,10},{9,11},{10,... | collective-permute-start | bytes 884744 | tf_op jit(solution)/shard_map/ppermute | solution.py:469
  269.1 28.4 %collective-permute-start.42 = (bf16[2,48,1536]{2,1,0:T(8,128)(2,1)}, bf16[2,48,1536]{2,1,0:T(8,128)(2,1)}, u32[]{:S(2)}, u32[]{:S(2)}) collective-permute-start(bf16[2,48,1536]{2,1,0:T(8,128)(2,1)} %get-tuple-element.266), channel_id=1, source_target_pairs={{0,1},{1,0},{2,3},{3,2},{4,5},{5,4},{6,7},{7,6},{8,9},{9,8},{10,11... | collective-permute-start | bytes 884744 | tf_op jit(solution)/shard_map/ppermute | solution.py:469
  269.9 27.5 %collective-permute-start.43 = (bf16[2,48,1536]{2,1,0:T(8,128)(2,1)}, bf16[2,48,1536]{2,1,0:T(8,128)(2,1)}, u32[]{:S(2)}, u32[]{:S(2)}) collective-permute-start(bf16[2,48,1536]{2,1,0:T(8,128)(2,1)} %get-tuple-element.265), channel_id=1, source_target_pairs={{0,2},{1,3},{2,0},{3,1},{4,6},{5,7},{6,4},{7,5},{8,10},{9,11},{10,... | collective-permute-start | bytes 884744 | tf_op jit(solution)/shard_map/ppermute | solution.py:469
  288.2 77.8 %collective-permute-start.54 = (bf16[3072,384]{1,0:T(8,128)(2,1)}, bf16[3072,384]{1,0:T(8,128)(2,1)}, u32[]{:S(2)}, u32[]{:S(2)}) collective-permute-start(bf16[3072,384]{1,0:T(8,128)(2,1)} %get-tuple-element.158), channel_id=1, source_target_pairs={{0,16},{16,0},{1,17},{17,1},{2,18},{18,2},{3,19},{19,3},{4,20},{20... | collective-permute-start | bytes 7077896 | tf_op jit(solution)/shard_map/ppermute | solution.py:464
  296.0 26.3 %collective-permute-start.59 = (bf16[2,48,1536]{2,1,0:T(8,128)(2,1)}, bf16[2,48,1536]{2,1,0:T(8,128)(2,1)}, u32[]{:S(2)}, u32[]{:S(2)}) collective-permute-start(bf16[2,48,1536]{2,1,0:T(8,128)(2,1)} %get-tuple-element.163), channel_id=1, source_target_pairs={{0,2},{1,3},{2,0},{3,1},{4,6},{5,7},{6,4},{7,5},{8,10},{9,11},{10,... | collective-permute-start | bytes 884744 | tf_op jit(solution)/shard_map/ppermute | solution.py:469
  296.8 27.6 %collective-permute-start.60 = (bf16[2,48,1536]{2,1,0:T(8,128)(2,1)}, bf16[2,48,1536]{2,1,0:T(8,128)(2,1)}, u32[]{:S(2)}, u32[]{:S(2)}) collective-permute-start(bf16[2,48,1536]{2,1,0:T(8,128)(2,1)} %get-tuple-element.164), channel_id=1, source_target_pairs={{0,1},{1,0},{2,3},{3,2},{4,5},{5,4},{6,7},{7,6},{8,9},{9,8},{10,11... | collective-permute-start | bytes 884744 | tf_op jit(solution)/shard_map/ppermute | solution.py:469
  317.5 26.1 %collective-permute-start.48 = (bf16[4,192,384]{2,1,0:T(8,128)(2,1)}, bf16[4,192,384]{2,1,0:T(8,128)(2,1)}, u32[]{:S(2)}, u32[]{:S(2)}) collective-permute-start(bf16[4,192,384]{2,1,0:T(8,128)(2,1)} %pad_maximum_fusion.1), channel_id=1, source_target_pairs={{0,2},{1,3},{2,0},{3,1},{4,6},{5,7},{6,4},{7,5},{8,10},{9,11},{10,... | collective-permute-start | bytes 1769480 | tf_op jit(solution)/shard_map/ppermute | solution.py:469
  339.5 30.7 %collective-permute-start.61 = (bf16[768,1536]{1,0:T(8,128)(2,1)}, bf16[768,1536]{1,0:T(8,128)(2,1)}, u32[]{:S(2)}, u32[]{:S(2)}) collective-permute-start(bf16[768,1536]{1,0:T(8,128)(2,1)} %get-tuple-element.165), channel_id=1, source_target_pairs={{0,16},{16,0},{1,17},{17,1},{2,18},{18,2},{3,19},{19,3},{4,20},{20... | collective-permute-start | bytes 7077896 | tf_op jit(solution)/shard_map/ppermute | solution.py:464
  359.3 26.4 %collective-permute-start.49 = (bf16[192,384]{1,0:T(8,128)(2,1)S(1)}, bf16[192,384]{1,0:T(8,128)(2,1)S(1)}, u32[]{:S(2)}, u32[]{:S(2)}) collective-permute-start(bf16[192,384]{1,0:T(8,128)(2,1)S(1)} %get-tuple-element.153), channel_id=1, source_target_pairs={{0,4},{1,5},{2,6},{3,7},{4,8},{5,9},{6,10},{7,11},{8,12},{9,13},{1... | collective-permute-start | bytes 442376 | tf_op jit(solution)/shard_map/ppermute | solution.py:475
  362.7 24.6 %collective-permute-start.50 = (bf16[192,384]{1,0:T(8,128)(2,1)S(1)}, bf16[192,384]{1,0:T(8,128)(2,1)S(1)}, u32[]{:S(2)}, u32[]{:S(2)}) collective-permute-start(bf16[192,384]{1,0:T(8,128)(2,1)S(1)} %get-tuple-element.154), channel_id=1, source_target_pairs={{0,8},{1,9},{2,10},{3,11},{4,12},{5,13},{6,14},{7,15},{8,0},{9,1},... | collective-permute-start | bytes 442376 | tf_op jit(solution)/shard_map/ppermute | solution.py:475
  386.6 26.3 %collective-permute-start.63 = (bf16[4,48,1536]{2,1,0:T(8,128)(2,1)S(1)}, bf16[4,48,1536]{2,1,0:T(8,128)(2,1)S(1)}, u32[]{:S(2)}, u32[]{:S(2)}) collective-permute-start(bf16[4,48,1536]{2,1,0:T(8,128)(2,1)S(1)} %copy-done.55), channel_id=1, source_target_pairs={{0,2},{1,3},{2,0},{3,1},{4,6},{5,7},{6,4},{7,5},{8,10},{9,11},{10,... | collective-permute-start | bytes 1769480 | tf_op jit(solution)/shard_map/ppermute | solution.py:469
  387.3 25.9 %collective-permute-start.62 = (bf16[4,48,1536]{2,1,0:T(8,128)(2,1)S(1)}, bf16[4,48,1536]{2,1,0:T(8,128)(2,1)S(1)}, u32[]{:S(2)}, u32[]{:S(2)}) collective-permute-start(bf16[4,48,1536]{2,1,0:T(8,128)(2,1)S(1)} %copy-done.54), channel_id=1, source_target_pairs={{0,1},{1,0},{2,3},{3,2},{4,5},{5,4},{6,7},{7,6},{8,9},{9,8},{10,11... | collective-permute-start | bytes 1769480 | tf_op jit(solution)/shard_map/ppermute | solution.py:469
  387.8 28.0 %collective-permute-start.71 = (bf16[48,1536]{1,0:T(8,128)(2,1)S(1)}, bf16[48,1536]{1,0:T(8,128)(2,1)S(1)}, u32[]{:S(2)}, u32[]{:S(2)}) collective-permute-start(bf16[48,1536]{1,0:T(8,128)(2,1)S(1)} %get-tuple-element.177), channel_id=1, source_target_pairs={{0,4},{1,5},{2,6},{3,7},{4,8},{5,9},{6,10},{7,11},{8,12},{9,13},{1... | collective-permute-start | bytes 442376 | tf_op jit(solution)/shard_map/ppermute | solution.py:475
  387.9 28.0 %collective-permute-start.72 = (bf16[48,1536]{1,0:T(8,128)(2,1)S(1)}, bf16[48,1536]{1,0:T(8,128)(2,1)S(1)}, u32[]{:S(2)}, u32[]{:S(2)}) collective-permute-start(bf16[48,1536]{1,0:T(8,128)(2,1)S(1)} %get-tuple-element.178), channel_id=1, source_target_pairs={{0,8},{1,9},{2,10},{3,11},{4,12},{5,13},{6,14},{7,15},{8,0},{9,1},... | collective-permute-start | bytes 442376 | tf_op jit(solution)/shard_map/ppermute | solution.py:475
  424.9 44.5 %collective-permute-start.70 = (bf16[4,48,1536]{2,1,0:T(8,128)(2,1)S(1)}, bf16[4,48,1536]{2,1,0:T(8,128)(2,1)S(1)}, u32[]{:S(2)}, u32[]{:S(2)}) collective-permute-start(bf16[4,48,1536]{2,1,0:T(8,128)(2,1)S(1)} %pad_maximum_fusion.5), channel_id=1, source_target_pairs={{0,2},{1,3},{2,0},{3,1},{4,6},{5,7},{6,4},{7,5},{8,10},{9,11},{10,... | collective-permute-start | bytes 1769480 | tf_op jit(solution)/shard_map/ppermute | solution.py:469
  425.8 43.6 %collective-permute-start.69 = (bf16[4,48,1536]{2,1,0:T(8,128)(2,1)S(1)}, bf16[4,48,1536]{2,1,0:T(8,128)(2,1)S(1)}, u32[]{:S(2)}, u32[]{:S(2)}) collective-permute-start(bf16[4,48,1536]{2,1,0:T(8,128)(2,1)S(1)} %pad_maximum_fusion.4), channel_id=1, source_target_pairs={{0,1},{1,0},{2,3},{3,2},{4,5},{5,4},{6,7},{7,6},{8,9},{9,8},{10,11... | collective-permute-start | bytes 1769480 | tf_op jit(solution)/shard_map/ppermute | solution.py:469
  (151 other events, 1480.8 us)
Sparse Core Ops, SparseCore 0:
  13.5 133.7 all-gather.1

commit v5 on v2

--- a/solution.py
+++ b/solution.py
@@ -10,7 +10,8 @@
 HD = 64
 ROT = 16
 LANES = 128
-TILES = 3
+TILES = 4
+PARTS = 16
 
 
 eps = 1e-05
@@ -135,8 +136,12 @@
         )
 
 
-def whole_blocks(count):
-    return [pl.BlockSpec(memory_space=pltpu.VMEM)] * count
+def fixed(*shape):
+    return pl.BlockSpec(shape, lambda *at: (0,) * len(shape))
+
+
+def fixed_like(*arrays):
+    return [fixed(*array.shape) for array in arrays]
 
 
 def attn_forward(side, rows, tables, mask, small, mine, other):
@@ -151,8 +156,16 @@
             jax.ShapeDtypeStruct((length, features), jnp.bfloat16),
             jax.ShapeDtypeStruct((length, features), jnp.float32),
         ),
-        in_specs=[pl.BlockSpec(memory_space=pltpu.SMEM)] + whole_blocks(8),
-        out_specs=tuple(whole_blocks(4)),
+        grid=(1,),
+        in_specs=[pl.BlockSpec(memory_space=pltpu.SMEM)]
+        + fixed_like(rows, tables, mask, small["norms"], small["qkv"], small["out"])
+        + [fixed(features, 4 * width)] * 2,
+        out_specs=(
+            fixed(2, length, 3 * width),
+            fixed(2, heads, length),
+            fixed(length, features),
+            fixed(length, features),
+        ),
         compiler_params=pltpu.CompilerParams(vmem_limit_bytes=vmem_bytes),
         cost_estimate=pl.CostEstimate(
             flops=2 * length * features * features * 5,
@@ -174,6 +187,20 @@
 
 def second_tile(step):
     return jnp.maximum(step - TILES, 0)
+
+
+def folded_cuts(shape, width):
+    rows = shape[0] // 2
+    for part in range(2):
+        for column in range(shape[1] // width):
+            yield (
+                slice(part * rows, (part + 1) * rows),
+                slice(column * width, (column + 1) * width),
+            )
+
+
+def unfolded(block, width):
+    return jnp.concatenate([block[cut] for cut in folded_cuts(block.shape, width)], axis=0)
 
 
 def mlp_forward_kernel(
@@ -196,12 +223,12 @@
     slope[...] = bell + hidden * density
     lit = (hidden * bell).astype(jnp.bfloat16)
     active[...] = lit
-    sum_mine[...] += product(lit, down_mine[...])
-    sum_other[...] += product(lit, down_other[...])
+    width = sum_mine.shape[1]
+    sum_mine[...] += product(lit, unfolded(down_mine, width))
+    sum_other[...] += product(lit, unfolded(down_other, width))
 
     @pl.when(step == 2 * TILES - 1)
     def _():
-        width = sum_mine.shape[1]
         for half, total in ((side[0], sum_mine), (1 - side[0], sum_other)):
             lanes = lane_half(half, width)
             produced[:, lanes] = (
@@ -209,18 +236,18 @@
             ).astype(produced.dtype)
 
 
-def mlp_forward(side, rows, passed, small, weights, kind):
+def mlp_forward(side, rows, passed, small, weights, places, kind):
     up_mine, up_other, down_mine, down_other = weights
+    up_at, down_at = places
     length, features = rows.shape
-    hidden = down_mine.shape[0]
-    tile = hidden // (2 * TILES)
     width = features // 2
-
-    def fixed(*shape):
-        return pl.BlockSpec(shape, lambda step, side: (0,) * len(shape))
-
+    tile = width
+    hidden = 2 * TILES * tile
+    folded = features // (2 * TILES)
     tiled = pl.BlockSpec((length, tile), lambda step, side: (0, tile_of(step, side)))
-    down_spec = pl.BlockSpec((tile, width), lambda step, side: (tile_of(step, side), 0))
+    down_spec = pl.BlockSpec(
+        (folded, TILES * width), lambda step, side: (tile_of(step, side), down_at)
+    )
     return pl.pallas_call(
         mlp_forward_kernel,
         out_shape=(
@@ -237,8 +264,8 @@
                 fixed(4, features),
                 pl.BlockSpec((1, tile), lambda step, side: (0, tile_of(step, side))),
                 fixed(2, features),
-                pl.BlockSpec((features, tile), lambda step, side: (0, first_tile(step))),
-                pl.BlockSpec((features, tile), lambda step, side: (0, second_tile(step))),
+                pl.BlockSpec((features, tile), lambda step, side: (0, up_at + first_tile(step))),
+                pl.BlockSpec((features, tile), lambda step, side: (0, up_at + second_tile(step))),
                 down_spec,
                 down_spec,
             ],
@@ -267,7 +294,8 @@
     up_kept, up_sent, down_kept, down_sent, bias_grad, grad_normed, normed
 ):
     step = pl.program_id(0)
-    width = down_mine.shape[1]
+    width = grad.shape[1] // 2
+    cuts = list(folded_cuts(down_mine.shape, width))
 
     @pl.when(step == 0)
     def _():
@@ -279,10 +307,13 @@
     grad_other = grad[:, lane_half(1 - side[0], width)]
     weight = jnp.where(step < TILES, up_mine[...], up_other[...])
     lit = active[...].T
-    down_kept[...] = product(lit, grad_mine).astype(jnp.bfloat16)
-    down_sent[...] = product(lit, grad_other).astype(jnp.bfloat16)
-    back = product_transposed(grad_mine, down_mine[...])
-    back += product_transposed(grad_other, down_other[...])
+    for grad_half, result in ((grad_mine, down_kept), (grad_other, down_sent)):
+        made = product(lit, grad_half).astype(jnp.bfloat16)
+        rows_each = made.shape[0] // len(cuts)
+        for index, cut in enumerate(cuts):
+            result[cut] = made[index * rows_each : (index + 1) * rows_each]
+    back = product_transposed(grad_mine, unfolded(down_mine, width))
+    back += product_transposed(grad_other, unfolded(down_other, width))
     back = (back * slope[...]).astype(jnp.bfloat16)
     bias_grad[...] = jnp.sum(back.astype(jnp.float32), axis=0, keepdims=True)
     up_grad = product(normed[...], back).astype(jnp.bfloat16)
@@ -298,28 +329,31 @@
     grad_normed[...] += product_transposed(back, weight)
 
 
-def mlp_backward(side, rows, grad, small, saved, weights):
+def mlp_backward(side, rows, grad, small, saved, weights, places):
     active, slope = saved
     up_mine, up_other, down_mine, down_other = weights
+    up_at, down_at = places
     length, features = rows.shape
-    hidden = down_mine.shape[0]
-    tile = hidden // (2 * TILES)
     width = features // 2
-
-    def fixed(*shape):
-        return pl.BlockSpec(shape, lambda step, side: (0,) * len(shape))
-
+    tile = width
+    hidden = 2 * TILES * tile
+    folded = features // (2 * TILES)
     tiled = pl.BlockSpec((length, tile), lambda step, side: (0, tile_of(step, side)))
-    down_spec = pl.BlockSpec((tile, width), lambda step, side: (tile_of(step, side), 0))
+    down_spec = pl.BlockSpec(
+        (folded, TILES * width), lambda step, side: (tile_of(step, side), down_at)
+    )
     up_first = pl.BlockSpec((features, tile), lambda step, side: (0, first_tile(step)))
     up_second = pl.BlockSpec((features, tile), lambda step, side: (0, second_tile(step)))
+    down_out = pl.BlockSpec(
+        (folded, TILES * width), lambda step, side: (tile_of(step, side), 0)
+    )
     return pl.pallas_call(
         mlp_backward_kernel,
         out_shape=(
             jax.ShapeDtypeStruct((features, hidden // 2), jnp.bfloat16),
             jax.ShapeDtypeStruct((features, hidden // 2), jnp.bfloat16),
-            jax.ShapeDtypeStruct((hidden, width), jnp.bfloat16),
-            jax.ShapeDtypeStruct((hidden, width), jnp.bfloat16),
+            jax.ShapeDtypeStruct((features, TILES * width), jnp.bfloat16),
+            jax.ShapeDtypeStruct((features, TILES * width), jnp.bfloat16),
             jax.ShapeDtypeStruct((1, hidden), jnp.float32),
             jax.ShapeDtypeStruct((length, features), jnp.float32),
         ),
@@ -332,16 +366,16 @@
                 fixed(4, features),
                 tiled,
                 tiled,
-                up_first,
-                up_second,
+                pl.BlockSpec((features, tile), lambda step, side: (0, up_at + first_tile(step))),
+                pl.BlockSpec((features, tile), lambda step, side: (0, up_at + second_tile(step))),
                 down_spec,
                 down_spec,
             ],
             out_specs=(
                 up_first,
                 up_second,
-                down_spec,
-                down_spec,
+                down_out,
+                down_out,
                 pl.BlockSpec((1, tile), lambda step, side: (0, tile_of(step, side))),
                 fixed(length, features),
             ),
@@ -434,14 +468,23 @@
     return pl.pallas_call(
         attn_backward_kernel,
         out_shape=(
-            jax.ShapeDtypeStruct(mine.shape, jnp.bfloat16),
-            jax.ShapeDtypeStruct(mine.shape, jnp.bfloat16),
+            jax.ShapeDtypeStruct((features, 2 * features), jnp.bfloat16),
+            jax.ShapeDtypeStruct((features, 2 * features), jnp.bfloat16),
             jax.ShapeDtypeStruct((2, 3 * features // 2), jnp.float32),
             jax.ShapeDtypeStruct((5, features), jnp.float32),
             jax.ShapeDtypeStruct((length, features), kind),
         ),
-        in_specs=[pl.BlockSpec(memory_space=pltpu.SMEM)] + whole_blocks(11),
-        out_specs=tuple(whole_blocks(5)),
+        grid=(1,),
+        in_specs=[pl.BlockSpec(memory_space=pltpu.SMEM)]
+        + fixed_like(rows, grad, tables, mask, small["norms"], qkv, logs, attended, grad_mlp)
+        + [fixed(features, 2 * features)] * 2,
+        out_specs=(
+            fixed(features, 2 * features),
+            fixed(features, 2 * features),
+            fixed(2, 3 * features // 2),
+            fixed(5, features),
+            fixed(length, features),
+        ),
         scratch_shapes=[pltpu.VMEM((length, features), jnp.bfloat16)],
         compiler_params=pltpu.CompilerParams(vmem_limit_bytes=vmem_bytes),
         cost_estimate=pl.CostEstimate(
@@ -468,13 +511,30 @@
     return lax.ppermute(value, "dp", [(i, i ^ bit) for i in range(count)])
 
 
-def ring_on(value):
+def shift_ring(value, steps):
     count = lax.axis_size("dp")
-    return lax.ppermute(value, "dp", [(i, (i + SQUARE) % count) for i in range(count)])
+    pairs = [(i, (i + SQUARE * steps) % count) for i in range(count)]
+    return lax.ppermute(value, "dp", pairs)
 
 
 def small_slice():
     return lax.axis_size("dp") == SQUARE * RING
+
+
+def after(values, earlier):
+    flat, shape = jax.tree.flatten(values)
+    waited = jax.tree.leaves(earlier)
+    tied = lax.optimization_barrier(tuple(flat) + tuple(waited))
+    return jax.tree.unflatten(shape, tied[: len(flat)])
+
+
+def own_place():
+    place = lax.axis_index("dp").astype(jnp.int32)
+    return (place // SQUARE, place % SQUARE)
+
+
+def any_space(count):
+    return [pl.BlockSpec(memory_space=pl.ANY)] * count
 
 
 def place_kernel(spot_ref, own, first, second, far_low, far_high, out, sems):
@@ -493,74 +553,260 @@
         copy.wait()
 
 
-def place_blocks(spot, blocks):
+def place_blocks(blocks):
+    spot = own_place()[1].reshape(1)
     _, rows, columns = blocks[0].shape
-    any_space = pl.BlockSpec(memory_space=pl.ANY)
-    return pl.pallas_call(
+    placed = pl.pallas_call(
         place_kernel,
         out_shape=jax.ShapeDtypeStruct((RING, SQUARE, rows, columns), blocks[0].dtype),
-        in_specs=[pl.BlockSpec(memory_space=pltpu.SMEM)] + [any_space] * 5,
+        in_specs=[pl.BlockSpec(memory_space=pltpu.SMEM)] + any_space(5),
         out_specs=pl.BlockSpec(memory_space=pltpu.VMEM),
         scratch_shapes=[pltpu.SemaphoreType.DMA((5,))],
         compiler_params=pltpu.CompilerParams(vmem_limit_bytes=vmem_bytes),
         name="place_blocks",
     )(spot, *blocks)
-
-
-def gather_rows(piece):
-    rows, columns = piece.shape
+    return placed.reshape(RING * SQUARE * rows, columns)
+
+
+def line_kernel(order_ref, *refs):
+    held, out, sems = refs[:-2], refs[-2], refs[-1]
+    copies = [
+        pltpu.make_async_copy(part, out.at[order_ref[at]], sems.at[at])
+        for at, part in enumerate(held)
+    ]
+    for copy in copies:
+        copy.start()
+    for copy in copies:
+        copy.wait()
+
+
+def line_placed(order, held):
+    return pl.pallas_call(
+        line_kernel,
+        out_shape=jax.ShapeDtypeStruct((len(held),) + held[0].shape, held[0].dtype),
+        in_specs=[pl.BlockSpec(memory_space=pltpu.SMEM)] + any_space(len(held)),
+        out_specs=pl.BlockSpec(memory_space=pltpu.VMEM),
+        scratch_shapes=[pltpu.SemaphoreType.DMA((len(held),))],
+        compiler_params=pltpu.CompilerParams(vmem_limit_bytes=vmem_bytes),
+        name="place_line",
+    )(order, *held)
+
+
+def ring_order():
+    return (own_place()[0] + RING - jnp.arange(RING, dtype=jnp.int32)) % RING
+
+
+def square_order():
+    return own_place()[1] ^ jnp.arange(SQUARE, dtype=jnp.int32)
+
+
+def gather_whole(piece):
+    return lax.all_gather(piece, "dp", axis=0, tiled=True)
+
+
+def ring_moved(piece):
+    return [shift_ring(piece, steps) for steps in range(1, RING)]
+
+
+def square_moved(piece):
+    return [swap_square(piece, bit) for bit in range(1, SQUARE)]
+
+
+def column_of(piece, moved):
+    return line_placed(ring_order(), [piece] + moved)
+
+
+def near_moved(column):
+    return (swap_square(column, 1), swap_square(column, 2))
+
+
+def far_moved(near):
+    half = RING // 2
+    return (swap_square(near[0][:half], 2), swap_square(near[1][half:], 1))
+
+
+def ring_around(blocks):
+    held = [blocks]
+    for _ in range(RING - 1):
+        held.append(shift_ring(held[-1], 1))
+    return held
+
+
+def gather_small(piece):
     if not small_slice():
-        return lax.all_gather(piece, "dp", axis=0, tiled=True)
-    place = lax.axis_index("dp")
-    level = place // SQUARE
-    spot = (place % SQUARE).astype(jnp.int32).reshape(1)
-    held = [piece]
-    for _ in range(RING - 1):
-        held.append(ring_on(held[-1]))
-    doubled = jnp.stack([held[3], held[2], held[1], held[0], held[3], held[2], held[1]])
-    column = lax.dynamic_slice_in_dim(doubled, RING - 1 - level, RING, 0)
-    first = swap_square(column, 1)
-    second = swap_square(column, 2)
+        return gather_whole(piece)
+    column = jnp.take(jnp.stack([piece] + ring_moved(piece)), ring_order(), axis=0)
+    stacked = jnp.stack([column] + square_moved(column), axis=1)
+    stacked = jnp.take(stacked, square_order(), axis=1)
+    return stacked.reshape(RING * SQUARE * piece.shape[0], -1)
+
+
+def far_kernel(place_ref, *refs):
+    pairs, (low, high) = refs[:-2], refs[-2:]
     half = RING // 2
-    far_low = swap_square(first[:half], 2)
-    far_high = swap_square(second[half:], 1)
-    whole = place_blocks(spot, (column, first, second, far_low, far_high))
-    return whole.reshape(RING * SQUARE * rows, columns)
-
-
-def scatter_rows(summed):
-    rows = summed.shape[0] // lax.axis_size("dp")
-    columns = summed.shape[1]
+    columns = pairs[0].shape[-1]
+    for at in range(0, len(pairs), 2):
+        cut = slice(at // 2 * columns, (at // 2 + 1) * columns)
+        total = pairs[at][...].astype(jnp.float32) + pairs[at + 1][...].astype(jnp.float32)
+        total = total[:, 0].astype(low.dtype)
+        low[:, :, cut] = total[:half]
+        high[:, :, cut] = total[half:]
+
+
+def near_kernel(place_ref, *refs):
+    pairs, (far_low, far_high), (first, second) = refs[:-4], refs[-4:-2], refs[-2:]
+    half = RING // 2
+    columns = pairs[0].shape[-1]
+    for at in range(0, len(pairs), 4):
+        cut = slice(at // 4 * columns, (at // 4 + 1) * columns)
+        one, two, three, four = (pair[...].astype(jnp.float32)[:, 0] for pair in pairs[at : at + 4])
+        total = one + two
+        first[:half, :, cut] = total[:half].astype(first.dtype)
+        high = far_high[:, :, cut].astype(jnp.float32)
+        first[half:, :, cut] = (total[half:] + high).astype(first.dtype)
+        total = three + four
+        low = far_low[:, :, cut].astype(jnp.float32)
+        second[:half, :, cut] = (total[:half] + low).astype(first.dtype)
+        second[half:, :, cut] = total[half:].astype(first.dtype)
+
+
+def column_kernel(place_ref, *refs):
+    pairs, (first, second), outs = refs[: -2 - RING], refs[-2 - RING : -RING], refs[-RING:]
+    columns = pairs[0].shape[-1]
+    for steps, out in enumerate(outs):
+        level = lax.rem(place_ref[0] + steps, RING)
+        for at in range(0, len(pairs), 2):
+            cut = slice(at // 2 * columns, (at // 2 + 1) * columns)
+            total = pairs[at][level, 0].astype(jnp.float32)
+            total += pairs[at + 1][level, 0].astype(jnp.float32)
+            total += first[level, :, cut].astype(jnp.float32)
+            total += second[level, :, cut].astype(jnp.float32)
+            out[:, cut] = total.astype(out.dtype)
+
+
+def block_spec(rows, columns, bit):
+    return pl.BlockSpec(
+        (RING, 1, rows, columns), lambda step, place: (0, place[1] ^ bit, 0, 0)
+    )
+
+
+def scatter_call(body, name, pairs, bits, extra, outs):
+    rows, columns = pairs[0].shape[0] // PARTS, pairs[0].shape[1]
+    blocks, specs = [], []
+    for at in range(0, len(pairs), 2):
+        for bit in bits:
+            for array in pairs[at : at + 2]:
+                blocks.append(array.reshape(RING, SQUARE, rows, columns))
+                specs.append(block_spec(rows, columns, bit))
+    return pl.pallas_call(
+        body,
+        out_shape=tuple(outs),
+        grid_spec=pltpu.PrefetchScalarGridSpec(
+            num_scalar_prefetch=1,
+            grid=(1,),
+            in_specs=specs + fixed_like(*extra),
+            out_specs=tuple(fixed_like(*outs)),
+        ),
+        compiler_params=pltpu.CompilerParams(vmem_limit_bytes=vmem_bytes),
+        name=name,
+    )(jnp.stack(own_place()), *blocks, *extra)
+
+
+def wide_shape(pairs, count, kind=jnp.bfloat16):
+    rows, columns = pairs[0].shape[0] // PARTS, pairs[0].shape[1] * len(pairs) // 2
+    lead = (count,) if count else ()
+    return jax.ShapeDtypeStruct(lead + (rows, columns), kind)
+
+
+def far_blocks(pairs):
+    half = wide_shape(pairs, RING // 2)
+    return scatter_call(far_kernel, "far_blocks", pairs, (3,), (), [half, half])
+
+
+def near_blocks(pairs, far):
+    full = wide_shape(pairs, RING)
+    return scatter_call(near_kernel, "near_blocks", pairs, (1, 2), far, [full, full])
+
+
+def sent_both(blocks):
+    return (swap_square(blocks[0], 1), swap_square(blocks[1], 2))
+
+
+def column_sent(pairs, near):
+    outs = [wide_shape(pairs, 0, jnp.float32)] + [wide_shape(pairs, 0)] * (RING - 1)
+    own, *leaving = scatter_call(column_kernel, "column_blocks", pairs, (0,), near, outs)
+    return [own] + [shift_ring(part, steps + 1) for steps, part in enumerate(leaving)]
+
+
+def total_of(parts):
+    total = parts[0].astype(jnp.float32)
+    for part in parts[1:]:
+        total = total + part.astype(jnp.float32)
+    return total
+
+
+def ring_steps(kept, received):
+    rows, columns = kept.shape[0] // PARTS, kept.shape[1]
+    kept = kept.reshape(RING, SQUARE, rows, columns)
+    received = received.reshape(RING, SQUARE, rows, columns)
+    level, _ = own_place()
+
+    def rung(back):
+        index = (level + RING - back) % RING
+        parts = [lax.dynamic_index_in_dim(array, index, 0, False) for array in (kept, received)]
+        return total_of(parts)
+
+    moving = rung(1).astype(jnp.bfloat16)
+    for step in range(1, RING):
+        moved = shift_ring(moving, 1)
+        yield moved
+        total = moved.astype(jnp.float32) + rung(step + 1)
+        moving = total.astype(jnp.bfloat16)
+    yield total
+
+
+def square_sent(blocks):
+    _, spot = own_place()
+
+    def block(index):
+        return lax.dynamic_index_in_dim(blocks, index, 0, keepdims=False)
+
+    moved = [
+        swap_square(block(spot ^ bit).astype(jnp.bfloat16), bit) for bit in range(1, SQUARE)
+    ]
+    return [block(spot)] + moved
+
+
+def scatter_small(kept, sent):
+    summed = kept + swap_cores(sent)
     if not small_slice():
         return lax.psum_scatter(summed, "dp", scatter_dimension=0, tiled=True)
-    place = lax.axis_index("dp")
-    level = place // SQUARE
-    spot = place % SQUARE
-    blocks = summed.reshape(RING, SQUARE, rows, columns)
+    level, spot = own_place()
+    blocks = summed.reshape(RING, SQUARE, -1)
 
     def block(index):
         return lax.dynamic_index_in_dim(blocks, index, 1, keepdims=False)
 
-    half = RING // 2
-    wire = jnp.bfloat16
-    far = block(spot ^ 3).astype(wire)
-    far_low = swap_square(far[:half], 1)
-    far_high = swap_square(far[half:], 2)
-    first = block(spot ^ 1)
-    second = block(spot ^ 2)
-    first = jnp.concatenate([first[:half], first[half:] + far_high.astype(jnp.float32)])
-    second = jnp.concatenate([second[:half] + far_low.astype(jnp.float32), second[half:]])
-    from_first = swap_square(first.astype(wire), 1)
-    from_second = swap_square(second.astype(wire), 2)
-    column = block(spot) + from_first.astype(jnp.float32) + from_second.astype(jnp.float32)
-
-    def rung(back):
-        return lax.dynamic_index_in_dim(column, (level - back) % RING, 0, keepdims=False)
-
-    travelling = rung(1)
-    for step in range(1, RING):
-        travelling = ring_on(travelling.astype(wire)).astype(jnp.float32) + rung(step + 1)
-    return travelling
+    column = block(spot)
+    for bit in range(1, SQUARE):
+        column = column + swap_square(block(spot ^ bit), bit)
+    total = lax.dynamic_index_in_dim(column, level, 0, keepdims=True)
+    for steps in range(1, RING):
+        part = lax.dynamic_index_in_dim(column, (level + steps) % RING, 0, keepdims=True)
+        total = total + shift_ring(part, steps)
+    return total
+
+
+def folded(rows, parts):
+    width = rows.shape[1]
+    split = rows.reshape(parts, TILES, -1, width).transpose(0, 2, 1, 3)
+    return split.reshape(-1, TILES * width)
+
+
+def unfolded_rows(rows, parts):
+    width = rows.shape[1] // TILES
+    split = rows.reshape(parts, -1, TILES, width).transpose(0, 2, 1, 3)
+    return split.reshape(-1, width)
 
 
 def half_of(array, which):
@@ -635,7 +881,7 @@
         [a[0].reshape(-1) for a in (qkv_bias, up_bias, out_biases, norm_gains, norm_biases)]
     )
     small_both = jnp.concatenate(ordered(is_first, small_own, swap_cores(small_own)))
-    small_full = gather_rows(small_both[None])
+    small_full = gather_small(small_both[None])
     small_full = small_full.reshape(count, 2, small_own.shape[0]).astype(jnp.float32)
 
     def small_of(layer):
@@ -660,66 +906,171 @@
             norms=jnp.concatenate([gains, shifts]),
         )
 
-    gathered = []
-    for layer in range(2):
-        found = []
-        for piece in pieces:
-            mine = gather_rows(piece[layer])
-            found.append((mine, swap_cores(mine)))
-        gathered.append(found)
     small = [small_of(layer) for layer in range(2)]
-
-    def forward(rows, layer, kind):
-        narrow, up, down = gathered[layer]
-        qkv, logs, attended, passed = attn_forward(side, rows, tables, mask, small[layer], *narrow)
-        active, slope, produced = mlp_forward(
-            side, rows, passed, small[layer], up + down, kind
+    kept_forward = {}
+    slabs = {}
+
+    def attn_step(layer, rows):
+        kept_forward[layer, "rows"] = rows
+        made = attn_forward(side, rows, tables, mask, small[layer], *slabs[layer, "narrow"])
+        kept_forward[layer, "attn"] = made
+        return made
+
+    def mlp_step(layer, kind):
+        passed = kept_forward[layer, "attn"][3]
+        rows = kept_forward[layer, "rows"]
+        made = mlp_forward(
+            side, rows, passed, small[layer], slabs[layer, "mlp"], places[layer], kind
         )
-        return (produced, (qkv, logs, attended), (active, slope))
-
-    def backward(rows, grad, layer, attn_saved, mlp_saved, kind):
-        narrow, up, down = gathered[layer]
-        up_kept, up_sent, down_kept, down_sent, bias_up, grad_mlp = mlp_backward(
-            side, rows, grad, small[layer], mlp_saved, up + down
+        kept_forward[layer, "mlp"] = made
+        return made
+
+    def mlp_back(layer, grad):
+        rows = kept_forward[layer, "rows"]
+        return mlp_backward(
+            side, rows, grad, small[layer], kept_forward[layer, "mlp"][:2],
+            slabs[layer, "mlp"], places[layer],
         )
-        kept, sent, bias_qkv, sums, passed = attn_backward(
-            side, rows, grad, tables, mask, small[layer], attn_saved, grad_mlp, *narrow, kind
+
+    def attn_back(layer, grad, grad_mlp, kind):
+        return attn_backward(
+            side, kept_forward[layer, "rows"], grad, tables, mask, small[layer],
+            kept_forward[layer, "attn"][:3], grad_mlp, *slabs[layer, "narrow"], kind,
         )
+
+    def vectors_of(bias_qkv, bias_up, sums):
         bias_qkv = jnp.where(is_first, bias_qkv, bias_qkv[::-1])
         bias_qkv = bias_qkv.reshape(2, 3, width).transpose(1, 0, 2).reshape(1, 6 * width)
-        vectors = (
-            bias_qkv,
-            bias_up,
-            jnp.concatenate([sums[4:5], sums[4:5]]),
-            sums[0:2],
-            sums[2:4],
+        double = jnp.concatenate([sums[4:5], sums[4:5]])
+        return (bias_qkv, bias_up, double, sums[0:2], sums[2:4])
+
+    places = ((0, 1), (TILES, 0))
+    if small_slice():
+        narrow, up, down = pieces
+        lower_mlp = jnp.concatenate([up[0], folded(down[0], 1)], axis=1)
+        upper_wide = jnp.concatenate([narrow[1], up[1]], axis=1)
+        upper_down = folded(down[1], 1)
+
+        ring_a = ring_moved(narrow[0])
+        square_d = square_moved(upper_down)
+        column_a = column_of(narrow[0], ring_a)
+        near_a = near_moved(column_a)
+        ring_b = ring_moved(after(lower_mlp, ring_a))
+        column_b = column_of(lower_mlp, ring_b)
+        far_a = far_moved(near_a)
+        near_b = near_moved(column_b)
+        ring_c = ring_moved(after(upper_wide, ring_b))
+        whole_a = place_blocks((column_a,) + near_a + far_a)
+        slabs[0, "narrow"] = (whole_a, swap_cores(whole_a))
+        far_b = far_moved(near_b)
+        column_c = column_of(upper_wide, ring_c)
+        near_c = near_moved(after(column_c, near_b))
+        blocks_d = line_placed(square_order(), [upper_down] + square_d)
+        held_d = ring_around(after(blocks_d, ring_c))
+        attn_rows, _ = after((entry, entry), (column_c, slabs[0, "narrow"], near_b))
+        attn_step(0, attn_rows)
+        whole_b = place_blocks((column_b,) + near_b + far_b)
+        whole_b = after(whole_b, kept_forward[0, "attn"][3])
+        swapped_b = swap_cores(whole_b)
+        slabs[0, "mlp"] = (whole_b, swapped_b, whole_b, swapped_b)
+        mlp_step(0, jnp.bfloat16)
+        far_c = far_moved(near_c)
+        whole_c = place_blocks((column_c,) + near_c + far_c)
+        swapped_c = swap_cores(whole_c)
+        slabs[1, "narrow"] = (whole_c, swapped_c)
+        whole_d = line_placed(ring_order(), held_d).reshape(whole_a.shape)
+        swapped_d = swap_cores(whole_d)
+        slabs[1, "mlp"] = (whole_c, swapped_c, whole_d, swapped_d)
+        attn_step(1, kept_forward[0, "mlp"][2])
+        mlp_step(1, jnp.float32)
+    else:
+        for layer in range(2):
+            narrow, up, down = (gather_whole(piece[layer]) for piece in pieces)
+            down = folded(down, PARTS)
+            joined = (narrow, up, down)
+            if layer == 0:
+                joined = (narrow, jnp.concatenate([up, down], axis=1))
+            else:
+                joined = (jnp.concatenate([narrow, up], axis=1), down)
+            first, second = ((part, swap_cores(part)) for part in joined)
+            slabs[layer, "narrow"] = first
+            slabs[layer, "mlp"] = (second if layer == 0 else first) + second
+        attn_step(0, entry)
+        mlp_step(0, jnp.bfloat16)
+        attn_step(1, kept_forward[0, "mlp"][2])
+        mlp_step(1, jnp.float32)
+    produced = kept_forward[1, "mlp"][2]
+
+    def mlp_pairs(made):
+        return (made[0], swap_cores(made[1]), made[2], swap_cores(made[3]))
+
+    if small_slice():
+        upper = mlp_back(1, cotangent)
+        pairs_a = mlp_pairs(upper)
+        upper_attn = attn_back(1, cotangent, upper[5], jnp.bfloat16)
+        leaving_a = far_blocks(after(pairs_a, upper_attn[2]))
+        far_a = sent_both(leaving_a)
+        grad_middle, received_b = after(
+            (upper_attn[4], swap_cores(upper_attn[1])), leaving_a
         )
-        return (passed, ((down_kept, down_sent), (up_kept, up_sent), (kept, sent)), vectors)
-
-    middle, attn_lower, mlp_lower = forward(entry, 0, jnp.bfloat16)
-    produced, attn_upper, mlp_upper = forward(middle, 1, jnp.float32)
-    grad_middle, grads_upper, vectors_upper = backward(
-        middle, cotangent, 1, attn_upper, mlp_upper, jnp.bfloat16
-    )
-    grad_entry, grads_lower, vectors_lower = backward(
-        entry, grad_middle, 0, attn_lower, mlp_lower, jnp.float32
-    )
-
-    def reduce_half(kept, sent):
-        return scatter_rows(kept.astype(jnp.float32) + swap_cores(sent).astype(jnp.float32))
-
-    reduced_upper = [reduce_half(*pair) for pair in grads_upper]
-    reduced_lower = [reduce_half(*pair) for pair in grads_lower]
+        lower = mlp_back(0, grad_middle)
+        near_a = near_blocks(pairs_a, after(far_a, lower[4]))
+        steps_b = ring_steps(upper_attn[0], after(received_b, lower[4]))
+        moved_b = next(steps_b)
+        pairs_c = mlp_pairs(lower)
+        grad_mlp = after(lower[5], near_a)
+        near_a = sent_both(near_a)
+        lower_attn = attn_back(0, grad_middle, grad_mlp, jnp.float32)
+        pairs_c = after(pairs_c, (lower_attn[2], near_a, moved_b))
+        far_c = sent_both(far_blocks(pairs_c))
+        pairs_d = (lower_attn[0], swap_cores(lower_attn[1]))
+        moved_b = next(steps_b)
+        far_d = sent_both(far_blocks(after(pairs_d, moved_b)))
+        parts_a = column_sent(pairs_a, near_a)
+        near_c = sent_both(near_blocks(pairs_c, far_c))
+        moved_b = next(steps_b)
+        blocks_b = next(steps_b)
+        parts_b = square_sent(blocks_b)
+        near_d = sent_both(near_blocks(pairs_d, far_d))
+        parts_c = column_sent(pairs_c, near_c)
+        parts_d = column_sent(pairs_d, near_d)
+        reduced = (
+            (total_of(parts_d), total_of(parts_b)),
+            (total_of(parts_c), total_of(parts_a)),
+        )
+    else:
+        upper = mlp_back(1, cotangent)
+        upper_attn = attn_back(1, cotangent, upper[5], jnp.bfloat16)
+        lower = mlp_back(0, upper_attn[4])
+        lower_attn = attn_back(0, upper_attn[4], lower[5], jnp.float32)
+
+        def spread(kept, received):
+            summed = kept.astype(jnp.float32) + received.astype(jnp.float32)
+            return lax.psum_scatter(summed, "dp", scatter_dimension=0, tiled=True)
+
+        def spread_mlp(made):
+            up_kept, up_got, down_kept, down_got = mlp_pairs(made)
+            down = spread(unfolded_rows(down_kept, PARTS), unfolded_rows(down_got, PARTS))
+            return jnp.concatenate([spread(up_kept, up_got), folded(down, 1)], axis=1)
+
+        reduced = (
+            tuple(spread(made[0], swap_cores(made[1])) for made in (lower_attn, upper_attn)),
+            tuple(spread_mlp(made) for made in (lower, upper)),
+        )
+    grad_entry = lower_attn[4]
+    vectors_upper = vectors_of(upper_attn[2], upper[4], upper_attn[3])
+    vectors_lower = vectors_of(lower_attn[2], lower[4], lower_attn[3])
 
     def finish(lower, upper):
         mine, leaving = ordered(is_first, lower, upper)
         return ordered(is_first, mine, swap_cores(leaving))
 
-    down_halves, up_halves, narrow_halves = (
-        finish(*pair) for pair in zip(reduced_lower, reduced_upper)
-    )
-    total_down = jnp.concatenate(down_halves, axis=1)
-    total_up = jnp.concatenate(up_halves, axis=1)
+    narrow_halves, mlp_halves = (finish(*pair) for pair in reduced)
+    up_width = up_weight.shape[2] // 2
+    total_up = jnp.concatenate([part[:, :up_width] for part in mlp_halves], axis=1)
+    total_down = jnp.concatenate(
+        [unfolded_rows(part[:, up_width:], 1) for part in mlp_halves], axis=1
+    )
     total_qkv = jnp.concatenate(
         [
             part[:, at * width : (at + 1) * width]
@@ -740,7 +1091,7 @@
     small_kept, small_sent = ordered(
         is_first, small_rows(vectors_lower), small_rows(vectors_upper)
     )
-    small_total = scatter_rows(small_kept + swap_cores(small_sent))[0]
+    small_total = scatter_small(small_kept, small_sent)[0]
     small_outs = []
     at = 0
     for shape in small_shapes:

time: 553 us -> 617 us (1.12)
  Pallas kernels: 105 us -> 141 us
  waiting for transfers between devices: 234 us -> 264 us
  starting transfers between devices: 122 us -> 99.8 us
  local copies, waits for them, and re-layouts: 52.2 us -> 69.6 us
    ppermute x42 -> x30, waiting for transfers between devices: 91.2 us -> 146 us  [shift_ring(): return lax.ppermute(value, 'dp', pairs)]
    ppermute x22 -> x19, starting transfers between devices: 63.2 us -> 27.1 us  [swap_cores(): return lax.ppermute(value, 'section', [(0, 1), (1, 0)])]
    pallas_call x2 -> x16, Pallas kernels: 24.7 us -> 58.7 us  [the longest x9 27.1 us: scatter_call(): pl.pallas_call(body, out_shape=tuple(outs), grid_spec=pltpu.PrefetchScala...]
    ppermute x42 -> x30, starting transfers between devices: 14.1 us -> 42 us  [shift_ring(): return lax.ppermute(value, 'dp', pairs)]
    ppermute x56 -> x36, waiting for transfers between devices: 142 us -> 117 us  [swap_square(): return lax.ppermute(value, 'dp', [(i, i ^ bit) for i in range(count)])]
    ppermute x56 -> x36, starting transfers between devices: 44.8 us -> 30.7 us  [swap_square(): return lax.ppermute(value, 'dp', [(i, i ^ bit) for i in range(count)])]
    add x15 -> x4, other arithmetic: 14.3 us -> 4.82 us  [the longest x1 2.64 us: ring_steps(): total = moved.astype(jnp.float32) + rung(step + 1)]
    slice x38 -> x12, local copies, waits for them, and re-layouts: 11.9 us -> 3.49 us  [the longest x6 3.39 us: far_moved(): return (swap_square(near[0][:half], 2), swap_square(near[1][half:], 1))]
  transfers between devices with their start and end apart: 120 -> 85, of which waited for: 54 -> 28; matrix products, arithmetic and copies ran while one was open for 10% -> 13% of each run, Pallas kernels for 7% -> 16%
where the time goes in v5:
time: 617 us; the launch traced here: 610 us
  waiting for transfers between devices  264 us (43%)
  Pallas kernels  141 us (23%)
  starting transfers between devices  99.8 us (16%)
  local copies, waits for them, and re-layouts  69.6 us (11%)
  other arithmetic  33.8 us (5%)
    ppermute x30, waiting for transfers between devices, shift_ring(): return lax.ppermute(value, 'dp', pairs)  146 us
    ppermute x36, waiting for transfers between devices, swap_square(): return lax.ppermute(value, 'dp', [(i, i ^ bit) for i in range(count)])  117 us
    ppermute x30, starting transfers between devices, shift_ring(): return lax.ppermute(value, 'dp', pairs)  42 us
    pallas_call x2, Pallas kernels, mlp_backward(): pl.pallas_call(mlp_backward_kernel, out_shape=(jax.ShapeDtypeStruct((feat...  35.3 us
    ppermute x36, starting transfers between devices, swap_square(): return lax.ppermute(value, 'dp', [(i, i ^ bit) for i in range(count)])  30.7 us
    pallas_call x9, Pallas kernels, scatter_call(): pl.pallas_call(body, out_shape=tuple(outs), grid_spec=pltpu.PrefetchScala...  27.1 us
    ppermute x19, starting transfers between devices, swap_cores(): return lax.ppermute(value, 'section', [(0, 1), (1, 0)])  27.1 us
    pallas_call x2, Pallas kernels, attn_backward(): pl.pallas_call(attn_backward_kernel, out_shape=(jax.ShapeDtypeStruct((fea...  25.1 us
  transfers between devices with their start and end apart: 85, of which 28 were waited for; matrix products, arithmetic and copies ran while one was open for 13% of the time, Pallas kernels for 16%

profile of v5, /device:TPU:1, one launch (start us, length us, event | category | flops | bytes accessed | tf_op | source)
XLA Modules:
  0.0 610.4 jit_solution(10188175888365469336)
XLA Ops:
  18.7 6.8 %collective-permute-done.5.refs_2_ = bf16[48,1536]{1,0:T(8,128)(2,1)S(1)} collective-permute-done((bf16[48,1536]{1,0:T(8,128)(2,1)S(1)}, bf16[48,1536]{1,0:T(8,128)(2,1)S(1)}, u32[]{:S(2)}, u32[]{:S(2)}) %collective-permute-start.5) | collective-permute-done | bytes 147488 | tf_op jit(solution)/shard_map/ppermute | solution.py:517
  36.5 12.8 %collective-permute-done.8.refs_2_ = bf16[48,3072]{1,0:T(8,128)(2,1)S(1)} collective-permute-done((bf16[48,3072]{1,0:T(8,128)(2,1)S(1)}, bf16[48,3072]{1,0:T(8,128)(2,1)S(1)}, u32[]{:S(2)}, u32[]{:S(2)}) %collective-permute-start.8) | collective-permute-done | bytes 294944 | tf_op jit(solution)/shard_map/ppermute | solution.py:517
  51.5 5.6 collective-permute-start.22
  67.6 26.8 %collective-permute-done.15.far_low = bf16[2,48,1536]{2,1,0:T(8,128)(2,1)S(1)} collective-permute-done((bf16[2,48,1536]{2,1,0:T(8,128)(2,1)S(1)}, bf16[2,48,1536]{2,1,0:T(8,128)(2,1)S(1)}, u32[]{:S(2)}, u32[]{:S(2)}) %collective-permute-start.15) | collective-permute-done | bytes 294944 | tf_op jit(solution)/shard_map/ppermute | solution.py:511
  102.6 7.2 %collective-permute-done.11.refs_2_ = bf16[48,3072]{1,0:T(8,128)(2,1)S(1)} collective-permute-done((bf16[48,3072]{1,0:T(8,128)(2,1)S(1)}, bf16[48,3072]{1,0:T(8,128)(2,1)S(1)}, u32[]{:S(2)}, u32[]{:S(2)}) %collective-permute-start.11) | collective-permute-done | bytes 294944 | tf_op jit(solution)/shard_map/ppermute | solution.py:517
  147.1 4.8 collective-permute-done.31.second
  155.5 9.0 %collective-permute-done.27.far_low = bf16[2,48,3072]{2,1,0:T(8,128)(2,1)S(1)} collective-permute-done((bf16[2,48,3072]{2,1,0:T(8,128)(2,1)S(1)}, bf16[2,48,3072]{2,1,0:T(8,128)(2,1)S(1)}, u32[]{:S(2)}, u32[]{:S(2)}) %collective-permute-start.27) | collective-permute-done | bytes 589856 | tf_op jit(solution)/shard_map/ppermute | solution.py:511
  168.2 8.0 %attn_forward.2 = (bf16[2,256,1152]{2,1,0:T(8,128)(2,1)S(1)}, f32[2,6,256]{2,1,0:T(8,128)S(1)}, bf16[256,768]{1,0:T(8,128)(2,1)S(1)}, f32[256,768]{1,0:T(8,128)S(1)}) custom-call(s32[1]{0:T(128)} %bitcast.side, bf16[256,768]{1,0:T(8,128)(2,1)S(1)} %get-tuple-element.94.rows, f32[3,256,128]{2,1,0:T(8,128)S(1)} %copy-done.11, f32[256,256]{1,0:T(8,128)S(1)} %copy-done.22, ...), custom_call_target="tpu_custom_call" | custom-call | flops 1509949440 | bytes 4718592 | tf_op jit(solution)/shard_map/attn_forward/pallas_call | solution.py:151
  180.9 4.1 place_blocks.5
  195.1 5.3 collective-permute-start.38
  200.4 14.6 %collective-permute-done.38.refs_1_ = bf16[4,48,1536]{2,1,0:T(8,128)(2,1)S(1)} collective-permute-done((bf16[4,48,1536]{2,1,0:T(8,128)(2,1)S(1)}, bf16[4,48,1536]{2,1,0:T(8,128)(2,1)S(1)}, u32[]{:S(2)}, u32[]{:S(2)}) %collective-permute-start.38) | collective-permute-done | bytes 589856 | tf_op jit(solution)/shard_map/ppermute | solution.py:517
  214.9 14.8 %collective-permute-done.39.refs_2_ = bf16[4,48,1536]{2,1,0:T(8,128)(2,1)S(1)} collective-permute-done((bf16[4,48,1536]{2,1,0:T(8,128)(2,1)S(1)}, bf16[4,48,1536]{2,1,0:T(8,128)(2,1)S(1)}, u32[]{:S(2)}, u32[]{:S(2)}) %collective-permute-start.39) | collective-permute-done | bytes 589856 | tf_op jit(solution)/shard_map/ppermute | solution.py:517
  230.2 13.8 %collective-permute-done.40.refs_3_ = bf16[4,48,1536]{2,1,0:T(8,128)(2,1)S(1)} collective-permute-done((bf16[4,48,1536]{2,1,0:T(8,128)(2,1)S(1)}, bf16[4,48,1536]{2,1,0:T(8,128)(2,1)S(1)}, u32[]{:S(2)}, u32[]{:S(2)}) %collective-permute-start.40) | collective-permute-done | bytes 589856 | tf_op jit(solution)/shard_map/ppermute | solution.py:517
  245.1 3.8 collective-permute-start.41
  259.3 11.2 %mlp_forward.2 = (bf16[256,3072]{1,0:T(8,128)(2,1)S(1)}, f32[256,3072]{1,0:T(8,128)}, bf16[256,768]{1,0:T(8,128)(2,1)S(1)}) custom-call(s32[1]{0:T(128)} %bitcast.side, bf16[256,768]{1,0:T(8,128)(2,1)S(1)} %get-tuple-element.94.rows, f32[256,768]{1,0:T(8,128)S(1)} %copy-done.33, f32[4,768]{1,0:T(4,128)S(1)} %pad_maximum_fusion.5.norms, ...), custom_call_target="tpu_custom_call" | custom-call | flops 2415919104 | bytes 14155776 | tf_op jit(solution)/shard_map/mlp_forward/pallas_call | solution.py:251
  270.5 9.2 %attn_forward.3 = (bf16[2,256,1152]{2,1,0:T(8,128)(2,1)S(1)}, f32[2,6,256]{2,1,0:T(8,128)S(1)}, bf16[256,768]{1,0:T(8,128)(2,1)S(1)}, f32[256,768]{1,0:T(8,128)S(1)}) custom-call(s32[1]{0:T(128)} %bitcast.side, bf16[256,768]{1,0:T(8,128)(2,1)S(1)} %get-tuple-element.97.rows, f32[3,256,128]{2,1,0:T(8,128)S(1)} %copy-done.11, f32[256,256]{1,0:T(8,128)S(1)} %copy-done.22, ...), custom_call_target="tpu_custom_call" | custom-call | flops 1509949440 | bytes 4718592 | tf_op jit(solution)/shard_map/attn_forward/pallas_call | solution.py:151
  279.8 10.8 %mlp_forward.3 = (bf16[256,3072]{1,0:T(8,128)(2,1)S(1)}, f32[256,3072]{1,0:T(8,128)}, f32[256,768]{1,0:T(8,128)S(1)}) custom-call(s32[1]{0:T(128)} %bitcast.side, bf16[256,768]{1,0:T(8,128)(2,1)S(1)} %get-tuple-element.97.rows, f32[256,768]{1,0:T(8,128)S(1)} %get-tuple-element.102.passed, f32[4,768]{1,0:T(4,128)S(1)} %pad_maximum_fusion.6.norms, ...), custom_call_target="tpu_custom_call" | custom-call | flops 2415919104 | bytes 14155776 | tf_op jit(solution)/shard_map/mlp_forward/pallas_call | solution.py:251
  291.5 17.7 %mlp_backward.2 = (bf16[768,1536]{1,0:T(8,128)(2,1)S(1)}, bf16[768,1536]{1,0:T(8,128)(2,1)}, bf16[768,1536]{1,0:T(8,128)(2,1)}, bf16[768,1536]{1,0:T(8,128)(2,1)...) custom-call(s32[1]{0:T(128)} %bitcast.side, bf16[256,768]{1,0:T(8,128)(2,1)S(1)} %get-tuple-element.97.rows, ...), custom_call_target="tpu_custom_call" | custom-call | flops 4831838208 | bytes 23592960 | tf_op jit(solution)/shard_map/mlp_backward/pallas_call | solution.py:350
  309.8 12.7 %attn_backward.2 = (bf16[768,1536]{1,0:T(8,128)(2,1)}, bf16[768,1536]{1,0:T(8,128)(2,1)}, f32[2,1152]{1,0:T(2,128)S(1)}, f32[5,768]{1,0:T(8,128)S(1)}, bf16[256,768]{1,0:T(8,128)(2,1)S(1)}) custom-call(s32[1]{0:T(128)} %bitcast.side, bf16[256,768]{1,0:T(8,128)(2,1)S(1)} %get-tuple-element.97.rows, bf16[256,768]{1,0:T(8,128)(2,1)S(1)} %copy-done.23, ...), custom_call_target="tpu_custom_call" | custom-call | flops 3623878656 | bytes 9437184 | tf_op jit(solution)/shard_map/attn_backward/pallas_call | solution.py:468
  330.0 17.6 %mlp_backward.3 = (bf16[768,1536]{1,0:T(8,128)(2,1)S(1)}, bf16[768,1536]{1,0:T(8,128)(2,1)}, bf16[768,1536]{1,0:T(8,128)(2,1)}, bf16[768,1536]{1,0:T(8,128)(2,1)...) custom-call(s32[1]{0:T(128)} %bitcast.side, bf16[256,768]{1,0:T(8,128)(2,1)S(1)} %get-tuple-element.94.rows, ...), custom_call_target="tpu_custom_call" | custom-call | flops 4831838208 | bytes 23592960 | tf_op jit(solution)/shard_map/mlp_backward/pallas_call | solution.py:350
  353.7 12.4 %attn_backward.3 = (bf16[768,1536]{1,0:T(8,128)(2,1)}, bf16[768,1536]{1,0:T(8,128)(2,1)}, f32[2,1152]{1,0:T(2,128)S(1)}, f32[5,768]{1,0:T(8,128)S(1)}, f32[256,768]{1,0:T(8,128)S(1)}) custom-call(s32[1]{0:T(128)} %bitcast.side, bf16[256,768]{1,0:T(8,128)(2,1)S(1)} %get-tuple-element.94.rows, bf16[256,768]{1,0:T(8,128)(2,1)S(1)} %copy-done.36, ...), custom_call_target="tpu_custom_call" | custom-call | flops 3623878656 | bytes 9437184 | tf_op jit(solution)/shard_map/attn_backward/pallas_call | solution.py:468
  372.7 13.4 %collective-permute-done.49 = bf16[4,48,1536]{2,1,0:T(8,128)(2,1)} collective-permute-done((bf16[4,48,1536]{2,1,0:T(8,128)(2,1)S(1)}, bf16[4,48,1536]{2,1,0:T(8,128)(2,1)}, u32[]{:S(2)}, u32[]{:S(2)}) %collective-permute-start.49) | collective-permute-done | bytes 589856 | tf_op jit(solution)/shard_map/ppermute | solution.py:517
  390.3 13.5 %collective-permute-done.50 = bf16[4,48,1536]{2,1,0:T(8,128)(2,1)} collective-permute-done((bf16[4,48,1536]{2,1,0:T(8,128)(2,1)S(1)}, bf16[4,48,1536]{2,1,0:T(8,128)(2,1)}, u32[]{:S(2)}, u32[]{:S(2)}) %collective-permute-start.50) | collective-permute-done | bytes 589856 | tf_op jit(solution)/shard_map/ppermute | solution.py:517
  414.3 22.4 %collective-permute-done.66 = f32[4,624]{1,0:T(4,128)S(1)} collective-permute-done((f32[4,624]{1,0:T(4,128)S(1)}, f32[4,624]{1,0:T(4,128)S(1)}, u32[]{:S(2)}, u32[]{:S(2)}) %collective-permute-start.66) | collective-permute-done | bytes 10016 | tf_op jit(solution)/shard_map/ppermute | solution.py:511
  446.2 25.0 %collective-permute-done.52.refs_5_ = bf16[2,48,1536]{2,1,0:T(8,128)(2,1)S(1)} collective-permute-done((bf16[2,48,1536]{2,1,0:T(8,128)(2,1)}, bf16[2,48,1536]{2,1,0:T(8,128)(2,1)S(1)}, u32[]{:S(2)}, u32[]{:S(2)}) %collective-permute-start.52) | collective-permute-done | bytes 294944 | tf_op jit(solution)/shard_map/ppermute | solution.py:511
  488.8 15.0 %collective-permute-done.54.refs_3_ = bf16[4,48,1536]{2,1,0:T(8,128)(2,1)S(1)} collective-permute-done((bf16[4,48,1536]{2,1,0:T(8,128)(2,1)S(1)}, bf16[4,48,1536]{2,1,0:T(8,128)(2,1)S(1)}, u32[]{:S(2)}, u32[]{:S(2)}) %collective-permute-start.54) | collective-permute-done | bytes 589856 | tf_op jit(solution)/shard_map/ppermute | solution.py:511
  513.3 4.6 near_blocks.5
  517.9 12.4 %collective-permute-start.47 = (f32[256,768]{1,0:T(8,128)}, f32[256,768]{1,0:T(8,128)}, u32[]{:S(2)}, u32[]{:S(2)}) collective-permute-start(f32[256,768]{1,0:T(8,128)} %broadcast_select_fusion.2), channel_id=1, source_target_pairs={{0,16},{16,0},{1,17},{17,1},{2,18},{18,2},{3,19},{19,3},{4,20},{20... | collective-permute-start | bytes 2359304 | tf_op jit(solution)/shard_map/ppermute | solution.py:506
  537.3 6.2 %collective-permute-done.56 = bf16[48,1536]{1,0:T(8,128)(2,1)} collective-permute-done((bf16[48,1536]{1,0:T(8,128)(2,1)}, bf16[48,1536]{1,0:T(8,128)(2,1)}, u32[]{:S(2)}, u32[]{:S(2)}) %collective-permute-start.56) | collective-permute-done | bytes 147488 | tf_op jit(solution)/shard_map/ppermute | solution.py:517
  553.7 4.5 collective-permute-done.76.refs_4_
  565.0 15.0 %collective-permute-done.82 = bf16[48,3072]{1,0:T(8,128)(2,1)S(1)} collective-permute-done((bf16[48,3072]{1,0:T(8,128)(2,1)S(1)}, bf16[48,3072]{1,0:T(8,128)(2,1)S(1)}, u32[]{:S(2)}, u32[]{:S(2)}) %collective-permute-start.82) | collective-permute-done | bytes 294944 | tf_op jit(solution)/shard_map/ppermute | solution.py:517
  580.5 24.8 %collective-permute-done.79 = bf16[48,3072]{1,0:T(8,128)(2,1)S(1)} collective-permute-done((bf16[48,3072]{1,0:T(8,128)(2,1)S(1)}, bf16[48,3072]{1,0:T(8,128)(2,1)S(1)}, u32[]{:S(2)}, u32[]{:S(2)}) %collective-permute-start.79) | collective-permute-done | bytes 294944 | tf_op jit(solution)/shard_map/ppermute | solution.py:517
  (502 shorter events, 222.4 us)
Async XLA Ops:
  4.8 28.8 %collective-permute-start.20 = (bf16[624]{0:T(1024)(128)(2,1)S(1)}, bf16[624]{0:T(1024)(128)(2,1)S(1)}, u32[]{:S(2)}, u32[]{:S(2)}) collective-permute-start(bf16[624]{0:T(1024)(128)(2,1)S(1)} %concatenate.55), channel_id=1, source_target_pairs={{0,16},{16,0},{1,17},{17,1},{2,18},{18,2},{3,19},{19,3},{4,20},{20... | collective-permute-start | bytes 3752 | tf_op jit(solution)/shard_map/ppermute | solution.py:506
  32.4 31.8 %collective-permute-start.13 = (bf16[4,48,1536]{2,1,0:T(8,128)(2,1)S(1)}, bf16[4,48,1536]{2,1,0:T(8,128)(2,1)S(1)}, u32[]{:S(2)}, u32[]{:S(2)}) collective-permute-start(bf16[4,48,1536]{2,1,0:T(8,128)(2,1)S(1)} %place_line.6.own), channel_id=1, source_target_pairs={{0,1},{1,0},{2,3},{3,2},{4,5},{5,4},{6,7},{7,6},{8,9},{9,8},{10,11... | collective-permute-start | bytes 1769480 | tf_op jit(solution)/shard_map/ppermute | solution.py:511
  33.7 30.8 %collective-permute-start.14 = (bf16[4,48,1536]{2,1,0:T(8,128)(2,1)S(1)}, bf16[4,48,1536]{2,1,0:T(8,128)(2,1)S(1)}, u32[]{:S(2)}, u32[]{:S(2)}) collective-permute-start(bf16[4,48,1536]{2,1,0:T(8,128)(2,1)S(1)} %place_line.6.own), channel_id=1, source_target_pairs={{0,2},{1,3},{2,0},{3,1},{4,6},{5,7},{6,4},{7,5},{8,10},{9,11},{10,... | collective-permute-start | bytes 1769480 | tf_op jit(solution)/shard_map/ppermute | solution.py:511
  50.2 61.1 %collective-permute-start.18 = (bf16[4,48,3072]{2,1,0:T(8,128)(2,1)S(1)}, bf16[4,48,3072]{2,1,0:T(8,128)(2,1)}, u32[]{:S(2)}, u32[]{:S(2)}) collective-permute-start(bf16[4,48,3072]{2,1,0:T(8,128)(2,1)S(1)} %place_line.7.own), channel_id=1, source_target_pairs={{0,1},{1,0},{2,3},{3,2},{4,5},{5,4},{6,7},{7,6},{8,9},{9,8},{10,11... | collective-permute-start | bytes 3538952 | tf_op jit(solution)/shard_map/ppermute | solution.py:511
  62.8 53.1 %collective-permute-start.19 = (bf16[4,48,3072]{2,1,0:T(8,128)(2,1)S(1)}, bf16[4,48,3072]{2,1,0:T(8,128)(2,1)S(1)}, u32[]{:S(2)}, u32[]{:S(2)}) collective-permute-start(bf16[4,48,3072]{2,1,0:T(8,128)(2,1)S(1)} %place_line.7.own), channel_id=1, source_target_pairs={{0,2},{1,3},{2,0},{3,1},{4,6},{5,7},{6,4},{7,5},{8,10},{9,11},{10,... | collective-permute-start | bytes 3538952 | tf_op jit(solution)/shard_map/ppermute | solution.py:511
  64.2 30.2 %collective-permute-start.15 = (bf16[2,48,1536]{2,1,0:T(8,128)(2,1)S(1)}, bf16[2,48,1536]{2,1,0:T(8,128)(2,1)S(1)}, u32[]{:S(2)}, u32[]{:S(2)}) collective-permute-start(bf16[2,48,1536]{2,1,0:T(8,128)(2,1)S(1)} %slice.190), channel_id=1, source_target_pairs={{0,2},{1,3},{2,0},{3,1},{4,6},{5,7},{6,4},{7,5},{8,10},{9,11},{10,... | collective-permute-start | bytes 884744 | tf_op jit(solution)/shard_map/ppermute | solution.py:511
  65.3 30.1 %collective-permute-start.16 = (bf16[2,48,1536]{2,1,0:T(8,128)(2,1)S(1)}, bf16[2,48,1536]{2,1,0:T(8,128)(2,1)S(1)}, u32[]{:S(2)}, u32[]{:S(2)}) collective-permute-start(bf16[2,48,1536]{2,1,0:T(8,128)(2,1)S(1)} %slice.191), channel_id=1, source_target_pairs={{0,1},{1,0},{2,3},{3,2},{4,5},{5,4},{6,7},{7,6},{8,9},{9,8},{10,11... | collective-permute-start | bytes 884744 | tf_op jit(solution)/shard_map/ppermute | solution.py:511
  66.6 34.8 %collective-permute-start.10 = (bf16[48,3072]{1,0:T(8,128)(2,1)S(1)}, bf16[48,3072]{1,0:T(8,128)(2,1)S(1)}, u32[]{:S(2)}, u32[]{:S(2)}) collective-permute-start(bf16[48,3072]{1,0:T(8,128)(2,1)S(1)} %pad_maximum_fusion.1.refs_0_), channel_id=1, source_target_pairs={{0,4},{1,5},{2,6},{3,7},{4,8},{5,9},{6,10},{7,11},{8,12},{9,13},{1... | collective-permute-start | bytes 884744 | tf_op jit(solution)/shard_map/ppermute | solution.py:517
  111.3 56.8 %collective-permute-start.17 = (bf16[768,1536]{1,0:T(8,128)(2,1)S(1)}, bf16[768,1536]{1,0:T(8,128)(2,1)}, u32[]{:S(2)}, u32[]{:S(2)}) collective-permute-start(bf16[768,1536]{1,0:T(8,128)(2,1)S(1)} %bitcast.198), channel_id=1, source_target_pairs={{0,16},{16,0},{1,17},{17,1},{2,18},{18,2},{3,19},{19,3},{4,20},{20... | collective-permute-start | bytes 7077896 | tf_op jit(solution)/shard_map/ppermute | solution.py:506
  116.9 36.3 %collective-permute-start = (bf16[256,768]{1,0:T(8,128)(2,1)}, bf16[256,768]{1,0:T(8,128)(2,1)}, u32[]{:S(2)}, u32[]{:S(2)}) collective-permute-start(bf16[256,768]{1,0:T(8,128)(2,1)} %dynamic-slice_bitcast_fusion), channel_id=1, source_target_pairs={{0,16},{16,0},{1,17},{17,1},{2,18},{18,2},{3,19},{19,3},{4,20},{20... | collective-permute-start | bytes 1179656 | tf_op jit(solution)/shard_map/ppermute | solution.py:506
  116.9 28.7 %collective-permute-start.30 = (bf16[4,48,3072]{2,1,0:T(8,128)(2,1)}, bf16[4,48,3072]{2,1,0:T(8,128)(2,1)}, u32[]{:S(2)}, u32[]{:S(2)}) collective-permute-start(bf16[4,48,3072]{2,1,0:T(8,128)(2,1)} %place_line.5.own), channel_id=1, source_target_pairs={{0,1},{1,0},{2,3},{3,2},{4,5},{5,4},{6,7},{7,6},{8,9},{9,8},{10,11... | collective-permute-start | bytes 3538952 | tf_op jit(solution)/shard_map/ppermute | solution.py:511
  124.8 27.2 %collective-permute-start.31 = (bf16[4,48,3072]{2,1,0:T(8,128)(2,1)}, bf16[4,48,3072]{2,1,0:T(8,128)(2,1)}, u32[]{:S(2)}, u32[]{:S(2)}) collective-permute-start(bf16[4,48,3072]{2,1,0:T(8,128)(2,1)} %place_line.5.own), channel_id=1, source_target_pairs={{0,2},{1,3},{2,0},{3,1},{4,6},{5,7},{6,4},{7,5},{8,10},{9,11},{10,... | collective-permute-start | bytes 3538952 | tf_op jit(solution)/shard_map/ppermute | solution.py:511
  151.9 28.9 %collective-permute-start.32 = (bf16[2,48,3072]{2,1,0:T(8,128)(2,1)S(1)}, bf16[2,48,3072]{2,1,0:T(8,128)(2,1)S(1)}, u32[]{:S(2)}, u32[]{:S(2)}) collective-permute-start(bf16[2,48,3072]{2,1,0:T(8,128)(2,1)S(1)} %slice.205), channel_id=1, source_target_pairs={{0,2},{1,3},{2,0},{3,1},{4,6},{5,7},{6,4},{7,5},{8,10},{9,11},{10,... | collective-permute-start | bytes 1769480 | tf_op jit(solution)/shard_map/ppermute | solution.py:511
  153.3 27.6 %collective-permute-start.33 = (bf16[2,48,3072]{2,1,0:T(8,128)(2,1)S(1)}, bf16[2,48,3072]{2,1,0:T(8,128)(2,1)S(1)}, u32[]{:S(2)}, u32[]{:S(2)}) collective-permute-start(bf16[2,48,3072]{2,1,0:T(8,128)(2,1)S(1)} %slice.206), channel_id=1, source_target_pairs={{0,1},{1,0},{2,3},{3,2},{4,5},{5,4},{6,7},{7,6},{8,9},{9,8},{10,11... | collective-permute-start | bytes 1769480 | tf_op jit(solution)/shard_map/ppermute | solution.py:511
  178.1 80.1 %collective-permute-start.29 = (bf16[768,3072]{1,0:T(8,128)(2,1)}, bf16[768,3072]{1,0:T(8,128)(2,1)}, u32[]{:S(2)}, u32[]{:S(2)}) collective-permute-start(bf16[768,3072]{1,0:T(8,128)(2,1)} %bitcast.41.up_mine.down_mine), channel_id=1, source_target_pairs={{0,16},{16,0},{1,17},{17,1},{2,18},{18,2},{3,19},{19,3},{4,20},{20... | collective-permute-start | bytes 14155784 | tf_op jit(solution)/shard_map/ppermute | solution.py:506
  185.0 85.5 %collective-permute-start.34 = (bf16[768,3072]{1,0:T(8,128)(2,1)}, bf16[768,3072]{1,0:T(8,128)(2,1)}, u32[]{:S(2)}, u32[]{:S(2)}) collective-permute-start(bf16[768,3072]{1,0:T(8,128)(2,1)} %bitcast.205), channel_id=1, source_target_pairs={{0,16},{16,0},{1,17},{17,1},{2,18},{18,2},{3,19},{19,3},{4,20},{20... | collective-permute-start | bytes 14155784 | tf_op jit(solution)/shard_map/ppermute | solution.py:506
  245.1 34.6 %collective-permute-start.41 = (bf16[768,1536]{1,0:T(8,128)(2,1)S(1)}, bf16[768,1536]{1,0:T(8,128)(2,1)}, u32[]{:S(2)}, u32[]{:S(2)}) collective-permute-start(bf16[768,1536]{1,0:T(8,128)(2,1)S(1)} %bitcast.195), channel_id=1, source_target_pairs={{0,16},{16,0},{1,17},{17,1},{2,18},{18,2},{3,19},{19,3},{4,20},{20... | collective-permute-start | bytes 7077896 | tf_op jit(solution)/shard_map/ppermute | solution.py:506
  367.1 38.4 %collective-permute-start.48 = (bf16[768,1536]{1,0:T(8,128)(2,1)}, bf16[768,1536]{1,0:T(8,128)(2,1)}, u32[]{:S(2)}, u32[]{:S(2)}) collective-permute-start(bf16[768,1536]{1,0:T(8,128)(2,1)} %get-tuple-element.136), channel_id=1, source_target_pairs={{0,16},{16,0},{1,17},{17,1},{2,18},{18,2},{3,19},{19,3},{4,20},{20... | collective-permute-start | bytes 7077896 | tf_op jit(solution)/shard_map/ppermute | solution.py:506
  372.2 108.6 %collective-permute-start.70 = (bf16[768,1536]{1,0:T(8,128)(2,1)}, bf16[768,1536]{1,0:T(8,128)(2,1)}, u32[]{:S(2)}, u32[]{:S(2)}) collective-permute-start(bf16[768,1536]{1,0:T(8,128)(2,1)} %get-tuple-element.155), channel_id=1, source_target_pairs={{0,16},{16,0},{1,17},{17,1},{2,18},{18,2},{3,19},{19,3},{4,20},{20... | collective-permute-start | bytes 7077896 | tf_op jit(solution)/shard_map/ppermute | solution.py:506
  372.2 108.6 %collective-permute-start.71 = (bf16[768,1536]{1,0:T(8,128)(2,1)}, bf16[768,1536]{1,0:T(8,128)(2,1)}, u32[]{:S(2)}, u32[]{:S(2)}) collective-permute-start(bf16[768,1536]{1,0:T(8,128)(2,1)} %get-tuple-element.157), channel_id=1, source_target_pairs={{0,16},{16,0},{1,17},{17,1},{2,18},{18,2},{3,19},{19,3},{4,20},{20... | collective-permute-start | bytes 7077896 | tf_op jit(solution)/shard_map/ppermute | solution.py:506
  403.7 72.6 %collective-permute-start.72 = (bf16[4,48,3072]{2,1,0:T(8,128)(2,1)}, bf16[4,48,3072]{2,1,0:T(8,128)(2,1)S(1)}, u32[]{:S(2)}, u32[]{:S(2)}) collective-permute-start(bf16[4,48,3072]{2,1,0:T(8,128)(2,1)} %copy-done.41), channel_id=1, source_target_pairs={{0,1},{1,0},{2,3},{3,2},{4,5},{5,4},{6,7},{7,6},{8,9},{9,8},{10,11... | collective-permute-start | bytes 3538952 | tf_op jit(solution)/shard_map/ppermute | solution.py:511
  408.6 34.7 %collective-permute-start.51 = (bf16[2,48,1536]{2,1,0:T(8,128)(2,1)}, bf16[2,48,1536]{2,1,0:T(8,128)(2,1)}, u32[]{:S(2)}, u32[]{:S(2)}) collective-permute-start(bf16[2,48,1536]{2,1,0:T(8,128)(2,1)} %get-tuple-element.142), channel_id=1, source_target_pairs={{0,1},{1,0},{2,3},{3,2},{4,5},{5,4},{6,7},{7,6},{8,9},{9,8},{10,11... | collective-permute-start | bytes 884744 | tf_op jit(solution)/shard_map/ppermute | solution.py:511
  442.3 35.2 %collective-permute-start.73 = (bf16[4,48,3072]{2,1,0:T(8,128)(2,1)}, bf16[4,48,3072]{2,1,0:T(8,128)(2,1)}, u32[]{:S(2)}, u32[]{:S(2)}) collective-permute-start(bf16[4,48,3072]{2,1,0:T(8,128)(2,1)} %copy-done.40), channel_id=1, source_target_pairs={{0,2},{1,3},{2,0},{3,1},{4,6},{5,7},{6,4},{7,5},{8,10},{9,11},{10,... | collective-permute-start | bytes 3538952 | tf_op jit(solution)/shard_map/ppermute | solution.py:511
  443.2 28.0 %collective-permute-start.52 = (bf16[2,48,1536]{2,1,0:T(8,128)(2,1)}, bf16[2,48,1536]{2,1,0:T(8,128)(2,1)S(1)}, u32[]{:S(2)}, u32[]{:S(2)}) collective-permute-start(bf16[2,48,1536]{2,1,0:T(8,128)(2,1)} %copy-done.46), channel_id=1, source_target_pairs={{0,2},{1,3},{2,0},{3,1},{4,6},{5,7},{6,4},{7,5},{8,10},{9,11},{10,... | collective-permute-start | bytes 884744 | tf_op jit(solution)/shard_map/ppermute | solution.py:511
  477.5 28.8 %collective-permute-start.69 = (f32[1,624]{1,0:T(1,128)S(1)}, f32[1,624]{1,0:T(1,128)S(1)}, u32[]{:S(2)}, u32[]{:S(2)}) collective-permute-start(f32[1,624]{1,0:T(1,128)S(1)} %get-tuple-element.238), channel_id=1, source_target_pairs={{0,12},{1,13},{2,14},{3,15},{4,0},{5,1},{6,2},{7,3},{8,4},{9,5},{1... | collective-permute-start | bytes 7496 | tf_op jit(solution)/shard_map/ppermute | solution.py:517
  483.1 25.7 %collective-permute-start.74 = (bf16[2,48,3072]{2,1,0:T(8,128)(2,1)S(1)}, bf16[2,48,3072]{2,1,0:T(8,128)(2,1)S(1)}, u32[]{:S(2)}, u32[]{:S(2)}) collective-permute-start(bf16[2,48,3072]{2,1,0:T(8,128)(2,1)S(1)} %get-tuple-element.162), channel_id=1, source_target_pairs={{0,1},{1,0},{2,3},{3,2},{4,5},{5,4},{6,7},{7,6},{8,9},{9,8},{10,11... | collective-permute-start | bytes 1769480 | tf_op jit(solution)/shard_map/ppermute | solution.py:511
  517.9 27.8 %collective-permute-start.47 = (f32[256,768]{1,0:T(8,128)}, f32[256,768]{1,0:T(8,128)}, u32[]{:S(2)}, u32[]{:S(2)}) collective-permute-start(f32[256,768]{1,0:T(8,128)} %broadcast_select_fusion.2), channel_id=1, source_target_pairs={{0,16},{16,0},{1,17},{17,1},{2,18},{18,2},{3,19},{19,3},{4,20},{20... | collective-permute-start | bytes 2359304 | tf_op jit(solution)/shard_map/ppermute | solution.py:506
  530.3 27.9 %collective-permute-start.76 = (bf16[4,48,3072]{2,1,0:T(8,128)(2,1)}, bf16[4,48,3072]{2,1,0:T(8,128)(2,1)S(1)}, u32[]{:S(2)}, u32[]{:S(2)}) collective-permute-start(bf16[4,48,3072]{2,1,0:T(8,128)(2,1)} %get-tuple-element.164), channel_id=1, source_target_pairs={{0,1},{1,0},{2,3},{3,2},{4,5},{5,4},{6,7},{7,6},{8,9},{9,8},{10,11... | collective-permute-start | bytes 3538952 | tf_op jit(solution)/shard_map/ppermute | solution.py:511
  531.3 27.5 %collective-permute-start.77 = (bf16[4,48,3072]{2,1,0:T(8,128)(2,1)}, bf16[4,48,3072]{2,1,0:T(8,128)(2,1)}, u32[]{:S(2)}, u32[]{:S(2)}) collective-permute-start(bf16[4,48,3072]{2,1,0:T(8,128)(2,1)} %get-tuple-element.165), channel_id=1, source_target_pairs={{0,2},{1,3},{2,0},{3,1},{4,6},{5,7},{6,4},{7,5},{8,10},{9,11},{10,... | collective-permute-start | bytes 3538952 | tf_op jit(solution)/shard_map/ppermute | solution.py:511
  552.5 27.5 %collective-permute-start.82 = (bf16[48,3072]{1,0:T(8,128)(2,1)S(1)}, bf16[48,3072]{1,0:T(8,128)(2,1)S(1)}, u32[]{:S(2)}, u32[]{:S(2)}) collective-permute-start(bf16[48,3072]{1,0:T(8,128)(2,1)S(1)} %get-tuple-element.172), channel_id=1, source_target_pairs={{0,8},{1,9},{2,10},{3,11},{4,12},{5,13},{6,14},{7,15},{8,0},{9,1},... | collective-permute-start | bytes 884744 | tf_op jit(solution)/shard_map/ppermute | solution.py:517
  564.5 40.8 %collective-permute-start.79 = (bf16[48,3072]{1,0:T(8,128)(2,1)S(1)}, bf16[48,3072]{1,0:T(8,128)(2,1)S(1)}, u32[]{:S(2)}, u32[]{:S(2)}) collective-permute-start(bf16[48,3072]{1,0:T(8,128)(2,1)S(1)} %get-tuple-element.168), channel_id=1, source_target_pairs={{0,8},{1,9},{2,10},{3,11},{4,12},{5,13},{6,14},{7,15},{8,0},{9,1},... | collective-permute-start | bytes 884744 | tf_op jit(solution)/shard_map/ppermute | solution.py:517
  564.6 40.7 %collective-permute-start.78 = (bf16[48,3072]{1,0:T(8,128)(2,1)S(1)}, bf16[48,3072]{1,0:T(8,128)(2,1)S(1)}, u32[]{:S(2)}, u32[]{:S(2)}) collective-permute-start(bf16[48,3072]{1,0:T(8,128)(2,1)S(1)} %get-tuple-element.167), channel_id=1, source_target_pairs={{0,4},{1,5},{2,6},{3,7},{4,8},{5,9},{6,10},{7,11},{8,12},{9,13},{1... | collective-permute-start | bytes 884744 | tf_op jit(solution)/shard_map/ppermute | solution.py:517
  (131 other events, 1587.8 us)

commit v6 on v5

--- a/solution.py
+++ b/solution.py
@@ -2,6 +2,7 @@
 
 import jax
 import jax.numpy as jnp
+import numpy as np
 from jax import lax
 from jax.experimental import pallas as pl
 from jax.experimental.pallas import tpu as pltpu
@@ -168,7 +169,7 @@
         ),
         compiler_params=pltpu.CompilerParams(vmem_limit_bytes=vmem_bytes),
         cost_estimate=pl.CostEstimate(
-            flops=2 * length * features * features * 5,
+            flops=2 * length * features * features * 30,
             bytes_accessed=8 * features * features,
             transcendentals=length * length * features // HD,
         ),
@@ -278,7 +279,7 @@
         ),
         compiler_params=pltpu.CompilerParams(vmem_limit_bytes=vmem_bytes),
         cost_estimate=pl.CostEstimate(
-            flops=4 * length * features * hidden,
+            flops=20 * length * features * hidden,
             bytes_accessed=4 * features * hidden + 6 * length * hidden,
             transcendentals=2 * length * hidden,
         ),
@@ -383,7 +384,7 @@
         ),
         compiler_params=pltpu.CompilerParams(vmem_limit_bytes=vmem_bytes),
         cost_estimate=pl.CostEstimate(
-            flops=8 * length * features * hidden,
+            flops=32 * length * features * hidden,
             bytes_accessed=8 * features * hidden + 6 * length * hidden,
             transcendentals=0,
         ),
@@ -443,7 +444,7 @@
         for index, part in enumerate((query_grad, key_grad, value_grad)):
             cut = slice(index * width, (index + 1) * width)
             part = part.astype(jnp.bfloat16)
-            bias_grad[at : at + 1, cut] = jnp.sum(
+            bias_grad[pl.ds(half, 1), cut] = jnp.sum(
                 part.astype(jnp.float32), axis=0, keepdims=True
             )
             result[:, cut] = product(normed, part).astype(jnp.bfloat16)
@@ -488,7 +489,7 @@
         scratch_shapes=[pltpu.VMEM((length, features), jnp.bfloat16)],
         compiler_params=pltpu.CompilerParams(vmem_limit_bytes=vmem_bytes),
         cost_estimate=pl.CostEstimate(
-            flops=2 * length * features * features * 12,
+            flops=2 * length * features * features * 48,
             bytes_accessed=16 * features * features,
             transcendentals=length * length * features // HD,
         ),
@@ -620,9 +621,13 @@
     return (swap_square(column, 1), swap_square(column, 2))
 
 
-def far_moved(near):
+def cut_near(near):
     half = RING // 2
-    return (swap_square(near[0][:half], 2), swap_square(near[1][half:], 1))
+    return (near[0][:half], near[1][half:])
+
+
+def far_moved(lows):
+    return (swap_square(lows[0], 2), swap_square(lows[1], 1))
 
 
 def ring_around(blocks):
@@ -632,13 +637,59 @@
     return held
 
 
-def gather_small(piece):
-    if not small_slice():
-        return gather_whole(piece)
-    column = jnp.take(jnp.stack([piece] + ring_moved(piece)), ring_order(), axis=0)
-    stacked = jnp.stack([column] + square_moved(column), axis=1)
-    stacked = jnp.take(stacked, square_order(), axis=1)
-    return stacked.reshape(RING * SQUARE * piece.shape[0], -1)
+def spread_kernel(side, rows, *refs):
+    picks, outs = refs[:6], refs[6:]
+    count = rows.shape[0]
+    width = outs[0].shape[2] // 3
+    size = rows.shape[1] // 2
+
+    def row(at, which):
+        pick, keep = picks[2 * which], picks[2 * which + 1]
+        found = product(rows[:, at : at + pick.shape[0]], pick[...])
+        return jnp.sum(found * keep[...], axis=0, keepdims=True)
+
+    for layer in range(2):
+        at = layer * size
+        found = row(at, 0)
+        for half in range(2):
+            parts = [
+                found[:, (2 * part + half) * width : (2 * part + half + 1) * width]
+                for part in range(3)
+            ]
+            outs[0][layer, pl.ds(half ^ side[0], 1), :] = jnp.concatenate(parts, axis=1)
+        at += picks[0].shape[0]
+        outs[1][layer] = row(at, 1)
+        at += picks[2].shape[0]
+        step = picks[4].shape[0]
+        for index in range(2):
+            outs[2][layer, index : index + 1, :] = row(at + index * step, 2)
+        for index in range(4):
+            outs[3][layer, index : index + 1, :] = row(at + (2 + index) * step, 2)
+
+
+def spread_small(side, rows, shards, features):
+    count = rows.shape[0]
+    picks = []
+    for shard in shards:
+        lane = np.arange(count * shard)
+        picks.append(jnp.asarray(np.arange(shard)[:, None] == lane % shard, jnp.bfloat16))
+        picks.append(jnp.asarray(np.arange(count)[:, None] == lane // shard, jnp.float32))
+    shapes = (
+        (2, 2, 3 * features // 2),
+        (2, 1, count * shards[1]),
+        (2, 2, features),
+        (2, 4, features),
+    )
+    outs = [jax.ShapeDtypeStruct(shape, jnp.float32) for shape in shapes]
+    return pl.pallas_call(
+        spread_kernel,
+        out_shape=tuple(outs),
+        grid=(1,),
+        in_specs=[pl.BlockSpec(memory_space=pltpu.SMEM)] + fixed_like(rows, *picks),
+        out_specs=tuple(fixed_like(*outs)),
+        compiler_params=pltpu.CompilerParams(vmem_limit_bytes=vmem_bytes),
+        name="spread_small",
+    )(side, rows, *picks)
 
 
 def far_kernel(place_ref, *refs):
@@ -775,26 +826,6 @@
         swap_square(block(spot ^ bit).astype(jnp.bfloat16), bit) for bit in range(1, SQUARE)
     ]
     return [block(spot)] + moved
-
-
-def scatter_small(kept, sent):
-    summed = kept + swap_cores(sent)
-    if not small_slice():
-        return lax.psum_scatter(summed, "dp", scatter_dimension=0, tiled=True)
-    level, spot = own_place()
-    blocks = summed.reshape(RING, SQUARE, -1)
-
-    def block(index):
-        return lax.dynamic_index_in_dim(blocks, index, 1, keepdims=False)
-
-    column = block(spot)
-    for bit in range(1, SQUARE):
-        column = column + swap_square(block(spot ^ bit), bit)
-    total = lax.dynamic_index_in_dim(column, level, 0, keepdims=True)
-    for steps in range(1, RING):
-        part = lax.dynamic_index_in_dim(column, (level + steps) % RING, 0, keepdims=True)
-        total = total + shift_ring(part, steps)
-    return total
 
 
 def folded(rows, parts):
@@ -881,32 +912,7 @@
         [a[0].reshape(-1) for a in (qkv_bias, up_bias, out_biases, norm_gains, norm_biases)]
     )
     small_both = jnp.concatenate(ordered(is_first, small_own, swap_cores(small_own)))
-    small_full = gather_small(small_both[None])
-    small_full = small_full.reshape(count, 2, small_own.shape[0]).astype(jnp.float32)
-
-    def small_of(layer):
-        rows = small_full[:, layer]
-        found = []
-        at = 0
-        for shape in small_shapes:
-            size = math.prod(shape)
-            part = rows[:, at : at + size].reshape((count,) + shape)
-            at += size
-            if len(shape) == 2:
-                part = part.transpose(1, 0, 2).reshape(shape[0], count * shape[1])
-            else:
-                part = part.reshape(1, count * shape[0])
-            found.append(part)
-        bias_qkv, bias_up, bias_out, gains, shifts = found
-        bias_qkv = bias_qkv.reshape(3, 2, width).transpose(1, 0, 2).reshape(2, 3 * width)
-        return dict(
-            qkv=jnp.where(is_first, bias_qkv, bias_qkv[::-1]),
-            up=bias_up,
-            out=bias_out,
-            norms=jnp.concatenate([gains, shifts]),
-        )
-
-    small = [small_of(layer) for layer in range(2)]
+    shards = (qkv_bias.shape[1], up_bias.shape[1], norm_gains.shape[2])
     kept_forward = {}
     slabs = {}
 
@@ -938,63 +944,74 @@
             kept_forward[layer, "attn"][:3], grad_mlp, *slabs[layer, "narrow"], kind,
         )
 
-    def vectors_of(bias_qkv, bias_up, sums):
-        bias_qkv = jnp.where(is_first, bias_qkv, bias_qkv[::-1])
-        bias_qkv = bias_qkv.reshape(2, 3, width).transpose(1, 0, 2).reshape(1, 6 * width)
-        double = jnp.concatenate([sums[4:5], sums[4:5]])
-        return (bias_qkv, bias_up, double, sums[0:2], sums[2:4])
-
-    places = ((0, 1), (TILES, 0))
+    def vector_of(bias_qkv, bias_up, sums):
+        parts = [
+            bias_qkv[half : half + 1, part * width : (part + 1) * width]
+            for part in range(3)
+            for half in range(2)
+        ]
+        order = (4, 4, 0, 1, 2, 3)
+        parts += [bias_up] + [sums[index : index + 1] for index in order]
+        return jnp.concatenate(parts, axis=1)
+
+    small = []
+
+    def spread_out(rows):
+        spread = spread_small(side, rows, shards, features)
+        for layer in range(2):
+            made = (part[layer] for part in spread)
+            small.append(dict(zip(("qkv", "up", "out", "norms"), made)))
+
+    places = ((TILES, 0), (TILES, 1))
     if small_slice():
         narrow, up, down = pieces
-        lower_mlp = jnp.concatenate([up[0], folded(down[0], 1)], axis=1)
-        upper_wide = jnp.concatenate([narrow[1], up[1]], axis=1)
-        upper_down = folded(down[1], 1)
-
-        ring_a = ring_moved(narrow[0])
-        square_d = square_moved(upper_down)
-        column_a = column_of(narrow[0], ring_a)
+        wide = [jnp.concatenate([narrow[layer], up[layer]], axis=1) for layer in range(2)]
+        deep = jnp.concatenate([folded(down[layer], 1) for layer in range(2)], axis=1)
+        whole_b = gather_whole(deep)
+        ring_a = ring_moved(wide[0])
+        line = small_both[None]
+        ring_s = ring_moved(line)
+        column_s = line_placed(ring_order(), [line] + ring_s)
+        column_a = column_of(wide[0], ring_a)
+        column_a, next_c, column_s = after((column_a, wide[1], column_s), (ring_a, ring_s))
         near_a = near_moved(column_a)
-        ring_b = ring_moved(after(lower_mlp, ring_a))
-        column_b = column_of(lower_mlp, ring_b)
-        far_a = far_moved(near_a)
-        near_b = near_moved(column_b)
-        ring_c = ring_moved(after(upper_wide, ring_b))
+        square_s = square_moved(column_s)
+        ring_c = ring_moved(next_c)
+        column_c = column_of(next_c, ring_c)
+        lows, column_c, square_s = after(
+            (cut_near(near_a), column_c, square_s), (near_a, ring_c, square_s)
+        )
+        far_a = far_moved(lows)
+        near_c = near_moved(column_c)
+        rows_s = line_placed(square_order(), [column_s] + square_s)
+        spread_out(rows_s.transpose(1, 0, 2, 3).reshape(PARTS, -1))
         whole_a = place_blocks((column_a,) + near_a + far_a)
-        slabs[0, "narrow"] = (whole_a, swap_cores(whole_a))
-        far_b = far_moved(near_b)
-        column_c = column_of(upper_wide, ring_c)
-        near_c = near_moved(after(column_c, near_b))
-        blocks_d = line_placed(square_order(), [upper_down] + square_d)
-        held_d = ring_around(after(blocks_d, ring_c))
-        attn_rows, _ = after((entry, entry), (column_c, slabs[0, "narrow"], near_b))
-        attn_step(0, attn_rows)
-        whole_b = place_blocks((column_b,) + near_b + far_b)
-        whole_b = after(whole_b, kept_forward[0, "attn"][3])
+        lows, whole_a = after((cut_near(near_c), whole_a), (far_a, near_c, small))
+        far_c = far_moved(lows)
+        swapped_a = swap_cores(whole_a)
+        slabs[0, "narrow"] = (whole_a, swapped_a)
+        whole_b = after(whole_b, far_a)
         swapped_b = swap_cores(whole_b)
-        slabs[0, "mlp"] = (whole_b, swapped_b, whole_b, swapped_b)
+        slabs[0, "mlp"] = (whole_a, swapped_a, whole_b, swapped_b)
+        attn_step(0, entry)
         mlp_step(0, jnp.bfloat16)
-        far_c = far_moved(near_c)
         whole_c = place_blocks((column_c,) + near_c + far_c)
         swapped_c = swap_cores(whole_c)
         slabs[1, "narrow"] = (whole_c, swapped_c)
-        whole_d = line_placed(ring_order(), held_d).reshape(whole_a.shape)
-        swapped_d = swap_cores(whole_d)
-        slabs[1, "mlp"] = (whole_c, swapped_c, whole_d, swapped_d)
+        slabs[1, "mlp"] = (whole_c, swapped_c, whole_b, swapped_b)
         attn_step(1, kept_forward[0, "mlp"][2])
         mlp_step(1, jnp.float32)
     else:
+        spread_out(gather_whole(small_both[None]))
+        whole_b = jnp.concatenate(
+            [folded(gather_whole(pieces[2][layer]), PARTS) for layer in range(2)], axis=1
+        )
+        second = (whole_b, swap_cores(whole_b))
         for layer in range(2):
-            narrow, up, down = (gather_whole(piece[layer]) for piece in pieces)
-            down = folded(down, PARTS)
-            joined = (narrow, up, down)
-            if layer == 0:
-                joined = (narrow, jnp.concatenate([up, down], axis=1))
-            else:
-                joined = (jnp.concatenate([narrow, up], axis=1), down)
-            first, second = ((part, swap_cores(part)) for part in joined)
-            slabs[layer, "narrow"] = first
-            slabs[layer, "mlp"] = (second if layer == 0 else first) + second
+            narrow, up = (gather_whole(piece[layer]) for piece in pieces[:2])
+            wide = jnp.concatenate([narrow, up], axis=1)
+            slabs[layer, "narrow"] = (wide, swap_cores(wide))
+            slabs[layer, "mlp"] = slabs[layer, "narrow"] + second
         attn_step(0, entry)
         mlp_step(0, jnp.bfloat16)
         attn_step(1, kept_forward[0, "mlp"][2])
@@ -1010,30 +1027,31 @@
         upper_attn = attn_back(1, cotangent, upper[5], jnp.bfloat16)
         leaving_a = far_blocks(after(pairs_a, upper_attn[2]))
         far_a = sent_both(leaving_a)
-        grad_middle, received_b = after(
-            (upper_attn[4], swap_cores(upper_attn[1])), leaving_a
-        )
+        grad_middle = after(upper_attn[4], leaving_a)
+        received_b = swap_cores(upper_attn[1])
         lower = mlp_back(0, grad_middle)
-        near_a = near_blocks(pairs_a, after(far_a, lower[4]))
+        leaving_a = near_blocks(pairs_a, after(far_a, lower[4]))
+        near_a = sent_both(leaving_a)
         steps_b = ring_steps(upper_attn[0], after(received_b, lower[4]))
         moved_b = next(steps_b)
         pairs_c = mlp_pairs(lower)
-        grad_mlp = after(lower[5], near_a)
-        near_a = sent_both(near_a)
-        lower_attn = attn_back(0, grad_middle, grad_mlp, jnp.float32)
-        pairs_c = after(pairs_c, (lower_attn[2], near_a, moved_b))
-        far_c = sent_both(far_blocks(pairs_c))
+        lower_attn = attn_back(
+            0, grad_middle, after(lower[5], (leaving_a, received_b)), jnp.float32
+        )
         pairs_d = (lower_attn[0], swap_cores(lower_attn[1]))
         moved_b = next(steps_b)
-        far_d = sent_both(far_blocks(after(pairs_d, moved_b)))
-        parts_a = column_sent(pairs_a, near_a)
-        near_c = sent_both(near_blocks(pairs_c, far_c))
+        pairs_c = after(pairs_c, (lower_attn[2], near_a))
+        far_c = sent_both(far_blocks(pairs_c))
+        pairs_d = after(pairs_d, near_a)
+        far_d = sent_both(far_blocks(pairs_d))
         moved_b = next(steps_b)
+        parts_a = column_sent(pairs_a, after(near_a, far_c))
+        near_c = sent_both(near_blocks(pairs_c, after(far_c, far_d)))
         blocks_b = next(steps_b)
-        parts_b = square_sent(blocks_b)
-        near_d = sent_both(near_blocks(pairs_d, far_d))
+        near_d = sent_both(near_blocks(pairs_d, after(far_d, near_c)))
         parts_c = column_sent(pairs_c, near_c)
-        parts_d = column_sent(pairs_d, near_d)
+        parts_b = square_sent(after(blocks_b, near_c))
+        parts_d = column_sent(pairs_d, after(near_d, near_c))
         reduced = (
             (total_of(parts_d), total_of(parts_b)),
             (total_of(parts_c), total_of(parts_a)),
@@ -1058,9 +1076,6 @@
             tuple(spread_mlp(made) for made in (lower, upper)),
         )
     grad_entry = lower_attn[4]
-    vectors_upper = vectors_of(upper_attn[2], upper[4], upper_attn[3])
-    vectors_lower = vectors_of(lower_attn[2], lower[4], lower_attn[3])
-
     def finish(lower, upper):
         mine, leaving = ordered(is_first, lower, upper)
         return ordered(is_first, mine, swap_cores(leaving))
@@ -1081,23 +1096,26 @@
     )
     total_out = jnp.concatenate([part[:, 3 * width :] for part in narrow_halves], axis=1)
 
-    def small_rows(vectors):
-        parts = []
-        for grad in vectors:
-            part = grad.reshape(grad.shape[0], count, -1).transpose(1, 0, 2)
-            parts.append(part.reshape(count, -1))
-        return jnp.concatenate(parts, axis=1)
-
-    small_kept, small_sent = ordered(
-        is_first, small_rows(vectors_lower), small_rows(vectors_upper)
-    )
-    small_total = scatter_small(small_kept, small_sent)[0]
+    vectors = [
+        vector_of(attn[2], mlp[4], attn[3])
+        for mlp, attn in ((lower, lower_attn), (upper, upper_attn))
+    ]
+    vector_kept, vector_sent = ordered(is_first, *vectors)
+    if small_slice():
+        vector = vector_kept + swap_cores(vector_sent)
+        vector = total_of([vector] + square_moved(vector))
+        vector = total_of([vector] + ring_moved(after(vector, near_c)))
+    else:
+        vector = lax.psum(vector_kept + swap_cores(vector_sent), "dp")
+    place = lax.axis_index("dp")
     small_outs = []
     at = 0
     for shape in small_shapes:
-        size = math.prod(shape)
-        small_outs.append(small_total[at : at + size].reshape((1,) + shape))
-        at += size
+        lead, size = (1,) if len(shape) == 1 else (shape[0],), shape[-1]
+        rows = vector[0, at : at + lead[0] * size * count].reshape(lead[0], count * size)
+        at += lead[0] * size * count
+        part = lax.dynamic_slice_in_dim(rows, place * size, size, 1)
+        small_outs.append(part.reshape((1,) + shape))
 
     staying, leaving = ordered(is_first, grad_entry, produced)
     ends_out = jnp.concatenate(ordered(is_first, staying, swap_cores(leaving)))

time: 617 us -> 466 us (0.76)
  waiting for transfers between devices: 264 us -> 159 us
  local copies, waits for them, and re-layouts: 69.6 us -> 44.9 us
  other arithmetic: 33.8 us -> 17.9 us
  between operations: 2.25 us -> 15.5 us
  starting transfers between devices: 99.8 us -> 86.9 us
    ppermute x30 -> x24, waiting for transfers between devices: 146 us -> 71.2 us  [shift_ring(): return lax.ppermute(value, 'dp', pairs)]
    ppermute x36 -> x29, waiting for transfers between devices: 117 us -> 79.7 us  [swap_square(): return lax.ppermute(value, 'dp', [(i, i ^ bit) for i in range(count)])]
    reshape x36 -> x4, local copies, waits for them, and re-layouts: 15.3 us -> 5.28 us  [the longest x3 3.87 us: on_device(): small_outs.append(part.reshape((1,) + shape))]
    ppermute x36 -> x29, starting transfers between devices: 30.7 us -> 22.6 us  [swap_square(): return lax.ppermute(value, 'dp', [(i, i ^ bit) for i in range(count)])]
    ppermute x19 -> x18, waiting for transfers between devices: 0.92 us -> 8.33 us  [swap_cores(): return lax.ppermute(value, 'section', [(0, 1), (1, 0)])]
    ppermute x19 -> x18, starting transfers between devices: 27.1 us -> 20.6 us  [swap_cores(): return lax.ppermute(value, 'section', [(0, 1), (1, 0)])]
    rev x4 -> x0, local copies, waits for them, and re-layouts: 6.36 us -> none  [the longest x2 5.89 us: small_of(): bias_qkv[::-1]]
    unnamed x166 -> x156, local copies, waits for them, and re-layouts: 20.9 us -> 23 us
  transfers between devices with their start and end apart: 85 -> 72, of which waited for: 28 -> 21; matrix products, arithmetic and copies ran while one was open for 13% -> 8% of each run, Pallas kernels for 16% -> 22%
where the time goes in v6:
time: 466 us; the launch traced here: 462 us
  waiting for transfers between devices  159 us (34%)
  Pallas kernels  137 us (29%)
  starting transfers between devices  86.9 us (19%)
  local copies, waits for them, and re-layouts  44.9 us (10%)
  other arithmetic  17.9 us (4%)
  between operations  15.5 us (3%)
    ppermute x29, waiting for transfers between devices, swap_square(): return lax.ppermute(value, 'dp', [(i, i ^ bit) for i in range(count)])  79.7 us
    ppermute x24, waiting for transfers between devices, shift_ring(): return lax.ppermute(value, 'dp', pairs)  71.2 us
    ppermute x24, starting transfers between devices, shift_ring(): return lax.ppermute(value, 'dp', pairs)  43.6 us
    pallas_call x2, Pallas kernels, mlp_backward(): pl.pallas_call(mlp_backward_kernel, out_shape=(jax.ShapeDtypeStruct((feat...  35.3 us
    pallas_call x2, Pallas kernels, attn_backward(): pl.pallas_call(attn_backward_kernel, out_shape=(jax.ShapeDtypeStruct((fea...  25.7 us
    pallas_call x9, Pallas kernels, scatter_call(): pl.pallas_call(body, out_shape=tuple(outs), grid_spec=pltpu.PrefetchScala...  24.3 us
    pallas_call x2, Pallas kernels, mlp_forward(): pl.pallas_call(mlp_forward_kernel, out_shape=(jax.ShapeDtypeStruct((lengt...  23.3 us
    unnamed x156, local copies, waits for them, and re-layouts  23 us
  transfers between devices with their start and end apart: 72, of which 21 were waited for; matrix products, arithmetic and copies ran while one was open for 8% of the time, Pallas kernels for 22%

profile of v6, /device:TPU:1, one launch (start us, length us, event | category | flops | bytes accessed | tf_op | source)
XLA Modules:
  0.0 461.8 jit_solution(231946385457426002)
XLA Ops:
  25.2 10.5 %collective-permute-done.3.refs_1_ = bf16[48,3072]{1,0:T(8,128)(2,1)S(1)} collective-permute-done((bf16[48,3072]{1,0:T(8,128)(2,1)S(1)}, bf16[48,3072]{1,0:T(8,128)(2,1)S(1)}, u32[]{:S(2)}, u32[]{:S(2)}) %collective-permute-start.3) | collective-permute-done | bytes 294944 | tf_op jit(solution)/shard_map/ppermute | solution.py:518
  35.7 15.7 %collective-permute-done.4.refs_2_ = bf16[48,3072]{1,0:T(8,128)(2,1)S(1)} collective-permute-done((bf16[48,3072]{1,0:T(8,128)(2,1)S(1)}, bf16[48,3072]{1,0:T(8,128)(2,1)S(1)}, u32[]{:S(2)}, u32[]{:S(2)}) %collective-permute-start.4) | collective-permute-done | bytes 294944 | tf_op jit(solution)/shard_map/ppermute | solution.py:518
  54.7 6.6 %collective-permute-start.12 = (bf16[48,3072]{1,0:T(8,128)(2,1)S(1)}, bf16[48,3072]{1,0:T(8,128)(2,1)S(1)}, u32[]{:S(2)}, u32[]{:S(2)}) collective-permute-start(bf16[48,3072]{1,0:T(8,128)(2,1)S(1)} %pad_maximum_fusion.2.refs_0_), channel_id=1, source_target_pairs={{0,4},{1,5},{2,6},{3,7},{4,8},{5,9},{6,10},{7,11},{8,12},{9,13},{1... | collective-permute-start | bytes 884744 | tf_op jit(solution)/shard_map/ppermute | solution.py:518
  63.7 8.8 %collective-permute-done.12.refs_1_ = bf16[48,3072]{1,0:T(8,128)(2,1)S(1)} collective-permute-done((bf16[48,3072]{1,0:T(8,128)(2,1)S(1)}, bf16[48,3072]{1,0:T(8,128)(2,1)S(1)}, u32[]{:S(2)}, u32[]{:S(2)}) %collective-permute-start.12) | collective-permute-done | bytes 294944 | tf_op jit(solution)/shard_map/ppermute | solution.py:518
  73.7 16.7 %collective-permute-done.13.refs_2_ = bf16[48,3072]{1,0:T(8,128)(2,1)S(1)} collective-permute-done((bf16[48,3072]{1,0:T(8,128)(2,1)S(1)}, bf16[48,3072]{1,0:T(8,128)(2,1)S(1)}, u32[]{:S(2)}, u32[]{:S(2)}) %collective-permute-start.13) | collective-permute-done | bytes 294944 | tf_op jit(solution)/shard_map/ppermute | solution.py:518
  117.3 36.1 %collective-permute-done.20.far_low = bf16[2,48,3072]{2,1,0:T(8,128)(2,1)S(1)} collective-permute-done((bf16[2,48,3072]{2,1,0:T(8,128)(2,1)S(1)}, bf16[2,48,3072]{2,1,0:T(8,128)(2,1)S(1)}, u32[]{:S(2)}, u32[]{:S(2)}) %collective-permute-start.20) | collective-permute-done | bytes 589856 | tf_op jit(solution)/shard_map/ppermute | solution.py:512
  153.5 3.7 place_blocks.2
  162.1 13.0 %collective-permute-done.25.far_low = bf16[2,48,3072]{2,1,0:T(8,128)(2,1)S(1)} collective-permute-done((bf16[2,48,3072]{2,1,0:T(8,128)(2,1)S(1)}, bf16[2,48,3072]{2,1,0:T(8,128)(2,1)S(1)}, u32[]{:S(2)}, u32[]{:S(2)}) %collective-permute-start.25) | collective-permute-done | bytes 589856 | tf_op jit(solution)/shard_map/ppermute | solution.py:512
  176.0 3.9 place_blocks.3
  182.9 6.5 %collective-permute-done = bf16[256,768]{1,0:T(8,128)(2,1)S(1)} collective-permute-done((bf16[256,768]{1,0:T(8,128)(2,1)S(1)}, bf16[256,768]{1,0:T(8,128)(2,1)S(1)}, u32[]{:S(2)}, u32[]{:S(2)}) %collective-permute-start) | collective-permute-done | bytes 393248 | tf_op jit(solution)/shard_map/ppermute | solution.py:507
  189.6 8.8 %attn_forward.2 = (bf16[2,256,1152]{2,1,0:T(8,128)(2,1)S(1)}, f32[2,6,256]{2,1,0:T(8,128)S(1)}, bf16[256,768]{1,0:T(8,128)(2,1)S(1)}, f32[256,768]{1,0:T(8,128)S(1)}) custom-call(s32[1]{0:T(128)} %bitcast.side, bf16[256,768]{1,0:T(8,128)(2,1)S(1)} %get-tuple-element.233.rows, f32[3,256,128]{2,1,0:T(8,128)S(1)} %pad_maximum_fusion.tables, ...), custom_call_target="tpu_custom_call" | custom-call | flops 9059696640 | bytes 4718592 | tf_op jit(solution)/shard_map/attn_forward/pallas_call | solution.py:152
  198.5 12.0 %mlp_forward.2 = (bf16[256,3072]{1,0:T(8,128)(2,1)S(1)}, f32[256,3072]{1,0:T(8,128)}, bf16[256,768]{1,0:T(8,128)(2,1)S(1)}) custom-call(s32[1]{0:T(128)} %bitcast.side, bf16[256,768]{1,0:T(8,128)(2,1)S(1)} %get-tuple-element.233.rows, f32[256,768]{1,0:T(8,128)S(1)} %get-tuple-element.126.passed, f32[4,768]{1,0:T(4,128)S(1)} %get-tuple-element.264.norms, ...), custom_call_target="tpu_custom_call" | custom-call | flops 12079595520 | bytes 14155776 | tf_op jit(solution)/shard_map/mlp_forward/pallas_call | solution.py:252
  210.6 8.7 %attn_forward.3 = (bf16[2,256,1152]{2,1,0:T(8,128)(2,1)S(1)}, f32[2,6,256]{2,1,0:T(8,128)S(1)}, bf16[256,768]{1,0:T(8,128)(2,1)S(1)}, f32[256,768]{1,0:T(8,128)S(1)}) custom-call(s32[1]{0:T(128)} %bitcast.side, bf16[256,768]{1,0:T(8,128)(2,1)S(1)} %get-tuple-element.128.rows, f32[3,256,128]{2,1,0:T(8,128)S(1)} %pad_maximum_fusion.tables, ...), custom_call_target="tpu_custom_call" | custom-call | flops 9059696640 | bytes 4718592 | tf_op jit(solution)/shard_map/attn_forward/pallas_call | solution.py:152
  219.3 11.2 %mlp_forward.3 = (bf16[256,3072]{1,0:T(8,128)(2,1)S(1)}, f32[256,3072]{1,0:T(8,128)}, f32[256,768]{1,0:T(8,128)S(1)}) custom-call(s32[1]{0:T(128)} %bitcast.side, bf16[256,768]{1,0:T(8,128)(2,1)S(1)} %get-tuple-element.128.rows, f32[256,768]{1,0:T(8,128)S(1)} %get-tuple-element.134.passed, f32[4,768]{1,0:T(4,128)S(1)} %copy-done.32, ...), custom_call_target="tpu_custom_call" | custom-call | flops 12079595520 | bytes 14155776 | tf_op jit(solution)/shard_map/mlp_forward/pallas_call | solution.py:252
  230.5 17.8 %mlp_backward.2 = (bf16[768,1536]{1,0:T(8,128)(2,1)S(1)}, bf16[768,1536]{1,0:T(8,128)(2,1)}, bf16[768,1536]{1,0:T(8,128)(2,1)}, bf16[768,1536]{1,0:T(8,128)(2,1)...) custom-call(s32[1]{0:T(128)} %bitcast.side, bf16[256,768]{1,0:T(8,128)(2,1)S(1)} %get-tuple-element.128.rows, ...), custom_call_target="tpu_custom_call" | custom-call | flops 19327352832 | bytes 23592960 | tf_op jit(solution)/shard_map/mlp_backward/pallas_call | solution.py:351
  248.9 12.3 %attn_backward.2 = (bf16[768,1536]{1,0:T(8,128)(2,1)}, bf16[768,1536]{1,0:T(8,128)(2,1)}, f32[2,1152]{1,0:T(2,128)S(1)}, f32[5,768]{1,0:T(8,128)S(1)}, bf16[256,768]{1,0:T(8,128)(2,1)S(1)}) custom-call(s32[1]{0:T(128)} %bitcast.side, bf16[256,768]{1,0:T(8,128)(2,1)S(1)} %get-tuple-element.128.rows, bf16[256,768]{1,0:T(8,128)(2,1)S(1)} %get-tuple-element.232.grad, ...), custom_call_target="tpu_custom_call" | custom-call | flops 14495514624 | bytes 9437184 | tf_op jit(solution)/shard_map/attn_backward/pallas_call | solution.py:469
  265.3 17.5 %mlp_backward.3 = (bf16[768,1536]{1,0:T(8,128)(2,1)S(1)}, bf16[768,1536]{1,0:T(8,128)(2,1)}, bf16[768,1536]{1,0:T(8,128)(2,1)}, bf16[768,1536]{1,0:T(8,128)(2,1)...) custom-call(s32[1]{0:T(128)} %bitcast.side, bf16[256,768]{1,0:T(8,128)(2,1)S(1)} %get-tuple-element.233.rows, ...), custom_call_target="tpu_custom_call" | custom-call | flops 19327352832 | bytes 23592960 | tf_op jit(solution)/shard_map/mlp_backward/pallas_call | solution.py:351
  288.7 3.3 near_blocks.3
  293.4 13.3 %attn_backward.3 = (bf16[768,1536]{1,0:T(8,128)(2,1)}, bf16[768,1536]{1,0:T(8,128)(2,1)}, f32[2,1152]{1,0:T(2,128)S(1)}, f32[5,768]{1,0:T(8,128)S(1)}, f32[256,768]{1,0:T(8,128)S(1)}) custom-call(s32[1]{0:T(128)} %bitcast.side, bf16[256,768]{1,0:T(8,128)(2,1)S(1)} %copy-done.18, bf16[256,768]{1,0:T(8,128)(2,1)S(1)} %get-tuple-element.150.grad, ...), custom_call_target="tpu_custom_call" | custom-call | flops 14495514624 | bytes 9437184 | tf_op jit(solution)/shard_map/attn_backward/pallas_call | solution.py:469
  311.6 7.1 %collective-permute-done.35.refs_4_ = bf16[4,48,3072]{2,1,0:T(8,128)(2,1)S(1)} collective-permute-done((bf16[4,48,3072]{2,1,0:T(8,128)(2,1)S(1)}, bf16[4,48,3072]{2,1,0:T(8,128)(2,1)S(1)}, u32[]{:S(2)}, u32[]{:S(2)}) %collective-permute-start.35) | collective-permute-done | bytes 1179680 | tf_op jit(solution)/shard_map/ppermute | solution.py:512
  333.0 6.2 %collective-permute-done.51 = bf16[4,48,1536]{2,1,0:T(8,128)(2,1)} collective-permute-done((bf16[4,48,1536]{2,1,0:T(8,128)(2,1)}, bf16[4,48,1536]{2,1,0:T(8,128)(2,1)}, u32[]{:S(2)}, u32[]{:S(2)}) %collective-permute-start.51) | collective-permute-done | bytes 589856 | tf_op jit(solution)/shard_map/ppermute | solution.py:518
  339.5 3.9 collective-permute-done.41.refs_8_
  346.2 3.5 collective-permute-done.37.refs_4_
  354.6 4.6 near_blocks.4
  361.9 7.6 %collective-permute-done.52 = bf16[4,48,1536]{2,1,0:T(8,128)(2,1)S(1)} collective-permute-done((bf16[4,48,1536]{2,1,0:T(8,128)(2,1)S(1)}, bf16[4,48,1536]{2,1,0:T(8,128)(2,1)S(1)}, u32[]{:S(2)}, u32[]{:S(2)}) %collective-permute-start.52) | collective-permute-done | bytes 589856 | tf_op jit(solution)/shard_map/ppermute | solution.py:518
  371.0 3.3 column_blocks.5
  375.4 11.1 %collective-permute-done.43.refs_4_ = bf16[4,48,3072]{2,1,0:T(8,128)(2,1)S(1)} collective-permute-done((bf16[4,48,3072]{2,1,0:T(8,128)(2,1)}, bf16[4,48,3072]{2,1,0:T(8,128)(2,1)S(1)}, u32[]{:S(2)}, u32[]{:S(2)}) %collective-permute-start.43) | collective-permute-done | bytes 1179680 | tf_op jit(solution)/shard_map/ppermute | solution.py:512
  407.9 4.1 collective-permute-done.45.refs_2_
  424.1 4.2 collective-permute-done.65
  428.4 10.8 %collective-permute-start.47 = (bf16[48,1536]{1,0:T(8,128)(2,1)S(1)}, bf16[48,1536]{1,0:T(8,128)(2,1)S(1)}, u32[]{:S(2)}, u32[]{:S(2)}) collective-permute-start(bf16[48,1536]{1,0:T(8,128)(2,1)S(1)} %get-tuple-element.194), channel_id=1, source_target_pairs={{0,4},{1,5},{2,6},{3,7},{4,8},{5,9},{6,10},{7,11},{8,12},{9,13},{1... | collective-permute-start | bytes 442376 | tf_op jit(solution)/shard_map/ppermute | solution.py:518
  440.7 3.6 collective-permute-start.70
  446.0 5.4 %collective-permute-start.56 = (f32[48,1536]{1,0:T(8,128)S(1)}, f32[48,1536]{1,0:T(8,128)S(1)}, u32[]{:S(2)}, u32[]{:S(2)}) collective-permute-start(f32[48,1536]{1,0:T(8,128)S(1)} %get-tuple-element.222), channel_id=1, source_target_pairs={{0,16},{16,0},{1,17},{17,1},{2,18},{18,2},{3,19},{19,3},{4,20},{20... | collective-permute-start | bytes 884744 | tf_op jit(solution)/shard_map/ppermute | solution.py:507
  (382 shorter events, 144.4 us)
Async XLA Ops:
  7.2 153.3 %all-gather.2.cloned.1.call-start = ((), (), s32[]{:S(2)}) async-start(), calls=%async_computation | async-start | bytes 5013504 | tf_op jit(solution)/shard_map/all_gather | solution.py:605
  22.2 29.1 %collective-permute-start.4 = (bf16[48,3072]{1,0:T(8,128)(2,1)S(1)}, bf16[48,3072]{1,0:T(8,128)(2,1)S(1)}, u32[]{:S(2)}, u32[]{:S(2)}) collective-permute-start(bf16[48,3072]{1,0:T(8,128)(2,1)S(1)} %pad_maximum_fusion.1.refs_0_), channel_id=1, source_target_pairs={{0,8},{1,9},{2,10},{3,11},{4,12},{5,13},{6,14},{7,15},{8,0},{9,1},... | collective-permute-start | bytes 884744 | tf_op jit(solution)/shard_map/ppermute | solution.py:518
  25.0 26.3 %collective-permute-start.5 = (bf16[48,3072]{1,0:T(8,128)(2,1)S(1)}, bf16[48,3072]{1,0:T(8,128)(2,1)S(1)}, u32[]{:S(2)}, u32[]{:S(2)}) collective-permute-start(bf16[48,3072]{1,0:T(8,128)(2,1)S(1)} %pad_maximum_fusion.1.refs_0_), channel_id=1, source_target_pairs={{0,12},{1,13},{2,14},{3,15},{4,0},{5,1},{6,2},{7,3},{8,4},{9,5},{1... | collective-permute-start | bytes 884744 | tf_op jit(solution)/shard_map/ppermute | solution.py:518
  52.2 46.7 %collective-permute-start.10 = (bf16[4,48,3072]{2,1,0:T(8,128)(2,1)S(1)}, bf16[4,48,3072]{2,1,0:T(8,128)(2,1)S(1)}, u32[]{:S(2)}, u32[]{:S(2)}) collective-permute-start(bf16[4,48,3072]{2,1,0:T(8,128)(2,1)S(1)} %place_line.4.own), channel_id=1, source_target_pairs={{0,1},{1,0},{2,3},{3,2},{4,5},{5,4},{6,7},{7,6},{8,9},{9,8},{10,11... | collective-permute-start | bytes 3538952 | tf_op jit(solution)/shard_map/ppermute | solution.py:512
  53.5 46.3 %collective-permute-start.11 = (bf16[4,48,3072]{2,1,0:T(8,128)(2,1)S(1)}, bf16[4,48,3072]{2,1,0:T(8,128)(2,1)}, u32[]{:S(2)}, u32[]{:S(2)}) collective-permute-start(bf16[4,48,3072]{2,1,0:T(8,128)(2,1)S(1)} %place_line.4.own), channel_id=1, source_target_pairs={{0,2},{1,3},{2,0},{3,1},{4,6},{5,7},{6,4},{7,5},{8,10},{9,11},{10,... | collective-permute-start | bytes 3538952 | tf_op jit(solution)/shard_map/ppermute | solution.py:512
  61.3 29.0 %collective-permute-start.13 = (bf16[48,3072]{1,0:T(8,128)(2,1)S(1)}, bf16[48,3072]{1,0:T(8,128)(2,1)S(1)}, u32[]{:S(2)}, u32[]{:S(2)}) collective-permute-start(bf16[48,3072]{1,0:T(8,128)(2,1)S(1)} %pad_maximum_fusion.2.refs_0_), channel_id=1, source_target_pairs={{0,8},{1,9},{2,10},{3,11},{4,12},{5,13},{6,14},{7,15},{8,0},{9,1},... | collective-permute-start | bytes 884744 | tf_op jit(solution)/shard_map/ppermute | solution.py:518
  61.3 30.9 %collective-permute-start.14 = (bf16[48,3072]{1,0:T(8,128)(2,1)S(1)}, bf16[48,3072]{1,0:T(8,128)(2,1)S(1)}, u32[]{:S(2)}, u32[]{:S(2)}) collective-permute-start(bf16[48,3072]{1,0:T(8,128)(2,1)S(1)} %pad_maximum_fusion.2.refs_0_), channel_id=1, source_target_pairs={{0,12},{1,13},{2,14},{3,15},{4,0},{5,1},{6,2},{7,3},{8,4},{9,5},{1... | collective-permute-start | bytes 884744 | tf_op jit(solution)/shard_map/ppermute | solution.py:518
  73.1 28.6 %collective-permute-start.15 = (bf16[4,1,1248]{2,1,0:T(2,128)(2,1)}, bf16[4,1,1248]{2,1,0:T(2,128)(2,1)S(1)}, u32[]{:S(2)}, u32[]{:S(2)}) collective-permute-start(bf16[4,1,1248]{2,1,0:T(2,128)(2,1)} %copy-done.28), channel_id=1, source_target_pairs={{0,1},{1,0},{2,3},{3,2},{4,5},{5,4},{6,7},{7,6},{8,9},{9,8},{10,11... | collective-permute-start | bytes 29960 | tf_op jit(solution)/shard_map/ppermute | solution.py:512
  101.7 55.5 %collective-permute-start.18 = (bf16[4,48,3072]{2,1,0:T(8,128)(2,1)S(1)}, bf16[4,48,3072]{2,1,0:T(8,128)(2,1)}, u32[]{:S(2)}, u32[]{:S(2)}) collective-permute-start(bf16[4,48,3072]{2,1,0:T(8,128)(2,1)S(1)} %place_line.6.own), channel_id=1, source_target_pairs={{0,1},{1,0},{2,3},{3,2},{4,5},{5,4},{6,7},{7,6},{8,9},{9,8},{10,11... | collective-permute-start | bytes 3538952 | tf_op jit(solution)/shard_map/ppermute | solution.py:512
  102.0 56.3 %collective-permute-start.19 = (bf16[4,48,3072]{2,1,0:T(8,128)(2,1)S(1)}, bf16[4,48,3072]{2,1,0:T(8,128)(2,1)}, u32[]{:S(2)}, u32[]{:S(2)}) collective-permute-start(bf16[4,48,3072]{2,1,0:T(8,128)(2,1)S(1)} %place_line.6.own), channel_id=1, source_target_pairs={{0,2},{1,3},{2,0},{3,1},{4,6},{5,7},{6,4},{7,5},{8,10},{9,11},{10,... | collective-permute-start | bytes 3538952 | tf_op jit(solution)/shard_map/ppermute | solution.py:512
  114.6 38.8 %collective-permute-start.20 = (bf16[2,48,3072]{2,1,0:T(8,128)(2,1)S(1)}, bf16[2,48,3072]{2,1,0:T(8,128)(2,1)S(1)}, u32[]{:S(2)}, u32[]{:S(2)}) collective-permute-start(bf16[2,48,3072]{2,1,0:T(8,128)(2,1)S(1)} %copy-done.48), channel_id=1, source_target_pairs={{0,2},{1,3},{2,0},{3,1},{4,6},{5,7},{6,4},{7,5},{8,10},{9,11},{10,... | collective-permute-start | bytes 1769480 | tf_op jit(solution)/shard_map/ppermute | solution.py:512
  114.9 38.6 %collective-permute-start.21 = (bf16[2,48,3072]{2,1,0:T(8,128)(2,1)S(1)}, bf16[2,48,3072]{2,1,0:T(8,128)(2,1)S(1)}, u32[]{:S(2)}, u32[]{:S(2)}) collective-permute-start(bf16[2,48,3072]{2,1,0:T(8,128)(2,1)S(1)} %copy-done.49), channel_id=1, source_target_pairs={{0,1},{1,0},{2,3},{3,2},{4,5},{5,4},{6,7},{7,6},{8,9},{9,8},{10,11... | collective-permute-start | bytes 1769480 | tf_op jit(solution)/shard_map/ppermute | solution.py:512
  159.5 30.1 %collective-permute-start.22 = (bf16[768,3072]{1,0:T(8,128)(2,1)}, bf16[768,3072]{1,0:T(8,128)(2,1)}, u32[]{:S(2)}, u32[]{:S(2)}) collective-permute-start(bf16[768,3072]{1,0:T(8,128)(2,1)} %bitcast.165), channel_id=1, source_target_pairs={{0,16},{16,0},{1,17},{17,1},{2,18},{18,2},{3,19},{19,3},{4,20},{20... | collective-permute-start | bytes 14155784 | tf_op jit(solution)/shard_map/ppermute | solution.py:507
  160.5 37.9 %collective-permute-start.24 = (bf16[768,3072]{1,0:T(8,128)(2,1)}, bf16[768,3072]{1,0:T(8,128)(2,1)}, u32[]{:S(2)}, u32[]{:S(2)}) collective-permute-start(bf16[768,3072]{1,0:T(8,128)(2,1)} %all-gather.2.cloned.1.call-done.down_mine), channel_id=1, source_target_pairs={{0,16},{16,0},{1,17},{17,1},{2,18},{18,2},{3,19},{19,3},{4,20},{20... | collective-permute-start | bytes 14155784 | tf_op jit(solution)/shard_map/ppermute | solution.py:507
  180.0 30.6 %collective-permute-start.27 = (bf16[768,3072]{1,0:T(8,128)(2,1)}, bf16[768,3072]{1,0:T(8,128)(2,1)}, u32[]{:S(2)}, u32[]{:S(2)}) collective-permute-start(bf16[768,3072]{1,0:T(8,128)(2,1)} %bitcast.170), channel_id=1, source_target_pairs={{0,16},{16,0},{1,17},{17,1},{2,18},{18,2},{3,19},{19,3},{4,20},{20... | collective-permute-start | bytes 14155784 | tf_op jit(solution)/shard_map/ppermute | solution.py:507
  261.2 24.2 %collective-permute-start.32 = (bf16[768,1536]{1,0:T(8,128)(2,1)}, bf16[768,1536]{1,0:T(8,128)(2,1)}, u32[]{:S(2)}, u32[]{:S(2)}) collective-permute-start(bf16[768,1536]{1,0:T(8,128)(2,1)} %get-tuple-element.162), channel_id=1, source_target_pairs={{0,16},{16,0},{1,17},{17,1},{2,18},{18,2},{3,19},{19,3},{4,20},{20... | collective-permute-start | bytes 7077896 | tf_op jit(solution)/shard_map/ppermute | solution.py:507
  263.8 24.9 %collective-permute-start.30 = (bf16[2,48,3072]{2,1,0:T(8,128)(2,1)S(1)}, bf16[2,48,3072]{2,1,0:T(8,128)(2,1)S(1)}, u32[]{:S(2)}, u32[]{:S(2)}) collective-permute-start(bf16[2,48,3072]{2,1,0:T(8,128)(2,1)S(1)} %get-tuple-element.148), channel_id=1, source_target_pairs={{0,1},{1,0},{2,3},{3,2},{4,5},{5,4},{6,7},{7,6},{8,9},{9,8},{10,11... | collective-permute-start | bytes 1769480 | tf_op jit(solution)/shard_map/ppermute | solution.py:512
  264.1 24.5 %collective-permute-start.31 = (bf16[2,48,3072]{2,1,0:T(8,128)(2,1)S(1)}, bf16[2,48,3072]{2,1,0:T(8,128)(2,1)S(1)}, u32[]{:S(2)}, u32[]{:S(2)}) collective-permute-start(bf16[2,48,3072]{2,1,0:T(8,128)(2,1)S(1)} %get-tuple-element.149), channel_id=1, source_target_pairs={{0,2},{1,3},{2,0},{3,1},{4,6},{5,7},{6,4},{7,5},{8,10},{9,11},{10,... | collective-permute-start | bytes 1769480 | tf_op jit(solution)/shard_map/ppermute | solution.py:512
  284.3 39.1 %collective-permute-start.39 = (bf16[768,1536]{1,0:T(8,128)(2,1)}, bf16[768,1536]{1,0:T(8,128)(2,1)S(1)}, u32[]{:S(2)}, u32[]{:S(2)}) collective-permute-start(bf16[768,1536]{1,0:T(8,128)(2,1)} %get-tuple-element.173), channel_id=1, source_target_pairs={{0,16},{16,0},{1,17},{17,1},{2,18},{18,2},{3,19},{19,3},{4,20},{20... | collective-permute-start | bytes 7077896 | tf_op jit(solution)/shard_map/ppermute | solution.py:507
  285.3 39.5 %collective-permute-start.40 = (bf16[768,1536]{1,0:T(8,128)(2,1)}, bf16[768,1536]{1,0:T(8,128)(2,1)}, u32[]{:S(2)}, u32[]{:S(2)}) collective-permute-start(bf16[768,1536]{1,0:T(8,128)(2,1)} %get-tuple-element.175), channel_id=1, source_target_pairs={{0,16},{16,0},{1,17},{17,1},{2,18},{18,2},{3,19},{19,3},{4,20},{20... | collective-permute-start | bytes 7077896 | tf_op jit(solution)/shard_map/ppermute | solution.py:507
  291.9 26.8 %collective-permute-start.35 = (bf16[4,48,3072]{2,1,0:T(8,128)(2,1)S(1)}, bf16[4,48,3072]{2,1,0:T(8,128)(2,1)S(1)}, u32[]{:S(2)}, u32[]{:S(2)}) collective-permute-start(bf16[4,48,3072]{2,1,0:T(8,128)(2,1)S(1)} %get-tuple-element.160), channel_id=1, source_target_pairs={{0,1},{1,0},{2,3},{3,2},{4,5},{5,4},{6,7},{7,6},{8,9},{9,8},{10,11... | collective-permute-start | bytes 3538952 | tf_op jit(solution)/shard_map/ppermute | solution.py:512
  292.3 29.1 %collective-permute-start.36 = (bf16[4,48,3072]{2,1,0:T(8,128)(2,1)S(1)}, bf16[4,48,3072]{2,1,0:T(8,128)(2,1)S(1)}, u32[]{:S(2)}, u32[]{:S(2)}) collective-permute-start(bf16[4,48,3072]{2,1,0:T(8,128)(2,1)S(1)} %get-tuple-element.161), channel_id=1, source_target_pairs={{0,2},{1,3},{2,0},{3,1},{4,6},{5,7},{6,4},{7,5},{8,10},{9,11},{10,... | collective-permute-start | bytes 3538952 | tf_op jit(solution)/shard_map/ppermute | solution.py:512
  307.8 23.8 %collective-permute-start.34 = (bf16[768,1536]{1,0:T(8,128)(2,1)}, bf16[768,1536]{1,0:T(8,128)(2,1)S(1)}, u32[]{:S(2)}, u32[]{:S(2)}) collective-permute-start(bf16[768,1536]{1,0:T(8,128)(2,1)} %get-tuple-element.167), channel_id=1, source_target_pairs={{0,16},{16,0},{1,17},{17,1},{2,18},{18,2},{3,19},{19,3},{4,20},{20... | collective-permute-start | bytes 7077896 | tf_op jit(solution)/shard_map/ppermute | solution.py:507
  330.1 29.1 %collective-permute-start.60 = (f32[1,9984]{1,0:T(1,128)S(1)}, f32[1,9984]{1,0:T(1,128)S(1)}, u32[]{:S(2)}, u32[]{:S(2)}) collective-permute-start(f32[1,9984]{1,0:T(1,128)S(1)} %fusion.14), channel_id=1, source_target_pairs={{0,3},{1,2},{2,1},{3,0},{4,7},{5,6},{6,5},{7,4},{8,11},{9,10},{10,... | collective-permute-start | bytes 119816 | tf_op jit(solution)/shard_map/ppermute | solution.py:512
  331.6 27.7 %collective-permute-start.59 = (f32[1,9984]{1,0:T(1,128)S(1)}, f32[1,9984]{1,0:T(1,128)S(1)}, u32[]{:S(2)}, u32[]{:S(2)}) collective-permute-start(f32[1,9984]{1,0:T(1,128)S(1)} %fusion.14), channel_id=1, source_target_pairs={{0,2},{1,3},{2,0},{3,1},{4,6},{5,7},{6,4},{7,5},{8,10},{9,11},{10,... | collective-permute-start | bytes 119816 | tf_op jit(solution)/shard_map/ppermute | solution.py:512
  359.2 27.3 %collective-permute-start.43 = (bf16[4,48,3072]{2,1,0:T(8,128)(2,1)}, bf16[4,48,3072]{2,1,0:T(8,128)(2,1)S(1)}, u32[]{:S(2)}, u32[]{:S(2)}) collective-permute-start(bf16[4,48,3072]{2,1,0:T(8,128)(2,1)} %get-tuple-element.185), channel_id=1, source_target_pairs={{0,1},{1,0},{2,3},{3,2},{4,5},{5,4},{6,7},{7,6},{8,9},{9,8},{10,11... | collective-permute-start | bytes 3538952 | tf_op jit(solution)/shard_map/ppermute | solution.py:512
  359.4 27.1 %collective-permute-start.44 = (bf16[4,48,3072]{2,1,0:T(8,128)(2,1)}, bf16[4,48,3072]{2,1,0:T(8,128)(2,1)S(1)}, u32[]{:S(2)}, u32[]{:S(2)}) collective-permute-start(bf16[4,48,3072]{2,1,0:T(8,128)(2,1)} %get-tuple-element.186), channel_id=1, source_target_pairs={{0,2},{1,3},{2,0},{3,1},{4,6},{5,7},{6,4},{7,5},{8,10},{9,11},{10,... | collective-permute-start | bytes 3538952 | tf_op jit(solution)/shard_map/ppermute | solution.py:512
  374.3 32.0 %collective-permute-start.69 = (bf16[48,3072]{1,0:T(8,128)(2,1)}, bf16[48,3072]{1,0:T(8,128)(2,1)}, u32[]{:S(2)}, u32[]{:S(2)}) collective-permute-start(bf16[48,3072]{1,0:T(8,128)(2,1)} %get-tuple-element.213), channel_id=1, source_target_pairs={{0,12},{1,13},{2,14},{3,15},{4,0},{5,1},{6,2},{7,3},{8,4},{9,5},{1... | collective-permute-start | bytes 884744 | tf_op jit(solution)/shard_map/ppermute | solution.py:518
  374.8 33.0 %collective-permute-start.68 = (bf16[48,3072]{1,0:T(8,128)(2,1)}, bf16[48,3072]{1,0:T(8,128)(2,1)}, u32[]{:S(2)}, u32[]{:S(2)}) collective-permute-start(bf16[48,3072]{1,0:T(8,128)(2,1)} %get-tuple-element.212), channel_id=1, source_target_pairs={{0,8},{1,9},{2,10},{3,11},{4,12},{5,13},{6,14},{7,15},{8,0},{9,1},... | collective-permute-start | bytes 884744 | tf_op jit(solution)/shard_map/ppermute | solution.py:518
  418.5 22.2 %collective-permute-start.54 = (bf16[48,1536]{1,0:T(8,128)(2,1)S(1)}, bf16[48,1536]{1,0:T(8,128)(2,1)S(1)}, u32[]{:S(2)}, u32[]{:S(2)}) collective-permute-start(bf16[48,1536]{1,0:T(8,128)(2,1)S(1)} %copy-done.54), channel_id=1, source_target_pairs={{0,2},{1,3},{2,0},{3,1},{4,6},{5,7},{6,4},{7,5},{8,10},{9,11},{10,... | collective-permute-start | bytes 442376 | tf_op jit(solution)/shard_map/ppermute | solution.py:512
  420.7 24.2 %collective-permute-start.53 = (bf16[48,1536]{1,0:T(8,128)(2,1)S(1)}, bf16[48,1536]{1,0:T(8,128)(2,1)S(1)}, u32[]{:S(2)}, u32[]{:S(2)}) collective-permute-start(bf16[48,1536]{1,0:T(8,128)(2,1)S(1)} %copy-done.53), channel_id=1, source_target_pairs={{0,1},{1,0},{2,3},{3,2},{4,5},{5,4},{6,7},{7,6},{8,9},{9,8},{10,11... | collective-permute-start | bytes 442376 | tf_op jit(solution)/shard_map/ppermute | solution.py:512
  421.2 23.7 %collective-permute-start.49 = (bf16[48,1536]{1,0:T(8,128)(2,1)S(1)}, bf16[48,1536]{1,0:T(8,128)(2,1)S(1)}, u32[]{:S(2)}, u32[]{:S(2)}) collective-permute-start(bf16[48,1536]{1,0:T(8,128)(2,1)S(1)} %get-tuple-element.196), channel_id=1, source_target_pairs={{0,12},{1,13},{2,14},{3,15},{4,0},{5,1},{6,2},{7,3},{8,4},{9,5},{1... | collective-permute-start | bytes 442376 | tf_op jit(solution)/shard_map/ppermute | solution.py:518
  (104 other events, 951.6 us)
Sparse Core Ops, SparseCore 0:
  11.8 125.3 all-gather.1

commit v7 on v6

--- a/solution.py
+++ b/solution.py
@@ -11,7 +11,8 @@
 HD = 64
 ROT = 16
 LANES = 128
-TILES = 4
+TILES = 2
+FOLD = 4
 PARTS = 16
 
 
@@ -191,8 +192,8 @@
 
 
 def folded_cuts(shape, width):
-    rows = shape[0] // 2
-    for part in range(2):
+    rows = 2 * width // PARTS
+    for part in range(shape[0] // rows):
         for column in range(shape[1] // width):
             yield (
                 slice(part * rows, (part + 1) * rows),
@@ -204,9 +205,13 @@
     return jnp.concatenate([block[cut] for cut in folded_cuts(block.shape, width)], axis=0)
 
 
+def down_joined(mine, other, width):
+    return jnp.concatenate([unfolded(mine, width), unfolded(other, width)], axis=1)
+
+
 def mlp_forward_kernel(
     side, rows, passed, norms, bias_up, bias_out, up_mine, up_other, down_mine, down_other,
-    active, slope, produced, normed, sum_mine, sum_other
+    active, slope, produced, normed, total
 ):
     step = pl.program_id(0)
 
@@ -214,8 +219,7 @@
     def _():
         unit, _ = unit_rows(rows[...].astype(jnp.float32))
         normed[...] = (unit * norms[1:2] + norms[3:4]).astype(jnp.bfloat16)
-        sum_mine[...] = jnp.zeros_like(sum_mine)
-        sum_other[...] = jnp.zeros_like(sum_other)
+        total[...] = jnp.zeros_like(total)
 
     weight = jnp.where(step < TILES, up_mine[...], up_other[...])
     hidden = product(normed[...], weight) + bias_up[...]
@@ -224,16 +228,16 @@
     slope[...] = bell + hidden * density
     lit = (hidden * bell).astype(jnp.bfloat16)
     active[...] = lit
-    width = sum_mine.shape[1]
-    sum_mine[...] += product(lit, unfolded(down_mine, width))
-    sum_other[...] += product(lit, unfolded(down_other, width))
+    width = total.shape[1] // 2
+    total[...] += product(lit, down_joined(down_mine, down_other, width))
 
     @pl.when(step == 2 * TILES - 1)
     def _():
-        for half, total in ((side[0], sum_mine), (1 - side[0], sum_other)):
+        for at, half in enumerate((side[0], 1 - side[0])):
             lanes = lane_half(half, width)
+            part = total[:, at * width : (at + 1) * width]
             produced[:, lanes] = (
-                passed[:, lanes] + total[...] + bias_out[1:2, lanes]
+                passed[:, lanes] + part + bias_out[1:2, lanes]
             ).astype(produced.dtype)
 
 
@@ -242,12 +246,12 @@
     up_at, down_at = places
     length, features = rows.shape
     width = features // 2
-    tile = width
+    tile = FOLD * width // TILES
     hidden = 2 * TILES * tile
     folded = features // (2 * TILES)
     tiled = pl.BlockSpec((length, tile), lambda step, side: (0, tile_of(step, side)))
     down_spec = pl.BlockSpec(
-        (folded, TILES * width), lambda step, side: (tile_of(step, side), down_at)
+        (folded, FOLD * width), lambda step, side: (tile_of(step, side), down_at)
     )
     return pl.pallas_call(
         mlp_forward_kernel,
@@ -273,8 +277,7 @@
             out_specs=(tiled, tiled, fixed(length, features)),
             scratch_shapes=[
                 pltpu.VMEM((length, features), jnp.bfloat16),
-                pltpu.VMEM((length, width), jnp.float32),
-                pltpu.VMEM((length, width), jnp.float32),
+                pltpu.VMEM((length, features), jnp.float32),
             ],
         ),
         compiler_params=pltpu.CompilerParams(vmem_limit_bytes=vmem_bytes),
@@ -292,7 +295,7 @@
 
 def mlp_backward_kernel(
     side, rows, grad, norms, active, slope, up_mine, up_other, down_mine, down_other,
-    up_kept, up_sent, down_kept, down_sent, bias_grad, grad_normed, normed
+    up_kept, up_sent, down_kept, down_sent, bias_grad, grad_normed, normed, grads
 ):
     step = pl.program_id(0)
     width = grad.shape[1] // 2
@@ -303,18 +306,18 @@
         unit, _ = unit_rows(rows[...].astype(jnp.float32))
         normed[...] = (unit * norms[1:2] + norms[3:4]).T.astype(jnp.bfloat16)
         grad_normed[...] = jnp.zeros_like(grad_normed)
-
-    grad_mine = grad[:, lane_half(side[0], width)]
-    grad_other = grad[:, lane_half(1 - side[0], width)]
+        grads[:, :width] = grad[:, lane_half(side[0], width)]
+        grads[:, width:] = grad[:, lane_half(1 - side[0], width)]
+
     weight = jnp.where(step < TILES, up_mine[...], up_other[...])
     lit = active[...].T
-    for grad_half, result in ((grad_mine, down_kept), (grad_other, down_sent)):
-        made = product(lit, grad_half).astype(jnp.bfloat16)
-        rows_each = made.shape[0] // len(cuts)
-        for index, cut in enumerate(cuts):
-            result[cut] = made[index * rows_each : (index + 1) * rows_each]
-    back = product_transposed(grad_mine, unfolded(down_mine, width))
-    back += product_transposed(grad_other, unfolded(down_other, width))
+    made = product(lit, grads[...]).astype(jnp.bfloat16)
+    rows_each = made.shape[0] // len(cuts)
+    for index, cut in enumerate(cuts):
+        part = made[index * rows_each : (index + 1) * rows_each]
+        down_kept[cut] = part[:, :width]
+        down_sent[cut] = part[:, width:]
+    back = product_transposed(grads[...], down_joined(down_mine, down_other, width))
     back = (back * slope[...]).astype(jnp.bfloat16)
     bias_grad[...] = jnp.sum(back.astype(jnp.float32), axis=0, keepdims=True)
     up_grad = product(normed[...], back).astype(jnp.bfloat16)
@@ -336,25 +339,25 @@
     up_at, down_at = places
     length, features = rows.shape
     width = features // 2
-    tile = width
+    tile = FOLD * width // TILES
     hidden = 2 * TILES * tile
     folded = features // (2 * TILES)
     tiled = pl.BlockSpec((length, tile), lambda step, side: (0, tile_of(step, side)))
     down_spec = pl.BlockSpec(
-        (folded, TILES * width), lambda step, side: (tile_of(step, side), down_at)
+        (folded, FOLD * width), lambda step, side: (tile_of(step, side), down_at)
     )
     up_first = pl.BlockSpec((features, tile), lambda step, side: (0, first_tile(step)))
     up_second = pl.BlockSpec((features, tile), lambda step, side: (0, second_tile(step)))
     down_out = pl.BlockSpec(
-        (folded, TILES * width), lambda step, side: (tile_of(step, side), 0)
+        (folded, FOLD * width), lambda step, side: (tile_of(step, side), 0)
     )
     return pl.pallas_call(
         mlp_backward_kernel,
         out_shape=(
             jax.ShapeDtypeStruct((features, hidden // 2), jnp.bfloat16),
             jax.ShapeDtypeStruct((features, hidden // 2), jnp.bfloat16),
-            jax.ShapeDtypeStruct((features, TILES * width), jnp.bfloat16),
-            jax.ShapeDtypeStruct((features, TILES * width), jnp.bfloat16),
+            jax.ShapeDtypeStruct((features, FOLD * width), jnp.bfloat16),
+            jax.ShapeDtypeStruct((features, FOLD * width), jnp.bfloat16),
             jax.ShapeDtypeStruct((1, hidden), jnp.float32),
             jax.ShapeDtypeStruct((length, features), jnp.float32),
         ),
@@ -380,7 +383,10 @@
                 pl.BlockSpec((1, tile), lambda step, side: (0, tile_of(step, side))),
                 fixed(length, features),
             ),
-            scratch_shapes=[pltpu.VMEM((features, length), jnp.bfloat16)],
+            scratch_shapes=[
+                pltpu.VMEM((features, length), jnp.bfloat16),
+                pltpu.VMEM((length, features), jnp.bfloat16),
+            ],
         ),
         compiler_params=pltpu.CompilerParams(vmem_limit_bytes=vmem_bytes),
         cost_estimate=pl.CostEstimate(
@@ -538,35 +544,51 @@
     return [pl.BlockSpec(memory_space=pl.ANY)] * count
 
 
-def place_kernel(spot_ref, own, first, second, far_low, far_high, out, sems):
+def place_kernel(spot_ref, *refs):
+    blocks, outs, sems = refs[:5], refs[5:-1], refs[-1]
+    own, first, second, far_low, far_high = blocks
     spot = spot_ref[0]
     half = RING // 2
-    copies = [
-        pltpu.make_async_copy(own, out.at[:, spot], sems.at[0]),
-        pltpu.make_async_copy(first, out.at[:, spot ^ 1], sems.at[1]),
-        pltpu.make_async_copy(second, out.at[:, spot ^ 2], sems.at[2]),
-        pltpu.make_async_copy(far_low, out.at[pl.ds(0, half), spot ^ 3], sems.at[3]),
-        pltpu.make_async_copy(far_high, out.at[pl.ds(half, half), spot ^ 3], sems.at[4]),
-    ]
+    copies = []
+    at = 0
+    for index, out in enumerate(outs):
+        lanes = pl.ds(at, out.shape[3])
+        at += out.shape[3]
+        pairs = (
+            (own, out.at[:, spot]),
+            (first, out.at[:, spot ^ 1]),
+            (second, out.at[:, spot ^ 2]),
+            (far_low, out.at[pl.ds(0, half), spot ^ 3]),
+            (far_high, out.at[pl.ds(half, half), spot ^ 3]),
+        )
+        for place, (block, target) in enumerate(pairs):
+            copies.append(
+                pltpu.make_async_copy(
+                    block.at[:, :, lanes], target, sems.at[5 * index + place]
+                )
+            )
     for copy in copies:
         copy.start()
     for copy in copies:
         copy.wait()
 
 
-def place_blocks(blocks):
+def place_blocks(blocks, widths):
     spot = own_place()[1].reshape(1)
-    _, rows, columns = blocks[0].shape
+    rows = blocks[0].shape[1]
     placed = pl.pallas_call(
         place_kernel,
-        out_shape=jax.ShapeDtypeStruct((RING, SQUARE, rows, columns), blocks[0].dtype),
+        out_shape=tuple(
+            jax.ShapeDtypeStruct((RING, SQUARE, rows, columns), blocks[0].dtype)
+            for columns in widths
+        ),
         in_specs=[pl.BlockSpec(memory_space=pltpu.SMEM)] + any_space(5),
-        out_specs=pl.BlockSpec(memory_space=pltpu.VMEM),
-        scratch_shapes=[pltpu.SemaphoreType.DMA((5,))],
+        out_specs=tuple([pl.BlockSpec(memory_space=pltpu.VMEM)] * len(widths)),
+        scratch_shapes=[pltpu.SemaphoreType.DMA((5 * len(widths),))],
         compiler_params=pltpu.CompilerParams(vmem_limit_bytes=vmem_bytes),
         name="place_blocks",
     )(spot, *blocks)
-    return placed.reshape(RING * SQUARE * rows, columns)
+    return [part.reshape(PARTS * rows, -1) for part in placed]
 
 
 def line_kernel(order_ref, *refs):
@@ -830,13 +852,13 @@
 
 def folded(rows, parts):
     width = rows.shape[1]
-    split = rows.reshape(parts, TILES, -1, width).transpose(0, 2, 1, 3)
-    return split.reshape(-1, TILES * width)
+    split = rows.reshape(parts, FOLD, -1, width).transpose(0, 2, 1, 3)
+    return split.reshape(-1, FOLD * width)
 
 
 def unfolded_rows(rows, parts):
-    width = rows.shape[1] // TILES
-    split = rows.reshape(parts, -1, TILES, width).transpose(0, 2, 1, 3)
+    width = rows.shape[1] // FOLD
+    split = rows.reshape(parts, -1, FOLD, width).transpose(0, 2, 1, 3)
     return split.reshape(-1, width)
 
 
@@ -962,18 +984,23 @@
             made = (part[layer] for part in spread)
             small.append(dict(zip(("qkv", "up", "out", "norms"), made)))
 
-    places = ((TILES, 0), (TILES, 1))
+    places = ((0, 1), (0, 1))
     if small_slice():
         narrow, up, down = pieces
-        wide = [jnp.concatenate([narrow[layer], up[layer]], axis=1) for layer in range(2)]
-        deep = jnp.concatenate([folded(down[layer], 1) for layer in range(2)], axis=1)
-        whole_b = gather_whole(deep)
-        ring_a = ring_moved(wide[0])
+        wide = [
+            jnp.concatenate([up[layer], folded(down[layer], 1)], axis=1) for layer in range(2)
+        ]
+        lower = jnp.concatenate([narrow[0], wide[0]], axis=1)
+        columns = narrow[0].shape[1]
+        whole_b = gather_whole(wide[1])
+        ring_a = ring_moved(lower)
         line = small_both[None]
         ring_s = ring_moved(line)
         column_s = line_placed(ring_order(), [line] + ring_s)
-        column_a = column_of(wide[0], ring_a)
-        column_a, next_c, column_s = after((column_a, wide[1], column_s), (ring_a, ring_s))
+        column_a = column_of(lower, ring_a)
+        column_a, next_c, column_s, entry, cotangent = after(
+            (column_a, narrow[1], column_s, entry, cotangent), (ring_a, ring_s)
+        )
         near_a = near_moved(column_a)
         square_s = square_moved(column_s)
         ring_c = ring_moved(next_c)
@@ -985,33 +1012,30 @@
         near_c = near_moved(column_c)
         rows_s = line_placed(square_order(), [column_s] + square_s)
         spread_out(rows_s.transpose(1, 0, 2, 3).reshape(PARTS, -1))
-        whole_a = place_blocks((column_a,) + near_a + far_a)
-        lows, whole_a = after((cut_near(near_c), whole_a), (far_a, near_c, small))
+        parts_a = (column_a,) + near_a + far_a
+        lows, parts_a, small = after(
+            (cut_near(near_c), parts_a, small), (far_a, near_c, small, whole_b)
+        )
+        whole_a = place_blocks(parts_a, (columns, 2 * columns))
         far_c = far_moved(lows)
-        swapped_a = swap_cores(whole_a)
-        slabs[0, "narrow"] = (whole_a, swapped_a)
-        whole_b = after(whole_b, far_a)
+        slabs[0, "narrow"] = (whole_a[0], swap_cores(whole_a[0]))
+        swapped_a = swap_cores(whole_a[1])
+        slabs[0, "mlp"] = (whole_a[1], swapped_a) * 2
+        attn_step(0, entry)
+        (whole_c,) = place_blocks((column_c,) + near_c + far_c, (columns,))
+        slabs[1, "narrow"] = (whole_c, swap_cores(whole_c))
         swapped_b = swap_cores(whole_b)
-        slabs[0, "mlp"] = (whole_a, swapped_a, whole_b, swapped_b)
-        attn_step(0, entry)
+        slabs[1, "mlp"] = (whole_b, swapped_b) * 2
         mlp_step(0, jnp.bfloat16)
-        whole_c = place_blocks((column_c,) + near_c + far_c)
-        swapped_c = swap_cores(whole_c)
-        slabs[1, "narrow"] = (whole_c, swapped_c)
-        slabs[1, "mlp"] = (whole_c, swapped_c, whole_b, swapped_b)
         attn_step(1, kept_forward[0, "mlp"][2])
         mlp_step(1, jnp.float32)
     else:
         spread_out(gather_whole(small_both[None]))
-        whole_b = jnp.concatenate(
-            [folded(gather_whole(pieces[2][layer]), PARTS) for layer in range(2)], axis=1
-        )
-        second = (whole_b, swap_cores(whole_b))
         for layer in range(2):
-            narrow, up = (gather_whole(piece[layer]) for piece in pieces[:2])
-            wide = jnp.concatenate([narrow, up], axis=1)
-            slabs[layer, "narrow"] = (wide, swap_cores(wide))
-            slabs[layer, "mlp"] = slabs[layer, "narrow"] + second
+            narrow, up, down = (gather_whole(piece[layer]) for piece in pieces)
+            wide = jnp.concatenate([up, folded(down, PARTS)], axis=1)
+            slabs[layer, "narrow"] = (narrow, swap_cores(narrow))
+            slabs[layer, "mlp"] = (wide, swap_cores(wide)) * 2
         attn_step(0, entry)
         mlp_step(0, jnp.bfloat16)
         attn_step(1, kept_forward[0, "mlp"][2])

time: 466 us -> 450 us (0.966)
  waiting for transfers between devices: 159 us -> 144 us
  Pallas kernels: 137 us -> 123 us
  starting transfers between devices: 86.9 us -> 96.5 us
    pallas_call x2, Pallas kernels: 35.3 us -> 26 us  [mlp_backward(): pl.pallas_call(mlp_backward_kernel, out_shape=(jax.ShapeDtypeStruct((feat...]
    ppermute x24, waiting for transfers between devices: 71.2 us -> 62.6 us  [shift_ring(): return lax.ppermute(value, 'dp', pairs)]
    ppermute x18 -> x19, waiting for transfers between devices: 8.33 us -> 0.05 us  [swap_cores(): return lax.ppermute(value, 'section', [(0, 1), (1, 0)])]
    ppermute x18 -> x19, starting transfers between devices: 20.6 us -> 26.6 us  [swap_cores(): return lax.ppermute(value, 'section', [(0, 1), (1, 0)])]
    ppermute x29, starting transfers between devices: 22.6 us -> 28.3 us  [swap_square(): return lax.ppermute(value, 'dp', [(i, i ^ bit) for i in range(count)])]
    pallas_call x2, Pallas kernels: 23.3 us -> 18 us  [mlp_forward(): pl.pallas_call(mlp_forward_kernel, out_shape=(jax.ShapeDtypeStruct((lengt...]
    unnamed x156 -> x154, local copies, waits for them, and re-layouts: 23 us -> 22.4 us
  transfers between devices with their start and end apart: 72 -> 73, of which waited for: 21 -> 19; matrix products, arithmetic and copies ran while one was open for 8% -> 10% of each run, Pallas kernels for 22% -> 21%
where the time goes in v7:
time: 450 us; the launch traced here: 446 us
  waiting for transfers between devices  144 us (32%)
  Pallas kernels  123 us (27%)
  starting transfers between devices  96.5 us (21%)
  local copies, waits for them, and re-layouts  48.1 us (11%)
  other arithmetic  19.5 us (4%)
  between operations  15.4 us (3%)
    ppermute x29, waiting for transfers between devices, swap_square(): return lax.ppermute(value, 'dp', [(i, i ^ bit) for i in range(count)])  81 us
    ppermute x24, waiting for transfers between devices, shift_ring(): return lax.ppermute(value, 'dp', pairs)  62.6 us
    ppermute x24, starting transfers between devices, shift_ring(): return lax.ppermute(value, 'dp', pairs)  41.5 us
    ppermute x29, starting transfers between devices, swap_square(): return lax.ppermute(value, 'dp', [(i, i ^ bit) for i in range(count)])  28.3 us
    ppermute x19, starting transfers between devices, swap_cores(): return lax.ppermute(value, 'section', [(0, 1), (1, 0)])  26.6 us
    pallas_call x2, Pallas kernels, mlp_backward(): pl.pallas_call(mlp_backward_kernel, out_shape=(jax.ShapeDtypeStruct((feat...  26 us
    pallas_call x2, Pallas kernels, attn_backward(): pl.pallas_call(attn_backward_kernel, out_shape=(jax.ShapeDtypeStruct((fea...  25.7 us
    pallas_call x9, Pallas kernels, scatter_call(): pl.pallas_call(body, out_shape=tuple(outs), grid_spec=pltpu.PrefetchScala...  24.4 us
  transfers between devices with their start and end apart: 73, of which 19 were waited for; matrix products, arithmetic and copies ran while one was open for 10% of the time, Pallas kernels for 21%

profile of v7, /device:TPU:1, one launch (start us, length us, event | category | flops | bytes accessed | tf_op | source)
XLA Modules:
  0.0 445.8 jit_solution(4919886062382566867)
XLA Ops:
  21.3 33.8 %collective-permute-done.7.refs_1_ = bf16[1,1248]{1,0:T(2,128)(2,1)S(1)} collective-permute-done((bf16[1,1248]{1,0:T(2,128)(2,1)S(1)}, bf16[1,1248]{1,0:T(2,128)(2,1)S(1)}, u32[]{:S(2)}, u32[]{:S(2)}) %collective-permute-start.7) | collective-permute-done | bytes 2528 | tf_op jit(solution)/shard_map/ppermute | solution.py:524
  55.1 9.5 %collective-permute-start.8 = (bf16[1,1248]{1,0:T(2,128)(2,1)S(1)}, bf16[1,1248]{1,0:T(2,128)(2,1)S(1)}, u32[]{:S(2)}, u32[]{:S(2)}) collective-permute-start(bf16[1,1248]{1,0:T(2,128)(2,1)S(1)} %broadcast_in_dim.59.refs_0_), channel_id=1, source_target_pairs={{0,8},{1,9},{2,10},{3,11},{4,12},{5,13},{6,14},{7,15},{8,0},{9,1},... | collective-permute-start | bytes 7496 | tf_op jit(solution)/shard_map/ppermute | solution.py:524
  79.5 3.0 collective-permute-done.13.refs_1_
  89.8 34.6 %collective-permute-done.11.refs_1_ = bf16[4,48,4608]{2,1,0:T(8,128)(2,1)S(1)} collective-permute-done((bf16[4,48,4608]{2,1,0:T(8,128)(2,1)S(1)}, bf16[4,48,4608]{2,1,0:T(8,128)(2,1)S(1)}, u32[]{:S(2)}, u32[]{:S(2)}) %collective-permute-start.11) | collective-permute-done | bytes 1769504 | tf_op jit(solution)/shard_map/ppermute | solution.py:518
  147.5 10.2 %collective-permute-done.21.refs_3_ = bf16[2,48,4608]{2,1,0:T(8,128)(2,1)} collective-permute-done((bf16[2,48,4608]{2,1,0:T(8,128)(2,1)}, bf16[2,48,4608]{2,1,0:T(8,128)(2,1)}, u32[]{:S(2)}, u32[]{:S(2)}) %collective-permute-start.21) | collective-permute-done | bytes 884768 | tf_op jit(solution)/shard_map/ppermute | solution.py:518
  157.7 5.0 %place_blocks.2 = (bf16[4,4,48,1536]{3,2,1,0:T(8,128)(2,1)}, bf16[4,4,48,3072]{3,2,1,0:T(8,128)(2,1)}) custom-call(s32[1]{0:T(128)} %bitcast.31.spot_ref, bf16[4,48,4608]{2,1,0:T(8,128)(2,1)S(1)} %place_line.4.refs_0_, bf16[4,48,4608]{2,1,0:T(8,128)(2,1)S(1)} %collective-permute-done.11.refs_1_, bf16[4,48,4608]{2,1,0:T(8,128)(2,1)} %collective-permute-done.12.refs_2_, ...), custom_call_target="tpu_custom_call" | custom-call | tf_op jit(solution)/shard_map/place_blocks/pallas_call | solution.py:579
  162.7 7.0 %collective-permute-start.24 = (bf16[768,3072]{1,0:T(8,128)(2,1)}, bf16[768,3072]{1,0:T(8,128)(2,1)}, u32[]{:S(2)}, u32[]{:S(2)}) collective-permute-start(bf16[768,3072]{1,0:T(8,128)(2,1)} %bitcast.192), channel_id=1, source_target_pairs={{0,16},{16,0},{1,17},{17,1},{2,18},{18,2},{3,19},{19,3},{4,20},{20... | collective-permute-start | bytes 14155784 | tf_op jit(solution)/shard_map/ppermute | solution.py:513
  173.7 6.5 %collective-permute-done.25.refs_3_ = bf16[2,48,1536]{2,1,0:T(8,128)(2,1)S(1)} collective-permute-done((bf16[2,48,1536]{2,1,0:T(8,128)(2,1)}, bf16[2,48,1536]{2,1,0:T(8,128)(2,1)S(1)}, u32[]{:S(2)}, u32[]{:S(2)}) %collective-permute-start.25) | collective-permute-done | bytes 294944 | tf_op jit(solution)/shard_map/ppermute | solution.py:518
  185.8 8.0 %attn_forward.2 = (bf16[2,256,1152]{2,1,0:T(8,128)(2,1)S(1)}, f32[2,6,256]{2,1,0:T(8,128)S(1)}, bf16[256,768]{1,0:T(8,128)(2,1)S(1)}, f32[256,768]{1,0:T(8,128)S(1)}) custom-call(s32[1]{0:T(128)} %bitcast.side, bf16[256,768]{1,0:T(8,128)(2,1)S(1)} %copy-done.16, f32[3,256,128]{2,1,0:T(8,128)S(1)} %pad_maximum_fusion.1.tables, f32[256,256]{1,0:T(8,128)S(1)} %fusion.6.mask, ...), custom_call_target="tpu_custom_call" | custom-call | flops 9059696640 | bytes 4718592 | tf_op jit(solution)/shard_map/attn_forward/pallas_call | solution.py:153
  194.8 9.2 %mlp_forward.2 = (bf16[256,3072]{1,0:T(8,128)(2,1)S(1)}, f32[256,3072]{1,0:T(8,128)}, bf16[256,768]{1,0:T(8,128)(2,1)S(1)}) custom-call(s32[1]{0:T(128)} %bitcast.side, bf16[256,768]{1,0:T(8,128)(2,1)S(1)} %copy-done.16, f32[256,768]{1,0:T(8,128)S(1)} %get-tuple-element.150.passed, f32[4,768]{1,0:T(4,128)S(1)} %get-tuple-element.141.norms, ...), custom_call_target="tpu_custom_call" | custom-call | flops 12079595520 | bytes 14155776 | tf_op jit(solution)/shard_map/mlp_forward/pallas_call | solution.py:256
  205.2 8.0 %attn_forward.3 = (bf16[2,256,1152]{2,1,0:T(8,128)(2,1)S(1)}, f32[2,6,256]{2,1,0:T(8,128)S(1)}, bf16[256,768]{1,0:T(8,128)(2,1)S(1)}, f32[256,768]{1,0:T(8,128)S(1)}) custom-call(s32[1]{0:T(128)} %bitcast.side, bf16[256,768]{1,0:T(8,128)(2,1)S(1)} %get-tuple-element.153.rows, f32[3,256,128]{2,1,0:T(8,128)S(1)} %pad_maximum_fusion.1.tables, ...), custom_call_target="tpu_custom_call" | custom-call | flops 9059696640 | bytes 4718592 | tf_op jit(solution)/shard_map/attn_forward/pallas_call | solution.py:153
  213.2 8.8 %mlp_forward.3 = (bf16[256,3072]{1,0:T(8,128)(2,1)S(1)}, f32[256,3072]{1,0:T(8,128)}, f32[256,768]{1,0:T(8,128)S(1)}) custom-call(s32[1]{0:T(128)} %bitcast.side, bf16[256,768]{1,0:T(8,128)(2,1)S(1)} %get-tuple-element.153.rows, f32[256,768]{1,0:T(8,128)S(1)} %get-tuple-element.163.passed, f32[4,768]{1,0:T(4,128)S(1)} %copy-done.26, ...), custom_call_target="tpu_custom_call" | custom-call | flops 12079595520 | bytes 14155776 | tf_op jit(solution)/shard_map/mlp_forward/pallas_call | solution.py:256
  221.9 13.1 %mlp_backward.2 = (bf16[768,1536]{1,0:T(8,128)(2,1)S(1)}, bf16[768,1536]{1,0:T(8,128)(2,1)}, bf16[768,1536]{1,0:T(8,128)(2,1)}, bf16[768,1536]{1,0:T(8,128)(2,1)...) custom-call(s32[1]{0:T(128)} %bitcast.side, bf16[256,768]{1,0:T(8,128)(2,1)S(1)} %get-tuple-element.153.rows, ...), custom_call_target="tpu_custom_call" | custom-call | flops 19327352832 | bytes 23592960 | tf_op jit(solution)/shard_map/mlp_backward/pallas_call | solution.py:354
  235.7 12.4 %attn_backward.2 = (bf16[768,1536]{1,0:T(8,128)(2,1)}, bf16[768,1536]{1,0:T(8,128)(2,1)}, f32[2,1152]{1,0:T(2,128)S(1)}, f32[5,768]{1,0:T(8,128)S(1)}, bf16[256,768]{1,0:T(8,128)(2,1)S(1)}) custom-call(s32[1]{0:T(128)} %bitcast.side, bf16[256,768]{1,0:T(8,128)(2,1)S(1)} %get-tuple-element.153.rows, bf16[256,768]{1,0:T(8,128)(2,1)S(1)} %copy-done.18, ...), custom_call_target="tpu_custom_call" | custom-call | flops 14495514624 | bytes 9437184 | tf_op jit(solution)/shard_map/attn_backward/pallas_call | solution.py:475
  253.1 12.9 %mlp_backward.3 = (bf16[768,1536]{1,0:T(8,128)(2,1)S(1)}, bf16[768,1536]{1,0:T(8,128)(2,1)}, bf16[768,1536]{1,0:T(8,128)(2,1)}, bf16[768,1536]{1,0:T(8,128)(2,1)...) custom-call(s32[1]{0:T(128)} %bitcast.side, bf16[256,768]{1,0:T(8,128)(2,1)S(1)} %copy-done.17, ...), custom_call_target="tpu_custom_call" | custom-call | flops 19327352832 | bytes 23592960 | tf_op jit(solution)/shard_map/mlp_backward/pallas_call | solution.py:354
  271.0 3.3 near_blocks.3
  276.7 13.4 %attn_backward.3 = (bf16[768,1536]{1,0:T(8,128)(2,1)}, bf16[768,1536]{1,0:T(8,128)(2,1)}, f32[2,1152]{1,0:T(2,128)S(1)}, f32[5,768]{1,0:T(8,128)S(1)}, f32[256,768]{1,0:T(8,128)S(1)}) custom-call(s32[1]{0:T(128)} %bitcast.side, bf16[256,768]{1,0:T(8,128)(2,1)S(1)} %copy-done.17, bf16[256,768]{1,0:T(8,128)(2,1)S(1)} %copy-done.44, ...), custom_call_target="tpu_custom_call" | custom-call | flops 14495514624 | bytes 9437184 | tf_op jit(solution)/shard_map/attn_backward/pallas_call | solution.py:475
  294.9 6.1 %collective-permute-done.36.refs_4_ = bf16[4,48,3072]{2,1,0:T(8,128)(2,1)S(1)} collective-permute-done((bf16[4,48,3072]{2,1,0:T(8,128)(2,1)S(1)}, bf16[4,48,3072]{2,1,0:T(8,128)(2,1)S(1)}, u32[]{:S(2)}, u32[]{:S(2)}) %collective-permute-start.36) | collective-permute-done | bytes 1179680 | tf_op jit(solution)/shard_map/ppermute | solution.py:518
  316.1 5.7 %collective-permute-done.52 = bf16[4,48,1536]{2,1,0:T(8,128)(2,1)} collective-permute-done((bf16[4,48,1536]{2,1,0:T(8,128)(2,1)}, bf16[4,48,1536]{2,1,0:T(8,128)(2,1)}, u32[]{:S(2)}, u32[]{:S(2)}) %collective-permute-start.52) | collective-permute-done | bytes 589856 | tf_op jit(solution)/shard_map/ppermute | solution.py:524
  322.8 3.4 collective-permute-done.42.refs_8_
  332.7 2.9 collective-permute-start.34
  336.6 4.7 %near_blocks.4 = (bf16[4,48,3072]{2,1,0:T(8,128)(2,1)}, bf16[4,48,3072]{2,1,0:T(8,128)(2,1)}) custom-call(s32[2]{0:T(128)S(1)} %pad_add_fusion.place_ref, bf16[4,4,48,1536]{3,2,1,0:T(8,128)(2,1)S(1)} %bitcast.150, bf16[4,4,48,1536]{3,2,1,0:T(8,128)(2,1)} %bitcast.153, bf16[4,4,48,1536]{3,2,1,0:T(8,128)(2,1)S(1)} %bitcast.151, ...), custom_call_target="tpu_custom_call" | custom-call | tf_op jit(solution)/shard_map/near_blocks/pallas_call | solution.py:774
  344.9 6.7 %collective-permute-done.53 = bf16[4,48,1536]{2,1,0:T(8,128)(2,1)S(1)} collective-permute-done((bf16[4,48,1536]{2,1,0:T(8,128)(2,1)S(1)}, bf16[4,48,1536]{2,1,0:T(8,128)(2,1)S(1)}, u32[]{:S(2)}, u32[]{:S(2)}) %collective-permute-start.53) | collective-permute-done | bytes 589856 | tf_op jit(solution)/shard_map/ppermute | solution.py:524
  353.1 3.3 column_blocks.5
  356.4 11.2 %collective-permute-done.44.refs_4_ = bf16[4,48,3072]{2,1,0:T(8,128)(2,1)S(1)} collective-permute-done((bf16[4,48,3072]{2,1,0:T(8,128)(2,1)}, bf16[4,48,3072]{2,1,0:T(8,128)(2,1)S(1)}, u32[]{:S(2)}, u32[]{:S(2)}) %collective-permute-start.44) | collective-permute-done | bytes 1179680 | tf_op jit(solution)/shard_map/ppermute | solution.py:518
  372.6 3.1 near_blocks.5
  391.7 2.7 collective-permute-done.46.refs_2_
  404.8 2.9 collective-permute-start.50
  407.7 7.2 %collective-permute-done.66 = bf16[48,3072]{1,0:T(8,128)(2,1)S(1)} collective-permute-done((bf16[48,3072]{1,0:T(8,128)(2,1)}, bf16[48,3072]{1,0:T(8,128)(2,1)S(1)}, u32[]{:S(2)}, u32[]{:S(2)}) %collective-permute-start.66) | collective-permute-done | bytes 294944 | tf_op jit(solution)/shard_map/ppermute | solution.py:524
  414.9 8.7 %collective-permute-start.48 = (bf16[48,1536]{1,0:T(8,128)(2,1)S(1)}, bf16[48,1536]{1,0:T(8,128)(2,1)S(1)}, u32[]{:S(2)}, u32[]{:S(2)}) collective-permute-start(bf16[48,1536]{1,0:T(8,128)(2,1)S(1)} %get-tuple-element.224), channel_id=1, source_target_pairs={{0,4},{1,5},{2,6},{3,7},{4,8},{5,9},{6,10},{7,11},{8,12},{9,13},{1... | collective-permute-start | bytes 442376 | tf_op jit(solution)/shard_map/ppermute | solution.py:524
  425.1 3.2 collective-permute-start.71
  430.1 5.4 %collective-permute-start.57 = (f32[48,1536]{1,0:T(8,128)S(1)}, f32[48,1536]{1,0:T(8,128)S(1)}, u32[]{:S(2)}, u32[]{:S(2)}) collective-permute-start(f32[48,1536]{1,0:T(8,128)S(1)} %get-tuple-element.252), channel_id=1, source_target_pairs={{0,16},{16,0},{1,17},{17,1},{2,18},{18,2},{3,19},{19,3},{4,20},{20... | collective-permute-start | bytes 884744 | tf_op jit(solution)/shard_map/ppermute | solution.py:513
  (381 shorter events, 154.5 us)
Async XLA Ops:
  7.2 150.5 %all-gather.2.cloned.1.call-start = ((), (), s32[]{:S(2)}) async-start(), calls=%async_computation | async-start | bytes 5013504 | tf_op jit(solution)/shard_map/all_gather | solution.py:627
  13.7 56.2 %collective-permute-start.10 = (bf16[256,768]{1,0:T(8,128)(2,1)}, bf16[256,768]{1,0:T(8,128)(2,1)S(1)}, u32[]{:S(2)}, u32[]{:S(2)}) collective-permute-start(bf16[256,768]{1,0:T(8,128)(2,1)} %dynamic-slice_bitcast_fusion), channel_id=1, source_target_pairs={{0,16},{16,0},{1,17},{17,1},{2,18},{18,2},{3,19},{19,3},{4,20},{20... | collective-permute-start | bytes 1179656 | tf_op jit(solution)/shard_map/ppermute | solution.py:513
  14.8 56.2 %collective-permute-start.3 = (bf16[48,4608]{1,0:T(8,128)(2,1)S(1)}, bf16[48,4608]{1,0:T(8,128)(2,1)S(1)}, u32[]{:S(2)}, u32[]{:S(2)}) collective-permute-start(bf16[48,4608]{1,0:T(8,128)(2,1)S(1)} %pad_maximum_fusion.refs_0_), channel_id=1, source_target_pairs={{0,4},{1,5},{2,6},{3,7},{4,8},{5,9},{6,10},{7,11},{8,12},{9,13},{1... | collective-permute-start | bytes 1327112 | tf_op jit(solution)/shard_map/ppermute | solution.py:524
  17.5 53.6 %collective-permute-start.4 = (bf16[48,4608]{1,0:T(8,128)(2,1)S(1)}, bf16[48,4608]{1,0:T(8,128)(2,1)S(1)}, u32[]{:S(2)}, u32[]{:S(2)}) collective-permute-start(bf16[48,4608]{1,0:T(8,128)(2,1)S(1)} %pad_maximum_fusion.refs_0_), channel_id=1, source_target_pairs={{0,8},{1,9},{2,10},{3,11},{4,12},{5,13},{6,14},{7,15},{8,0},{9,1},... | collective-permute-start | bytes 1327112 | tf_op jit(solution)/shard_map/ppermute | solution.py:524
  19.8 51.3 %collective-permute-start.5 = (bf16[48,4608]{1,0:T(8,128)(2,1)S(1)}, bf16[48,4608]{1,0:T(8,128)(2,1)S(1)}, u32[]{:S(2)}, u32[]{:S(2)}) collective-permute-start(bf16[48,4608]{1,0:T(8,128)(2,1)S(1)} %pad_maximum_fusion.refs_0_), channel_id=1, source_target_pairs={{0,12},{1,13},{2,14},{3,15},{4,0},{5,1},{6,2},{7,3},{8,4},{9,5},{1... | collective-permute-start | bytes 1327112 | tf_op jit(solution)/shard_map/ppermute | solution.py:524
  20.9 34.2 %collective-permute-start.7 = (bf16[1,1248]{1,0:T(2,128)(2,1)S(1)}, bf16[1,1248]{1,0:T(2,128)(2,1)S(1)}, u32[]{:S(2)}, u32[]{:S(2)}) collective-permute-start(bf16[1,1248]{1,0:T(2,128)(2,1)S(1)} %broadcast_in_dim.59.refs_0_), channel_id=1, source_target_pairs={{0,4},{1,5},{2,6},{3,7},{4,8},{5,9},{6,10},{7,11},{8,12},{9,13},{1... | collective-permute-start | bytes 7496 | tf_op jit(solution)/shard_map/ppermute | solution.py:524
  72.6 51.7 %collective-permute-start.11 = (bf16[4,48,4608]{2,1,0:T(8,128)(2,1)S(1)}, bf16[4,48,4608]{2,1,0:T(8,128)(2,1)S(1)}, u32[]{:S(2)}, u32[]{:S(2)}) collective-permute-start(bf16[4,48,4608]{2,1,0:T(8,128)(2,1)S(1)} %place_line.4.refs_0_), channel_id=1, source_target_pairs={{0,1},{1,0},{2,3},{3,2},{4,5},{5,4},{6,7},{7,6},{8,9},{9,8},{10,11... | collective-permute-start | bytes 5308424 | tf_op jit(solution)/shard_map/ppermute | solution.py:518
  73.9 52.3 %collective-permute-start.12 = (bf16[4,48,4608]{2,1,0:T(8,128)(2,1)S(1)}, bf16[4,48,4608]{2,1,0:T(8,128)(2,1)}, u32[]{:S(2)}, u32[]{:S(2)}) collective-permute-start(bf16[4,48,4608]{2,1,0:T(8,128)(2,1)S(1)} %place_line.4.refs_0_), channel_id=1, source_target_pairs={{0,2},{1,3},{2,0},{3,1},{4,6},{5,7},{6,4},{7,5},{8,10},{9,11},{10,... | collective-permute-start | bytes 5308424 | tf_op jit(solution)/shard_map/ppermute | solution.py:518
  82.5 45.8 %collective-permute-start.16 = (bf16[4,1,1248]{2,1,0:T(2,128)(2,1)}, bf16[4,1,1248]{2,1,0:T(2,128)(2,1)S(1)}, u32[]{:S(2)}, u32[]{:S(2)}) collective-permute-start(bf16[4,1,1248]{2,1,0:T(2,128)(2,1)} %copy-done.22), channel_id=1, source_target_pairs={{0,1},{1,0},{2,3},{3,2},{4,5},{5,4},{6,7},{7,6},{8,9},{9,8},{10,11... | collective-permute-start | bytes 29960 | tf_op jit(solution)/shard_map/ppermute | solution.py:518
  84.9 43.5 %collective-permute-start.17 = (bf16[4,1,1248]{2,1,0:T(2,128)(2,1)}, bf16[4,1,1248]{2,1,0:T(2,128)(2,1)S(1)}, u32[]{:S(2)}, u32[]{:S(2)}) collective-permute-start(bf16[4,1,1248]{2,1,0:T(2,128)(2,1)} %copy-done.22), channel_id=1, source_target_pairs={{0,2},{1,3},{2,0},{3,1},{4,6},{5,7},{6,4},{7,5},{8,10},{9,11},{10,... | collective-permute-start | bytes 29960 | tf_op jit(solution)/shard_map/ppermute | solution.py:518
  87.3 41.1 %collective-permute-start.18 = (bf16[4,1,1248]{2,1,0:T(2,128)(2,1)}, bf16[4,1,1248]{2,1,0:T(2,128)(2,1)S(1)}, u32[]{:S(2)}, u32[]{:S(2)}) collective-permute-start(bf16[4,1,1248]{2,1,0:T(2,128)(2,1)} %copy-done.22), channel_id=1, source_target_pairs={{0,3},{1,2},{2,1},{3,0},{4,7},{5,6},{6,5},{7,4},{8,11},{9,10},{10,... | collective-permute-start | bytes 29960 | tf_op jit(solution)/shard_map/ppermute | solution.py:518
  131.0 26.7 %collective-permute-start.21 = (bf16[2,48,4608]{2,1,0:T(8,128)(2,1)}, bf16[2,48,4608]{2,1,0:T(8,128)(2,1)}, u32[]{:S(2)}, u32[]{:S(2)}) collective-permute-start(bf16[2,48,4608]{2,1,0:T(8,128)(2,1)} %slice.221), channel_id=1, source_target_pairs={{0,2},{1,3},{2,0},{3,1},{4,6},{5,7},{6,4},{7,5},{8,10},{9,11},{10,... | collective-permute-start | bytes 2654216 | tf_op jit(solution)/shard_map/ppermute | solution.py:518
  131.1 26.6 %collective-permute-start.22 = (bf16[2,48,4608]{2,1,0:T(8,128)(2,1)}, bf16[2,48,4608]{2,1,0:T(8,128)(2,1)}, u32[]{:S(2)}, u32[]{:S(2)}) collective-permute-start(bf16[2,48,4608]{2,1,0:T(8,128)(2,1)} %slice.222), channel_id=1, source_target_pairs={{0,1},{1,0},{2,3},{3,2},{4,5},{5,4},{6,7},{7,6},{8,9},{9,8},{10,11... | collective-permute-start | bytes 2654216 | tf_op jit(solution)/shard_map/ppermute | solution.py:518
  162.7 32.0 %collective-permute-start.24 = (bf16[768,3072]{1,0:T(8,128)(2,1)}, bf16[768,3072]{1,0:T(8,128)(2,1)}, u32[]{:S(2)}, u32[]{:S(2)}) collective-permute-start(bf16[768,3072]{1,0:T(8,128)(2,1)} %bitcast.192), channel_id=1, source_target_pairs={{0,16},{16,0},{1,17},{17,1},{2,18},{18,2},{3,19},{19,3},{4,20},{20... | collective-permute-start | bytes 14155784 | tf_op jit(solution)/shard_map/ppermute | solution.py:513
  169.9 43.3 %collective-permute-start.28 = (bf16[768,3072]{1,0:T(8,128)(2,1)}, bf16[768,3072]{1,0:T(8,128)(2,1)}, u32[]{:S(2)}, u32[]{:S(2)}) collective-permute-start(bf16[768,3072]{1,0:T(8,128)(2,1)} %all-gather.2.cloned.1.call-done.up_mine.down_mine), channel_id=1, source_target_pairs={{0,16},{16,0},{1,17},{17,1},{2,18},{18,2},{3,19},{19,3},{4,20},{20... | collective-permute-start | bytes 14155784 | tf_op jit(solution)/shard_map/ppermute | solution.py:513
  182.6 22.5 %collective-permute-start.27 = (bf16[768,1536]{1,0:T(8,128)(2,1)S(1)}, bf16[768,1536]{1,0:T(8,128)(2,1)}, u32[]{:S(2)}, u32[]{:S(2)}) collective-permute-start(bf16[768,1536]{1,0:T(8,128)(2,1)S(1)} %bitcast.157), channel_id=1, source_target_pairs={{0,16},{16,0},{1,17},{17,1},{2,18},{18,2},{3,19},{19,3},{4,20},{20... | collective-permute-start | bytes 7077896 | tf_op jit(solution)/shard_map/ppermute | solution.py:513
  268.3 37.9 %collective-permute-start.40 = (bf16[768,1536]{1,0:T(8,128)(2,1)}, bf16[768,1536]{1,0:T(8,128)(2,1)S(1)}, u32[]{:S(2)}, u32[]{:S(2)}) collective-permute-start(bf16[768,1536]{1,0:T(8,128)(2,1)} %get-tuple-element.203), channel_id=1, source_target_pairs={{0,16},{16,0},{1,17},{17,1},{2,18},{18,2},{3,19},{19,3},{4,20},{20... | collective-permute-start | bytes 7077896 | tf_op jit(solution)/shard_map/ppermute | solution.py:513
  269.0 38.7 %collective-permute-start.41 = (bf16[768,1536]{1,0:T(8,128)(2,1)}, bf16[768,1536]{1,0:T(8,128)(2,1)}, u32[]{:S(2)}, u32[]{:S(2)}) collective-permute-start(bf16[768,1536]{1,0:T(8,128)(2,1)} %get-tuple-element.205), channel_id=1, source_target_pairs={{0,16},{16,0},{1,17},{17,1},{2,18},{18,2},{3,19},{19,3},{4,20},{20... | collective-permute-start | bytes 7077896 | tf_op jit(solution)/shard_map/ppermute | solution.py:513
  274.3 26.8 %collective-permute-start.36 = (bf16[4,48,3072]{2,1,0:T(8,128)(2,1)S(1)}, bf16[4,48,3072]{2,1,0:T(8,128)(2,1)S(1)}, u32[]{:S(2)}, u32[]{:S(2)}) collective-permute-start(bf16[4,48,3072]{2,1,0:T(8,128)(2,1)S(1)} %get-tuple-element.190), channel_id=1, source_target_pairs={{0,1},{1,0},{2,3},{3,2},{4,5},{5,4},{6,7},{7,6},{8,9},{9,8},{10,11... | collective-permute-start | bytes 3538952 | tf_op jit(solution)/shard_map/ppermute | solution.py:518
  275.4 28.4 %collective-permute-start.37 = (bf16[4,48,3072]{2,1,0:T(8,128)(2,1)S(1)}, bf16[4,48,3072]{2,1,0:T(8,128)(2,1)S(1)}, u32[]{:S(2)}, u32[]{:S(2)}) collective-permute-start(bf16[4,48,3072]{2,1,0:T(8,128)(2,1)S(1)} %get-tuple-element.191), channel_id=1, source_target_pairs={{0,2},{1,3},{2,0},{3,1},{4,6},{5,7},{6,4},{7,5},{8,10},{9,11},{10,... | collective-permute-start | bytes 3538952 | tf_op jit(solution)/shard_map/ppermute | solution.py:518
  291.2 23.2 %collective-permute-start.35 = (bf16[768,1536]{1,0:T(8,128)(2,1)}, bf16[768,1536]{1,0:T(8,128)(2,1)S(1)}, u32[]{:S(2)}, u32[]{:S(2)}) collective-permute-start(bf16[768,1536]{1,0:T(8,128)(2,1)} %get-tuple-element.197), channel_id=1, source_target_pairs={{0,16},{16,0},{1,17},{17,1},{2,18},{18,2},{3,19},{19,3},{4,20},{20... | collective-permute-start | bytes 7077896 | tf_op jit(solution)/shard_map/ppermute | solution.py:513
  313.9 27.4 %collective-permute-start.61 = (f32[1,9984]{1,0:T(1,128)S(1)}, f32[1,9984]{1,0:T(1,128)S(1)}, u32[]{:S(2)}, u32[]{:S(2)}) collective-permute-start(f32[1,9984]{1,0:T(1,128)S(1)} %fusion.14), channel_id=1, source_target_pairs={{0,3},{1,2},{2,1},{3,0},{4,7},{5,6},{6,5},{7,4},{8,11},{9,10},{10,... | collective-permute-start | bytes 119816 | tf_op jit(solution)/shard_map/ppermute | solution.py:518
  314.4 28.0 %collective-permute-start.60 = (f32[1,9984]{1,0:T(1,128)S(1)}, f32[1,9984]{1,0:T(1,128)S(1)}, u32[]{:S(2)}, u32[]{:S(2)}) collective-permute-start(f32[1,9984]{1,0:T(1,128)S(1)} %fusion.14), channel_id=1, source_target_pairs={{0,2},{1,3},{2,0},{3,1},{4,6},{5,7},{6,4},{7,5},{8,10},{9,11},{10,... | collective-permute-start | bytes 119816 | tf_op jit(solution)/shard_map/ppermute | solution.py:518
  321.8 21.6 %collective-permute-start.59 = (f32[1,9984]{1,0:T(1,128)S(1)}, f32[1,9984]{1,0:T(1,128)S(1)}, u32[]{:S(2)}, u32[]{:S(2)}) collective-permute-start(f32[1,9984]{1,0:T(1,128)S(1)} %fusion.14), channel_id=1, source_target_pairs={{0,1},{1,0},{2,3},{3,2},{4,5},{5,4},{6,7},{7,6},{8,9},{9,8},{10,11... | collective-permute-start | bytes 119816 | tf_op jit(solution)/shard_map/ppermute | solution.py:518
  341.2 26.3 %collective-permute-start.44 = (bf16[4,48,3072]{2,1,0:T(8,128)(2,1)}, bf16[4,48,3072]{2,1,0:T(8,128)(2,1)S(1)}, u32[]{:S(2)}, u32[]{:S(2)}) collective-permute-start(bf16[4,48,3072]{2,1,0:T(8,128)(2,1)} %get-tuple-element.215), channel_id=1, source_target_pairs={{0,1},{1,0},{2,3},{3,2},{4,5},{5,4},{6,7},{7,6},{8,9},{9,8},{10,11... | collective-permute-start | bytes 3538952 | tf_op jit(solution)/shard_map/ppermute | solution.py:518
  342.4 26.9 %collective-permute-start.45 = (bf16[4,48,3072]{2,1,0:T(8,128)(2,1)}, bf16[4,48,3072]{2,1,0:T(8,128)(2,1)S(1)}, u32[]{:S(2)}, u32[]{:S(2)}) collective-permute-start(bf16[4,48,3072]{2,1,0:T(8,128)(2,1)} %get-tuple-element.216), channel_id=1, source_target_pairs={{0,2},{1,3},{2,0},{3,1},{4,6},{5,7},{6,4},{7,5},{8,10},{9,11},{10,... | collective-permute-start | bytes 3538952 | tf_op jit(solution)/shard_map/ppermute | solution.py:518
  356.4 34.1 %collective-permute-start.70 = (bf16[48,3072]{1,0:T(8,128)(2,1)}, bf16[48,3072]{1,0:T(8,128)(2,1)}, u32[]{:S(2)}, u32[]{:S(2)}) collective-permute-start(bf16[48,3072]{1,0:T(8,128)(2,1)} %get-tuple-element.243), channel_id=1, source_target_pairs={{0,12},{1,13},{2,14},{3,15},{4,0},{5,1},{6,2},{7,3},{8,4},{9,5},{1... | collective-permute-start | bytes 884744 | tf_op jit(solution)/shard_map/ppermute | solution.py:524
  356.4 35.3 %collective-permute-start.69 = (bf16[48,3072]{1,0:T(8,128)(2,1)}, bf16[48,3072]{1,0:T(8,128)(2,1)}, u32[]{:S(2)}, u32[]{:S(2)}) collective-permute-start(bf16[48,3072]{1,0:T(8,128)(2,1)} %get-tuple-element.242), channel_id=1, source_target_pairs={{0,8},{1,9},{2,10},{3,11},{4,12},{5,13},{6,14},{7,15},{8,0},{9,1},... | collective-permute-start | bytes 884744 | tf_op jit(solution)/shard_map/ppermute | solution.py:524
  380.5 23.3 %collective-permute-start.68 = (bf16[48,3072]{1,0:T(8,128)(2,1)}, bf16[48,3072]{1,0:T(8,128)(2,1)}, u32[]{:S(2)}, u32[]{:S(2)}) collective-permute-start(bf16[48,3072]{1,0:T(8,128)(2,1)} %get-tuple-element.241), channel_id=1, source_target_pairs={{0,4},{1,5},{2,6},{3,7},{4,8},{5,9},{6,10},{7,11},{8,12},{9,13},{1... | collective-permute-start | bytes 884744 | tf_op jit(solution)/shard_map/ppermute | solution.py:524
  391.6 23.2 %collective-permute-start.66 = (bf16[48,3072]{1,0:T(8,128)(2,1)}, bf16[48,3072]{1,0:T(8,128)(2,1)S(1)}, u32[]{:S(2)}, u32[]{:S(2)}) collective-permute-start(bf16[48,3072]{1,0:T(8,128)(2,1)} %copy-done.35), channel_id=1, source_target_pairs={{0,8},{1,9},{2,10},{3,11},{4,12},{5,13},{6,14},{7,15},{8,0},{9,1},... | collective-permute-start | bytes 884744 | tf_op jit(solution)/shard_map/ppermute | solution.py:524
  403.8 25.1 %collective-permute-start.54 = (bf16[48,1536]{1,0:T(8,128)(2,1)S(1)}, bf16[48,1536]{1,0:T(8,128)(2,1)S(1)}, u32[]{:S(2)}, u32[]{:S(2)}) collective-permute-start(bf16[48,1536]{1,0:T(8,128)(2,1)S(1)} %copy-done.53), channel_id=1, source_target_pairs={{0,1},{1,0},{2,3},{3,2},{4,5},{5,4},{6,7},{7,6},{8,9},{9,8},{10,11... | collective-permute-start | bytes 442376 | tf_op jit(solution)/shard_map/ppermute | solution.py:518
  404.8 24.2 %collective-permute-start.50 = (bf16[48,1536]{1,0:T(8,128)(2,1)S(1)}, bf16[48,1536]{1,0:T(8,128)(2,1)S(1)}, u32[]{:S(2)}, u32[]{:S(2)}) collective-permute-start(bf16[48,1536]{1,0:T(8,128)(2,1)S(1)} %get-tuple-element.226), channel_id=1, source_target_pairs={{0,12},{1,13},{2,14},{3,15},{4,0},{5,1},{6,2},{7,3},{8,4},{9,5},{1... | collective-permute-start | bytes 442376 | tf_op jit(solution)/shard_map/ppermute | solution.py:524
  (104 other events, 831.3 us)
Sparse Core Ops, SparseCore 0:
  11.9 121.2 all-gather.1

commit v8 on v7

--- a/solution.py
+++ b/solution.py
@@ -995,21 +995,21 @@
         whole_b = gather_whole(wide[1])
         ring_a = ring_moved(lower)
         line = small_both[None]
-        ring_s = ring_moved(line)
-        column_s = line_placed(ring_order(), [line] + ring_s)
         column_a = column_of(lower, ring_a)
-        column_a, next_c, column_s, entry, cotangent = after(
-            (column_a, narrow[1], column_s, entry, cotangent), (ring_a, ring_s)
+        column_a, next_c, line, entry, cotangent = after(
+            (column_a, narrow[1], line, entry, cotangent), ring_a
         )
         near_a = near_moved(column_a)
-        square_s = square_moved(column_s)
         ring_c = ring_moved(next_c)
+        ring_s = ring_moved(line)
         column_c = column_of(next_c, ring_c)
-        lows, column_c, square_s = after(
-            (cut_near(near_a), column_c, square_s), (near_a, ring_c, square_s)
+        column_s = line_placed(ring_order(), [line] + ring_s)
+        lows, column_c, column_s = after(
+            (cut_near(near_a), column_c, column_s), (near_a, ring_c, ring_s)
         )
         far_a = far_moved(lows)
         near_c = near_moved(column_c)
+        square_s = square_moved(column_s)
         rows_s = line_placed(square_order(), [column_s] + square_s)
         spread_out(rows_s.transpose(1, 0, 2, 3).reshape(PARTS, -1))
         parts_a = (column_a,) + near_a + far_a
@@ -1060,7 +1060,7 @@
         moved_b = next(steps_b)
         pairs_c = mlp_pairs(lower)
         lower_attn = attn_back(
-            0, grad_middle, after(lower[5], (leaving_a, received_b)), jnp.float32
+            0, grad_middle, lower[5], jnp.float32
         )
         pairs_d = (lower_attn[0], swap_cores(lower_attn[1]))
         moved_b = next(steps_b)

time: 450 us -> 463 us (1.029)
  waiting for transfers between devices: 144 us -> 152 us
  starting transfers between devices: 96.5 us -> 102 us
    ppermute x24, waiting for transfers between devices: 62.6 us -> 79.9 us  [shift_ring(): return lax.ppermute(value, 'dp', pairs)]
    ppermute x24, starting transfers between devices: 41.5 us -> 51.8 us  [shift_ring(): return lax.ppermute(value, 'dp', pairs)]
    ppermute x29, waiting for transfers between devices: 81 us -> 72 us  [swap_square(): return lax.ppermute(value, 'dp', [(i, i ^ bit) for i in range(count)])]
    unnamed x154 -> x136, local copies, waits for them, and re-layouts: 22.4 us -> 18.8 us
where the time goes in v8:
time: 463 us; the launch traced here: 459 us
  waiting for transfers between devices  152 us (33%)
  Pallas kernels  123 us (27%)
  starting transfers between devices  102 us (22%)
  local copies, waits for them, and re-layouts  45 us (10%)
  other arithmetic  21.6 us (5%)
  between operations  15.3 us (3%)
    ppermute x24, waiting for transfers between devices, shift_ring(): return lax.ppermute(value, 'dp', pairs)  79.9 us
    ppermute x29, waiting for transfers between devices, swap_square(): return lax.ppermute(value, 'dp', [(i, i ^ bit) for i in range(count)])  72 us
    ppermute x24, starting transfers between devices, shift_ring(): return lax.ppermute(value, 'dp', pairs)  51.8 us
    ppermute x29, starting transfers between devices, swap_square(): return lax.ppermute(value, 'dp', [(i, i ^ bit) for i in range(count)])  27 us
    pallas_call x2, Pallas kernels, mlp_backward(): pl.pallas_call(mlp_backward_kernel, out_shape=(jax.ShapeDtypeStruct((feat...  26.5 us
    pallas_call x2, Pallas kernels, attn_backward(): pl.pallas_call(attn_backward_kernel, out_shape=(jax.ShapeDtypeStruct((fea...  25.7 us
    pallas_call x9, Pallas kernels, scatter_call(): pl.pallas_call(body, out_shape=tuple(outs), grid_spec=pltpu.PrefetchScala...  23.7 us
    ppermute x19, starting transfers between devices, swap_cores(): return lax.ppermute(value, 'section', [(0, 1), (1, 0)])  22.9 us
  transfers between devices with their start and end apart: 73, of which 19 were waited for; matrix products, arithmetic and copies ran while one was open for 10% of the time, Pallas kernels for 21%

profile of v8, /device:TPU:1, one launch (start us, length us, event | category | flops | bytes accessed | tf_op | source)
XLA Modules:
  0.0 458.6 jit_solution(12976019344589537482)
XLA Ops:
  21.3 9.6 %collective-permute-done.3.refs_1_ = bf16[48,4608]{1,0:T(8,128)(2,1)S(1)} collective-permute-done((bf16[48,4608]{1,0:T(8,128)(2,1)S(1)}, bf16[48,4608]{1,0:T(8,128)(2,1)S(1)}, u32[]{:S(2)}, u32[]{:S(2)}) %collective-permute-start.3) | collective-permute-done | bytes 442400 | tf_op jit(solution)/shard_map/ppermute | solution.py:524
  30.9 23.9 %collective-permute-done.4.refs_2_ = bf16[48,4608]{1,0:T(8,128)(2,1)S(1)} collective-permute-done((bf16[48,4608]{1,0:T(8,128)(2,1)S(1)}, bf16[48,4608]{1,0:T(8,128)(2,1)S(1)}, u32[]{:S(2)}, u32[]{:S(2)}) %collective-permute-start.4) | collective-permute-done | bytes 442400 | tf_op jit(solution)/shard_map/ppermute | solution.py:524
  58.9 9.9 %collective-permute-start.13 = (bf16[1,1248]{1,0:T(2,128)(2,1)S(1)}, bf16[1,1248]{1,0:T(2,128)(2,1)S(1)}, u32[]{:S(2)}, u32[]{:S(2)}) collective-permute-start(bf16[1,1248]{1,0:T(2,128)(2,1)S(1)} %broadcast_in_dim.59.refs_0_), channel_id=1, source_target_pairs={{0,4},{1,5},{2,6},{3,7},{4,8},{5,9},{6,10},{7,11},{8,12},{9,13},{1... | collective-permute-start | bytes 7496 | tf_op jit(solution)/shard_map/ppermute | solution.py:524
  78.7 11.6 %collective-permute-done.11.refs_2_ = bf16[48,1536]{1,0:T(8,128)(2,1)} collective-permute-done((bf16[48,1536]{1,0:T(8,128)(2,1)}, bf16[48,1536]{1,0:T(8,128)(2,1)}, u32[]{:S(2)}, u32[]{:S(2)}) %collective-permute-start.11) | collective-permute-done | bytes 147488 | tf_op jit(solution)/shard_map/ppermute | solution.py:524
  92.9 18.7 %collective-permute-done.8.refs_1_ = bf16[4,48,4608]{2,1,0:T(8,128)(2,1)S(1)} collective-permute-done((bf16[4,48,4608]{2,1,0:T(8,128)(2,1)S(1)}, bf16[4,48,4608]{2,1,0:T(8,128)(2,1)S(1)}, u32[]{:S(2)}, u32[]{:S(2)}) %collective-permute-start.8) | collective-permute-done | bytes 1769504 | tf_op jit(solution)/shard_map/ppermute | solution.py:518
  138.1 12.1 %collective-permute-done.18.refs_3_ = bf16[2,48,4608]{2,1,0:T(8,128)(2,1)} collective-permute-done((bf16[2,48,4608]{2,1,0:T(8,128)(2,1)}, bf16[2,48,4608]{2,1,0:T(8,128)(2,1)}, u32[]{:S(2)}, u32[]{:S(2)}) %collective-permute-start.18) | collective-permute-done | bytes 884768 | tf_op jit(solution)/shard_map/ppermute | solution.py:518
  152.3 5.1 %place_blocks.2 = (bf16[4,4,48,1536]{3,2,1,0:T(8,128)(2,1)}, bf16[4,4,48,3072]{3,2,1,0:T(8,128)(2,1)}) custom-call(s32[1]{0:T(128)} %bitcast.31.spot_ref, bf16[4,48,4608]{2,1,0:T(8,128)(2,1)S(1)} %place_line.4.refs_0_, bf16[4,48,4608]{2,1,0:T(8,128)(2,1)S(1)} %collective-permute-done.8.refs_1_, bf16[4,48,4608]{2,1,0:T(8,128)(2,1)} %collective-permute-done.9.refs_2_, ...), custom_call_target="tpu_custom_call" | custom-call | tf_op jit(solution)/shard_map/place_blocks/pallas_call | solution.py:579
  165.1 5.7 %collective-permute-done.25.refs_3_ = bf16[2,48,1536]{2,1,0:T(8,128)(2,1)S(1)} collective-permute-done((bf16[2,48,1536]{2,1,0:T(8,128)(2,1)}, bf16[2,48,1536]{2,1,0:T(8,128)(2,1)S(1)}, u32[]{:S(2)}, u32[]{:S(2)}) %collective-permute-start.25) | collective-permute-done | bytes 294944 | tf_op jit(solution)/shard_map/ppermute | solution.py:518
  176.4 8.0 %attn_forward.2 = (bf16[2,256,1152]{2,1,0:T(8,128)(2,1)S(1)}, f32[2,6,256]{2,1,0:T(8,128)S(1)}, bf16[256,768]{1,0:T(8,128)(2,1)S(1)}, f32[256,768]{1,0:T(8,128)S(1)}) custom-call(s32[1]{0:T(128)} %bitcast.side, bf16[256,768]{1,0:T(8,128)(2,1)S(1)} %copy-done.10, f32[3,256,128]{2,1,0:T(8,128)S(1)} %pad_maximum_fusion.1.tables, f32[256,256]{1,0:T(8,128)S(1)} %fusion.6.mask, ...), custom_call_target="tpu_custom_call" | custom-call | flops 9059696640 | bytes 4718592 | tf_op jit(solution)/shard_map/attn_forward/pallas_call | solution.py:153
  185.2 9.6 %mlp_forward.2 = (bf16[256,3072]{1,0:T(8,128)(2,1)S(1)}, f32[256,3072]{1,0:T(8,128)}, bf16[256,768]{1,0:T(8,128)(2,1)S(1)}) custom-call(s32[1]{0:T(128)} %bitcast.side, bf16[256,768]{1,0:T(8,128)(2,1)S(1)} %copy-done.10, f32[256,768]{1,0:T(8,128)S(1)} %get-tuple-element.145.passed, f32[4,768]{1,0:T(4,128)S(1)} %get-tuple-element.136.norms, ...), custom_call_target="tpu_custom_call" | custom-call | flops 12079595520 | bytes 14155776 | tf_op jit(solution)/shard_map/mlp_forward/pallas_call | solution.py:256
  194.9 8.0 %attn_forward.3 = (bf16[2,256,1152]{2,1,0:T(8,128)(2,1)S(1)}, f32[2,6,256]{2,1,0:T(8,128)S(1)}, bf16[256,768]{1,0:T(8,128)(2,1)S(1)}, f32[256,768]{1,0:T(8,128)S(1)}) custom-call(s32[1]{0:T(128)} %bitcast.side, bf16[256,768]{1,0:T(8,128)(2,1)S(1)} %get-tuple-element.148.rows, f32[3,256,128]{2,1,0:T(8,128)S(1)} %pad_maximum_fusion.1.tables, ...), custom_call_target="tpu_custom_call" | custom-call | flops 9059696640 | bytes 4718592 | tf_op jit(solution)/shard_map/attn_forward/pallas_call | solution.py:153
  202.9 8.8 %mlp_forward.3 = (bf16[256,3072]{1,0:T(8,128)(2,1)S(1)}, f32[256,3072]{1,0:T(8,128)}, f32[256,768]{1,0:T(8,128)S(1)}) custom-call(s32[1]{0:T(128)} %bitcast.side, bf16[256,768]{1,0:T(8,128)(2,1)S(1)} %get-tuple-element.148.rows, f32[256,768]{1,0:T(8,128)S(1)} %get-tuple-element.158.passed, f32[4,768]{1,0:T(4,128)S(1)} %copy-done.19, ...), custom_call_target="tpu_custom_call" | custom-call | flops 12079595520 | bytes 14155776 | tf_op jit(solution)/shard_map/mlp_forward/pallas_call | solution.py:256
  211.6 13.2 %mlp_backward.2 = (bf16[768,1536]{1,0:T(8,128)(2,1)S(1)}, bf16[768,1536]{1,0:T(8,128)(2,1)}, bf16[768,1536]{1,0:T(8,128)(2,1)}, bf16[768,1536]{1,0:T(8,128)(2,1)...) custom-call(s32[1]{0:T(128)} %bitcast.side, bf16[256,768]{1,0:T(8,128)(2,1)S(1)} %get-tuple-element.148.rows, ...), custom_call_target="tpu_custom_call" | custom-call | flops 19327352832 | bytes 23592960 | tf_op jit(solution)/shard_map/mlp_backward/pallas_call | solution.py:354
  225.5 12.3 %attn_backward.2 = (bf16[768,1536]{1,0:T(8,128)(2,1)}, bf16[768,1536]{1,0:T(8,128)(2,1)}, f32[2,1152]{1,0:T(2,128)S(1)}, f32[5,768]{1,0:T(8,128)S(1)}, bf16[256,768]{1,0:T(8,128)(2,1)S(1)}) custom-call(s32[1]{0:T(128)} %bitcast.side, bf16[256,768]{1,0:T(8,128)(2,1)S(1)} %get-tuple-element.148.rows, bf16[256,768]{1,0:T(8,128)(2,1)S(1)} %copy-done.11, ...), custom_call_target="tpu_custom_call" | custom-call | flops 14495514624 | bytes 9437184 | tf_op jit(solution)/shard_map/attn_backward/pallas_call | solution.py:475
  242.3 13.3 %mlp_backward.3 = (bf16[768,1536]{1,0:T(8,128)(2,1)S(1)}, bf16[768,1536]{1,0:T(8,128)(2,1)}, bf16[768,1536]{1,0:T(8,128)(2,1)}, bf16[768,1536]{1,0:T(8,128)(2,1)...) custom-call(s32[1]{0:T(128)} %bitcast.side, bf16[256,768]{1,0:T(8,128)(2,1)S(1)} %copy-done.10, ...), custom_call_target="tpu_custom_call" | custom-call | flops 19327352832 | bytes 23592960 | tf_op jit(solution)/shard_map/mlp_backward/pallas_call | solution.py:354
  257.1 13.4 %attn_backward.3 = (bf16[768,1536]{1,0:T(8,128)(2,1)}, bf16[768,1536]{1,0:T(8,128)(2,1)}, f32[2,1152]{1,0:T(2,128)S(1)}, f32[5,768]{1,0:T(8,128)S(1)}, f32[256,768]{1,0:T(8,128)S(1)}) custom-call(s32[1]{0:T(128)} %bitcast.side, bf16[256,768]{1,0:T(8,128)(2,1)S(1)} %copy-done.10, bf16[256,768]{1,0:T(8,128)(2,1)S(1)} %get-tuple-element.175.grad, ...), custom_call_target="tpu_custom_call" | custom-call | flops 14495514624 | bytes 9437184 | tf_op jit(solution)/shard_map/attn_backward/pallas_call | solution.py:475
  272.5 9.1 %collective-permute-start.51 = (bf16[4,48,1536]{2,1,0:T(8,128)(2,1)S(1)}, bf16[4,48,1536]{2,1,0:T(8,128)(2,1)S(1)}, u32[]{:S(2)}, u32[]{:S(2)}) collective-permute-start(bf16[4,48,1536]{2,1,0:T(8,128)(2,1)S(1)} %fusion.2), channel_id=1, source_target_pairs={{0,4},{1,5},{2,6},{3,7},{4,8},{5,9},{6,10},{7,11},{8,12},{9,13},{1... | collective-permute-start | bytes 1769480 | tf_op jit(solution)/shard_map/ppermute | solution.py:524
  282.6 3.2 near_blocks.3
  286.2 10.0 %collective-permute-done.51 = bf16[4,48,1536]{2,1,0:T(8,128)(2,1)S(1)} collective-permute-done((bf16[4,48,1536]{2,1,0:T(8,128)(2,1)S(1)}, bf16[4,48,1536]{2,1,0:T(8,128)(2,1)S(1)}, u32[]{:S(2)}, u32[]{:S(2)}) %collective-permute-start.51) | collective-permute-done | bytes 589856 | tf_op jit(solution)/shard_map/ppermute | solution.py:524
  297.5 15.9 %collective-permute-done.35.refs_4_ = bf16[4,48,3072]{2,1,0:T(8,128)(2,1)S(1)} collective-permute-done((bf16[4,48,3072]{2,1,0:T(8,128)(2,1)S(1)}, bf16[4,48,3072]{2,1,0:T(8,128)(2,1)S(1)}, u32[]{:S(2)}, u32[]{:S(2)}) %collective-permute-start.35) | collective-permute-done | bytes 1179680 | tf_op jit(solution)/shard_map/ppermute | solution.py:518
  316.5 6.0 %collective-permute-done.36.refs_5_ = bf16[4,48,3072]{2,1,0:T(8,128)(2,1)S(1)} collective-permute-done((bf16[4,48,3072]{2,1,0:T(8,128)(2,1)S(1)}, bf16[4,48,3072]{2,1,0:T(8,128)(2,1)S(1)}, u32[]{:S(2)}, u32[]{:S(2)}) %collective-permute-start.36) | collective-permute-done | bytes 1179680 | tf_op jit(solution)/shard_map/ppermute | solution.py:518
  330.4 8.2 %collective-permute-done.52 = bf16[4,48,1536]{2,1,0:T(8,128)(2,1)} collective-permute-done((bf16[4,48,1536]{2,1,0:T(8,128)(2,1)}, bf16[4,48,1536]{2,1,0:T(8,128)(2,1)}, u32[]{:S(2)}, u32[]{:S(2)}) %collective-permute-start.52) | collective-permute-done | bytes 589856 | tf_op jit(solution)/shard_map/ppermute | solution.py:524
  344.2 3.7 collective-permute-start.31
  348.8 3.9 near_blocks.4
  356.9 8.1 %collective-permute-done.53 = bf16[4,48,1536]{2,1,0:T(8,128)(2,1)} collective-permute-done((bf16[4,48,1536]{2,1,0:T(8,128)(2,1)}, bf16[4,48,1536]{2,1,0:T(8,128)(2,1)}, u32[]{:S(2)}, u32[]{:S(2)}) %collective-permute-start.53) | collective-permute-done | bytes 589856 | tf_op jit(solution)/shard_map/ppermute | solution.py:524
  367.6 3.3 column_blocks.5
  372.4 7.3 %collective-permute-done.43.refs_4_ = bf16[4,48,3072]{2,1,0:T(8,128)(2,1)S(1)} collective-permute-done((bf16[4,48,3072]{2,1,0:T(8,128)(2,1)S(1)}, bf16[4,48,3072]{2,1,0:T(8,128)(2,1)S(1)}, u32[]{:S(2)}, u32[]{:S(2)}) %collective-permute-start.43) | collective-permute-done | bytes 1179680 | tf_op jit(solution)/shard_map/ppermute | solution.py:518
  386.1 3.1 near_blocks.5
  419.6 7.6 %collective-permute-done.66 = bf16[48,3072]{1,0:T(8,128)(2,1)S(1)} collective-permute-done((bf16[48,3072]{1,0:T(8,128)(2,1)}, bf16[48,3072]{1,0:T(8,128)(2,1)S(1)}, u32[]{:S(2)}, u32[]{:S(2)}) %collective-permute-start.66) | collective-permute-done | bytes 294944 | tf_op jit(solution)/shard_map/ppermute | solution.py:524
  427.2 8.2 %collective-permute-start.47 = (bf16[48,1536]{1,0:T(8,128)(2,1)S(1)}, bf16[48,1536]{1,0:T(8,128)(2,1)S(1)}, u32[]{:S(2)}, u32[]{:S(2)}) collective-permute-start(bf16[48,1536]{1,0:T(8,128)(2,1)S(1)} %get-tuple-element.217), channel_id=1, source_target_pairs={{0,4},{1,5},{2,6},{3,7},{4,8},{5,9},{6,10},{7,11},{8,12},{9,13},{1... | collective-permute-start | bytes 442376 | tf_op jit(solution)/shard_map/ppermute | solution.py:524
  437.0 4.1 collective-permute-start.71
  442.8 5.4 %collective-permute-start.57 = (f32[48,1536]{1,0:T(8,128)S(1)}, f32[48,1536]{1,0:T(8,128)S(1)}, u32[]{:S(2)}, u32[]{:S(2)}) collective-permute-start(f32[48,1536]{1,0:T(8,128)S(1)} %get-tuple-element.246), channel_id=1, source_target_pairs={{0,16},{16,0},{1,17},{17,1},{2,18},{18,2},{3,19},{19,3},{4,20},{20... | collective-permute-start | bytes 884744 | tf_op jit(solution)/shard_map/ppermute | solution.py:513
  (363 shorter events, 152.7 us)
Async XLA Ops:
  7.2 145.1 %all-gather.2.cloned.1.call-start = ((), (), s32[]{:S(2)}) async-start(), calls=%async_computation | async-start | bytes 5013504 | tf_op jit(solution)/shard_map/all_gather | solution.py:627
  16.8 38.0 %collective-permute-start.4 = (bf16[48,4608]{1,0:T(8,128)(2,1)S(1)}, bf16[48,4608]{1,0:T(8,128)(2,1)S(1)}, u32[]{:S(2)}, u32[]{:S(2)}) collective-permute-start(bf16[48,4608]{1,0:T(8,128)(2,1)S(1)} %pad_maximum_fusion.refs_0_), channel_id=1, source_target_pairs={{0,8},{1,9},{2,10},{3,11},{4,12},{5,13},{6,14},{7,15},{8,0},{9,1},... | collective-permute-start | bytes 1327112 | tf_op jit(solution)/shard_map/ppermute | solution.py:524
  19.1 35.7 %collective-permute-start.5 = (bf16[48,4608]{1,0:T(8,128)(2,1)S(1)}, bf16[48,4608]{1,0:T(8,128)(2,1)S(1)}, u32[]{:S(2)}, u32[]{:S(2)}) collective-permute-start(bf16[48,4608]{1,0:T(8,128)(2,1)S(1)} %pad_maximum_fusion.refs_0_), channel_id=1, source_target_pairs={{0,12},{1,13},{2,14},{3,15},{4,0},{5,1},{6,2},{7,3},{8,4},{9,5},{1... | collective-permute-start | bytes 1327112 | tf_op jit(solution)/shard_map/ppermute | solution.py:524
  56.4 55.3 %collective-permute-start.8 = (bf16[4,48,4608]{2,1,0:T(8,128)(2,1)S(1)}, bf16[4,48,4608]{2,1,0:T(8,128)(2,1)S(1)}, u32[]{:S(2)}, u32[]{:S(2)}) collective-permute-start(bf16[4,48,4608]{2,1,0:T(8,128)(2,1)S(1)} %place_line.4.refs_0_), channel_id=1, source_target_pairs={{0,1},{1,0},{2,3},{3,2},{4,5},{5,4},{6,7},{7,6},{8,9},{9,8},{10,11... | collective-permute-start | bytes 5308424 | tf_op jit(solution)/shard_map/ppermute | solution.py:518
  57.7 55.0 %collective-permute-start.9 = (bf16[4,48,4608]{2,1,0:T(8,128)(2,1)S(1)}, bf16[4,48,4608]{2,1,0:T(8,128)(2,1)}, u32[]{:S(2)}, u32[]{:S(2)}) collective-permute-start(bf16[4,48,4608]{2,1,0:T(8,128)(2,1)S(1)} %place_line.4.refs_0_), channel_id=1, source_target_pairs={{0,2},{1,3},{2,0},{3,1},{4,6},{5,7},{6,4},{7,5},{8,10},{9,11},{10,... | collective-permute-start | bytes 5308424 | tf_op jit(solution)/shard_map/ppermute | solution.py:518
  73.0 17.4 %collective-permute-start.11 = (bf16[48,1536]{1,0:T(8,128)(2,1)}, bf16[48,1536]{1,0:T(8,128)(2,1)}, u32[]{:S(2)}, u32[]{:S(2)}) collective-permute-start(bf16[48,1536]{1,0:T(8,128)(2,1)} %get-tuple-element.126.refs_0_), channel_id=1, source_target_pairs={{0,8},{1,9},{2,10},{3,11},{4,12},{5,13},{6,14},{7,15},{8,0},{9,1},... | collective-permute-start | bytes 442376 | tf_op jit(solution)/shard_map/ppermute | solution.py:524
  120.8 29.4 %collective-permute-start.18 = (bf16[2,48,4608]{2,1,0:T(8,128)(2,1)}, bf16[2,48,4608]{2,1,0:T(8,128)(2,1)}, u32[]{:S(2)}, u32[]{:S(2)}) collective-permute-start(bf16[2,48,4608]{2,1,0:T(8,128)(2,1)} %slice.221), channel_id=1, source_target_pairs={{0,2},{1,3},{2,0},{3,1},{4,6},{5,7},{6,4},{7,5},{8,10},{9,11},{10,... | collective-permute-start | bytes 2654216 | tf_op jit(solution)/shard_map/ppermute | solution.py:518
  121.2 31.1 %collective-permute-start.19 = (bf16[2,48,4608]{2,1,0:T(8,128)(2,1)}, bf16[2,48,4608]{2,1,0:T(8,128)(2,1)}, u32[]{:S(2)}, u32[]{:S(2)}) collective-permute-start(bf16[2,48,4608]{2,1,0:T(8,128)(2,1)} %slice.222), channel_id=1, source_target_pairs={{0,1},{1,0},{2,3},{3,2},{4,5},{5,4},{6,7},{7,6},{8,9},{9,8},{10,11... | collective-permute-start | bytes 2654216 | tf_op jit(solution)/shard_map/ppermute | solution.py:518
  157.4 27.7 %collective-permute-start.24 = (bf16[768,3072]{1,0:T(8,128)(2,1)}, bf16[768,3072]{1,0:T(8,128)(2,1)}, u32[]{:S(2)}, u32[]{:S(2)}) collective-permute-start(bf16[768,3072]{1,0:T(8,128)(2,1)} %bitcast.184), channel_id=1, source_target_pairs={{0,16},{16,0},{1,17},{17,1},{2,18},{18,2},{3,19},{19,3},{4,20},{20... | collective-permute-start | bytes 14155784 | tf_op jit(solution)/shard_map/ppermute | solution.py:513
  160.6 42.3 %collective-permute-start.28 = (bf16[768,3072]{1,0:T(8,128)(2,1)}, bf16[768,3072]{1,0:T(8,128)(2,1)}, u32[]{:S(2)}, u32[]{:S(2)}) collective-permute-start(bf16[768,3072]{1,0:T(8,128)(2,1)} %all-gather.2.cloned.1.call-done.up_mine.down_mine), channel_id=1, source_target_pairs={{0,16},{16,0},{1,17},{17,1},{2,18},{18,2},{3,19},{19,3},{4,20},{20... | collective-permute-start | bytes 14155784 | tf_op jit(solution)/shard_map/ppermute | solution.py:513
  173.2 21.6 %collective-permute-start.27 = (bf16[768,1536]{1,0:T(8,128)(2,1)S(1)}, bf16[768,1536]{1,0:T(8,128)(2,1)}, u32[]{:S(2)}, u32[]{:S(2)}) collective-permute-start(bf16[768,1536]{1,0:T(8,128)(2,1)S(1)} %bitcast.153), channel_id=1, source_target_pairs={{0,16},{16,0},{1,17},{17,1},{2,18},{18,2},{3,19},{19,3},{4,20},{20... | collective-permute-start | bytes 7077896 | tf_op jit(solution)/shard_map/ppermute | solution.py:513
  237.9 33.2 %collective-permute-start.50 = (bf16[768,1536]{1,0:T(8,128)(2,1)}, bf16[768,1536]{1,0:T(8,128)(2,1)}, u32[]{:S(2)}, u32[]{:S(2)}) collective-permute-start(bf16[768,1536]{1,0:T(8,128)(2,1)} %get-tuple-element.221), channel_id=1, source_target_pairs={{0,16},{16,0},{1,17},{17,1},{2,18},{18,2},{3,19},{19,3},{4,20},{20... | collective-permute-start | bytes 7077896 | tf_op jit(solution)/shard_map/ppermute | solution.py:513
  240.8 40.9 %collective-permute-start.33 = (bf16[2,48,3072]{2,1,0:T(8,128)(2,1)S(1)}, bf16[2,48,3072]{2,1,0:T(8,128)(2,1)S(1)}, u32[]{:S(2)}, u32[]{:S(2)}) collective-permute-start(bf16[2,48,3072]{2,1,0:T(8,128)(2,1)S(1)} %get-tuple-element.173), channel_id=1, source_target_pairs={{0,1},{1,0},{2,3},{3,2},{4,5},{5,4},{6,7},{7,6},{8,9},{9,8},{10,11... | collective-permute-start | bytes 1769480 | tf_op jit(solution)/shard_map/ppermute | solution.py:518
  242.1 40.5 %collective-permute-start.34 = (bf16[2,48,3072]{2,1,0:T(8,128)(2,1)S(1)}, bf16[2,48,3072]{2,1,0:T(8,128)(2,1)S(1)}, u32[]{:S(2)}, u32[]{:S(2)}) collective-permute-start(bf16[2,48,3072]{2,1,0:T(8,128)(2,1)S(1)} %get-tuple-element.174), channel_id=1, source_target_pairs={{0,2},{1,3},{2,0},{3,1},{4,6},{5,7},{6,4},{7,5},{8,10},{9,11},{10,... | collective-permute-start | bytes 1769480 | tf_op jit(solution)/shard_map/ppermute | solution.py:518
  270.5 53.1 %collective-permute-start.32 = (bf16[768,1536]{1,0:T(8,128)(2,1)}, bf16[768,1536]{1,0:T(8,128)(2,1)S(1)}, u32[]{:S(2)}, u32[]{:S(2)}) collective-permute-start(bf16[768,1536]{1,0:T(8,128)(2,1)} %get-tuple-element.185), channel_id=1, source_target_pairs={{0,16},{16,0},{1,17},{17,1},{2,18},{18,2},{3,19},{19,3},{4,20},{20... | collective-permute-start | bytes 7077896 | tf_op jit(solution)/shard_map/ppermute | solution.py:513
  271.1 54.3 %collective-permute-start.39 = (bf16[768,1536]{1,0:T(8,128)(2,1)}, bf16[768,1536]{1,0:T(8,128)(2,1)}, u32[]{:S(2)}, u32[]{:S(2)}) collective-permute-start(bf16[768,1536]{1,0:T(8,128)(2,1)} %get-tuple-element.196), channel_id=1, source_target_pairs={{0,16},{16,0},{1,17},{17,1},{2,18},{18,2},{3,19},{19,3},{4,20},{20... | collective-permute-start | bytes 7077896 | tf_op jit(solution)/shard_map/ppermute | solution.py:513
  272.5 23.7 %collective-permute-start.51 = (bf16[4,48,1536]{2,1,0:T(8,128)(2,1)S(1)}, bf16[4,48,1536]{2,1,0:T(8,128)(2,1)S(1)}, u32[]{:S(2)}, u32[]{:S(2)}) collective-permute-start(bf16[4,48,1536]{2,1,0:T(8,128)(2,1)S(1)} %fusion.2), channel_id=1, source_target_pairs={{0,4},{1,5},{2,6},{3,7},{4,8},{5,9},{6,10},{7,11},{8,12},{9,13},{1... | collective-permute-start | bytes 1769480 | tf_op jit(solution)/shard_map/ppermute | solution.py:524
  281.7 44.8 %collective-permute-start.40 = (bf16[768,1536]{1,0:T(8,128)(2,1)}, bf16[768,1536]{1,0:T(8,128)(2,1)}, u32[]{:S(2)}, u32[]{:S(2)}) collective-permute-start(bf16[768,1536]{1,0:T(8,128)(2,1)} %get-tuple-element.198), channel_id=1, source_target_pairs={{0,16},{16,0},{1,17},{17,1},{2,18},{18,2},{3,19},{19,3},{4,20},{20... | collective-permute-start | bytes 7077896 | tf_op jit(solution)/shard_map/ppermute | solution.py:513
  285.8 27.6 %collective-permute-start.35 = (bf16[4,48,3072]{2,1,0:T(8,128)(2,1)S(1)}, bf16[4,48,3072]{2,1,0:T(8,128)(2,1)S(1)}, u32[]{:S(2)}, u32[]{:S(2)}) collective-permute-start(bf16[4,48,3072]{2,1,0:T(8,128)(2,1)S(1)} %get-tuple-element.189), channel_id=1, source_target_pairs={{0,1},{1,0},{2,3},{3,2},{4,5},{5,4},{6,7},{7,6},{8,9},{9,8},{10,11... | collective-permute-start | bytes 3538952 | tf_op jit(solution)/shard_map/ppermute | solution.py:518
  296.2 26.4 %collective-permute-start.36 = (bf16[4,48,3072]{2,1,0:T(8,128)(2,1)S(1)}, bf16[4,48,3072]{2,1,0:T(8,128)(2,1)S(1)}, u32[]{:S(2)}, u32[]{:S(2)}) collective-permute-start(bf16[4,48,3072]{2,1,0:T(8,128)(2,1)S(1)} %get-tuple-element.190), channel_id=1, source_target_pairs={{0,2},{1,3},{2,0},{3,1},{4,6},{5,7},{6,4},{7,5},{8,10},{9,11},{10,... | collective-permute-start | bytes 3538952 | tf_op jit(solution)/shard_map/ppermute | solution.py:518
  330.1 17.9 %collective-permute-start.42 = (bf16[2,48,3072]{2,1,0:T(8,128)(2,1)S(1)}, bf16[2,48,3072]{2,1,0:T(8,128)(2,1)S(1)}, u32[]{:S(2)}, u32[]{:S(2)}) collective-permute-start(bf16[2,48,3072]{2,1,0:T(8,128)(2,1)S(1)} %get-tuple-element.205), channel_id=1, source_target_pairs={{0,2},{1,3},{2,0},{3,1},{4,6},{5,7},{6,4},{7,5},{8,10},{9,11},{10,... | collective-permute-start | bytes 1769480 | tf_op jit(solution)/shard_map/ppermute | solution.py:518
  348.0 17.0 %collective-permute-start.53 = (bf16[4,48,1536]{2,1,0:T(8,128)(2,1)}, bf16[4,48,1536]{2,1,0:T(8,128)(2,1)}, u32[]{:S(2)}, u32[]{:S(2)}) collective-permute-start(bf16[4,48,1536]{2,1,0:T(8,128)(2,1)} %fusion), channel_id=1, source_target_pairs={{0,4},{1,5},{2,6},{3,7},{4,8},{5,9},{6,10},{7,11},{8,12},{9,13},{1... | collective-permute-start | bytes 1769480 | tf_op jit(solution)/shard_map/ppermute | solution.py:524
  352.7 27.0 %collective-permute-start.43 = (bf16[4,48,3072]{2,1,0:T(8,128)(2,1)S(1)}, bf16[4,48,3072]{2,1,0:T(8,128)(2,1)S(1)}, u32[]{:S(2)}, u32[]{:S(2)}) collective-permute-start(bf16[4,48,3072]{2,1,0:T(8,128)(2,1)S(1)} %get-tuple-element.208), channel_id=1, source_target_pairs={{0,1},{1,0},{2,3},{3,2},{4,5},{5,4},{6,7},{7,6},{8,9},{9,8},{10,11... | collective-permute-start | bytes 3538952 | tf_op jit(solution)/shard_map/ppermute | solution.py:518
  353.0 26.7 %collective-permute-start.44 = (bf16[4,48,3072]{2,1,0:T(8,128)(2,1)}, bf16[4,48,3072]{2,1,0:T(8,128)(2,1)S(1)}, u32[]{:S(2)}, u32[]{:S(2)}) collective-permute-start(bf16[4,48,3072]{2,1,0:T(8,128)(2,1)} %get-tuple-element.209), channel_id=1, source_target_pairs={{0,2},{1,3},{2,0},{3,1},{4,6},{5,7},{6,4},{7,5},{8,10},{9,11},{10,... | collective-permute-start | bytes 3538952 | tf_op jit(solution)/shard_map/ppermute | solution.py:518
  370.9 32.1 %collective-permute-start.70 = (bf16[48,3072]{1,0:T(8,128)(2,1)}, bf16[48,3072]{1,0:T(8,128)(2,1)}, u32[]{:S(2)}, u32[]{:S(2)}) collective-permute-start(bf16[48,3072]{1,0:T(8,128)(2,1)} %get-tuple-element.237), channel_id=1, source_target_pairs={{0,12},{1,13},{2,14},{3,15},{4,0},{5,1},{6,2},{7,3},{8,4},{9,5},{1... | collective-permute-start | bytes 884744 | tf_op jit(solution)/shard_map/ppermute | solution.py:524
  372.4 32.9 %collective-permute-start.69 = (bf16[48,3072]{1,0:T(8,128)(2,1)}, bf16[48,3072]{1,0:T(8,128)(2,1)}, u32[]{:S(2)}, u32[]{:S(2)}) collective-permute-start(bf16[48,3072]{1,0:T(8,128)(2,1)} %get-tuple-element.236), channel_id=1, source_target_pairs={{0,8},{1,9},{2,10},{3,11},{4,12},{5,13},{6,14},{7,15},{8,0},{9,1},... | collective-permute-start | bytes 884744 | tf_op jit(solution)/shard_map/ppermute | solution.py:524
  394.0 21.5 %collective-permute-start.68 = (bf16[48,3072]{1,0:T(8,128)(2,1)}, bf16[48,3072]{1,0:T(8,128)(2,1)}, u32[]{:S(2)}, u32[]{:S(2)}) collective-permute-start(bf16[48,3072]{1,0:T(8,128)(2,1)} %get-tuple-element.235), channel_id=1, source_target_pairs={{0,4},{1,5},{2,6},{3,7},{4,8},{5,9},{6,10},{7,11},{8,12},{9,13},{1... | collective-permute-start | bytes 884744 | tf_op jit(solution)/shard_map/ppermute | solution.py:524
  405.2 22.0 %collective-permute-start.66 = (bf16[48,3072]{1,0:T(8,128)(2,1)}, bf16[48,3072]{1,0:T(8,128)(2,1)S(1)}, u32[]{:S(2)}, u32[]{:S(2)}) collective-permute-start(bf16[48,3072]{1,0:T(8,128)(2,1)} %copy-done.34), channel_id=1, source_target_pairs={{0,8},{1,9},{2,10},{3,11},{4,12},{5,13},{6,14},{7,15},{8,0},{9,1},... | collective-permute-start | bytes 884744 | tf_op jit(solution)/shard_map/ppermute | solution.py:524
  407.2 20.0 %collective-permute-start.65 = (bf16[48,3072]{1,0:T(8,128)(2,1)}, bf16[48,3072]{1,0:T(8,128)(2,1)S(1)}, u32[]{:S(2)}, u32[]{:S(2)}) collective-permute-start(bf16[48,3072]{1,0:T(8,128)(2,1)} %copy-done.33), channel_id=1, source_target_pairs={{0,4},{1,5},{2,6},{3,7},{4,8},{5,9},{6,10},{7,11},{8,12},{9,13},{1... | collective-permute-start | bytes 884744 | tf_op jit(solution)/shard_map/ppermute | solution.py:524
  415.5 21.5 %collective-permute-start.55 = (bf16[48,1536]{1,0:T(8,128)(2,1)S(1)}, bf16[48,1536]{1,0:T(8,128)(2,1)S(1)}, u32[]{:S(2)}, u32[]{:S(2)}) collective-permute-start(bf16[48,1536]{1,0:T(8,128)(2,1)S(1)} %copy-done.45), channel_id=1, source_target_pairs={{0,2},{1,3},{2,0},{3,1},{4,6},{5,7},{6,4},{7,5},{8,10},{9,11},{10,... | collective-permute-start | bytes 442376 | tf_op jit(solution)/shard_map/ppermute | solution.py:518
  416.6 25.0 %collective-permute-start.54 = (bf16[48,1536]{1,0:T(8,128)(2,1)S(1)}, bf16[48,1536]{1,0:T(8,128)(2,1)S(1)}, u32[]{:S(2)}, u32[]{:S(2)}) collective-permute-start(bf16[48,1536]{1,0:T(8,128)(2,1)S(1)} %copy-done.44), channel_id=1, source_target_pairs={{0,1},{1,0},{2,3},{3,2},{4,5},{5,4},{6,7},{7,6},{8,9},{9,8},{10,11... | collective-permute-start | bytes 442376 | tf_op jit(solution)/shard_map/ppermute | solution.py:518
  416.7 25.0 %collective-permute-start.49 = (bf16[48,1536]{1,0:T(8,128)(2,1)S(1)}, bf16[48,1536]{1,0:T(8,128)(2,1)S(1)}, u32[]{:S(2)}, u32[]{:S(2)}) collective-permute-start(bf16[48,1536]{1,0:T(8,128)(2,1)S(1)} %get-tuple-element.219), channel_id=1, source_target_pairs={{0,12},{1,13},{2,14},{3,15},{4,0},{5,1},{6,2},{7,3},{8,4},{9,5},{1... | collective-permute-start | bytes 442376 | tf_op jit(solution)/shard_map/ppermute | solution.py:524
  (95 other events, 761.6 us)
Sparse Core Ops, SparseCore 0:
  11.9 126.2 all-gather.1
